TPU v7x, 32 devices: a whole 2x2x4 slice. The times are simulated.
32 devices in a mesh: wide: 8 (over z, y), narrow: 4 (over x, core).
Axes of the slice: x: 2, y: 2, z: 4, core: 2. Of those that a mesh axis runs over, the one named last changes fastest.
Arguments:
- clean_mel: float32 [16384, 80], P(('wide', 'narrow')), may hold values from -6 to 6
- gauss_noise: float32 [16384, 80], P(('wide', 'narrow')), may hold values from -6 to 6
- flow_time: float32 [32], P(('wide', 'narrow')), may hold values from 0 to 1
- phone_ids: int32 [16384], P(('wide', 'narrow')), may hold values from 0 to 127
- lengths: int32 [32], P(('wide', 'narrow')), may hold values from 32 to 512, as said below
- span_start: int32 [32], P(('wide', 'narrow')), may hold values from 0 to 154, as said below
- span_end: int32 [32], P(('wide', 'narrow')), may hold values from 1 to 512, as said below
- speaker: int32 [32], P(('wide', 'narrow')), may hold values from 0 to 15, as said below
- skip_states: bfloat16 [16384, 1024], P(('wide', 'narrow')), may hold values from -6 to 6
- w_input: float32 [672, 1024], P(None, ('wide', 'narrow')), may hold values from -0.25 to 0.25
- phone_table: float32 [128, 512], P(None, ('wide', 'narrow')), may hold values from -5 to 5
- w_skip: float32 [2048, 1024], P(('wide', 'narrow')), may hold values from -0.125 to 0.125
- w_attend: float32 [1024, 3072], P(('wide', 'narrow')), may hold values from -0.1875 to 0.1875
- w_output: float32 [1024, 1024], P(('wide', 'narrow')), may hold values from -0.375 to 0.375
- w_expand: float32 [1024, 4096], P(('wide', 'narrow')), may hold values from -0.1875 to 0.1875
- w_reduce: float32 [4096, 1024], P(('wide', 'narrow')), may hold values from -0.09375 to 0.09375
- w_head: float32 [1024, 80], P(('wide', 'narrow')), may hold values from -0.1875 to 0.1875
- norm_gains: float32 [3, 1024], P(None, ('wide', 'narrow'))
- moment_input: float32 [672, 1024], P(None, ('wide', 'narrow')), may hold values from -0.0014648438 to 0.0014648438
- moment_table: float32 [128, 512], P(None, ('wide', 'narrow')), may hold values from -6.1035156e-05 to 6.1035156e-05
- moment_skip: float32 [2048, 1024], P(('wide', 'narrow')), may hold values from -0.0014648438 to 0.0014648438
- moment_attend: float32 [1024, 3072], P(('wide', 'narrow')), may hold values from -0.0014648438 to 0.0014648438
- moment_output: float32 [1024, 1024], P(('wide', 'narrow')), may hold values from -0.0014648438 to 0.0014648438
- moment_expand: float32 [1024, 4096], P(('wide', 'narrow')), may hold values from -0.0014648438 to 0.0014648438
- moment_reduce: float32 [4096, 1024], P(('wide', 'narrow')), may hold values from -0.0014648438 to 0.0014648438
- moment_head: float32 [1024, 80], P(('wide', 'narrow')), may hold values from -0.0014648438 to 0.0014648438
- moment_gains: float32 [3, 1024], P(None, ('wide', 'narrow')), may hold values from -0.005859375 to 0.005859375
- square_input: float32 [672, 1024], P(None, ('wide', 'narrow')), may hold values from 6.4438304e-08 to 2.5775321e-07
- square_table: float32 [128, 512], P(None, ('wide', 'narrow')), may hold values from 9.205472e-11 to 3.758901e-10
- square_skip: float32 [2048, 1024], P(('wide', 'narrow')), may hold values from 6.4438304e-08 to 2.5775321e-07
- square_attend: float32 [1024, 3072], P(('wide', 'narrow')), may hold values from 6.4438304e-08 to 2.5775321e-07
- square_output: float32 [1024, 1024], P(('wide', 'narrow')), may hold values from 6.4438304e-08 to 2.5775321e-07
- square_expand: float32 [1024, 4096], P(('wide', 'narrow')), may hold values from 6.4438304e-08 to 2.5775321e-07
- square_reduce: float32 [4096, 1024], P(('wide', 'narrow')), may hold values from 6.4438304e-08 to 2.5775321e-07
- square_head: float32 [1024, 80], P(('wide', 'narrow')), may hold values from 6.4438304e-08 to 2.5775321e-07
- square_gains: float32 [3, 1024], P(None, ('wide', 'narrow')), may hold values from 1.0310129e-06 to 4.1240514e-06
Outputs:
- loss_value: float32 [], replicated
- grad_norm: float32 [], replicated
- next_w_input: float32 [672, 1024], P(None, ('wide', 'narrow'))
- next_phone_table: float32 [128, 512], P(None, ('wide', 'narrow'))
- next_w_skip: float32 [2048, 1024], P(('wide', 'narrow'))
- next_w_attend: float32 [1024, 3072], P(('wide', 'narrow'))
- next_w_output: float32 [1024, 1024], P(('wide', 'narrow'))
- next_w_expand: float32 [1024, 4096], P(('wide', 'narrow'))
- next_w_reduce: float32 [4096, 1024], P(('wide', 'narrow'))
- next_w_head: float32 [1024, 80], P(('wide', 'narrow'))
- next_norm_gains: float32 [3, 1024], P(None, ('wide', 'narrow'))
- next_moment_input: float32 [672, 1024], P(None, ('wide', 'narrow'))
- next_moment_table: float32 [128, 512], P(None, ('wide', 'narrow'))
- next_moment_skip: float32 [2048, 1024], P(('wide', 'narrow'))
- next_moment_attend: float32 [1024, 3072], P(('wide', 'narrow'))
- next_moment_output: float32 [1024, 1024], P(('wide', 'narrow'))
- next_moment_expand: float32 [1024, 4096], P(('wide', 'narrow'))
- next_moment_reduce: float32 [4096, 1024], P(('wide', 'narrow'))
- next_moment_head: float32 [1024, 80], P(('wide', 'narrow'))
- next_moment_gains: float32 [3, 1024], P(None, ('wide', 'narrow'))
- next_square_input: float32 [672, 1024], P(None, ('wide', 'narrow'))
- next_square_table: float32 [128, 512], P(None, ('wide', 'narrow'))
- next_square_skip: float32 [2048, 1024], P(('wide', 'narrow'))
- next_square_attend: float32 [1024, 3072], P(('wide', 'narrow'))
- next_square_output: float32 [1024, 1024], P(('wide', 'narrow'))
- next_square_expand: float32 [1024, 4096], P(('wide', 'narrow'))
- next_square_reduce: float32 [4096, 1024], P(('wide', 'narrow'))
- next_square_head: float32 [1024, 80], P(('wide', 'narrow'))
- next_square_gains: float32 [3, 1024], P(None, ('wide', 'narrow'))
Inputs may be any that keep to these rules, and one draw needn't show every extreme that they name: `lengths`: utterance u's length; exactly one utterance has 512 frames. span_start < span_end <= lengths; a span covers 70 to 100 percent of its utterance (rounded down, at least one frame). `span_end`: the end of each span; one span ends at 512. Some speaker group has no utterance.
All inputs are finite; a program needn't handle non-finite values.
Results may differ from a plain program's by a relative error of at most 0.012.
The roundings to bfloat16 on the way count: a program that leaves them out, or rounds other values in their place, can miss the bound.
Values may be sent and summed in bfloat16 or wider, within the bound.
No kernel may reach another device: no remote copies, remote signals or barrier semaphores. Data moves between devices by JAX's collectives and lax.ppermute only.
A program may use at most 256 MiB of HBM per device.

v0:
```python
from functools import partial
import math

import jax
import jax.numpy as jnp
from jax import lax
from jax.sharding import PartitionSpec as P

HD = 64
SPK = 16
STEP = 10


SIGMA = 1e-05
NORM_EPS = 1e-05
LEARN_RATE = 0.01
GAIN_RATE = 0.3
BETA_ONE = 0.5
BETA_TWO = 0.5
DECAY = 0.01
ADAM_EPS = 1e-08
MASKED = -1000000000.0


def as_low(x):
    return x.astype(jnp.bfloat16)


def matmul(left, right):
    return jnp.dot(left, right, preferred_element_type=jnp.float32)


def contract_rows(left, right):
    return lax.dot_general(
        left, right, (((0,), (0,)), ((), ())), preferred_element_type=jnp.float32
    )


def contract_cols(left, right):
    return lax.dot_general(
        left, right, (((1,), (1,)), ((), ())), preferred_element_type=jnp.float32
    )


def time_features(flow, width):
    half = width // 2
    freqs = jnp.exp(-math.log(10000.0) * jnp.arange(half, dtype=jnp.float32) / half)
    angle = 1000.0 * flow * freqs
    return jnp.concatenate([jnp.sin(angle), jnp.cos(angle)])


def normalize(x):
    centered = x - jnp.mean(x, -1, keepdims=True)
    inverse = lax.rsqrt(jnp.mean(centered * centered, -1, keepdims=True) + NORM_EPS)
    return (centered * inverse, inverse)


def normalize_back(grad, normed, inverse):
    return inverse * (
        grad
        - jnp.mean(grad, -1, keepdims=True)
        - normed * jnp.mean(grad * normed, -1, keepdims=True)
    )


def head_slopes(heads):
    return 2.0 ** (-8.0 * (jnp.arange(heads, dtype=jnp.float32) + 1.0) / heads)


def attention_scores(query, keys, frame_valid):
    frames, heads = (query.shape[0], query.shape[1])
    position = jnp.arange(frames)
    dist = jnp.abs(position[:, None] - position[None, :]).astype(jnp.float32)
    scores = jnp.einsum("qhd,khd->hqk", query, keys, preferred_element_type=jnp.float32) * HD ** (
        -0.5
    )
    scores = scores - head_slopes(heads)[:, None, None] * dist[None]
    return jnp.where(frame_valid[None, None, :] > 0, scores, MASKED)


def adam_step(master, grad, moment, square, rate):
    moment = BETA_ONE * moment + (1.0 - BETA_ONE) * grad
    square = BETA_TWO * square + (1.0 - BETA_TWO) * grad * grad
    moment_hat = moment / (1.0 - BETA_ONE**STEP)
    square_hat = square / (1.0 - BETA_TWO**STEP)
    master = master - rate * (moment_hat / (jnp.sqrt(square_hat) + ADAM_EPS) + DECAY * master)
    return (master, moment, square)


def shards(
    clean_mel,
    gauss_noise,
    flow_time,
    phone_ids,
    lengths,
    span_start,
    span_end,
    speaker,
    skip_states,
    w_input,
    phone_table,
    w_skip,
    w_attend,
    w_output,
    w_expand,
    w_reduce,
    w_head,
    norm_gains,
    moment_input,
    moment_table,
    moment_skip,
    moment_attend,
    moment_output,
    moment_expand,
    moment_reduce,
    moment_head,
    moment_gains,
    square_input,
    square_table,
    square_skip,
    square_attend,
    square_output,
    square_expand,
    square_reduce,
    square_head,
    square_gains,
):
    masters = (
        w_input,
        phone_table,
        w_skip,
        w_attend,
        w_output,
        w_expand,
        w_reduce,
        w_head,
        norm_gains,
    )
    moments = (
        moment_input,
        moment_table,
        moment_skip,
        moment_attend,
        moment_output,
        moment_expand,
        moment_reduce,
        moment_head,
        moment_gains,
    )
    squares = (
        square_input,
        square_table,
        square_skip,
        square_attend,
        square_output,
        square_expand,
        square_reduce,
        square_head,
        square_gains,
    )
    rates = (
        LEARN_RATE,
        GAIN_RATE,
        LEARN_RATE,
        LEARN_RATE,
        LEARN_RATE,
        LEARN_RATE,
        LEARN_RATE,
        LEARN_RATE,
        GAIN_RATE,
    )
    frames = clean_mel.shape[0]
    mel_bins = clean_mel.shape[1]
    position = jnp.arange(frames)
    frame_valid = (position < lengths[0]).astype(jnp.float32)
    frame_inside = ((position >= span_start[0]) & (position < span_end[0])).astype(
        jnp.float32
    ) * frame_valid
    speaker_hot = (speaker[0] == jnp.arange(SPK)).astype(jnp.float32)
    local_count = speaker_hot * jnp.sum(frame_inside)
    gathered = (
        lax.all_gather(as_low(w_input), ("wide", "narrow"), axis=1, tiled=True),
        lax.all_gather(as_low(phone_table), ("wide", "narrow"), axis=1, tiled=True),
        lax.all_gather(as_low(w_skip), ("wide", "narrow"), axis=0, tiled=True),
        lax.all_gather(as_low(w_attend), ("wide", "narrow"), axis=0, tiled=True),
        lax.all_gather(as_low(w_output), ("wide", "narrow"), axis=0, tiled=True),
        lax.all_gather(as_low(w_expand), ("wide", "narrow"), axis=0, tiled=True),
        lax.all_gather(as_low(w_reduce), ("wide", "narrow"), axis=0, tiled=True),
        lax.all_gather(as_low(w_head), ("wide", "narrow"), axis=0, tiled=True),
        lax.all_gather(as_low(norm_gains), ("wide", "narrow"), axis=1, tiled=True),
    )
    (
        input_full,
        table_full,
        skip_full,
        attend_full,
        output_full,
        expand_full,
        reduce_full,
        head_full,
        gains_full,
    ) = gathered
    width = skip_full.shape[1]
    heads = width // HD
    gains_wide = gains_full.astype(jnp.float32)
    flow = flow_time[0]
    noisy_mel = (1.0 - (1.0 - SIGMA) * flow) * gauss_noise + flow * clean_mel
    context = clean_mel * (frame_valid - frame_inside)[:, None]
    target = clean_mel - (1.0 - SIGMA) * gauss_noise
    phone_hot = as_low(phone_ids[:, None] == jnp.arange(table_full.shape[0])[None, :])
    embedded = as_low(matmul(phone_hot, table_full))
    features = jnp.concatenate([as_low(noisy_mel), as_low(context), embedded], 1)
    start_state = matmul(features, input_full) + time_features(flow, width)[None, :]
    joined = jnp.concatenate([as_low(start_state), skip_states], 1)
    stream = matmul(joined, skip_full)
    normed_one, inverse_one = normalize(stream)
    attn_in = as_low(normed_one * gains_wide[0])
    packed = as_low(matmul(attn_in, attend_full))
    query = packed[:, :width].reshape(frames, heads, HD)
    keys = packed[:, width : 2 * width].reshape(frames, heads, HD)
    values = packed[:, 2 * width :].reshape(frames, heads, HD)
    scores = attention_scores(query, keys, frame_valid)
    top_score = jnp.max(scores, -1, keepdims=True)
    expo = jnp.exp(scores - top_score)
    exp_total = jnp.sum(expo, -1, keepdims=True)
    log_total = top_score + jnp.log(exp_total)
    attn_probs = as_low(expo / exp_total)
    mixed = as_low(
        jnp.einsum("hqk,khd->qhd", attn_probs, values, preferred_element_type=jnp.float32).reshape(
            frames, width
        )
    )
    stream_mid = stream + matmul(mixed, output_full)
    normed_two, inverse_two = normalize(stream_mid)
    ffn_in = as_low(normed_two * gains_wide[1])
    hidden = matmul(ffn_in, expand_full)
    activated = as_low(jax.nn.gelu(hidden, approximate=False))
    stream_out = stream_mid + matmul(activated, reduce_full)
    normed_three, inverse_three = normalize(stream_out)
    head_in = as_low(normed_three * gains_wide[2])
    prediction = matmul(head_in, head_full)
    error = prediction - target
    frame_error = jnp.sum(error * error, 1) * frame_inside
    local_sum = speaker_hot * jnp.sum(frame_error)
    sums, counts = lax.psum((local_sum, local_count), ("wide", "narrow"))
    regathered = (
        lax.all_gather(as_low(w_input), ("wide", "narrow"), axis=1, tiled=True),
        lax.all_gather(as_low(phone_table), ("wide", "narrow"), axis=1, tiled=True),
        lax.all_gather(as_low(w_skip), ("wide", "narrow"), axis=0, tiled=True),
        lax.all_gather(as_low(w_attend), ("wide", "narrow"), axis=0, tiled=True),
        lax.all_gather(as_low(w_output), ("wide", "narrow"), axis=0, tiled=True),
        lax.all_gather(as_low(w_expand), ("wide", "narrow"), axis=0, tiled=True),
        lax.all_gather(as_low(w_reduce), ("wide", "narrow"), axis=0, tiled=True),
        lax.all_gather(as_low(w_head), ("wide", "narrow"), axis=0, tiled=True),
        lax.all_gather(as_low(norm_gains), ("wide", "narrow"), axis=1, tiled=True),
    )
    (
        input_full,
        table_full,
        skip_full,
        attend_full,
        output_full,
        expand_full,
        reduce_full,
        head_full,
        gains_full,
    ) = regathered
    gains_wide = gains_full.astype(jnp.float32)
    share = jnp.sum(speaker_hot / jnp.maximum(counts, 1.0)) / SPK
    d_prediction = as_low(2.0 * share * error * frame_inside[:, None])
    grad_head = contract_rows(head_in, d_prediction)
    d_head_in = contract_cols(d_prediction, head_full)
    grad_gain_three = jnp.sum(d_head_in * normed_three, 0)
    d_stream_out = normalize_back(d_head_in * gains_wide[2], normed_three, inverse_three)
    d_branch = as_low(d_stream_out)
    grad_reduce = contract_rows(activated, d_branch)
    d_activated = contract_cols(d_branch, reduce_full)
    gelu_pull = jax.vjp(partial(jax.nn.gelu, approximate=False), hidden)[1]
    d_hidden = as_low(gelu_pull(d_activated)[0])
    grad_expand = contract_rows(ffn_in, d_hidden)
    d_ffn_in = contract_cols(d_hidden, expand_full)
    grad_gain_two = jnp.sum(d_ffn_in * normed_two, 0)
    d_stream_mid = d_stream_out + normalize_back(d_ffn_in * gains_wide[1], normed_two, inverse_two)
    d_out = as_low(d_stream_mid)
    grad_output = contract_rows(mixed, d_out)
    d_mixed = as_low(contract_cols(d_out, output_full)).reshape(frames, heads, HD)
    probs_full = jnp.exp(attention_scores(query, keys, frame_valid) - log_total)
    d_probs = jnp.einsum("qhd,khd->hqk", d_mixed, values, preferred_element_type=jnp.float32)
    d_values = jnp.einsum("hqk,qhd->khd", attn_probs, d_mixed, preferred_element_type=jnp.float32)
    row_dot = jnp.sum(d_probs * probs_full, -1, keepdims=True)
    d_scores = as_low(probs_full * (d_probs - row_dot))
    d_query = jnp.einsum(
        "hqk,khd->qhd", d_scores, keys, preferred_element_type=jnp.float32
    ) * HD ** (-0.5)
    d_keys = jnp.einsum(
        "hqk,qhd->khd", d_scores, query, preferred_element_type=jnp.float32
    ) * HD ** (-0.5)
    d_packed = as_low(
        jnp.concatenate(
            [
                d_query.reshape(frames, width),
                d_keys.reshape(frames, width),
                d_values.reshape(frames, width),
            ],
            1,
        )
    )
    grad_attend = contract_rows(attn_in, d_packed)
    d_attn_in = contract_cols(d_packed, attend_full)
    grad_gain_one = jnp.sum(d_attn_in * normed_one, 0)
    d_stream = d_stream_mid + normalize_back(d_attn_in * gains_wide[0], normed_one, inverse_one)
    d_joined_in = as_low(d_stream)
    grad_skip = contract_rows(joined, d_joined_in)
    d_start = as_low(contract_cols(d_joined_in, skip_full)[:, :width])
    grad_input = contract_rows(features, d_start)
    d_phones = as_low(contract_cols(d_start, input_full)[:, 2 * mel_bins :])
    grad_table = contract_rows(phone_hot, d_phones)
    grad_gains = jnp.stack([grad_gain_one, grad_gain_two, grad_gain_three])
    shares = (
        lax.psum_scatter(grad_input, ("wide", "narrow"), scatter_dimension=1, tiled=True),
        lax.psum_scatter(grad_table, ("wide", "narrow"), scatter_dimension=1, tiled=True),
        lax.psum_scatter(grad_skip, ("wide", "narrow"), scatter_dimension=0, tiled=True),
        lax.psum_scatter(grad_attend, ("wide", "narrow"), scatter_dimension=0, tiled=True),
        lax.psum_scatter(grad_output, ("wide", "narrow"), scatter_dimension=0, tiled=True),
        lax.psum_scatter(grad_expand, ("wide", "narrow"), scatter_dimension=0, tiled=True),
        lax.psum_scatter(grad_reduce, ("wide", "narrow"), scatter_dimension=0, tiled=True),
        lax.psum_scatter(grad_head, ("wide", "narrow"), scatter_dimension=0, tiled=True),
        lax.psum_scatter(grad_gains, ("wide", "narrow"), scatter_dimension=1, tiled=True),
    )
    local_square = sum((jnp.sum(g * g) for g in shares))
    total_square = lax.psum(local_square, ("wide", "narrow"))
    loss_value = jnp.mean(sums / jnp.maximum(counts, 1.0))
    grad_norm = jnp.sqrt(total_square)
    clip = jnp.minimum(1.0, 1.0 / (grad_norm + 1e-06))
    results = [
        adam_step(w, g * clip, m, s, r)
        for w, g, m, s, r in zip(masters, shares, moments, squares, rates)
    ]
    next_weights = tuple((r[0] for r in results))
    next_moments = tuple((r[1] for r in results))
    next_squares = tuple((r[2] for r in results))
    return (loss_value, grad_norm) + next_weights + next_moments + next_squares


def solution(mesh):
    in_specs = (
        P(("wide", "narrow"), None),
        P(("wide", "narrow"), None),
        P(("wide", "narrow")),
        P(("wide", "narrow")),
        P(("wide", "narrow")),
        P(("wide", "narrow")),
        P(("wide", "narrow")),
        P(("wide", "narrow")),
        P(("wide", "narrow"), None),
        P(None, ("wide", "narrow")),
        P(None, ("wide", "narrow")),
        P(("wide", "narrow"), None),
        P(("wide", "narrow"), None),
        P(("wide", "narrow"), None),
        P(("wide", "narrow"), None),
        P(("wide", "narrow"), None),
        P(("wide", "narrow"), None),
        P(None, ("wide", "narrow")),
        P(None, ("wide", "narrow")),
        P(None, ("wide", "narrow")),
        P(("wide", "narrow"), None),
        P(("wide", "narrow"), None),
        P(("wide", "narrow"), None),
        P(("wide", "narrow"), None),
        P(("wide", "narrow"), None),
        P(("wide", "narrow"), None),
        P(None, ("wide", "narrow")),
        P(None, ("wide", "narrow")),
        P(None, ("wide", "narrow")),
        P(("wide", "narrow"), None),
        P(("wide", "narrow"), None),
        P(("wide", "narrow"), None),
        P(("wide", "narrow"), None),
        P(("wide", "narrow"), None),
        P(("wide", "narrow"), None),
        P(None, ("wide", "narrow")),
    )
    out_specs = (
        P(),
        P(),
        P(None, ("wide", "narrow")),
        P(None, ("wide", "narrow")),
        P(("wide", "narrow"), None),
        P(("wide", "narrow"), None),
        P(("wide", "narrow"), None),
        P(("wide", "narrow"), None),
        P(("wide", "narrow"), None),
        P(("wide", "narrow"), None),
        P(None, ("wide", "narrow")),
        P(None, ("wide", "narrow")),
        P(None, ("wide", "narrow")),
        P(("wide", "narrow"), None),
        P(("wide", "narrow"), None),
        P(("wide", "narrow"), None),
        P(("wide", "narrow"), None),
        P(("wide", "narrow"), None),
        P(("wide", "narrow"), None),
        P(None, ("wide", "narrow")),
        P(None, ("wide", "narrow")),
        P(None, ("wide", "narrow")),
        P(("wide", "narrow"), None),
        P(("wide", "narrow"), None),
        P(("wide", "narrow"), None),
        P(("wide", "narrow"), None),
        P(("wide", "narrow"), None),
        P(("wide", "narrow"), None),
        P(None, ("wide", "narrow")),
    )
    return jax.shard_map(shards, mesh=mesh, in_specs=in_specs, out_specs=out_specs, check_vma=False)
```

profile of v0, /device:TPU:0, one launch (start us, length us, event | category | flops | bytes accessed | tf_op | source)
XLA Modules:
  0.0 1953.7 jit_solution(11142917095237842303)
XLA Ops:
  7.3 1.6 convert_element_type.141
  9.0 1.6 convert_element_type.143
  10.7 1.7 convert_element_type.147
  12.5 1.5 convert_element_type.154
  14.1 1.8 convert_element_type.156
  15.9 1.8 convert_element_type.158
  22.9 43.3 %all-gather = bf16[32,32,3]{1,2,0:T(4,128)(2,1)S(1)} all-gather(bf16[1,32,3]{1,2,0:T(4,128)(2,1)S(1)} %convert_bitcast_fusion), channel_id=1, replica_groups=mesh['wide'=8,'narrow'=4] {'wide','narrow'}, dimensions={0}, use_global_device_ids=true | all-gather | bytes 6336 | tf_op jit(solution)/shard_map/all_gather | solution.py:190
  66.9 37.1 %all_gather.35 = bf16[128,512]{0,1:T(8,128)(2,1)S(1)} all-gather(bf16[128,16]{0,1:T(8,128)(2,1)S(1)} %convert_element_type.139), channel_id=1, replica_groups=mesh['wide'=8,'narrow'=4] {'wide','narrow'}, dimensions={1}, use_global_device_ids=true | all-gather | bytes 135168 | tf_op jit(solution)/shard_map/all_gather | solution.py:183
  103.9 41.8 %all_gather.43 = bf16[1024,80]{1,0:T(8,128)(2,1)} all-gather(bf16[32,80]{1,0:T(8,128)(2,1)S(1)} %convert_element_type.160), channel_id=1, replica_groups=mesh['wide'=8,'narrow'=4] {'wide','narrow'}, dimensions={0}, use_global_device_ids=true | all-gather | bytes 168960 | tf_op jit(solution)/shard_map/all_gather | solution.py:189
  148.0 3.6 add_convert_fusion.2
  151.6 4.9 fusion.63
  157.0 49.0 %all-gather.12.cloned.1.call-done = bf16[1024,3072]{1,0:T(8,128)(2,1)} async-done(((bf16[32,3072]{1,0:T(8,128)(2,1)}), bf16[1024,3072]{1,0:T(8,128)(2,1)}) %all-gather.12.cloned.1.call-update) | async-done | bytes 6291472 | tf_op jit(solution)/shard_map/all_gather | solution.py:185
  206.0 6.8 convolution_convert_fusion
  212.8 1.7 fusion.61
  216.5 1.9 copy.96
  218.4 9.2 fusion.64
  227.7 8.3 fusion
  236.0 7.2 divide_convert_fusion
  243.3 3.2 copy-done
  248.0 16.2 all-gather.14.cloned.1.call-done
  264.2 3.6 fusion.65
  269.5 74.3 %all-gather.16.cloned.1.call-done = bf16[1024,4096]{1,0:T(8,128)(2,1)} async-done(((bf16[32,4096]{1,0:T(8,128)(2,1)}), bf16[1024,4096]{1,0:T(8,128)(2,1)}) %all-gather.16.cloned.1.call-update) | async-done | bytes 8388624 | tf_op jit(solution)/shard_map/all_gather | solution.py:187
  343.8 26.8 %multiply_convert_fusion.1 = (bf16[512,4096]{1,0:T(8,128)(2,1)}, f32[512,4096]{1,0:T(8,128)}, f32[512,4096]{1,0:T(8,128)}) fusion(bf16[1024,4096]{1,0:T(8,128)(2,1)} %all-gather.16.cloned.1.call-done, f32[512,1024]{1,0:T(8,128)} %copy-done.9, f32[1024]{0:T(1024)S(1)} %bitcast.113, f32[512]{0:T(512)S(1)} %add_rsqrt_fusion.1, f32[512]{0:T(512)S(1)} %broadcast_multiply_fusion.7), kind=kOutput, calls=%fused_computation.10 | convolution fusion | flops 4433379328 | bytes 31465472 | tf_op jit(solution)/shard_map/dot_general | solution.py:30
  370.6 52.6 %all-gather.18.cloned.1.call-done = bf16[4096,1024]{1,0:T(8,128)(2,1)} async-done(((bf16[128,1024]{1,0:T(8,128)(2,1)}), bf16[4096,1024]{1,0:T(8,128)(2,1)}) %all-gather.18.cloned.1.call-update) | async-done | bytes 8388624 | tf_op jit(solution)/shard_map/all_gather | solution.py:188
  423.2 9.7 fusion.66
  437.7 39.6 %all-reduce = (f32[16]{0:T(128)S(1)}, f32[16]{0:T(128)S(1)}) all-reduce(f32[16]{0:T(128)S(1)} %copy-done.78, f32[16]{0:T(128)S(1)} %fusion.40), channel_id=1, replica_groups=mesh['wide'=8,'narrow'=4] {'wide','narrow'}, use_global_device_ids=true, to_apply=%region_12.13 | all-reduce | flops 32 | bytes 256 | tf_op jit(solution)/shard_map/psum | solution.py:245
  478.6 2.5 multiply_reduce_fusion.1
  481.7 15.2 add_convert_fusion
  496.9 9.4 multiply_reduce_fusion.2
  511.3 7.2 convolution_convert_fusion.1
  518.5 14.7 multiply_reduce_fusion
  534.1 10.6 multiply_convert_fusion
  544.7 6.2 multiply_convert_fusion.2
  554.5 5.2 multiply_reduce_fusion.3
  561.1 3.0 add_convert_fusion.1
  564.6 2.4 fusion.67
  571.2 4.1 fusion.23
  575.4 3.3 fusion.14
  580.5 5.7 fusion.7
  588.0 9.8 fusion.9
  597.9 1.5 copy-done.11
  599.4 10.5 fusion.49
  610.0 1.5 copy-done.13
  611.5 10.4 fusion.17
  622.0 73.0 %reduce-scatter.28.cloned.1.call-done = f32[32,3]{1,0:T(8,128)} async-done(((f32[1024,3]{1,0:T(8,128)}), f32[32,3]{1,0:T(8,128)}) %reduce-scatter.28.cloned.1.call-update) | async-done | bytes 400
  696.5 130.7 %reduce-scatter.14.cloned.1.call-done = f32[128,16]{0,1:T(8,128)} async-done(((f32[128,512]{0,1:T(8,128)}), f32[128,16]{0,1:T(8,128)}) %reduce-scatter.14.cloned.1.call-update) | async-done | bytes 8208 | tf_op jit(solution)/shard_map/reduce_scatter | solution.py:321
  828.5 131.1 %reduce-scatter.26.cloned.1.call-done = f32[32,80]{1,0:T(8,128)} async-done(((f32[1024,80]{1,0:T(8,128)}), f32[32,80]{1,0:T(8,128)}) %reduce-scatter.26.cloned.1.call-update) | async-done | bytes 10256 | tf_op jit(solution)/shard_map/reduce_scatter | solution.py:327
  960.9 102.3 %reduce-scatter.12.cloned.1.call-done = f32[672,32]{0,1:T(8,128)} async-done(((f32[672,1024]{0,1:T(8,128)}), f32[672,32]{0,1:T(8,128)}) %reduce-scatter.12.cloned.1.call-update) | async-done | bytes 86032 | tf_op jit(solution)/shard_map/reduce_scatter | solution.py:320
  1063.2 1.5 multiply_reduce_fusion.19
  1066.0 139.7 %reduce-scatter.20.cloned.1.call-done = f32[32,1024]{1,0:T(8,128)} async-done(((f32[1024,1024]{1,0:T(8,128)}), f32[32,1024]{1,0:T(8,128)}) %reduce-scatter.20.cloned.1.call-update) | async-done | bytes 131088 | tf_op jit(solution)/shard_map/reduce_scatter | solution.py:324
  1205.7 1.5 multiply_reduce_fusion.18
  1207.3 145.1 %reduce-scatter.16.cloned.1.call-done = f32[64,1024]{1,0:T(8,128)} async-done(((f32[2048,1024]{1,0:T(8,128)}), f32[64,1024]{1,0:T(8,128)}) %reduce-scatter.16.cloned.1.call-update) | async-done | bytes 262160 | tf_op jit(solution)/shard_map/reduce_scatter | solution.py:322
  1352.4 1.6 multiply_reduce_fusion.16
  1354.7 156.5 %reduce-scatter.18.cloned.1.call-done = f32[32,3072]{1,0:T(8,128)} async-done(((f32[1024,3072]{1,0:T(8,128)}), f32[32,3072]{1,0:T(8,128)}) %reduce-scatter.18.cloned.1.call-update) | async-done | bytes 393232 | tf_op jit(solution)/shard_map/reduce_scatter | solution.py:323
  1511.2 1.8 multiply_reduce_fusion.15
  1514.3 181.1 %reduce-scatter.22.cloned.1.call-done = f32[32,4096]{1,0:T(8,128)} async-done(((f32[1024,4096]{1,0:T(8,128)}), f32[32,4096]{1,0:T(8,128)}) %reduce-scatter.22.cloned.1.call-update) | async-done | bytes 524304 | tf_op jit(solution)/shard_map/reduce_scatter | solution.py:325
  1695.4 1.8 multiply_reduce_fusion.14
  1697.8 184.1 %reduce-scatter.24.cloned.1.call-done = f32[128,1024]{1,0:T(8,128)} async-done(((f32[4096,1024]{1,0:T(8,128)}), f32[128,1024]{1,0:T(8,128)}) %reduce-scatter.24.cloned.1.call-update) | async-done | bytes 524304 | tf_op jit(solution)/shard_map/reduce_scatter | solution.py:326
  1881.9 1.9 multiply_reduce_fusion.13
  1886.4 42.3 %psum.23 = f32[]{:T(128)} all-reduce(f32[]{:T(128)S(6)} %add.268), channel_id=1, replica_groups=mesh['wide'=8,'narrow'=4] {'wide','narrow'}, use_global_device_ids=true, to_apply=%region_43.44 | all-reduce | flops 1 | bytes 8 | tf_op jit(solution)/shard_map/psum | solution.py:331
  1933.4 1.7 multiply_subtract_fusion.5
  1935.2 1.8 multiply_subtract_fusion.4
  1937.0 2.3 multiply_subtract_fusion.3
  1939.3 2.3 multiply_subtract_fusion.2
  (264 shorter events, 47.0 us)
Async XLA Ops:
  7.2 15.6 copy-start.66
  7.2 15.6 copy-start.54
  7.2 15.6 copy-start.52
  7.2 140.2 %copy-start.71 = (s32[512]{0:T(512)S(1)}, s32[512]{0:T(512)}, u32[]{:S(2)}) copy-start(s32[512]{0:T(512)} %param.39) | copy-start | bytes 6148
  7.3 140.7 %copy-start.38 = (f32[512,80]{0,1:T(8,128)S(1)}, f32[512,80]{0,1:T(8,128)}, u32[]{:S(2)}) copy-start(f32[512,80]{0,1:T(8,128)} %param.37) | copy-start | bytes 491524
  7.3 140.7 %copy-start.36 = (f32[512,80]{0,1:T(8,128)S(1)}, f32[512,80]{0,1:T(8,128)}, u32[]{:S(2)}) copy-start(f32[512,80]{0,1:T(8,128)} %param.36) | copy-start | bytes 491524
  7.3 140.7 %all-gather.8.cloned.1.call-start = ((), (), s32[]{:S(2)}) async-start(), calls=%async_computation.9 | async-start | bytes 1622016 | tf_op jit(solution)/shard_map/all_gather | solution.py:182
  9.0 142.7 %all-gather.10.cloned.1.call-start = ((), (), s32[]{:S(2)}) async-start(), calls=%async_computation.10 | async-start | bytes 4325376 | tf_op jit(solution)/shard_map/all_gather | solution.py:184
  10.7 195.3 %all-gather.12.cloned.1.call-start = ((), (), s32[]{:S(2)}) async-start(), calls=%async_computation.11 | async-start | bytes 6488064 | tf_op jit(solution)/shard_map/all_gather | solution.py:185
  12.4 251.8 %all-gather.14.cloned.1.call-start = ((), (), s32[]{:S(2)}) async-start(), calls=%async_computation.12 | async-start | bytes 2162688 | tf_op jit(solution)/shard_map/all_gather | solution.py:186
  14.1 329.8 %all-gather.16.cloned.1.call-start = ((), (), s32[]{:S(2)}) async-start(), calls=%async_computation.13 | async-start | bytes 8650752 | tf_op jit(solution)/shard_map/all_gather | solution.py:187
  15.9 407.3 %all-gather.18.cloned.1.call-start = ((), (), s32[]{:S(2)}) async-start(), calls=%async_computation.14 | async-start | bytes 8650752 | tf_op jit(solution)/shard_map/all_gather | solution.py:188
  17.8 677.2 %reduce-scatter.28.cloned.1.call-start = ((), (), s32[]{:S(2)}) async-start(), calls=%async_computation.23 | async-start | bytes 540672
  66.9 139.1 %copy-start.61 = (f32[1,1024]{1,0:T(1,128)}, f32[1,1024]{1,0:T(1,128)S(1)}, u32[]{:S(2)}) copy-start(f32[1,1024]{1,0:T(1,128)S(1)} %get-tuple-element.78) | copy-start | bytes 12292
  156.6 56.2 %copy-start.14 = (f32[512,1024]{1,0:T(8,128)}, f32[512,1024]{1,0:T(8,128)S(1)}, u32[]{:S(2)}) copy-start(f32[512,1024]{1,0:T(8,128)S(1)} %get-tuple-element.80) | copy-start | bytes 6291460
  156.6 49.4 %copy-start.56 = (f32[512]{0:T(512)}, f32[512]{0:T(512)S(1)}, u32[]{:S(2)}) copy-start(f32[512]{0:T(512)S(1)} %broadcast_multiply_fusion.8) | copy-start | bytes 6148
  157.0 49.0 %copy-start.68 = (f32[512]{0:T(512)}, f32[512]{0:T(512)S(1)}, u32[]{:S(2)}) copy-start(f32[512]{0:T(512)S(1)} %add_rsqrt_fusion.2) | copy-start | bytes 6148
  216.0 11.7 copy-start.17
  216.5 11.1 copy-start.19
  248.0 21.6 %copy-start.4 = (bf16[16,64,512]{2,1,0:T(8,128)(2,1)}, bf16[16,64,512]{2,1,0:T(8,128)(2,1)S(1)}, u32[]{:S(2)}) copy-start(bf16[16,64,512]{2,1,0:T(8,128)(2,1)S(1)} %convolution_convert_fusion.2) | copy-start | bytes 3145732
  264.2 79.6 %copy-start.59 = (f32[1,1024]{1,0:T(1,128)S(1)}, f32[1,1024]{1,0:T(1,128)}, u32[]{:S(2)}) copy-start(f32[1,1024]{1,0:T(1,128)} %get-tuple-element.77) | copy-start | bytes 12292
  269.5 236.7 %copy-start.64 = (f32[512]{0:T(512)}, f32[512]{0:T(512)S(1)}, u32[]{:S(2)}) copy-start(f32[512]{0:T(512)S(1)} %add_rsqrt_fusion.1) | copy-start | bytes 6148
  433.0 4.8 copy-start.78
  481.7 24.6 %copy-start.12 = (f32[512,1024]{1,0:T(8,128)}, f32[512,1024]{1,0:T(8,128)S(1)}, u32[]{:S(2)}) copy-start(f32[512,1024]{1,0:T(8,128)S(1)} %subtract_multiply_fusion) | copy-start | bytes 6291460
  481.7 15.2 copy-start.10
  511.3 21.9 %slice-start = ((s8[16777216]{0:T(1024)(128)(4,1)}), s8[4194304]{0:T(1024)(128)(4,1)S(1)}, s32[]{:S(2)}) async-start(s8[16777216]{0:T(1024)(128)(4,1)} %bitcast.89), calls=%async_computation.24 | async-start | bytes 8388608
  518.5 14.7 slice-start.1
  518.5 14.7 slice-start.2
  518.5 15.6 slice-start.3
  534.1 10.6 copy-start.20
  544.7 6.2 copy-start.1
  544.7 6.2 copy-start.18
  544.7 7.8 slice-start.4
  552.4 7.3 copy-start.21
  554.5 5.3 copy-start.58
  554.5 5.3 copy-start.70
  554.5 6.6 copy-start.3
  560.8 266.4 %reduce-scatter.14.cloned.1.call-start = ((), (), s32[]{:S(2)}) async-start(), calls=%async_computation.16 | async-start | bytes 270336 | tf_op jit(solution)/shard_map/reduce_scatter | solution.py:321
  569.7 389.8 %reduce-scatter.26.cloned.1.call-start = ((), (), s32[]{:S(2)}) async-start(), calls=%async_computation.22 | async-start | bytes 540672 | tf_op jit(solution)/shard_map/reduce_scatter | solution.py:327
  571.1 4.3 copy-start.5
  571.1 492.1 %reduce-scatter.12.cloned.1.call-start = ((), (), s32[]{:S(2)}) async-start(), calls=%async_computation.15 | async-start | bytes 3244032 | tf_op jit(solution)/shard_map/reduce_scatter | solution.py:320
  575.3 630.4 %reduce-scatter.20.cloned.1.call-start = ((), (), s32[]{:S(2)}) async-start(), calls=%async_computation.19 | async-start | bytes 4325376 | tf_op jit(solution)/shard_map/reduce_scatter | solution.py:324
  578.7 773.7 %reduce-scatter.16.cloned.1.call-start = ((), (), s32[]{:S(2)}) async-start(), calls=%async_computation.17 | async-start | bytes 8650752 | tf_op jit(solution)/shard_map/reduce_scatter | solution.py:322
  586.2 925.0 %reduce-scatter.18.cloned.1.call-start = ((), (), s32[]{:S(2)}) async-start(), calls=%async_computation.18 | async-start | bytes 12976128 | tf_op jit(solution)/shard_map/reduce_scatter | solution.py:323
  597.8 1097.5 %reduce-scatter.22.cloned.1.call-start = ((), (), s32[]{:S(2)}) async-start(), calls=%async_computation.20 | async-start | bytes 17301504 | tf_op jit(solution)/shard_map/reduce_scatter | solution.py:325
  609.9 1272.0 %reduce-scatter.24.cloned.1.call-start = ((), (), s32[]{:S(2)}) async-start(), calls=%async_computation.21 | async-start | bytes 17301504 | tf_op jit(solution)/shard_map/reduce_scatter | solution.py:326
  621.9 1307.5 %copy-start.67 = (f32[3,32]{1,0:T(4,128)S(1)}, f32[3,32]{1,0:T(4,128)}, u32[]{:S(2)}) copy-start(f32[3,32]{1,0:T(4,128)} %param.53) | copy-start | bytes 1156
  621.9 1308.8 %copy-start.55 = (f32[128,16]{0,1:T(8,128)S(1)}, f32[128,16]{0,1:T(8,128)}, u32[]{:S(2)}) copy-start(f32[128,16]{0,1:T(8,128)} %param.46) | copy-start | bytes 24580
  621.9 1310.2 %copy-start.53 = (f32[32,80]{1,0:T(8,128)S(1)}, f32[32,80]{1,0:T(8,128)}, u32[]{:S(2)}) copy-start(f32[32,80]{1,0:T(8,128)} %param.52) | copy-start | bytes 30724
  621.9 1310.2 %copy-start.63 = (f32[32,80]{1,0:T(8,128)S(1)}, f32[32,80]{1,0:T(8,128)}, u32[]{:S(2)}) copy-start(f32[32,80]{1,0:T(8,128)} %param.61) | copy-start | bytes 30724
  621.9 1311.6 %copy-start.46 = (f32[672,32]{0,1:T(8,128)S(1)}, f32[672,32]{0,1:T(8,128)}, u32[]{:S(2)}) copy-start(f32[672,32]{0,1:T(8,128)} %param.45) | copy-start | bytes 258052
  621.9 1313.3 %copy-start.41 = (f32[32,1024]{1,0:T(8,128)S(1)}, f32[32,1024]{1,0:T(8,128)}, u32[]{:S(2)}) copy-start(f32[32,1024]{1,0:T(8,128)} %param.49) | copy-start | bytes 393220
  621.9 1313.3 %copy-start.47 = (f32[32,1024]{1,0:T(8,128)S(1)}, f32[32,1024]{1,0:T(8,128)}, u32[]{:S(2)}) copy-start(f32[32,1024]{1,0:T(8,128)} %param.58) | copy-start | bytes 393220
  621.9 1315.0 %copy-start.33 = (f32[64,1024]{1,0:T(8,128)S(1)}, f32[64,1024]{1,0:T(8,128)}, u32[]{:S(2)}) copy-start(f32[64,1024]{1,0:T(8,128)} %param.47) | copy-start | bytes 786436
  622.0 1317.3 %copy-start.28 = (f32[32,3072]{1,0:T(8,128)S(1)}, f32[32,3072]{1,0:T(8,128)}, u32[]{:S(2)}) copy-start(f32[32,3072]{1,0:T(8,128)} %param.48) | copy-start | bytes 1179652
  694.9 1246.7 %copy-start.24 = (f32[128,1024]{1,0:T(8,128)S(1)}, f32[128,1024]{1,0:T(8,128)}, u32[]{:S(2)}) copy-start(f32[128,1024]{1,0:T(8,128)} %param.51) | copy-start | bytes 1572868
  694.9 1246.7 %copy-start.42 = (f32[128,1024]{1,0:T(8,128)S(1)}, f32[128,1024]{1,0:T(8,128)}, u32[]{:S(2)}) copy-start(f32[128,1024]{1,0:T(8,128)} %param.60) | copy-start | bytes 1572868
  694.9 1246.7 %copy-start.43 = (f32[128,1024]{1,0:T(8,128)S(1)}, f32[128,1024]{1,0:T(8,128)}, u32[]{:S(2)}) copy-start(f32[128,1024]{1,0:T(8,128)} %param.69) | copy-start | bytes 1572868
  1511.2 428.1 %copy-start.29 = (f32[32,3072]{1,0:T(8,128)S(1)}, f32[32,3072]{1,0:T(8,128)}, u32[]{:S(2)}) copy-start(f32[32,3072]{1,0:T(8,128)} %reduce-scatter.18.cloned.1.call-done) | copy-start | bytes 1179652
  1881.9 59.7 %copy-start.27 = (f32[128,1024]{1,0:T(8,128)S(1)}, f32[128,1024]{1,0:T(8,128)}, u32[]{:S(2)}) copy-start(f32[128,1024]{1,0:T(8,128)} %reduce-scatter.24.cloned.1.call-done) | copy-start | bytes 1572868
  1937.0 6.1 copy-start.25
  1937.0 6.1 copy-start.26
  1937.0 6.1 copy-start.44
  1937.0 6.1 copy-start.45
  (38 other events, 86.4 us)
Sparse Core Ops, SparseCore 0:
  11.5 57.6 all-gather.7
  72.7 61.5 all-gather.9
  137.8 68.1 all-gather.11
  209.3 54.9 all-gather.13
  267.5 76.2 all-gather.15
  347.1 76.0 all-gather.17
  561.0 133.9 reduce-scatter.27
  697.8 129.3 reduce-scatter.13
  830.0 129.5 reduce-scatter.25
  965.7 97.4 reduce-scatter.11
  1065.6 140.0 reduce-scatter.19
  1208.0 144.3 reduce-scatter.15
  1359.5 151.6 reduce-scatter.17
  1513.3 181.9 reduce-scatter.21
  1697.5 184.3 reduce-scatter.23
where the time goes:
time: 1960 us; the launch traced here: 1950 us
  waiting for transfers between devices  1440 us (73%)
  blocking collectives  204 us (10%)
  matrix products  180 us (9%)
  other arithmetic  76.4 us (4%)
  between operations  28.7 us (1%)
  local copies, waits for them, and re-layouts  27 us (1%)
    reduce_scatter x1, waiting for transfers between devices, shards(): lax.psum_scatter(grad_reduce, ('wide', 'narrow'), scatter_dimension=0, ti...  184 us
    reduce_scatter x1, waiting for transfers between devices, shards(): lax.psum_scatter(grad_expand, ('wide', 'narrow'), scatter_dimension=0, ti...  181 us
    reduce_scatter x1, waiting for transfers between devices, shards(): lax.psum_scatter(grad_attend, ('wide', 'narrow'), scatter_dimension=0, ti...  157 us
    reduce_scatter x1, waiting for transfers between devices, shards(): lax.psum_scatter(grad_skip, ('wide', 'narrow'), scatter_dimension=0, tile...  145 us
    reduce_scatter x1, waiting for transfers between devices, shards(): lax.psum_scatter(grad_output, ('wide', 'narrow'), scatter_dimension=0, ti...  140 us
    reduce_scatter x1, waiting for transfers between devices, shards(): lax.psum_scatter(grad_head, ('wide', 'narrow'), scatter_dimension=0, tile...  131 us
    reduce_scatter x1, waiting for transfers between devices, shards(): lax.psum_scatter(grad_table, ('wide', 'narrow'), scatter_dimension=1, til...  131 us
    reduce_scatter x1, waiting for transfers between devices, shards(): lax.psum_scatter(grad_input, ('wide', 'narrow'), scatter_dimension=1, til...  102 us
  transfers between devices with their start and end apart: 15, of which 13 were waited for; matrix products, arithmetic and copies ran while one was open for 8% of the time, Pallas kernels for 0%

commit v1 on v0

v1 whole, which is shorter than its diff:
```python
from functools import partial
import math

import jax
import jax.numpy as jnp
from jax import lax
from jax.experimental import pallas as pl
from jax.experimental.pallas import tpu as pltpu
from jax.sharding import PartitionSpec as P

HD = 64
SPK = 16
STEP = 10


SIGMA = 1e-05
NORM_EPS = 1e-05
LEARN_RATE = 0.01
GAIN_RATE = 0.3
BETA_ONE = 0.5
BETA_TWO = 0.5
DECAY = 0.01
ADAM_EPS = 1e-08
MASKED = -1000000000.0
VMEM = 48 * 1024 * 1024


def as_low(x):
    return x.astype(jnp.bfloat16)


def matmul(left, right):
    return jnp.dot(left, right, preferred_element_type=jnp.float32)


def contract_rows(left, right):
    return lax.dot_general(
        left, right, (((0,), (0,)), ((), ())), preferred_element_type=jnp.float32
    )


def contract_cols(left, right):
    return lax.dot_general(
        left, right, (((1,), (1,)), ((), ())), preferred_element_type=jnp.float32
    )


def time_features(flow, width):
    half = width // 2
    freqs = jnp.exp(-math.log(10000.0) * jnp.arange(half, dtype=jnp.float32) / half)
    angle = 1000.0 * flow * freqs
    return jnp.concatenate([jnp.sin(angle), jnp.cos(angle)])


def normalize(x):
    centered = x - jnp.mean(x, -1, keepdims=True)
    inverse = lax.rsqrt(jnp.mean(centered * centered, -1, keepdims=True) + NORM_EPS)
    return (centered * inverse, inverse)


def normalize_back(grad, normed, inverse):
    return inverse * (
        grad
        - jnp.mean(grad, -1, keepdims=True)
        - normed * jnp.mean(grad * normed, -1, keepdims=True)
    )


def head_slopes(heads):
    return 2.0 ** (-8.0 * (jnp.arange(heads, dtype=jnp.float32) + 1.0) / heads)


def attention_scores(query, keys, frame_valid):
    frames, heads = (query.shape[0], query.shape[1])
    position = jnp.arange(frames)
    dist = jnp.abs(position[:, None] - position[None, :]).astype(jnp.float32)
    scores = jnp.einsum("qhd,khd->hqk", query, keys, preferred_element_type=jnp.float32) * HD ** (
        -0.5
    )
    scores = scores - head_slopes(heads)[:, None, None] * dist[None]
    return jnp.where(frame_valid[None, None, :] > 0, scores, MASKED)


def adam_step(master, grad, moment, square, rate):
    moment = BETA_ONE * moment + (1.0 - BETA_ONE) * grad
    square = BETA_TWO * square + (1.0 - BETA_TWO) * grad * grad
    moment_hat = moment / (1.0 - BETA_ONE**STEP)
    square_hat = square / (1.0 - BETA_TWO**STEP)
    master = master - rate * (moment_hat / (jnp.sqrt(square_hat) + ADAM_EPS) + DECAY * master)
    return (master, moment, square)


AXES = ("wide", "narrow")


def grid_sizes(wide, narrow):
    low = 1
    while (2 * low) * (2 * low) <= wide:
        low *= 2
    return (wide // low, low, narrow // 2, 2)


class Grid:
    def __init__(self, mesh):
        self.sizes = grid_sizes(mesh.shape["wide"], mesh.shape["narrow"])
        self.total = mesh.shape["wide"] * mesh.shape["narrow"]

    def coords(self, index):
        out = []
        for size in reversed(self.sizes):
            out.append(index % size)
            index = index // size
        return out[::-1]

    def index(self, coords):
        index = 0
        for size, value in zip(self.sizes, coords):
            index = index * size + value
        return index

    def mixed(self):
        return self.sizes[1] == self.sizes[2]

    def axis(self, role, core):
        if role == "z":
            return 0
        if role == "core":
            return 3
        if self.mixed():
            return (2, 1)[core] if role == "far" else (1, 2)[core]
        return 2 if role == "far" else 1

    def size(self, role):
        return self.sizes[self.axis(role, 0)]

    def pairs(self, role, step):
        out = []
        for source in range(self.total):
            coords = self.coords(source)
            axis = self.axis(role, coords[3])
            coords[axis] = (coords[axis] + step) % self.sizes[axis]
            out.append((source, self.index(coords)))
        return out

    def owners(self, core_step, direction):
        me = self.coords(lax.axis_index(AXES))
        core = (me[3] + core_step) % 2
        far, near, deep = (self.size(r) for r in ("far", "near", "z"))
        f, n, k = jnp.meshgrid(jnp.arange(far), jnp.arange(near), jnp.arange(deep), indexing="ij")
        z = (me[0] + direction * k) % self.sizes[0]
        if self.mixed():
            y = jnp.where(core == 0, me[1] + direction * n, me[1] + direction * f) % self.sizes[1]
            x = jnp.where(core == 0, me[2] + direction * f, me[2] + direction * n) % self.sizes[2]
        else:
            y = (me[1] + direction * n) % self.sizes[1]
            x = (me[2] + direction * f) % self.sizes[2]
        return self.index((z, y, x, core)).reshape(-1).astype(jnp.int32)


def shift(grid, x, role, step):
    return lax.ppermute(x, AXES, grid.pairs(role, step))


def tied(x, *others):
    return lax.optimization_barrier((x,) + others)[0]


def spread(grid, x, role):
    return [x] + [shift(grid, x, role, step) for step in range(1, grid.size(role))]


def gather(grid, x, after):
    if after is not None:
        x = tied(x, after)
    deep = jnp.stack(spread(grid, x, "z"))
    near = jnp.concatenate(spread(grid, deep, "near"))
    far = jnp.concatenate(spread(grid, near, "far"))
    other = shift(grid, far, "core", 1)
    return far, other, deep


def place_kernel(rows, own_ref, other_ref, far_ref, core_ref, *refs):
    outs, sem = refs[:-1], refs[-1]
    copies = []
    for idx, source in ((own_ref, far_ref), (other_ref, core_ref)):
        for i in range(source.shape[0]):
            start = 0
            for out, count in zip(outs, rows):
                copy = pltpu.make_async_copy(
                    source.at[i, pl.ds(start, count)], out.at[idx[i]], sem
                )
                copy.start()
                copies.append(copy)
                start += count
    for copy in copies:
        copy.wait()


def place(rows, own, other, far, core):
    total = 2 * far.shape[0]
    width = far.shape[2]
    return pl.pallas_call(
        partial(place_kernel, rows),
        out_shape=[jax.ShapeDtypeStruct((total, r, width), far.dtype) for r in rows],
        in_specs=[pl.BlockSpec(memory_space=pltpu.SMEM)] * 2 + [pl.BlockSpec(memory_space=pl.ANY)] * 2,
        out_specs=[pl.BlockSpec(memory_space=pltpu.VMEM)] * len(rows),
        scratch_shapes=[pltpu.SemaphoreType.DMA],
        compiler_params=pltpu.CompilerParams(vmem_limit_bytes=VMEM),
        cost_estimate=pl.CostEstimate(
            flops=0, transcendentals=0, bytes_accessed=4 * total * sum(rows) * width
        ),
        name="place",
    )(own, other, far, core)


def pick_kernel(rows, idx_ref, *refs):
    out = refs[-1]
    start = 0
    for ref, count in zip(refs[:-1], rows):
        out[0, start : start + count] = ref[0]
        start += count


def pick(parts, idx):
    rows = [p.shape[1] for p in parts]
    width = parts[0].shape[2]
    count = idx.shape[0]
    return pl.pallas_call(
        partial(pick_kernel, rows),
        grid_spec=pltpu.PrefetchScalarGridSpec(
            num_scalar_prefetch=1,
            grid=(count,),
            in_specs=[pl.BlockSpec((1, r, width), lambda i, idx: (idx[i], 0, 0)) for r in rows],
            out_specs=pl.BlockSpec((1, sum(rows), width), lambda i, idx: (i, 0, 0)),
        ),
        out_shape=jax.ShapeDtypeStruct((count, sum(rows), width), parts[0].dtype),
        cost_estimate=pl.CostEstimate(
            flops=0, transcendentals=0, bytes_accessed=4 * count * sum(rows) * width
        ),
        name="pick",
    )(idx, *parts)


def fold_kernel(rows, far, idx_ref, *refs):
    outs = refs[-far:]
    came = refs[-2 * far : -far]
    start = 0
    for w, count in enumerate(rows):
        for f in range(far):
            part = refs[w * far + f]
            total = part[0].astype(jnp.float32) + came[f][0, start : start + count].astype(jnp.float32)
            outs[f][0, start : start + count] = total.astype(outs[f].dtype)
        start += count


def fold(parts, came, idx, far):
    rows = [p.shape[1] for p in parts]
    width = parts[0].shape[2]
    count = idx.shape[0] // far
    height = sum(rows)

    def part_map(f, i, idx):
        return (idx[f * count + i], 0, 0)

    def came_map(f, i, idx):
        return (f * count + i, 0, 0)

    return pl.pallas_call(
        partial(fold_kernel, rows, far),
        grid_spec=pltpu.PrefetchScalarGridSpec(
            num_scalar_prefetch=1,
            grid=(count,),
            in_specs=[
                pl.BlockSpec((1, r, width), partial(part_map, f)) for r in rows for f in range(far)
            ]
            + [pl.BlockSpec((1, height, width), partial(came_map, f)) for f in range(far)],
            out_specs=[pl.BlockSpec((1, height, width), lambda i, idx: (i, 0, 0))] * far,
        ),
        out_shape=[jax.ShapeDtypeStruct((count, height, width), jnp.bfloat16)] * far,
        compiler_params=pltpu.CompilerParams(vmem_limit_bytes=VMEM),
        cost_estimate=pl.CostEstimate(
            flops=0, transcendentals=0, bytes_accessed=6 * far * count * height * width
        ),
        name="fold",
    )(idx, *[p for p in parts for _ in range(far)], *[came] * far)


def scatter(grid, parts, mine, theirs, after):
    sent = pick(parts, theirs)
    if after is not None:
        sent = tied(sent, after)
    came = shift(grid, sent, "core", 1)
    far, near, deep = (grid.size(r) for r in ("far", "near", "z"))
    legs = fold(parts, came, mine, far)
    moved = [shift(grid, legs[f], "far", f) for f in range(1, far)]
    legs = [
        as_low(
            sum(leg[n * deep : (n + 1) * deep].astype(jnp.float32) for leg in [legs[0]] + moved)
        )
        for n in range(near)
    ]
    first = moved[0] if moved else None
    moved = [shift(grid, legs[n], "near", n) for n in range(1, near)]
    legs = [sum(leg[k].astype(jnp.float32) for leg in [legs[0]] + moved) for k in range(deep)]
    moved = [shift(grid, as_low(legs[k]), "z", k) for k in range(1, deep)]
    return sum((m.astype(jnp.float32) for m in moved), legs[0]), first


def all_sum(grid, x):
    step = 1
    while step < grid.total:
        x = x + lax.ppermute(x, AXES, [(i, i ^ step) for i in range(grid.total)])
        step *= 2
    return x


def shards(
    grid,
    fast,
    clean_mel,
    gauss_noise,
    flow_time,
    phone_ids,
    lengths,
    span_start,
    span_end,
    speaker,
    skip_states,
    w_input,
    phone_table,
    w_skip,
    w_attend,
    w_output,
    w_expand,
    w_reduce,
    w_head,
    norm_gains,
    moment_input,
    moment_table,
    moment_skip,
    moment_attend,
    moment_output,
    moment_expand,
    moment_reduce,
    moment_head,
    moment_gains,
    square_input,
    square_table,
    square_skip,
    square_attend,
    square_output,
    square_expand,
    square_reduce,
    square_head,
    square_gains,
):
    masters = (w_input, phone_table, w_skip, w_attend, w_output, w_expand, w_reduce, w_head, norm_gains)
    moments = (
        moment_input, moment_table, moment_skip, moment_attend, moment_output,
        moment_expand, moment_reduce, moment_head, moment_gains,
    )
    squares = (
        square_input, square_table, square_skip, square_attend, square_output,
        square_expand, square_reduce, square_head, square_gains,
    )
    rates = (LEARN_RATE, GAIN_RATE) + (LEARN_RATE,) * 6 + (GAIN_RATE,)
    frames, mel_bins = clean_mel.shape
    width = w_skip.shape[1]
    heads = width // HD
    devices = grid.total
    unit = width // devices
    inputs = w_input.shape[0]
    phones = phone_table.shape[0]
    phone_width = phone_table.shape[1] * devices
    table_lanes = phone_table.shape[0] * phone_table.shape[1] // unit
    at_table = inputs
    at_head = at_table + table_lanes
    at_gain = at_head + mel_bins
    at_count = at_gain + 3
    position = jnp.arange(frames)
    frame_valid = (position < lengths[0]).astype(jnp.float32)
    frame_inside = ((position >= span_start[0]) & (position < span_end[0])).astype(
        jnp.float32
    ) * frame_valid
    speaker_hot = (speaker[0] == jnp.arange(SPK)).astype(jnp.float32)
    count = jnp.sum(frame_inside)
    count_high = jnp.floor(count / 16.0)
    tally = jnp.stack([speaker[0].astype(jnp.float32), count_high, count - 16.0 * count_high])

    small = jnp.concatenate(
        [
            w_input.T,
            phone_table.T.reshape(unit, table_lanes),
            w_head,
            norm_gains.T,
            jnp.broadcast_to(tally[None, :], (unit, 3)),
            jnp.zeros((unit, width - at_count - 3), jnp.float32),
        ],
        1,
    )

    def blocks(x):
        return [as_low(x[:, j : j + width]) for j in range(0, x.shape[1], width)]

    attend_rows = blocks(w_attend)
    expand_rows = blocks(w_expand)
    half = len(expand_rows) // 2
    stages = [
        [as_low(small), as_low(w_skip)],
        attend_rows,
        [as_low(w_output)] + expand_rows[:half],
        expand_rows[half:],
        [as_low(w_reduce)],
    ]
    if fast:
        own, other = grid.owners(0, -1), grid.owners(1, -1)
    fulls = []
    after = None
    for stage in stages:
        rows = [w.shape[0] for w in stage]
        load = jnp.concatenate(stage, 0)
        if fast:
            far, core, after = gather(grid, load, after)
            full = place(rows, own, other, far, core)
        else:
            whole = lax.all_gather(load, AXES, axis=0, tiled=False)
            ends = [sum(rows[:j]) for j in range(len(rows) + 1)]
            full = [whole[:, a:b] for a, b in zip(ends, ends[1:])]
        fulls.append([f.reshape(-1, width) for f in full])
    small_full, skip_full = fulls[0]
    attend_full = fulls[1]
    output_full = fulls[2][0]
    expand_full = fulls[2][1:] + fulls[3]
    reduce_full = fulls[4][0]
    input_turned = small_full[:, :inputs]
    table_full = small_full[:, at_table:at_head].reshape(phone_width, phones).T
    head_full = small_full[:, at_head:at_gain]
    gains_wide = small_full[:, at_gain:at_count].astype(jnp.float32).T
    tallies = small_full.reshape(devices, unit, width)[:, 0, at_count : at_count + 3].astype(
        jnp.float32
    )
    counts = jnp.sum(
        (tallies[:, :1] == jnp.arange(SPK, dtype=jnp.float32)[None, :])
        * (16.0 * tallies[:, 1:2] + tallies[:, 2:3]),
        0,
    )

    flow = flow_time[0]
    noisy_mel = (1.0 - (1.0 - SIGMA) * flow) * gauss_noise + flow * clean_mel
    context = clean_mel * (frame_valid - frame_inside)[:, None]
    target = clean_mel - (1.0 - SIGMA) * gauss_noise
    phone_hot = as_low(phone_ids[:, None] == jnp.arange(phones)[None, :])
    embedded = as_low(matmul(phone_hot, table_full))
    features = jnp.concatenate([as_low(noisy_mel), as_low(context), embedded], 1)
    start_state = contract_cols(features, input_turned) + time_features(flow, width)[None, :]
    joined = jnp.concatenate([as_low(start_state), skip_states], 1)
    stream = matmul(joined, skip_full)
    normed_one, inverse_one = normalize(stream)
    attn_in = as_low(normed_one * gains_wide[0])
    query, keys, values = [
        as_low(matmul(attn_in, w)).reshape(frames, heads, HD) for w in attend_full
    ]
    scores = attention_scores(query, keys, frame_valid)
    top_score = jnp.max(scores, -1, keepdims=True)
    expo = jnp.exp(scores - top_score)
    exp_total = jnp.sum(expo, -1, keepdims=True)
    log_total = top_score + jnp.log(exp_total)
    attn_probs = as_low(expo / exp_total)
    mixed = as_low(
        jnp.einsum("hqk,khd->qhd", attn_probs, values, preferred_element_type=jnp.float32).reshape(
            frames, width
        )
    )
    stream_mid = stream + matmul(mixed, output_full)
    normed_two, inverse_two = normalize(stream_mid)
    ffn_in = as_low(normed_two * gains_wide[1])
    hidden = [matmul(ffn_in, w) for w in expand_full]
    activated = [as_low(jax.nn.gelu(h, approximate=False)) for h in hidden]
    stream_out = stream_mid + matmul(jnp.concatenate(activated, 1), reduce_full)
    normed_three, inverse_three = normalize(stream_out)
    head_in = as_low(normed_three * gains_wide[2])
    prediction = matmul(head_in, head_full)
    error = prediction - target
    frame_error = jnp.sum(error * error, 1) * frame_inside
    local_sum = speaker_hot * jnp.sum(frame_error)
    share = jnp.sum(speaker_hot / jnp.maximum(counts, 1.0)) / SPK
    d_prediction = as_low(2.0 * share * error * frame_inside[:, None])
    grad_head = contract_rows(head_in, d_prediction)
    d_head_in = contract_cols(d_prediction, head_full)
    grad_gain_three = jnp.sum(d_head_in * normed_three, 0)
    d_stream_out = normalize_back(d_head_in * gains_wide[2], normed_three, inverse_three)
    d_branch = as_low(d_stream_out)
    if fast:
        mine, theirs = grid.owners(0, 1), grid.owners(1, 1)
    chain = [None]

    def send(parts):
        rows = [p.shape[0] // devices for p in parts]
        if fast:
            low_parts = [as_low(p).reshape(devices, r, width) for p, r in zip(parts, rows)]
            total, chain[0] = scatter(grid, low_parts, mine, theirs, chain[0])
        else:
            parts = [p.reshape(devices, r, width) for p, r in zip(parts, rows)]
            total = lax.psum_scatter(jnp.concatenate(parts, 1), AXES, scatter_dimension=0)
        ends = [sum(rows[:j]) for j in range(len(rows) + 1)]
        return [total[a:b] for a, b in zip(ends, ends[1:])]

    (share_reduce,) = send([jnp.concatenate([contract_rows(a, d_branch) for a in activated], 0)])
    count_wide = len(activated)
    d_hidden = []
    for j in range(count_wide):
        d_activated = contract_cols(d_branch, reduce_full[j * width : (j + 1) * width])
        gelu_pull = jax.vjp(partial(jax.nn.gelu, approximate=False), hidden[j])[1]
        d_hidden.append(as_low(gelu_pull(d_activated)[0]))
    share_expand = send([contract_rows(ffn_in, d) for d in d_hidden])
    d_ffn_in = sum(contract_cols(d, w) for d, w in zip(d_hidden, expand_full))
    grad_gain_two = jnp.sum(d_ffn_in * normed_two, 0)
    d_stream_mid = d_stream_out + normalize_back(d_ffn_in * gains_wide[1], normed_two, inverse_two)
    d_out = as_low(d_stream_mid)
    grad_output = contract_rows(mixed, d_out)
    d_mixed = as_low(contract_cols(d_out, output_full)).reshape(frames, heads, HD)
    probs_full = jnp.exp(attention_scores(query, keys, frame_valid) - log_total)
    d_probs = jnp.einsum("qhd,khd->hqk", d_mixed, values, preferred_element_type=jnp.float32)
    d_values = jnp.einsum("hqk,qhd->khd", attn_probs, d_mixed, preferred_element_type=jnp.float32)
    row_dot = jnp.sum(d_probs * probs_full, -1, keepdims=True)
    d_scores = as_low(probs_full * (d_probs - row_dot))
    d_query = jnp.einsum(
        "hqk,khd->qhd", d_scores, keys, preferred_element_type=jnp.float32
    ) * HD ** (-0.5)
    d_keys = jnp.einsum(
        "hqk,qhd->khd", d_scores, query, preferred_element_type=jnp.float32
    ) * HD ** (-0.5)
    d_packed = [as_low(d.reshape(frames, width)) for d in (d_query, d_keys, d_values)]
    share_output, *share_attend = send([grad_output] + [contract_rows(attn_in, d) for d in d_packed])
    d_attn_in = sum(contract_cols(d, w) for d, w in zip(d_packed, attend_full))
    grad_gain_one = jnp.sum(d_attn_in * normed_one, 0)
    d_stream = d_stream_mid + normalize_back(d_attn_in * gains_wide[0], normed_one, inverse_one)
    d_joined_in = as_low(d_stream)
    grad_skip = contract_rows(joined, d_joined_in)
    d_start = as_low(contract_cols(d_joined_in, skip_full[:width]))
    grad_input = contract_rows(d_start, features)
    d_phones = as_low(matmul(d_start, input_turned[:, 2 * mel_bins :]))
    grad_table = contract_rows(d_phones, phone_hot)
    grad_small = jnp.concatenate(
        [
            grad_input,
            grad_table.reshape(width, table_lanes),
            grad_head,
            jnp.stack([grad_gain_one, grad_gain_two, grad_gain_three], 1),
            jnp.zeros((width, width - at_count), jnp.float32),
        ],
        1,
    )
    share_skip, share_small = send([grad_skip, grad_small])
    shares = (
        share_small[:, :inputs].T,
        share_small[:, at_table:at_head].reshape(phone_width // devices, phones).T,
        share_skip,
        jnp.concatenate(share_attend, 1),
        share_output,
        jnp.concatenate(share_expand, 1),
        share_reduce,
        share_small[:, at_head:at_gain],
        share_small[:, at_gain:at_count].T,
    )
    local_square = sum((jnp.sum(g * g) for g in shares))
    totals = all_sum(grid, jnp.concatenate([local_sum, local_square[None]]))
    sums, total_square = totals[:SPK], totals[SPK]
    loss_value = jnp.mean(sums / jnp.maximum(counts, 1.0))
    grad_norm = jnp.sqrt(total_square)
    clip = jnp.minimum(1.0, 1.0 / (grad_norm + 1e-06))
    results = [
        adam_step(w, g * clip, m, s, r)
        for w, g, m, s, r in zip(masters, shares, moments, squares, rates)
    ]
    next_weights = tuple((r[0] for r in results))
    next_moments = tuple((r[1] for r in results))
    next_squares = tuple((r[2] for r in results))
    return (loss_value, grad_norm) + next_weights + next_moments + next_squares


def solution(mesh):
    grid = Grid(mesh)
    in_specs = (
        P(("wide", "narrow"), None),
        P(("wide", "narrow"), None),
        P(("wide", "narrow")),
        P(("wide", "narrow")),
        P(("wide", "narrow")),
        P(("wide", "narrow")),
        P(("wide", "narrow")),
        P(("wide", "narrow")),
        P(("wide", "narrow"), None),
        P(None, ("wide", "narrow")),
        P(None, ("wide", "narrow")),
        P(("wide", "narrow"), None),
        P(("wide", "narrow"), None),
        P(("wide", "narrow"), None),
        P(("wide", "narrow"), None),
        P(("wide", "narrow"), None),
        P(("wide", "narrow"), None),
        P(None, ("wide", "narrow")),
        P(None, ("wide", "narrow")),
        P(None, ("wide", "narrow")),
        P(("wide", "narrow"), None),
        P(("wide", "narrow"), None),
        P(("wide", "narrow"), None),
        P(("wide", "narrow"), None),
        P(("wide", "narrow"), None),
        P(("wide", "narrow"), None),
        P(None, ("wide", "narrow")),
        P(None, ("wide", "narrow")),
        P(None, ("wide", "narrow")),
        P(("wide", "narrow"), None),
        P(("wide", "narrow"), None),
        P(("wide", "narrow"), None),
        P(("wide", "narrow"), None),
        P(("wide", "narrow"), None),
        P(("wide", "narrow"), None),
        P(None, ("wide", "narrow")),
    )
    out_specs = (
        P(),
        P(),
        P(None, ("wide", "narrow")),
        P(None, ("wide", "narrow")),
        P(("wide", "narrow"), None),
        P(("wide", "narrow"), None),
        P(("wide", "narrow"), None),
        P(("wide", "narrow"), None),
        P(("wide", "narrow"), None),
        P(("wide", "narrow"), None),
        P(None, ("wide", "narrow")),
        P(None, ("wide", "narrow")),
        P(None, ("wide", "narrow")),
        P(("wide", "narrow"), None),
        P(("wide", "narrow"), None),
        P(("wide", "narrow"), None),
        P(("wide", "narrow"), None),
        P(("wide", "narrow"), None),
        P(("wide", "narrow"), None),
        P(None, ("wide", "narrow")),
        P(None, ("wide", "narrow")),
        P(None, ("wide", "narrow")),
        P(("wide", "narrow"), None),
        P(("wide", "narrow"), None),
        P(("wide", "narrow"), None),
        P(("wide", "narrow"), None),
        P(("wide", "narrow"), None),
        P(("wide", "narrow"), None),
        P(None, ("wide", "narrow")),
    )

    def body(*args):
        unit = args[11].shape[1] // grid.total
        return shards(grid, unit % 32 == 0, *args)

    return jax.shard_map(body, mesh=mesh, in_specs=in_specs, out_specs=out_specs, check_vma=False)
```

time: 1960 us -> 738 us (0.38)
  waiting for transfers between devices: 1440 us -> 201 us
  blocking collectives: 204 us -> 0 us
  Pallas kernels: 0 us -> 101 us
  starting transfers between devices: 1.09 us -> 67.7 us
  local copies, waits for them, and re-layouts: 27 us -> 91 us
  matrix products: 180 us -> 154 us
    reduce_scatter x8 -> x0, waiting for transfers between devices: 1170 us -> none  [the longest x1 184 us: shards(): lax.psum_scatter(grad_reduce, ('wide', 'narrow'), scatter_dimension=0, ti...]
    ppermute x0 -> x59, waiting for transfers between devices: none -> 201 us  [the longest x54 190 us: shift(): return lax.ppermute(x, AXES, grid.pairs(role, step))]
    all_gather x6 -> x0, waiting for transfers between devices: 192 us -> none  [the longest x1 74.3 us: shards(): lax.all_gather(as_low(w_expand), ('wide', 'narrow'), axis=0, tiled=True)]
    all_gather x3 -> x0, blocking collectives: 122 us -> none  [the longest x1 43.3 us: shards(): lax.all_gather(as_low(norm_gains), ('wide', 'narrow'), axis=1, tiled=True)]
    pallas_call x0 -> x13, Pallas kernels: none -> 101 us  [the longest x4 42.7 us: pick(): pl.pallas_call(partial(pick_kernel, rows), grid_spec=pltpu.PrefetchScalar...]
    psum x2 -> x0, blocking collectives: 81.9 us -> none  [the longest x1 42.3 us: shards(): total_square = lax.psum(local_square, ('wide', 'narrow'))]
    unnamed x16 -> x0, waiting for transfers between devices: 73.2 us -> none
    ppermute x0 -> x59, starting transfers between devices: none -> 67.7 us  [the longest x54 64.2 us: shift(): return lax.ppermute(x, AXES, grid.pairs(role, step))]
  transfers between devices with their start and end apart: 15 -> 59, of which waited for: 13 -> 29; matrix products, arithmetic and copies ran while one was open for 8% -> 36% of each run, Pallas kernels for 0% -> 8%
where the time goes in v1:
time: 738 us; the launch traced here: 728 us
  waiting for transfers between devices  201 us (27%)
  matrix products  154 us (21%)
  Pallas kernels  101 us (14%)
  other arithmetic  96 us (13%)
  local copies, waits for them, and re-layouts  91 us (12%)
  starting transfers between devices  67.7 us (9%)
  between operations  17.5 us (2%)
    ppermute x54, waiting for transfers between devices, shift(): return lax.ppermute(x, AXES, grid.pairs(role, step))  190 us
    ppermute x54, starting transfers between devices, shift(): return lax.ppermute(x, AXES, grid.pairs(role, step))  64.2 us
    dot_general x12, matrix products, matmul(): return jnp.dot(left, right, preferred_element_type=jnp.float32)  52.7 us
    unnamed x302, local copies, waits for them, and re-layouts  43.7 us
    pallas_call x4, Pallas kernels, pick(): pl.pallas_call(partial(pick_kernel, rows), grid_spec=pltpu.PrefetchScalar...  42.7 us
    convert_element_type x19, other arithmetic, as_low(): return x.astype(jnp.bfloat16)  38.8 us
    dot_general x16, matrix products, contract_rows(): lax.dot_general(left, right, (((0,), (0,)), ((), ())), preferred_element_...  38.3 us
    dot_general x15, matrix products, contract_cols(): lax.dot_general(left, right, (((1,), (1,)), ((), ())), preferred_element_...  30.7 us
  transfers between devices with their start and end apart: 59, of which 29 were waited for; matrix products, arithmetic and copies ran while one was open for 36% of the time, Pallas kernels for 8%

profile of v1, /device:TPU:0, one launch (start us, length us, event | category | flops | bytes accessed | tf_op | source)
XLA Modules:
  0.0 728.3 jit_solution(3110631713259017119)
XLA Ops:
  11.1 4.0 collective-permute-start.1
  25.7 3.9 collective-permute-done.1
  33.7 3.2 collective-permute-start.7
  44.0 10.6 %collective-permute-done.7 = bf16[96,1024]{1,0:T(8,128)(2,1)S(1)} collective-permute-done((bf16[96,1024]{1,0:T(8,128)(2,1)S(1)}, bf16[96,1024]{1,0:T(8,128)(2,1)S(1)}, u32[]{:S(2)}, u32[]{:S(2)}) %collective-permute-start.7) | collective-permute-done | bytes 196640 | tf_op jit(solution)/shard_map/ppermute | solution.py:161
  62.3 9.2 %collective-permute-done.13 = bf16[96,1024]{1,0:T(8,128)(2,1)S(1)} collective-permute-done((bf16[96,1024]{1,0:T(8,128)(2,1)S(1)}, bf16[96,1024]{1,0:T(8,128)(2,1)S(1)}, u32[]{:S(2)}, u32[]{:S(2)}) %collective-permute-start.13) | collective-permute-done | bytes 196640 | tf_op jit(solution)/shard_map/ppermute | solution.py:161
  71.8 3.3 collective-permute-start.19
  81.8 5.3 collective-permute-done.19
  93.0 3.2 collective-permute-done.26
  97.8 12.7 %collective-permute-done.25 = bf16[128,1024]{1,0:T(8,128)(2,1)S(1)} collective-permute-done((bf16[128,1024]{1,0:T(8,128)(2,1)S(1)}, bf16[128,1024]{1,0:T(8,128)(2,1)S(1)}, u32[]{:S(2)}, u32[]{:S(2)}) %collective-permute-start.25) | collective-permute-done | bytes 262176 | tf_op jit(solution)/shard_map/ppermute | solution.py:161
  118.6 26.4 %collective-permute-done.27 = bf16[4,128,1024]{2,1,0:T(8,128)(2,1)S(1)} collective-permute-done((bf16[4,128,1024]{2,1,0:T(8,128)(2,1)S(1)}, bf16[4,128,1024]{2,1,0:T(8,128)(2,1)S(1)}, u32[]{:S(2)}, u32[]{:S(2)}) %collective-permute-start.27) | collective-permute-done | bytes 1048608 | tf_op jit(solution)/shard_map/ppermute | solution.py:161
  158.2 31.6 %collective-permute-done.10 = bf16[8,96,1024]{2,1,0:T(8,128)(2,1)} collective-permute-done((bf16[8,96,1024]{2,1,0:T(8,128)(2,1)}, bf16[8,96,1024]{2,1,0:T(8,128)(2,1)}, u32[]{:S(2)}, u32[]{:S(2)}) %collective-permute-start.10) | collective-permute-done | bytes 1572896 | tf_op jit(solution)/shard_map/ppermute | solution.py:161
  192.6 14.1 %collective-permute-done.16 = bf16[8,96,1024]{2,1,0:T(8,128)(2,1)} collective-permute-done((bf16[8,96,1024]{2,1,0:T(8,128)(2,1)}, bf16[8,96,1024]{2,1,0:T(8,128)(2,1)}, u32[]{:S(2)}, u32[]{:S(2)}) %collective-permute-start.16) | collective-permute-done | bytes 1572896 | tf_op jit(solution)/shard_map/ppermute | solution.py:161
  209.4 3.1 constant_dynamic-update-slice_fusion.49.far_ref
  218.4 8.9 %place.5 = (bf16[32,32,1024]{2,1,0:T(8,128)(2,1)S(1)}, bf16[32,64,1024]{2,1,0:T(8,128)(2,1)}) custom-call(s32[16]{0:T(128)S(1)} %multiply_add_fusion.13.own_ref, s32[16]{0:T(128)S(1)} %get-tuple-element.245.other_ref, bf16[16,96,1024]{2,1,0:T(8,128)(2,1)S(1)} %constant_dynamic-update-slice_fusion.5.far_ref, bf16[16,96,1024]{2,1,0:T(8,128)(2,1)} %collective-permute-done.5.core_ref), custom_call_target="tpu_custom_call" | custom-call | bytes 12582912 | tf_op jit(solution)/shard_map/place/pallas_call | solution.py:202
  240.8 4.7 place.6
  251.4 3.9 convolution_convert_fusion.20
  256.8 3.9 convolution_convert_fusion.18
  262.4 10.0 %fusion.134 = (f32[16,512]{1,0:T(8,128)S(1)}, f32[16,512,512]{1,2,0:T(8,128)}) fusion(f32[512,512]{0,1:T(8,128)} %abs_convert_fusion, f32[16]{0:T(128)S(1)} %copy-done.121, bf16[512,16,64]{0,2,1:T(8,128)(2,1)S(1)} %bitcast.351, bf16[512,16,64]{0,2,1:T(8,128)(2,1)S(1)} %bitcast.346, pred[512]{0:T(512)(128)(4,1)S(1)} %convert_compare_fusion), kind=kOutput, calls=%fused_computation.446 | convolution fusion | flops 557834240 | bytes 19956288 | tf_op jit(solution)/shard_map/qhd,khd->hqk/dot_general | solution.py:77
  272.3 8.3 %fusion = f32[16,512]{1,0:T(8,128)S(1)} fusion(f32[16,512,512]{1,2,0:T(8,128)} %get-tuple-element.360, f32[16,512]{1,0:T(8,128)S(1)} %get-tuple-element.359), kind=kLoop, calls=%fused_computation.6 | loop fusion | flops 8380416 | bytes 16842752 | tf_op jit(solution)/shard_map/reduce_sum | solution.py:466
  281.2 7.2 divide_convert_fusion
  291.8 5.1 place.7
  299.5 6.9 multiply_convert_fusion.7
  306.5 6.9 multiply_convert_fusion.6
  313.4 7.1 multiply_convert_fusion.5
  320.5 6.9 multiply_convert_fusion.4
  327.5 7.3 place.9
  334.8 8.0 %fusion.136 = (f32[512]{0:T(512)S(1)}, f32[512,1024]{1,0:T(8,128)S(1)}) fusion(f32[512,1024]{1,0:T(8,128)S(1)} %get-tuple-element.362, bf16[4096,1024]{1,0:T(8,128)(2,1)} %bitcast.317, bf16[512,1024]{1,0:T(8,128)(2,1)S(1)} %get-tuple-element.243, bf16[512,1024]{1,0:T(8,128)(2,1)S(1)} %get-tuple-element.241, bf16[512,1024]{1,0:T(8,128)(2,1)S(1)} %get-tuple-element.239, ...), kind=kOutput, calls=%fused_computation.448 | convolution fusion | flops 4312792576 | bytes 16779264 | tf_op jit(solution)/shard_map/dot_general | solution.py:33
  356.2 4.3 pad_maximum_fusion
  360.6 10.8 %pick.7 = bf16[16,128,1024]{2,1,0:T(8,128)(2,1)} custom-call(s32[16]{0:T(128)} %get-tuple-element.347.idx_ref, bf16[32,128,1024]{2,1,0:T(8,128)(2,1)} %bitcast.311), custom_call_target="tpu_custom_call" | custom-call | bytes 8388608 | tf_op jit(solution)/shard_map/pick/pallas_call | solution.py:228
  371.5 4.6 fusion.128
  388.0 2.8 convolution_convert_fusion.6
  400.2 7.5 %fold.4 = (bf16[8,128,1024]{2,1,0:T(8,128)(2,1)S(1)}, bf16[8,128,1024]{2,1,0:T(8,128)(2,1)}) custom-call(s32[16]{0:T(128)S(1)} %get-tuple-element.348.idx_ref, bf16[32,128,1024]{2,1,0:T(8,128)(2,1)} %bitcast.312, bf16[32,128,1024]{2,1,0:T(8,128)(2,1)} %bitcast.313, bf16[16,128,1024]{2,1,0:T(8,128)(2,1)} %copy-done.26, bf16[16,128,1024]{2,1,0:T(8,128)(2,1)} %copy-done.26), custom_call_target="tpu_custom_call" | custom-call | bytes 12582912 | tf_op jit(solution)/shard_map/fold/pallas_call | solution.py:268
  411.8 10.8 %pick.6 = bf16[16,128,1024]{2,1,0:T(8,128)(2,1)} custom-call(s32[16]{0:T(128)} %get-tuple-element.347.idx_ref, bf16[32,32,1024]{2,1,0:T(8,128)(2,1)} %bitcast.321, bf16[32,32,1024]{2,1,0:T(8,128)(2,1)} %bitcast.330, bf16[32,32,1024]{2,1,0:T(8,128)(2,1)} %bitcast.324, bf16[32,32,1024]{2,1,0:T(8,128)(2,1)} %bitcast.318), custom_call_target="tpu_custom_call" | custom-call | bytes 8388608 | tf_op jit(solution)/shard_map/pick/pallas_call | solution.py:228
  422.6 3.3 fusion.138
  430.0 4.0 collective-permute-done.31
  437.8 6.1 convolution_convert_fusion.14
  447.5 11.2 %multiply_reduce_fusion = (f32[16,512]{1,0:T(8,128)S(1)}, f32[16,512,512]{1,2,0:T(8,128)}) fusion(f32[16,512,512]{1,2,0:T(8,128)} %get-tuple-element.360, f32[16,512]{1,0:T(8,128)S(1)} %copy-done.82, bf16[512,16,64]{0,2,1:T(8,128)(2,1)S(1)} %bitcast.345, bf16[512,16,64]{0,2,1:T(8,128)(2,1)S(1)} %bitcast.343), kind=kOutput, calls=%fused_computation.1 | convolution fusion | flops 549445632 | bytes 35717120 | tf_op jit(solution)/shard_map/qhd,khd->hqk/dot_general | solution.py:523
  458.8 11.7 %multiply_convert_fusion = bf16[16,512,512]{1,2,0:T(8,128)(2,1)S(1)} fusion(f32[16,512,512]{1,2,0:T(8,128)} %get-tuple-element.371, f32[16,512,512]{1,2,0:T(8,128)} %get-tuple-element.360, f32[16,512]{1,0:T(8,128)S(1)} %get-tuple-element.370, f32[16,512]{1,0:T(8,128)S(1)} %copy-done.82), kind=kLoop, calls=%fused_computation | loop fusion | flops 16777216 | bytes 42008576 | tf_op jit(solution)/shard_map/convert_element_type | solution.py:29
  470.5 7.8 %fold.5 = (bf16[8,128,1024]{2,1,0:T(8,128)(2,1)S(1)}, bf16[8,128,1024]{2,1,0:T(8,128)(2,1)}) custom-call(s32[16]{0:T(128)S(1)} %get-tuple-element.348.idx_ref, bf16[32,32,1024]{2,1,0:T(8,128)(2,1)} %bitcast.322, bf16[32,32,1024]{2,1,0:T(8,128)(2,1)} %bitcast.323, bf16[32,32,1024]{2,1,0:T(8,128)(2,1)} %bitcast.331, bf16[32,32,1024]{2,1,0:T(8,128)(2,1)} %bitcast.332, ...), custom_call_target="tpu_custom_call" | custom-call | bytes 12582912 | tf_op jit(solution)/shard_map/fold/pallas_call | solution.py:268
  492.0 10.8 %pick.5 = bf16[16,128,1024]{2,1,0:T(8,128)(2,1)} custom-call(s32[16]{0:T(128)} %get-tuple-element.347.idx_ref, bf16[32,32,1024]{2,1,0:T(8,128)(2,1)} %bitcast.339, bf16[32,32,1024]{2,1,0:T(8,128)(2,1)} %bitcast.333, bf16[32,32,1024]{2,1,0:T(8,128)(2,1)} %bitcast.336, bf16[32,32,1024]{2,1,0:T(8,128)(2,1)} %bitcast.327), custom_call_target="tpu_custom_call" | custom-call | bytes 8388608 | tf_op jit(solution)/shard_map/pick/pallas_call | solution.py:228
  504.7 3.2 slice.318
  512.7 3.2 multiply_reduce_fusion.3
  517.9 8.0 %fold.6 = (bf16[8,128,1024]{2,1,0:T(8,128)(2,1)S(1)}, bf16[8,128,1024]{2,1,0:T(8,128)(2,1)}) custom-call(s32[16]{0:T(128)S(1)} %get-tuple-element.348.idx_ref, bf16[32,32,1024]{2,1,0:T(8,128)(2,1)} %bitcast.340, bf16[32,32,1024]{2,1,0:T(8,128)(2,1)} %bitcast.341, bf16[32,32,1024]{2,1,0:T(8,128)(2,1)} %bitcast.334, bf16[32,32,1024]{2,1,0:T(8,128)(2,1)} %bitcast.335, ...), custom_call_target="tpu_custom_call" | custom-call | bytes 12582912 | tf_op jit(solution)/shard_map/fold/pallas_call | solution.py:268
  531.9 3.7 add_convert_fusion.6
  537.9 2.9 fusion.39
  546.0 5.2 concatenate.123.refs_1_.refs_2_.refs_3_
  551.2 6.3 convolution_convert_fusion
  557.5 10.4 %pick.4 = bf16[16,96,1024]{2,1,0:T(8,128)(2,1)} custom-call(s32[16]{0:T(128)} %get-tuple-element.347.idx_ref, bf16[32,64,1024]{2,1,0:T(8,128)(2,1)} %bitcast.314, bf16[32,32,1024]{2,1,0:T(8,128)(2,1)} %concatenate.123.refs_1_.refs_2_.refs_3_), custom_call_target="tpu_custom_call" | custom-call | bytes 6291456 | tf_op jit(solution)/shard_map/pick/pallas_call | solution.py:228
  568.2 3.7 add_convert_fusion.1
  578.9 5.8 fold.7
  587.9 4.0 collective-permute-start.53
  594.4 14.6 %collective-permute-done.46 = bf16[4,128,1024]{2,1,0:T(8,128)(2,1)S(1)} collective-permute-done((bf16[4,128,1024]{2,1,0:T(8,128)(2,1)S(1)}, bf16[4,128,1024]{2,1,0:T(8,128)(2,1)S(1)}, u32[]{:S(2)}, u32[]{:S(2)}) %collective-permute-start.46) | collective-permute-done | bytes 1048608 | tf_op jit(solution)/shard_map/ppermute | solution.py:161
  610.4 3.8 collective-permute-start.49
  614.2 3.0 collective-permute-done.52
  618.0 3.5 collective-permute-done.47
  623.2 11.1 %collective-permute-done.48 = bf16[128,1024]{1,0:T(8,128)(2,1)S(1)} collective-permute-done((bf16[128,1024]{1,0:T(8,128)(2,1)S(1)}, bf16[128,1024]{1,0:T(8,128)(2,1)S(1)}, u32[]{:S(2)}, u32[]{:S(2)}) %collective-permute-start.48) | collective-permute-done | bytes 262176 | tf_op jit(solution)/shard_map/ppermute | solution.py:161
  636.4 3.8 collective-permute-start.45
  641.0 6.5 collective-permute-done.43
  649.3 9.5 %collective-permute-done.44 = bf16[128,1024]{1,0:T(8,128)(2,1)S(1)} collective-permute-done((bf16[128,1024]{1,0:T(8,128)(2,1)S(1)}, bf16[128,1024]{1,0:T(8,128)(2,1)S(1)}, u32[]{:S(2)}, u32[]{:S(2)}) %collective-permute-start.44) | collective-permute-done | bytes 262176 | tf_op jit(solution)/shard_map/ppermute | solution.py:161
  659.3 3.8 collective-permute-start.41
  664.5 4.6 collective-permute-done.39
  669.1 7.4 %collective-permute-done.40 = bf16[96,1024]{1,0:T(8,128)(2,1)S(1)} collective-permute-done((bf16[96,1024]{1,0:T(8,128)(2,1)S(1)}, bf16[96,1024]{1,0:T(8,128)(2,1)S(1)}, u32[]{:S(2)}, u32[]{:S(2)}) %collective-permute-start.40) | collective-permute-done | bytes 196640 | tf_op jit(solution)/shard_map/ppermute | solution.py:161
  697.0 3.0 collective-permute-done.57
  701.3 3.7 collective-permute-done.58
  (583 shorter events, 254.8 us)
Async XLA Ops:
  11.1 18.6 %collective-permute-start.1 = (bf16[96,1024]{1,0:T(8,128)(2,1)}, bf16[96,1024]{1,0:T(8,128)(2,1)}, u32[]{:S(2)}, u32[]{:S(2)}) collective-permute-start(bf16[96,1024]{1,0:T(8,128)(2,1)} %get-tuple-element.329), channel_id=1, source_target_pairs={{0,16},{1,17},{2,18},{3,19},{4,20},{5,21},{6,22},{7,23},{8,24},{9,... | collective-permute-start | bytes 589832 | tf_op jit(solution)/shard_map/ppermute | solution.py:161
  15.1 14.5 %collective-permute-start = (bf16[96,1024]{1,0:T(8,128)(2,1)}, bf16[96,1024]{1,0:T(8,128)(2,1)}, u32[]{:S(2)}, u32[]{:S(2)}) collective-permute-start(bf16[96,1024]{1,0:T(8,128)(2,1)} %get-tuple-element.329), channel_id=1, source_target_pairs={{0,8},{1,9},{2,10},{3,11},{4,12},{5,13},{6,14},{7,15},{8,16},{9,17... | collective-permute-start | bytes 589832 | tf_op jit(solution)/shard_map/ppermute | solution.py:161
  16.7 13.7 %collective-permute-start.2 = (bf16[96,1024]{1,0:T(8,128)(2,1)}, bf16[96,1024]{1,0:T(8,128)(2,1)}, u32[]{:S(2)}, u32[]{:S(2)}) collective-permute-start(bf16[96,1024]{1,0:T(8,128)(2,1)} %get-tuple-element.329), channel_id=1, source_target_pairs={{0,24},{1,25},{2,26},{3,27},{4,28},{5,29},{6,30},{7,31},{8,0},{9,1... | collective-permute-start | bytes 589832 | tf_op jit(solution)/shard_map/ppermute | solution.py:161
  31.5 12.5 %collective-permute-start.8 = (bf16[96,1024]{1,0:T(8,128)(2,1)S(1)}, bf16[96,1024]{1,0:T(8,128)(2,1)S(1)}, u32[]{:S(2)}, u32[]{:S(2)}) collective-permute-start(bf16[96,1024]{1,0:T(8,128)(2,1)S(1)} %pad_maximum_fusion.15), channel_id=1, source_target_pairs={{0,24},{1,25},{2,26},{3,27},{4,28},{5,29},{6,30},{7,31},{8,0},{9,1... | collective-permute-start | bytes 589832 | tf_op jit(solution)/shard_map/ppermute | solution.py:161
  33.7 20.9 %collective-permute-start.7 = (bf16[96,1024]{1,0:T(8,128)(2,1)S(1)}, bf16[96,1024]{1,0:T(8,128)(2,1)S(1)}, u32[]{:S(2)}, u32[]{:S(2)}) collective-permute-start(bf16[96,1024]{1,0:T(8,128)(2,1)S(1)} %pad_maximum_fusion.15), channel_id=1, source_target_pairs={{0,16},{1,17},{2,18},{3,19},{4,20},{5,21},{6,22},{7,23},{8,24},{9,... | collective-permute-start | bytes 589832 | tf_op jit(solution)/shard_map/ppermute | solution.py:161
  36.9 17.6 %collective-permute-start.6 = (bf16[96,1024]{1,0:T(8,128)(2,1)S(1)}, bf16[96,1024]{1,0:T(8,128)(2,1)S(1)}, u32[]{:S(2)}, u32[]{:S(2)}) collective-permute-start(bf16[96,1024]{1,0:T(8,128)(2,1)S(1)} %pad_maximum_fusion.15), channel_id=1, source_target_pairs={{0,8},{1,9},{2,10},{3,11},{4,12},{5,13},{6,14},{7,15},{8,16},{9,17... | collective-permute-start | bytes 589832 | tf_op jit(solution)/shard_map/ppermute | solution.py:161
  38.9 40.6 %collective-permute-start.3 = (bf16[4,96,1024]{2,1,0:T(8,128)(2,1)S(1)}, bf16[4,96,1024]{2,1,0:T(8,128)(2,1)S(1)}, u32[]{:S(2)}, u32[]{:S(2)}) collective-permute-start(bf16[4,96,1024]{2,1,0:T(8,128)(2,1)S(1)} %pad_maximum_fusion.5), channel_id=1, source_target_pairs={{0,4},{1,3},{2,6},{3,1},{4,0},{5,7},{6,2},{7,5},{8,12},{9,11},{10,... | collective-permute-start | bytes 2359304 | tf_op jit(solution)/shard_map/ppermute | solution.py:161
  54.7 7.6 %collective-permute-start.14 = (bf16[96,1024]{1,0:T(8,128)(2,1)S(1)}, bf16[96,1024]{1,0:T(8,128)(2,1)S(1)}, u32[]{:S(2)}, u32[]{:S(2)}) collective-permute-start(bf16[96,1024]{1,0:T(8,128)(2,1)S(1)} %pad_maximum_fusion.16), channel_id=1, source_target_pairs={{0,24},{1,25},{2,26},{3,27},{4,28},{5,29},{6,30},{7,31},{8,0},{9,1... | collective-permute-start | bytes 589832 | tf_op jit(solution)/shard_map/ppermute | solution.py:161
  54.8 16.7 %collective-permute-start.13 = (bf16[96,1024]{1,0:T(8,128)(2,1)S(1)}, bf16[96,1024]{1,0:T(8,128)(2,1)S(1)}, u32[]{:S(2)}, u32[]{:S(2)}) collective-permute-start(bf16[96,1024]{1,0:T(8,128)(2,1)S(1)} %pad_maximum_fusion.16), channel_id=1, source_target_pairs={{0,16},{1,17},{2,18},{3,19},{4,20},{5,21},{6,22},{7,23},{8,24},{9,... | collective-permute-start | bytes 589832 | tf_op jit(solution)/shard_map/ppermute | solution.py:161
  54.8 16.7 %collective-permute-start.12 = (bf16[96,1024]{1,0:T(8,128)(2,1)S(1)}, bf16[96,1024]{1,0:T(8,128)(2,1)S(1)}, u32[]{:S(2)}, u32[]{:S(2)}) collective-permute-start(bf16[96,1024]{1,0:T(8,128)(2,1)S(1)} %pad_maximum_fusion.16), channel_id=1, source_target_pairs={{0,8},{1,9},{2,10},{3,11},{4,12},{5,13},{6,14},{7,15},{8,16},{9,17... | collective-permute-start | bytes 589832 | tf_op jit(solution)/shard_map/ppermute | solution.py:161
  71.6 10.2 %collective-permute-start.20 = (bf16[64,1024]{1,0:T(8,128)(2,1)S(1)}, bf16[64,1024]{1,0:T(8,128)(2,1)S(1)}, u32[]{:S(2)}, u32[]{:S(2)}) collective-permute-start(bf16[64,1024]{1,0:T(8,128)(2,1)S(1)} %pad_maximum_fusion.17), channel_id=1, source_target_pairs={{0,24},{1,25},{2,26},{3,27},{4,28},{5,29},{6,30},{7,31},{8,0},{9,1... | collective-permute-start | bytes 393224 | tf_op jit(solution)/shard_map/ppermute | solution.py:161
  71.8 15.3 %collective-permute-start.19 = (bf16[64,1024]{1,0:T(8,128)(2,1)S(1)}, bf16[64,1024]{1,0:T(8,128)(2,1)S(1)}, u32[]{:S(2)}, u32[]{:S(2)}) collective-permute-start(bf16[64,1024]{1,0:T(8,128)(2,1)S(1)} %pad_maximum_fusion.17), channel_id=1, source_target_pairs={{0,16},{1,17},{2,18},{3,19},{4,20},{5,21},{6,22},{7,23},{8,24},{9,... | collective-permute-start | bytes 393224 | tf_op jit(solution)/shard_map/ppermute | solution.py:161
  75.1 12.0 %collective-permute-start.18 = (bf16[64,1024]{1,0:T(8,128)(2,1)S(1)}, bf16[64,1024]{1,0:T(8,128)(2,1)S(1)}, u32[]{:S(2)}, u32[]{:S(2)}) collective-permute-start(bf16[64,1024]{1,0:T(8,128)(2,1)S(1)} %pad_maximum_fusion.17), channel_id=1, source_target_pairs={{0,8},{1,9},{2,10},{3,11},{4,12},{5,13},{6,14},{7,15},{8,16},{9,17... | collective-permute-start | bytes 393224 | tf_op jit(solution)/shard_map/ppermute | solution.py:161
  79.6 36.2 %collective-permute-start.4 = (bf16[8,96,1024]{2,1,0:T(8,128)(2,1)S(1)}, bf16[8,96,1024]{2,1,0:T(8,128)(2,1)S(1)}, u32[]{:S(2)}, u32[]{:S(2)}) collective-permute-start(bf16[8,96,1024]{2,1,0:T(8,128)(2,1)S(1)} %get-tuple-element.277), channel_id=1, source_target_pairs={{0,2},{1,5},{2,0},{3,7},{4,6},{5,1},{6,4},{7,3},{8,10},{9,13},{10,... | collective-permute-start | bytes 4718600 | tf_op jit(solution)/shard_map/ppermute | solution.py:161
  87.2 9.0 %collective-permute-start.26 = (bf16[128,1024]{1,0:T(8,128)(2,1)S(1)}, bf16[128,1024]{1,0:T(8,128)(2,1)S(1)}, u32[]{:S(2)}, u32[]{:S(2)}) collective-permute-start(bf16[128,1024]{1,0:T(8,128)(2,1)S(1)} %convert_element_type.551), channel_id=1, source_target_pairs={{0,24},{1,25},{2,26},{3,27},{4,28},{5,29},{6,30},{7,31},{8,0},{9,1... | collective-permute-start | bytes 786440 | tf_op jit(solution)/shard_map/ppermute | solution.py:161
  87.3 23.2 %collective-permute-start.25 = (bf16[128,1024]{1,0:T(8,128)(2,1)S(1)}, bf16[128,1024]{1,0:T(8,128)(2,1)S(1)}, u32[]{:S(2)}, u32[]{:S(2)}) collective-permute-start(bf16[128,1024]{1,0:T(8,128)(2,1)S(1)} %convert_element_type.551), channel_id=1, source_target_pairs={{0,16},{1,17},{2,18},{3,19},{4,20},{5,21},{6,22},{7,23},{8,24},{9,... | collective-permute-start | bytes 786440 | tf_op jit(solution)/shard_map/ppermute | solution.py:161
  87.4 24.7 %collective-permute-start.24 = (bf16[128,1024]{1,0:T(8,128)(2,1)S(1)}, bf16[128,1024]{1,0:T(8,128)(2,1)S(1)}, u32[]{:S(2)}, u32[]{:S(2)}) collective-permute-start(bf16[128,1024]{1,0:T(8,128)(2,1)S(1)} %convert_element_type.551), channel_id=1, source_target_pairs={{0,8},{1,9},{2,10},{3,11},{4,12},{5,13},{6,14},{7,15},{8,16},{9,17... | collective-permute-start | bytes 786440 | tf_op jit(solution)/shard_map/ppermute | solution.py:161
  89.3 24.1 %collective-permute-start.21 = (bf16[4,64,1024]{2,1,0:T(8,128)(2,1)S(1)}, bf16[4,64,1024]{2,1,0:T(8,128)(2,1)S(1)}, u32[]{:S(2)}, u32[]{:S(2)}) collective-permute-start(bf16[4,64,1024]{2,1,0:T(8,128)(2,1)S(1)} %pad_maximum_fusion.9), channel_id=1, source_target_pairs={{0,4},{1,3},{2,6},{3,1},{4,0},{5,7},{6,2},{7,5},{8,12},{9,11},{10,... | collective-permute-start | bytes 1572872 | tf_op jit(solution)/shard_map/ppermute | solution.py:161
  96.2 51.9 %collective-permute-start.9 = (bf16[4,96,1024]{2,1,0:T(8,128)(2,1)S(1)}, bf16[4,96,1024]{2,1,0:T(8,128)(2,1)S(1)}, u32[]{:S(2)}, u32[]{:S(2)}) collective-permute-start(bf16[4,96,1024]{2,1,0:T(8,128)(2,1)S(1)} %pad_maximum_fusion.6), channel_id=1, source_target_pairs={{0,4},{1,3},{2,6},{3,1},{4,0},{5,7},{6,2},{7,5},{8,12},{9,11},{10,... | collective-permute-start | bytes 2359304 | tf_op jit(solution)/shard_map/ppermute | solution.py:161
  110.5 40.7 %collective-permute-start.15 = (bf16[4,96,1024]{2,1,0:T(8,128)(2,1)S(1)}, bf16[4,96,1024]{2,1,0:T(8,128)(2,1)S(1)}, u32[]{:S(2)}, u32[]{:S(2)}) collective-permute-start(bf16[4,96,1024]{2,1,0:T(8,128)(2,1)S(1)} %pad_maximum_fusion.7), channel_id=1, source_target_pairs={{0,4},{1,3},{2,6},{3,1},{4,0},{5,7},{6,2},{7,5},{8,12},{9,11},{10,... | collective-permute-start | bytes 2359304 | tf_op jit(solution)/shard_map/ppermute | solution.py:161
  112.2 32.8 %collective-permute-start.27 = (bf16[4,128,1024]{2,1,0:T(8,128)(2,1)S(1)}, bf16[4,128,1024]{2,1,0:T(8,128)(2,1)S(1)}, u32[]{:S(2)}, u32[]{:S(2)}) collective-permute-start(bf16[4,128,1024]{2,1,0:T(8,128)(2,1)S(1)} %pad_maximum_fusion.4), channel_id=1, source_target_pairs={{0,4},{1,3},{2,6},{3,1},{4,0},{5,7},{6,2},{7,5},{8,12},{9,11},{10,... | collective-permute-start | bytes 3145736 | tf_op jit(solution)/shard_map/ppermute | solution.py:161
  114.3 35.4 %collective-permute-start.22 = (bf16[8,64,1024]{2,1,0:T(8,128)(2,1)S(1)}, bf16[8,64,1024]{2,1,0:T(8,128)(2,1)S(1)}, u32[]{:S(2)}, u32[]{:S(2)}) collective-permute-start(bf16[8,64,1024]{2,1,0:T(8,128)(2,1)S(1)} %get-tuple-element.287), channel_id=1, source_target_pairs={{0,2},{1,5},{2,0},{3,7},{4,6},{5,1},{6,4},{7,3},{8,10},{9,13},{10,... | collective-permute-start | bytes 3145736 | tf_op jit(solution)/shard_map/ppermute | solution.py:161
  115.9 102.5 %collective-permute-start.5 = (bf16[16,96,1024]{2,1,0:T(8,128)(2,1)S(1)}, bf16[16,96,1024]{2,1,0:T(8,128)(2,1)}, u32[]{:S(2)}, u32[]{:S(2)}) collective-permute-start(bf16[16,96,1024]{2,1,0:T(8,128)(2,1)S(1)} %constant_dynamic-update-slice_fusion.5.far_ref), channel_id=1, source_target_pairs={{0,1},{1,0},{2,3},{3,2},{4,5},{5,4},{6,7},{7,6},{8,9},{9,8},{10,11... | collective-permute-start | bytes 9437192 | tf_op jit(solution)/shard_map/ppermute | solution.py:161
  146.7 62.7 %collective-permute-start.28 = (bf16[8,128,1024]{2,1,0:T(8,128)(2,1)}, bf16[8,128,1024]{2,1,0:T(8,128)(2,1)}, u32[]{:S(2)}, u32[]{:S(2)}) collective-permute-start(bf16[8,128,1024]{2,1,0:T(8,128)(2,1)} %get-tuple-element.271), channel_id=1, source_target_pairs={{0,2},{1,5},{2,0},{3,7},{4,6},{5,1},{6,4},{7,3},{8,10},{9,13},{10,... | collective-permute-start | bytes 6291464 | tf_op jit(solution)/shard_map/ppermute | solution.py:161
  149.2 40.7 %collective-permute-start.10 = (bf16[8,96,1024]{2,1,0:T(8,128)(2,1)}, bf16[8,96,1024]{2,1,0:T(8,128)(2,1)}, u32[]{:S(2)}, u32[]{:S(2)}) collective-permute-start(bf16[8,96,1024]{2,1,0:T(8,128)(2,1)} %get-tuple-element.275), channel_id=1, source_target_pairs={{0,2},{1,5},{2,0},{3,7},{4,6},{5,1},{6,4},{7,3},{8,10},{9,13},{10,... | collective-permute-start | bytes 4718600 | tf_op jit(solution)/shard_map/ppermute | solution.py:161
  151.2 61.8 %collective-permute-start.23 = (bf16[16,64,1024]{2,1,0:T(8,128)(2,1)}, bf16[16,64,1024]{2,1,0:T(8,128)(2,1)}, u32[]{:S(2)}, u32[]{:S(2)}) collective-permute-start(bf16[16,64,1024]{2,1,0:T(8,128)(2,1)} %constant_dynamic-update-slice_fusion.38.far_ref), channel_id=1, source_target_pairs={{0,1},{1,0},{2,3},{3,2},{4,5},{5,4},{6,7},{7,6},{8,9},{9,8},{10,11... | collective-permute-start | bytes 6291464 | tf_op jit(solution)/shard_map/ppermute | solution.py:161
  152.6 54.1 %collective-permute-start.16 = (bf16[8,96,1024]{2,1,0:T(8,128)(2,1)}, bf16[8,96,1024]{2,1,0:T(8,128)(2,1)}, u32[]{:S(2)}, u32[]{:S(2)}) collective-permute-start(bf16[8,96,1024]{2,1,0:T(8,128)(2,1)} %get-tuple-element.273), channel_id=1, source_target_pairs={{0,2},{1,5},{2,0},{3,7},{4,6},{5,1},{6,4},{7,3},{8,10},{9,13},{10,... | collective-permute-start | bytes 4718600 | tf_op jit(solution)/shard_map/ppermute | solution.py:161
  192.6 48.2 %collective-permute-start.11 = (bf16[16,96,1024]{2,1,0:T(8,128)(2,1)}, bf16[16,96,1024]{2,1,0:T(8,128)(2,1)}, u32[]{:S(2)}, u32[]{:S(2)}) collective-permute-start(bf16[16,96,1024]{2,1,0:T(8,128)(2,1)} %constant_dynamic-update-slice_fusion.16.far_ref), channel_id=1, source_target_pairs={{0,1},{1,0},{2,3},{3,2},{4,5},{5,4},{6,7},{7,6},{8,9},{9,8},{10,11... | collective-permute-start | bytes 9437192 | tf_op jit(solution)/shard_map/ppermute | solution.py:161
  209.4 82.5 %collective-permute-start.17 = (bf16[16,96,1024]{2,1,0:T(8,128)(2,1)}, bf16[16,96,1024]{2,1,0:T(8,128)(2,1)}, u32[]{:S(2)}, u32[]{:S(2)}) collective-permute-start(bf16[16,96,1024]{2,1,0:T(8,128)(2,1)} %constant_dynamic-update-slice_fusion.27.far_ref), channel_id=1, source_target_pairs={{0,1},{1,0},{2,3},{3,2},{4,5},{5,4},{6,7},{7,6},{8,9},{9,8},{10,11... | collective-permute-start | bytes 9437192 | tf_op jit(solution)/shard_map/ppermute | solution.py:161
  212.5 115.0 %collective-permute-start.29 = (bf16[16,128,1024]{2,1,0:T(8,128)(2,1)}, bf16[16,128,1024]{2,1,0:T(8,128)(2,1)}, u32[]{:S(2)}, u32[]{:S(2)}) collective-permute-start(bf16[16,128,1024]{2,1,0:T(8,128)(2,1)} %constant_dynamic-update-slice_fusion.49.far_ref), channel_id=1, source_target_pairs={{0,1},{1,0},{2,3},{3,2},{4,5},{5,4},{6,7},{7,6},{8,9},{9,8},{10,11... | collective-permute-start | bytes 12582920 | tf_op jit(solution)/shard_map/ppermute | solution.py:161
  240.2 58.6 %copy-start.88 = (f32[1,1024]{1,0:T(1,128)}, f32[1,1024]{1,0:T(1,128)S(1)}, u32[]{:S(2)}) copy-start(f32[1,1024]{1,0:T(1,128)S(1)} %get-tuple-element.341) | copy-start | bytes 12292
  371.4 26.7 %collective-permute-start.30 = (bf16[16,128,1024]{2,1,0:T(8,128)(2,1)}, bf16[16,128,1024]{2,1,0:T(8,128)(2,1)S(1)}, u32[]{:S(2)}, u32[]{:S(2)}) collective-permute-start(bf16[16,128,1024]{2,1,0:T(8,128)(2,1)} %pick.7), channel_id=1, source_target_pairs={{0,1},{1,0},{2,3},{3,2},{4,5},{5,4},{6,7},{7,6},{8,9},{9,8},{10,11... | collective-permute-start | bytes 12582920 | tf_op jit(solution)/shard_map/ppermute | solution.py:161
  407.7 26.4 %collective-permute-start.31 = (bf16[8,128,1024]{2,1,0:T(8,128)(2,1)}, bf16[8,128,1024]{2,1,0:T(8,128)(2,1)}, u32[]{:S(2)}, u32[]{:S(2)}) collective-permute-start(bf16[8,128,1024]{2,1,0:T(8,128)(2,1)} %get-tuple-element.68), channel_id=1, source_target_pairs={{0,2},{1,5},{2,0},{3,7},{4,6},{5,1},{6,4},{7,3},{8,10},{9,13},{10,... | collective-permute-start | bytes 6291464 | tf_op jit(solution)/shard_map/ppermute | solution.py:161
  434.0 36.4 %collective-permute-start.32 = (bf16[16,128,1024]{2,1,0:T(8,128)(2,1)}, bf16[16,128,1024]{2,1,0:T(8,128)(2,1)}, u32[]{:S(2)}, u32[]{:S(2)}) collective-permute-start(bf16[16,128,1024]{2,1,0:T(8,128)(2,1)} %pick.6), channel_id=1, source_target_pairs={{0,1},{1,0},{2,3},{3,2},{4,5},{5,4},{6,7},{7,6},{8,9},{9,8},{10,11... | collective-permute-start | bytes 12582920 | tf_op jit(solution)/shard_map/ppermute | solution.py:161
  478.3 26.4 %collective-permute-start.33 = (bf16[8,128,1024]{2,1,0:T(8,128)(2,1)}, bf16[8,128,1024]{2,1,0:T(8,128)(2,1)}, u32[]{:S(2)}, u32[]{:S(2)}) collective-permute-start(bf16[8,128,1024]{2,1,0:T(8,128)(2,1)} %get-tuple-element.70), channel_id=1, source_target_pairs={{0,2},{1,5},{2,0},{3,7},{4,6},{5,1},{6,4},{7,3},{8,10},{9,13},{10,... | collective-permute-start | bytes 6291464 | tf_op jit(solution)/shard_map/ppermute | solution.py:161
  504.7 11.1 %collective-permute-start.34 = (bf16[16,128,1024]{2,1,0:T(8,128)(2,1)}, bf16[16,128,1024]{2,1,0:T(8,128)(2,1)S(1)}, u32[]{:S(2)}, u32[]{:S(2)}) collective-permute-start(bf16[16,128,1024]{2,1,0:T(8,128)(2,1)} %pick.5), channel_id=1, source_target_pairs={{0,1},{1,0},{2,3},{3,2},{4,5},{5,4},{6,7},{7,6},{8,9},{9,8},{10,11... | collective-permute-start | bytes 12582920 | tf_op jit(solution)/shard_map/ppermute | solution.py:161
  527.3 40.6 %collective-permute-start.35 = (bf16[8,128,1024]{2,1,0:T(8,128)(2,1)}, bf16[8,128,1024]{2,1,0:T(8,128)(2,1)}, u32[]{:S(2)}, u32[]{:S(2)}) collective-permute-start(bf16[8,128,1024]{2,1,0:T(8,128)(2,1)} %get-tuple-element.72), channel_id=1, source_target_pairs={{0,2},{1,5},{2,0},{3,7},{4,6},{5,1},{6,4},{7,3},{8,10},{9,13},{10,... | collective-permute-start | bytes 6291464 | tf_op jit(solution)/shard_map/ppermute | solution.py:161
  567.9 9.3 %collective-permute-start.36 = (bf16[16,96,1024]{2,1,0:T(8,128)(2,1)}, bf16[16,96,1024]{2,1,0:T(8,128)(2,1)S(1)}, u32[]{:S(2)}, u32[]{:S(2)}) collective-permute-start(bf16[16,96,1024]{2,1,0:T(8,128)(2,1)} %pick.4), channel_id=1, source_target_pairs={{0,1},{1,0},{2,3},{3,2},{4,5},{5,4},{6,7},{7,6},{8,9},{9,8},{10,11... | collective-permute-start | bytes 9437192 | tf_op jit(solution)/shard_map/ppermute | solution.py:161
  571.8 15.7 %collective-permute-start.50 = (bf16[4,128,1024]{2,1,0:T(8,128)(2,1)}, bf16[4,128,1024]{2,1,0:T(8,128)(2,1)S(1)}, u32[]{:S(2)}, u32[]{:S(2)}) collective-permute-start(bf16[4,128,1024]{2,1,0:T(8,128)(2,1)} %get-tuple-element.252), channel_id=1, source_target_pairs={{0,4},{1,3},{2,6},{3,1},{4,0},{5,7},{6,2},{7,5},{8,12},{9,11},{10,... | collective-permute-start | bytes 3145736 | tf_op jit(solution)/shard_map/ppermute | solution.py:161
  575.8 33.2 %collective-permute-start.46 = (bf16[4,128,1024]{2,1,0:T(8,128)(2,1)S(1)}, bf16[4,128,1024]{2,1,0:T(8,128)(2,1)S(1)}, u32[]{:S(2)}, u32[]{:S(2)}) collective-permute-start(bf16[4,128,1024]{2,1,0:T(8,128)(2,1)S(1)} %get-tuple-element.254), channel_id=1, source_target_pairs={{0,4},{1,3},{2,6},{3,1},{4,0},{5,7},{6,2},{7,5},{8,12},{9,11},{10,... | collective-permute-start | bytes 3145736 | tf_op jit(solution)/shard_map/ppermute | solution.py:161
  584.7 49.8 %collective-permute-start.37 = (bf16[8,96,1024]{2,1,0:T(8,128)(2,1)S(1)}, bf16[8,96,1024]{2,1,0:T(8,128)(2,1)S(1)}, u32[]{:S(2)}, u32[]{:S(2)}) collective-permute-start(bf16[8,96,1024]{2,1,0:T(8,128)(2,1)S(1)} %get-tuple-element.75), channel_id=1, source_target_pairs={{0,2},{1,5},{2,0},{3,7},{4,6},{5,1},{6,4},{7,3},{8,10},{9,13},{10,... | collective-permute-start | bytes 4718600 | tf_op jit(solution)/shard_map/ppermute | solution.py:161
  587.8 22.5 %collective-permute-start.51 = (bf16[128,1024]{1,0:T(8,128)(2,1)S(1)}, bf16[128,1024]{1,0:T(8,128)(2,1)S(1)}, u32[]{:S(2)}, u32[]{:S(2)}) collective-permute-start(bf16[128,1024]{1,0:T(8,128)(2,1)S(1)} %get-tuple-element.259), channel_id=1, source_target_pairs={{0,8},{1,9},{2,10},{3,11},{4,12},{5,13},{6,14},{7,15},{8,16},{9,17... | collective-permute-start | bytes 786440 | tf_op jit(solution)/shard_map/ppermute | solution.py:161
  587.9 22.5 %collective-permute-start.53 = (bf16[128,1024]{1,0:T(8,128)(2,1)S(1)}, bf16[128,1024]{1,0:T(8,128)(2,1)S(1)}, u32[]{:S(2)}, u32[]{:S(2)}) collective-permute-start(bf16[128,1024]{1,0:T(8,128)(2,1)S(1)} %get-tuple-element.260), channel_id=1, source_target_pairs={{0,24},{1,25},{2,26},{3,27},{4,28},{5,29},{6,30},{7,31},{8,0},{9,1... | collective-permute-start | bytes 786440 | tf_op jit(solution)/shard_map/ppermute | solution.py:161
  591.9 25.3 %collective-permute-start.52 = (bf16[128,1024]{1,0:T(8,128)(2,1)S(1)}, bf16[128,1024]{1,0:T(8,128)(2,1)S(1)}, u32[]{:S(2)}, u32[]{:S(2)}) collective-permute-start(bf16[128,1024]{1,0:T(8,128)(2,1)S(1)} %get-tuple-element.261), channel_id=1, source_target_pairs={{0,16},{1,17},{2,18},{3,19},{4,20},{5,21},{6,22},{7,23},{8,24},{9,... | collective-permute-start | bytes 786440 | tf_op jit(solution)/shard_map/ppermute | solution.py:161
  609.0 27.0 %collective-permute-start.42 = (bf16[4,128,1024]{2,1,0:T(8,128)(2,1)S(1)}, bf16[4,128,1024]{2,1,0:T(8,128)(2,1)S(1)}, u32[]{:S(2)}, u32[]{:S(2)}) collective-permute-start(bf16[4,128,1024]{2,1,0:T(8,128)(2,1)S(1)} %get-tuple-element.256), channel_id=1, source_target_pairs={{0,4},{1,3},{2,6},{3,1},{4,0},{5,7},{6,2},{7,5},{8,12},{9,11},{10,... | collective-permute-start | bytes 3145736 | tf_op jit(solution)/shard_map/ppermute | solution.py:161
  610.3 11.2 %collective-permute-start.47 = (bf16[128,1024]{1,0:T(8,128)(2,1)S(1)}, bf16[128,1024]{1,0:T(8,128)(2,1)S(1)}, u32[]{:S(2)}, u32[]{:S(2)}) collective-permute-start(bf16[128,1024]{1,0:T(8,128)(2,1)S(1)} %get-tuple-element.262), channel_id=1, source_target_pairs={{0,8},{1,9},{2,10},{3,11},{4,12},{5,13},{6,14},{7,15},{8,16},{9,17... | collective-permute-start | bytes 786440 | tf_op jit(solution)/shard_map/ppermute | solution.py:161
  610.4 12.8 %collective-permute-start.49 = (bf16[128,1024]{1,0:T(8,128)(2,1)S(1)}, bf16[128,1024]{1,0:T(8,128)(2,1)S(1)}, u32[]{:S(2)}, u32[]{:S(2)}) collective-permute-start(bf16[128,1024]{1,0:T(8,128)(2,1)S(1)} %get-tuple-element.263), channel_id=1, source_target_pairs={{0,24},{1,25},{2,26},{3,27},{4,28},{5,29},{6,30},{7,31},{8,0},{9,1... | collective-permute-start | bytes 786440 | tf_op jit(solution)/shard_map/ppermute | solution.py:161
  617.2 17.1 %collective-permute-start.48 = (bf16[128,1024]{1,0:T(8,128)(2,1)S(1)}, bf16[128,1024]{1,0:T(8,128)(2,1)S(1)}, u32[]{:S(2)}, u32[]{:S(2)}) collective-permute-start(bf16[128,1024]{1,0:T(8,128)(2,1)S(1)} %get-tuple-element.264), channel_id=1, source_target_pairs={{0,16},{1,17},{2,18},{3,19},{4,20},{5,21},{6,22},{7,23},{8,24},{9,... | collective-permute-start | bytes 786440 | tf_op jit(solution)/shard_map/ppermute | solution.py:161
  635.2 23.8 %collective-permute-start.38 = (bf16[4,96,1024]{2,1,0:T(8,128)(2,1)S(1)}, bf16[4,96,1024]{2,1,0:T(8,128)(2,1)S(1)}, u32[]{:S(2)}, u32[]{:S(2)}) collective-permute-start(bf16[4,96,1024]{2,1,0:T(8,128)(2,1)S(1)} %get-tuple-element.258), channel_id=1, source_target_pairs={{0,4},{1,3},{2,6},{3,1},{4,0},{5,7},{6,2},{7,5},{8,12},{9,11},{10,... | collective-permute-start | bytes 2359304 | tf_op jit(solution)/shard_map/ppermute | solution.py:161
  636.3 11.2 %collective-permute-start.43 = (bf16[128,1024]{1,0:T(8,128)(2,1)S(1)}, bf16[128,1024]{1,0:T(8,128)(2,1)S(1)}, u32[]{:S(2)}, u32[]{:S(2)}) collective-permute-start(bf16[128,1024]{1,0:T(8,128)(2,1)S(1)} %get-tuple-element.265), channel_id=1, source_target_pairs={{0,8},{1,9},{2,10},{3,11},{4,12},{5,13},{6,14},{7,15},{8,16},{9,17... | collective-permute-start | bytes 786440 | tf_op jit(solution)/shard_map/ppermute | solution.py:161
  636.4 12.9 %collective-permute-start.45 = (bf16[128,1024]{1,0:T(8,128)(2,1)S(1)}, bf16[128,1024]{1,0:T(8,128)(2,1)S(1)}, u32[]{:S(2)}, u32[]{:S(2)}) collective-permute-start(bf16[128,1024]{1,0:T(8,128)(2,1)S(1)} %get-tuple-element.266), channel_id=1, source_target_pairs={{0,24},{1,25},{2,26},{3,27},{4,28},{5,29},{6,30},{7,31},{8,0},{9,1... | collective-permute-start | bytes 786440 | tf_op jit(solution)/shard_map/ppermute | solution.py:161
  640.2 18.6 %collective-permute-start.44 = (bf16[128,1024]{1,0:T(8,128)(2,1)S(1)}, bf16[128,1024]{1,0:T(8,128)(2,1)S(1)}, u32[]{:S(2)}, u32[]{:S(2)}) collective-permute-start(bf16[128,1024]{1,0:T(8,128)(2,1)S(1)} %get-tuple-element.267), channel_id=1, source_target_pairs={{0,16},{1,17},{2,18},{3,19},{4,20},{5,21},{6,22},{7,23},{8,24},{9,... | collective-permute-start | bytes 786440 | tf_op jit(solution)/shard_map/ppermute | solution.py:161
  659.3 54.7 %copy-start.74 = (f32[32,1024]{1,0:T(8,128)S(1)}, f32[32,1024]{1,0:T(8,128)}, u32[]{:S(2)}) copy-start(f32[32,1024]{1,0:T(8,128)} %param.49) | copy-start | bytes 393220
  659.3 9.8 %collective-permute-start.39 = (bf16[96,1024]{1,0:T(8,128)(2,1)S(1)}, bf16[96,1024]{1,0:T(8,128)(2,1)S(1)}, u32[]{:S(2)}, u32[]{:S(2)}) collective-permute-start(bf16[96,1024]{1,0:T(8,128)(2,1)S(1)} %get-tuple-element.268), channel_id=1, source_target_pairs={{0,8},{1,9},{2,10},{3,11},{4,12},{5,13},{6,14},{7,15},{8,16},{9,17... | collective-permute-start | bytes 589832 | tf_op jit(solution)/shard_map/ppermute | solution.py:161
  659.3 9.8 %collective-permute-start.41 = (bf16[96,1024]{1,0:T(8,128)(2,1)S(1)}, bf16[96,1024]{1,0:T(8,128)(2,1)S(1)}, u32[]{:S(2)}, u32[]{:S(2)}) collective-permute-start(bf16[96,1024]{1,0:T(8,128)(2,1)S(1)} %get-tuple-element.269), channel_id=1, source_target_pairs={{0,24},{1,25},{2,26},{3,27},{4,28},{5,29},{6,30},{7,31},{8,0},{9,1... | collective-permute-start | bytes 589832 | tf_op jit(solution)/shard_map/ppermute | solution.py:161
  663.1 54.1 %copy-start.79 = (f32[672,32]{0,1:T(8,128)S(1)}, f32[672,32]{0,1:T(8,128)}, u32[]{:S(2)}) copy-start(f32[672,32]{0,1:T(8,128)} %param.45) | copy-start | bytes 258052
  663.1 13.4 %collective-permute-start.40 = (bf16[96,1024]{1,0:T(8,128)(2,1)S(1)}, bf16[96,1024]{1,0:T(8,128)(2,1)S(1)}, u32[]{:S(2)}, u32[]{:S(2)}) collective-permute-start(bf16[96,1024]{1,0:T(8,128)(2,1)S(1)} %get-tuple-element.270), channel_id=1, source_target_pairs={{0,16},{1,17},{2,18},{3,19},{4,20},{5,21},{6,22},{7,23},{8,24},{9,... | collective-permute-start | bytes 589832 | tf_op jit(solution)/shard_map/ppermute | solution.py:161
  663.8 55.1 %copy-start.63 = (f32[64,1024]{1,0:T(8,128)S(1)}, f32[64,1024]{1,0:T(8,128)}, u32[]{:S(2)}) copy-start(f32[64,1024]{1,0:T(8,128)} %param.47) | copy-start | bytes 786436
  663.8 55.1 %copy-start.83 = (f32[64,1024]{1,0:T(8,128)S(1)}, f32[64,1024]{1,0:T(8,128)}, u32[]{:S(2)}) copy-start(f32[64,1024]{1,0:T(8,128)} %param.56) | copy-start | bytes 786436
  685.9 1.1 collective-permute-start.54
  687.6 3.8 collective-permute-start.55
  692.1 3.6 collective-permute-start.56
  696.3 3.6 collective-permute-start.57
  700.5 4.4 collective-permute-start.58
  (134 other events, 829.2 us)

commit v2 on v1

v2 whole, which is shorter than its diff:
```python
from functools import partial
import math

import jax
import jax.numpy as jnp
from jax import lax
from jax.experimental import pallas as pl
from jax.experimental.pallas import tpu as pltpu
from jax.sharding import PartitionSpec as P

HD = 64
SPK = 16
STEP = 10


SIGMA = 1e-05
NORM_EPS = 1e-05
LEARN_RATE = 0.01
GAIN_RATE = 0.3
BETA_ONE = 0.5
BETA_TWO = 0.5
DECAY = 0.01
ADAM_EPS = 1e-08
FAR_AWAY = -1e30
VMEM = 56 * 1024 * 1024
TABLE_AT = 768
HEAD_AT = 896


def as_low(x):
    return x.astype(jnp.bfloat16)


def contract_rows(left, right):
    return lax.dot_general(
        left, right, (((0,), (0,)), ((), ())), preferred_element_type=jnp.float32
    )


def time_features(flow, width):
    half = width // 2
    freqs = jnp.exp(-math.log(10000.0) * jnp.arange(half, dtype=jnp.float32) / half)
    angle = 1000.0 * flow * freqs
    return jnp.concatenate([jnp.sin(angle), jnp.cos(angle)])


def normalize(x):
    centered = x - jnp.mean(x, -1, keepdims=True)
    inverse = lax.rsqrt(jnp.mean(centered * centered, -1, keepdims=True) + NORM_EPS)
    return (centered * inverse, inverse)


def normalize_back(grad, normed, inverse):
    return inverse * (
        grad
        - jnp.mean(grad, -1, keepdims=True)
        - normed * jnp.mean(grad * normed, -1, keepdims=True)
    )


def head_slopes(heads):
    return 2.0 ** (-8.0 * (jnp.arange(heads, dtype=jnp.float32) + 1.0) / heads)


def adam_step(master, grad, moment, square, rate):
    moment = BETA_ONE * moment + (1.0 - BETA_ONE) * grad
    square = BETA_TWO * square + (1.0 - BETA_TWO) * grad * grad
    moment_hat = moment / (1.0 - BETA_ONE**STEP)
    square_hat = square / (1.0 - BETA_TWO**STEP)
    master = master - rate * (moment_hat / (jnp.sqrt(square_hat) + ADAM_EPS) + DECAY * master)
    return (master, moment, square)


AXES = ("wide", "narrow")


def grid_sizes(wide, narrow):
    low = 1
    while (2 * low) * (2 * low) <= wide:
        low *= 2
    return (wide // low, low, narrow // 2, 2)


class Grid:
    def __init__(self, mesh):
        self.sizes = grid_sizes(mesh.shape["wide"], mesh.shape["narrow"])
        self.total = mesh.shape["wide"] * mesh.shape["narrow"]

    def coords(self, index):
        out = []
        for size in reversed(self.sizes):
            out.append(index % size)
            index = index // size
        return out[::-1]

    def index(self, coords):
        index = 0
        for size, value in zip(self.sizes, coords):
            index = index * size + value
        return index

    def mixed(self):
        return self.sizes[1] == self.sizes[2]

    def axis(self, role, core):
        if role == "z":
            return 0
        if role == "core":
            return 3
        if self.mixed():
            return (2, 1)[core] if role == "far" else (1, 2)[core]
        return 2 if role == "far" else 1

    def size(self, role):
        return self.sizes[self.axis(role, 0)]

    def pairs(self, role, step):
        out = []
        for source in range(self.total):
            coords = self.coords(source)
            axis = self.axis(role, coords[3])
            coords[axis] = (coords[axis] + step) % self.sizes[axis]
            out.append((source, self.index(coords)))
        return out

    def lines(self):
        deep = self.total // self.sizes[0]
        return [[z * deep + rest for z in range(self.sizes[0])] for rest in range(deep)]

    def owners(self, core_step, direction):
        me = self.coords(lax.axis_index(AXES))
        core = (me[3] + core_step) % 2
        far, near, deep = (self.size(r) for r in ("far", "near", "z"))
        f, n, z = jnp.meshgrid(jnp.arange(far), jnp.arange(near), jnp.arange(deep), indexing="ij")
        if self.mixed():
            y = jnp.where(core == 0, me[1] + direction * n, me[1] + direction * f) % self.sizes[1]
            x = jnp.where(core == 0, me[2] + direction * f, me[2] + direction * n) % self.sizes[2]
        else:
            y = (me[1] + direction * n) % self.sizes[1]
            x = (me[2] + direction * f) % self.sizes[2]
        return self.index((z, y, x, core)).reshape(-1).astype(jnp.int32)


def shift(grid, x, role, step):
    return lax.ppermute(x, AXES, grid.pairs(role, step))


def tied(x, *others):
    return lax.optimization_barrier((x,) + others)[0]


def swap_deep(grid, x):
    return lax.all_to_all(x, AXES, 0, 0, axis_index_groups=grid.lines())


def join(*xs):
    return lax.optimization_barrier(xs)


def spread(grid, x, role):
    return [x] + [shift(grid, x, role, step) for step in range(1, grid.size(role))]


def all_sum(grid, x):
    step = 1
    while step < grid.total:
        x = x + lax.ppermute(x, AXES, [(i, i ^ step) for i in range(grid.total)])
        step *= 2
    return x


def dot_nn(a, b):
    return lax.dot_general(a, b, (((1,), (0,)), ((), ())), preferred_element_type=jnp.float32)


def dot_nt(a, b):
    return lax.dot_general(a, b, (((1,), (1,)), ((), ())), preferred_element_type=jnp.float32)


def dot_tn(a, b):
    return lax.dot_general(a, b, (((0,), (0,)), ((), ())), preferred_element_type=jnp.float32)


def params():
    return pltpu.CompilerParams(vmem_limit_bytes=VMEM)


def key_bias(length, frames):
    key = lax.broadcasted_iota(jnp.int32, (frames, frames), 0)
    query = lax.broadcasted_iota(jnp.int32, (frames, frames), 1)
    dist = -jnp.abs(key - query).astype(jnp.float32)
    return jnp.where(key < length, dist, FAR_AWAY)


def attend_kernel(length_ref, slope_ref, packed_ref, mixed_ref, lse_ref, bias_ref):
    step = pl.program_id(0)
    q_ref, k_ref, v_ref = (packed_ref.at[j] for j in range(3))
    frames = q_ref.shape[0]

    @pl.when(step == 0)
    def _():
        bias_ref[...] = key_bias(length_ref[0], frames)

    parts = []
    for h in range(2):
        lanes = slice(h * HD, (h + 1) * HD)
        scores = dot_nt(k_ref[:, lanes], q_ref[:, lanes] * jnp.bfloat16(HD**-0.5))
        scores = scores + slope_ref[2 * step + h] * bias_ref[...]
        top = jnp.max(scores, 0, keepdims=True)
        expo = jnp.exp(scores - top)
        total = jnp.sum(expo, 0, keepdims=True)
        lse_ref[0, h : h + 1] = top + jnp.log(total)
        probs = as_low(expo * (1.0 / total))
        parts.append(dot_tn(v_ref[:, lanes], probs))
    mixed_ref[...] = as_low(jnp.concatenate(parts, 0).T)


def attend(length, slopes, packed):
    _, frames, width = packed.shape
    pairs = width // (2 * HD)
    block = pl.BlockSpec((frames, 2 * HD), lambda i: (0, i))
    return pl.pallas_call(
        attend_kernel,
        grid=(pairs,),
        in_specs=[pl.BlockSpec(memory_space=pltpu.SMEM)] * 2
        + [pl.BlockSpec((3, frames, 2 * HD), lambda i: (0, 0, i))],
        out_specs=[block, pl.BlockSpec((1, 2, frames), lambda i: (i, 0, 0))],
        out_shape=[
            jax.ShapeDtypeStruct((frames, width), jnp.bfloat16),
            jax.ShapeDtypeStruct((pairs, 2, frames), jnp.float32),
        ],
        scratch_shapes=[pltpu.VMEM((frames, frames), jnp.float32)],
        compiler_params=params(),
        name="attend",
    )(length, slopes, packed)


def attend_back_kernel(length_ref, slope_ref, packed_ref, d_ref, lse_ref, out_ref, bias_ref):
    step = pl.program_id(0)
    q_ref, k_ref, v_ref = (packed_ref.at[j] for j in range(3))
    frames = q_ref.shape[0]

    @pl.when(step == 0)
    def _():
        bias_ref[...] = key_bias(length_ref[0], frames)

    d_query, d_keys, d_values = [], [], []
    for h in range(2):
        lanes = slice(h * HD, (h + 1) * HD)
        query = q_ref[:, lanes] * jnp.bfloat16(HD**-0.5)
        keys, values, d_mixed = k_ref[:, lanes], v_ref[:, lanes], d_ref[:, lanes]
        scores = dot_nt(keys, query) + slope_ref[2 * step + h] * bias_ref[...]
        probs = jnp.exp(scores - lse_ref[0, h : h + 1])
        d_probs = dot_nt(values, d_mixed)
        row_dot = jnp.sum(d_probs * probs, 0, keepdims=True)
        d_scores = as_low(probs * (d_probs - row_dot))
        d_values.append(dot_nn(as_low(probs), d_mixed))
        d_keys.append(dot_nn(d_scores, query))
        d_query.append(dot_tn(keys, d_scores))
    out_ref[0] = as_low((jnp.concatenate(d_query, 0) * HD**-0.5).T)
    out_ref[1] = as_low(jnp.concatenate(d_keys, 1))
    out_ref[2] = as_low(jnp.concatenate(d_values, 1))


def attend_back(length, slopes, packed, d_mixed, lse):
    _, frames, width = packed.shape
    pairs = width // (2 * HD)
    stacked = pl.BlockSpec((3, frames, 2 * HD), lambda i: (0, 0, i))
    return pl.pallas_call(
        attend_back_kernel,
        grid=(pairs,),
        in_specs=[pl.BlockSpec(memory_space=pltpu.SMEM)] * 2
        + [stacked, pl.BlockSpec((frames, 2 * HD), lambda i: (0, i))]
        + [pl.BlockSpec((1, 2, frames), lambda i: (i, 0, 0))],
        out_specs=stacked,
        out_shape=jax.ShapeDtypeStruct((3, frames, width), jnp.bfloat16),
        scratch_shapes=[pltpu.VMEM((frames, frames), jnp.float32)],
        compiler_params=params(),
        name="attend_back",
    )(length, slopes, packed, d_mixed, lse)


def gelu_both(x):
    z = jnp.abs(x) * (0.5**0.5)
    bell = jnp.exp(-z * z)
    t = 1.0 / (1.0 + 0.3275911 * z)
    poly = t * (0.254829592 + t * (-0.284496736 + t * (1.421413741 + t * (-1.453152027 + t * 1.061405429))))
    tail = 0.5 * poly * bell
    share = jnp.where(x >= 0, 1.0 - tail, tail)
    return x * share, share + x * bell * (0.5 / math.pi) ** 0.5


def expand_kernel(x_ref, w_ref, act_ref, turned_ref, slope_ref):
    hidden = dot_nn(x_ref[...], w_ref[0])
    act, slope = gelu_both(hidden)
    act = as_low(act)
    act_ref[...] = act
    turned_ref[...] = act.T
    slope_ref[...] = as_low(slope)


def expand(x, w, tile=1024):
    frames, width = x.shape
    count, _, wide = w.shape
    per = wide // tile
    total = count * wide
    return pl.pallas_call(
        expand_kernel,
        grid=(count * per,),
        in_specs=[
            pl.BlockSpec((frames, width), lambda i: (0, 0)),
            pl.BlockSpec((1, width, tile), lambda i: (i // per, 0, i % per)),
        ],
        out_specs=[
            pl.BlockSpec((frames, tile), lambda i: (0, i)),
            pl.BlockSpec((tile, frames), lambda i: (i, 0)),
            pl.BlockSpec((frames, tile), lambda i: (0, i)),
        ],
        out_shape=[
            jax.ShapeDtypeStruct((frames, total), jnp.bfloat16),
            jax.ShapeDtypeStruct((total, frames), jnp.bfloat16),
            jax.ShapeDtypeStruct((frames, total), jnp.bfloat16),
        ],
        compiler_params=params(),
        name="expand",
    )(x, w)


def front_kernel(
    small_ref, table_ref, skip_ref, states_ref, hot_ref, mel_ref, time_ref, gain_ref,
    embed_ref, stream_ref, start_ref, normed_ref, turned_ref,
):
    phones = embed_ref.shape[1]
    width = stream_ref.shape[1]
    embedded = as_low(dot_nt(hot_ref[...], table_ref[...]))
    embed_ref[...] = embedded
    start = dot_nt(embedded, small_ref[:, :phones])
    start = start + dot_nt(mel_ref[...], small_ref[:, phones:TABLE_AT]) + time_ref[...]
    start = as_low(start)
    start_ref[...] = start.T
    stream = dot_nn(start, skip_ref[:width]) + dot_nn(states_ref[...], skip_ref[width:])
    stream_ref[...] = stream
    normed = as_low(normalize(stream)[0] * gain_ref[...])
    normed_ref[...] = normed
    turned_ref[...] = normed.T


def front(small, table, skip, states, hot, mel, time, gain):
    frames, width = states.shape
    phones = table.shape[0]
    f32, low = jnp.float32, jnp.bfloat16
    return pl.pallas_call(
        front_kernel,
        out_shape=[
            jax.ShapeDtypeStruct((frames, phones), low),
            jax.ShapeDtypeStruct((frames, width), f32),
            jax.ShapeDtypeStruct((width, frames), low),
            jax.ShapeDtypeStruct((frames, width), low),
            jax.ShapeDtypeStruct((width, frames), low),
        ],
        compiler_params=params(),
        name="front",
    )(small, table, skip, states, hot, mel, time, gain)


def pack_kernel(x_ref, w_ref, out_ref):
    out_ref[0] = as_low(dot_nn(x_ref[...], w_ref[0]))


def pack(x, w):
    frames, width = x.shape
    return pl.pallas_call(
        pack_kernel,
        grid=(w.shape[0],),
        in_specs=[
            pl.BlockSpec((frames, width), lambda i: (0, 0)),
            pl.BlockSpec((1, width, width), lambda i: (i, 0, 0)),
        ],
        out_specs=pl.BlockSpec((1, frames, width), lambda i: (i, 0, 0)),
        out_shape=jax.ShapeDtypeStruct((w.shape[0], frames, width), jnp.bfloat16),
        compiler_params=params(),
        name="pack",
    )(x, w)


def mid_kernel(mixed_ref, w_ref, stream_ref, gain_ref, mid_ref, in_ref, turned_ref, mixed_turned_ref):
    mixed = mixed_ref[...]
    mid = stream_ref[...] + dot_nn(mixed, w_ref[...])
    mid_ref[...] = mid
    normed = as_low(normalize(mid)[0] * gain_ref[...])
    in_ref[...] = normed
    turned_ref[...] = normed.T
    mixed_turned_ref[...] = mixed.T


def mid_step(mixed, w, stream, gain):
    frames, width = stream.shape
    low = jnp.bfloat16
    return pl.pallas_call(
        mid_kernel,
        out_shape=[
            jax.ShapeDtypeStruct((frames, width), jnp.float32),
            jax.ShapeDtypeStruct((frames, width), low),
            jax.ShapeDtypeStruct((width, frames), low),
            jax.ShapeDtypeStruct((width, frames), low),
        ],
        compiler_params=params(),
        name="mid",
    )(mixed, w, stream, gain)


def head_kernel(
    share_ref, act_ref, w_ref, mid_ref, head_ref, target_ref, inside_ref, gain_ref,
    d_ref, low_ref, grad_ref, gain_grad_ref, error_ref, total_ref,
):
    step = pl.program_id(0)
    part = dot_nn(act_ref[...], w_ref[...])

    @pl.when(step == 0)
    def _():
        total_ref[...] = mid_ref[...] + part

    @pl.when(step > 0)
    def _():
        total_ref[...] += part

    @pl.when(step == pl.num_programs(0) - 1)
    def _():
        bins = target_ref.shape[1]
        normed, inverse = normalize(total_ref[...])
        gain = gain_ref[...]
        head_in = as_low(normed * gain)
        head = head_ref[:, :bins]
        inside = inside_ref[...]
        error = dot_nn(head_in, head) - target_ref[...]
        error_ref[...] = jnp.sum(jnp.sum(error * error, 1, keepdims=True) * inside, 0, keepdims=True)
        d_prediction = as_low((2.0 * share_ref[0]) * error * inside)
        grad_ref[...] = dot_tn(head_in, d_prediction)
        d_head_in = dot_nt(d_prediction, head)
        gain_grad_ref[...] = jnp.sum(d_head_in * normed, 0, keepdims=True)
        d_stream = normalize_back(d_head_in * gain, normed, inverse)
        d_ref[...] = d_stream
        low_ref[...] = as_low(d_stream)


def head_step(share, act, w, mid, head, target, inside, gain, tile=1024):
    frames, width = mid.shape
    bins = target.shape[1]
    whole = lambda *shape: pl.BlockSpec(shape, lambda i: (0,) * len(shape))
    return pl.pallas_call(
        head_kernel,
        grid=(act.shape[1] // tile,),
        in_specs=[
            pl.BlockSpec(memory_space=pltpu.SMEM),
            pl.BlockSpec((frames, tile), lambda i: (0, i)),
            pl.BlockSpec((tile, width), lambda i: (i, 0)),
            whole(frames, width), whole(*head.shape), whole(frames, bins), whole(frames, 1), whole(1, width),
        ],
        out_specs=[
            whole(frames, width), whole(frames, width), whole(width, bins), whole(1, width), whole(1, 1),
        ],
        out_shape=[
            jax.ShapeDtypeStruct((frames, width), jnp.float32),
            jax.ShapeDtypeStruct((frames, width), jnp.bfloat16),
            jax.ShapeDtypeStruct((width, bins), jnp.float32),
            jax.ShapeDtypeStruct((1, width), jnp.float32),
            jax.ShapeDtypeStruct((1, 1), jnp.float32),
        ],
        scratch_shapes=[pltpu.VMEM((frames, width), jnp.float32)],
        compiler_params=params(),
        name="head",
    )(share, act, w, mid, head, target, inside, gain)


def ffn_back_kernel(
    low_ref, d_ref, down_ref, slope_ref, up_ref, mid_ref, gain_ref,
    out_ref, out_low_ref, gain_grad_ref, hidden_ref, total_ref,
):
    step = pl.program_id(0)
    d_hidden = as_low(dot_nt(low_ref[...], down_ref[...]) * slope_ref[...].astype(jnp.float32))
    hidden_ref[0] = d_hidden
    part = dot_nt(d_hidden, up_ref[0])

    @pl.when(step == 0)
    def _():
        total_ref[...] = part

    @pl.when(step > 0)
    def _():
        total_ref[...] += part

    @pl.when(step == pl.num_programs(0) - 1)
    def _():
        normed, inverse = normalize(mid_ref[...])
        grad = total_ref[...]
        gain_grad_ref[...] = jnp.sum(grad * normed, 0, keepdims=True)
        out = d_ref[...] + normalize_back(grad * gain_ref[...], normed, inverse)
        out_ref[...] = out
        out_low_ref[...] = as_low(out)


def ffn_back(low, d, down, slope, up, mid, gain):
    frames, width = mid.shape
    count = up.shape[0]
    whole = lambda *shape: pl.BlockSpec(shape, lambda i: (0,) * len(shape))
    return pl.pallas_call(
        ffn_back_kernel,
        grid=(count,),
        in_specs=[
            whole(frames, width), whole(frames, width),
            pl.BlockSpec((width, width), lambda i: (i, 0)),
            pl.BlockSpec((frames, width), lambda i: (0, i)),
            pl.BlockSpec((1, width, width), lambda i: (i, 0, 0)),
            whole(frames, width), whole(1, width),
        ],
        out_specs=[whole(frames, width), whole(frames, width), whole(1, width)]
        + [pl.BlockSpec((1, frames, width), lambda i: (i, 0, 0))],
        out_shape=[
            jax.ShapeDtypeStruct((frames, width), jnp.float32),
            jax.ShapeDtypeStruct((frames, width), jnp.bfloat16),
            jax.ShapeDtypeStruct((1, width), jnp.float32),
        ]
        + [jax.ShapeDtypeStruct((count, frames, width), jnp.bfloat16)],
        scratch_shapes=[pltpu.VMEM((frames, width), jnp.float32)],
        compiler_params=params(),
        name="ffn_back",
    )(low, d, down, slope, up, mid, gain)


def pack_back_kernel(packed_ref, w_ref, d_ref, stream_ref, gain_ref, low_ref, gain_grad_ref):
    grad = sum(dot_nt(packed_ref[j], w_ref[j]) for j in range(w_ref.shape[0]))
    normed, inverse = normalize(stream_ref[...])
    gain_grad_ref[...] = jnp.sum(grad * normed, 0, keepdims=True)
    low_ref[...] = as_low(d_ref[...] + normalize_back(grad * gain_ref[...], normed, inverse))


def pack_back(packed, w, d, stream, gain):
    frames, width = stream.shape
    return pl.pallas_call(
        pack_back_kernel,
        out_shape=[
            jax.ShapeDtypeStruct((frames, width), jnp.bfloat16),
            jax.ShapeDtypeStruct((1, width), jnp.float32),
        ],
        compiler_params=params(),
        name="pack_back",
    )(packed, w, d, stream, gain)


def tail_kernel(d_ref, skip_ref, small_ref, embed_ref, mel_ref, hot_ref, main_ref, table_ref):
    phones = embed_ref.shape[1]
    d_start = as_low(dot_nt(d_ref[...], skip_ref[...]))
    d_phones = as_low(dot_nn(d_start, small_ref[:, :phones]))
    main_ref[:, :phones] = as_low(dot_tn(d_start, embed_ref[...]))
    main_ref[:, phones:] = as_low(dot_tn(d_start, mel_ref[...]))
    table_ref[...] = as_low(dot_tn(d_phones, hot_ref[...]))


def tail(d, skip, small, embed, mel, hot):
    width = d.shape[1]
    phones = embed.shape[1]
    whole = lambda x: pl.BlockSpec(x.shape, lambda i: (0, 0))
    return pl.pallas_call(
        tail_kernel,
        grid=(1,),
        in_specs=[whole(d), pl.BlockSpec((width, width), lambda i: (0, 0))]
        + [whole(x) for x in (small, embed, mel, hot)],
        out_specs=[
            pl.BlockSpec((width, TABLE_AT), lambda i: (0, 0)),
            pl.BlockSpec((phones, hot.shape[1]), lambda i: (0, 0)),
        ],
        out_shape=[
            jax.ShapeDtypeStruct((width, TABLE_AT), jnp.bfloat16),
            jax.ShapeDtypeStruct((phones, hot.shape[1]), jnp.bfloat16),
        ],
        compiler_params=params(),
        name="tail",
    )(d, skip, small, embed, mel, hot)


def grads_kernel(plan, count, rows, legs, came_too, idx_ref, *refs):
    refs, picked_ref, sems = refs[:-2], refs[-2], refs[-1]
    outs = refs[len(refs) - legs :]
    came_ref = refs[len(refs) - legs - 1] if came_too else None
    step = pl.program_id(0)
    each = count // legs

    def copies(c):
        lefts, rights, stride, offset = plan[c]
        if rights is None:
            return []
        slot = c % 2
        return [
            pltpu.make_async_copy(
                refs[left].at[pl.ds(pl.multiple_of(idx_ref[i] * stride + offset, rows), rows)],
                picked_ref.at[slot, side, pl.ds(i * rows, rows)],
                sems.at[slot],
            )
            for side, left in enumerate(lefts)
            for i in range(count)
        ]

    def chunk(c):
        lefts, rights, _, _ = plan[c]
        if c == 0:
            for copy in copies(0):
                copy.start()
        if c + 1 < len(plan):
            for copy in copies(c + 1):
                copy.start()
        for copy in copies(c):
            copy.wait()
        if rights is None:
            main, table, edge = (refs[r] for r in lefts)
            thick = table.shape[0] // (main.shape[0] // rows)
            blocks = []
            for i in range(count):
                start = pl.multiple_of(idx_ref[i] * rows, rows)
                short = pl.multiple_of(idx_ref[i] * thick, thick)
                lead = table[pl.ds(short, thick)]
                rest = jnp.zeros((rows - thick, lead.shape[1]), lead.dtype)
                middle = jnp.concatenate([lead, rest], 0) if thick < rows else lead
                block = [main[pl.ds(start, rows)], middle, edge[pl.ds(start, rows)]]
                blocks.append(jnp.concatenate(block, 1).astype(jnp.float32))
            total = jnp.stack(blocks)
            if came_too:
                total = total + came_ref[...].astype(jnp.float32)
        else:
            wide = outs[0].shape[2]
            total = sum(
                dot_nn(picked_ref[c % 2, side], refs[r][0] if len(refs[r].shape) == 3 else refs[r][...])
                for side, r in enumerate(rights)
            )
            total = total.reshape(count, rows, wide)
        for f in range(legs):
            outs[f][...] = as_low(total[f * each : (f + 1) * each])

    for c in range(len(plan)):
        pl.when(step == c)(partial(chunk, c))


def grads(plan, arrays, idx, frames, rows, width, legs, came=None):
    count = idx.shape[0]
    picked = [j for entry in plan if entry[1] is not None for j in entry[0]]

    def spec(j, x):
        if j in picked:
            return pl.BlockSpec(memory_space=pl.ANY)
        if len(x.shape) == 3:
            first = min(c for c, entry in enumerate(plan) if entry[1] is not None and j in entry[1])
            return pl.BlockSpec((1,) + x.shape[1:], lambda i: (jnp.maximum(i - first, 0), 0, 0))
        return pl.BlockSpec(x.shape, lambda i, n=len(x.shape): (0,) * n)

    specs = [spec(j, x) for j, x in enumerate(arrays)]
    if came is not None:
        specs.append(pl.BlockSpec((count, rows, width), lambda i: (0, 0, 0)))
        arrays = list(arrays) + [came]
    return pl.pallas_call(
        partial(grads_kernel, plan, count, rows, legs, came is not None),
        grid=(len(plan),),
        in_specs=[pl.BlockSpec(memory_space=pltpu.SMEM)] + specs,
        out_specs=[pl.BlockSpec((count // legs, rows, width), lambda i: (0, i, 0))] * legs,
        out_shape=[jax.ShapeDtypeStruct((count // legs, rows * len(plan), width), jnp.bfloat16)] * legs,
        scratch_shapes=[
            pltpu.VMEM((2, 2, count * rows, frames), jnp.bfloat16),
            pltpu.SemaphoreType.DMA((2,)),
        ],
        compiler_params=params(),
        name="grads",
    )(idx, *arrays)


def fold_kernel(legs, *refs):
    ins, outs = refs[:-legs], refs[-legs:]
    took = len(ins) // legs
    for j in range(legs):
        total = ins[j * took][...].astype(jnp.float32)
        for ref in ins[j * took + 1 : (j + 1) * took]:
            total = total + ref[...].astype(jnp.float32)
        outs[j][...] = as_low(total)


def fold(parts, legs):
    count, rows, width = parts[0].shape
    each = count // legs
    tile = rows // 2
    return pl.pallas_call(
        partial(fold_kernel, legs),
        grid=(rows // tile,),
        in_specs=[
            pl.BlockSpec((each, tile, width), lambda i, j=j: (j, i, 0)) for j in range(legs) for _ in parts
        ],
        out_specs=[pl.BlockSpec((each, tile, width), lambda i: (0, i, 0))] * legs,
        out_shape=[jax.ShapeDtypeStruct((each, rows, width), jnp.bfloat16)] * legs,
        compiler_params=params(),
        name="fold",
    )(*[p for _ in range(legs) for p in parts])


def stack_kernel(*refs):
    ins, out, sem = refs[:-2], refs[-2], refs[-1]
    copies = [pltpu.make_async_copy(ref, out.at[i], sem) for i, ref in enumerate(ins)]
    for copy in copies:
        copy.start()
    for copy in copies:
        copy.wait()


def stack(parts):
    return pl.pallas_call(
        stack_kernel,
        in_specs=[pl.BlockSpec(memory_space=pl.ANY)] * len(parts),
        out_specs=pl.BlockSpec(memory_space=pltpu.VMEM),
        out_shape=jax.ShapeDtypeStruct((len(parts),) + parts[0].shape, parts[0].dtype),
        scratch_shapes=[pltpu.SemaphoreType.DMA],
        compiler_params=params(),
        name="stack",
    )(*parts)


def place_kernel(layout, sources, count, *refs):
    idx_refs, sources_refs = refs[:2], refs[2 : 2 + sources]
    outs, sem = refs[2 + sources : -1], refs[-1]
    copies = []
    for s, source in enumerate(sources_refs):
        idx_ref = idx_refs[s // (sources // 2)]
        first = (s % (sources // 2)) * count
        for i in range(count):
            owner = idx_ref[first + i]
            start = 0
            for (out, block), rows in layout:
                ref = outs[out]
                goal = ref.at[owner] if block is None else ref.at[block, owner]
                copy = pltpu.make_async_copy(source.at[i, pl.ds(start, rows)], goal, sem)
                copy.start()
                copies.append(copy)
                start += rows
    for copy in copies:
        copy.wait()


def place(layout, shapes, own, other, pieces):
    width = pieces[0].shape[2]
    return pl.pallas_call(
        partial(place_kernel, layout, len(pieces), pieces[0].shape[0]),
        in_specs=[pl.BlockSpec(memory_space=pltpu.SMEM)] * 2
        + [pl.BlockSpec(memory_space=pl.ANY)] * len(pieces),
        out_specs=[pl.BlockSpec(memory_space=pltpu.VMEM)] * len(shapes),
        out_shape=[jax.ShapeDtypeStruct(s, jnp.bfloat16) for s in shapes],
        scratch_shapes=[pltpu.SemaphoreType.DMA],
        compiler_params=params(),
        name="place",
    )(own, other, *pieces)


def shards(
    grid,
    fast,
    clean_mel,
    gauss_noise,
    flow_time,
    phone_ids,
    lengths,
    span_start,
    span_end,
    speaker,
    skip_states,
    w_input,
    phone_table,
    w_skip,
    w_attend,
    w_output,
    w_expand,
    w_reduce,
    w_head,
    norm_gains,
    moment_input,
    moment_table,
    moment_skip,
    moment_attend,
    moment_output,
    moment_expand,
    moment_reduce,
    moment_head,
    moment_gains,
    square_input,
    square_table,
    square_skip,
    square_attend,
    square_output,
    square_expand,
    square_reduce,
    square_head,
    square_gains,
):
    masters = (w_input, phone_table, w_skip, w_attend, w_output, w_expand, w_reduce, w_head, norm_gains)
    moments = (
        moment_input, moment_table, moment_skip, moment_attend, moment_output,
        moment_expand, moment_reduce, moment_head, moment_gains,
    )
    squares = (
        square_input, square_table, square_skip, square_attend, square_output,
        square_expand, square_reduce, square_head, square_gains,
    )
    rates = (LEARN_RATE, GAIN_RATE) + (LEARN_RATE,) * 6 + (GAIN_RATE,)
    frames, mel_bins = clean_mel.shape
    width = w_skip.shape[1]
    heads = width // HD
    devices = grid.total
    unit = width // devices
    inputs = w_input.shape[0]
    phones = phone_table.shape[0]
    phone_wide = phone_table.shape[1]
    phone_width = phone_wide * devices
    mel_lanes = TABLE_AT - phone_width
    at_gain = HEAD_AT + mel_bins
    at_count = at_gain + 3
    position = jnp.arange(frames)
    frame_valid = (position < lengths[0]).astype(jnp.float32)
    frame_inside = ((position >= span_start[0]) & (position < span_end[0])).astype(
        jnp.float32
    ) * frame_valid
    speaker_hot = (speaker[0] == jnp.arange(SPK)).astype(jnp.float32)
    count = jnp.sum(frame_inside)
    count_high = jnp.floor(count / 16.0)
    tally = jnp.stack([speaker[0].astype(jnp.float32), count_high, count - 16.0 * count_high])

    low_input = as_low(w_input)
    small = jnp.concatenate(
        [
            low_input[2 * mel_bins :].T,
            low_input[: 2 * mel_bins].T,
            jnp.zeros((unit, TABLE_AT - inputs), jnp.bfloat16),
            jnp.pad(as_low(phone_table).T, ((0, unit - phone_wide), (0, 0))),
            as_low(w_head),
            as_low(norm_gains).T,
            jnp.broadcast_to(as_low(tally)[None, :], (unit, 3)),
            jnp.zeros((unit, width - at_count - 3), jnp.bfloat16),
        ],
        1,
    )

    def blocks(x):
        return [as_low(x[:, j : j + width]) for j in range(0, x.shape[1], width)]

    attend_blocks, expand_blocks = blocks(w_attend), blocks(w_expand)
    packs, wides = len(attend_blocks), len(expand_blocks)
    stages = [
        [("small", None, small), ("skip", None, as_low(w_skip))],
        [("attend", j, w) for j, w in enumerate(attend_blocks)],
        [("output", None, as_low(w_output))] + [("expand", j, w) for j, w in enumerate(expand_blocks)],
        [("reduce", None, as_low(w_reduce))],
    ]
    counts_of = {"attend": packs, "expand": wides}
    if fast:
        own, other = grid.owners(0, -1), grid.owners(1, -1)

    def named(stage):
        return list(dict.fromkeys(name for name, _, _ in stage))

    def load(stage):
        return jnp.concatenate([w for _, _, w in stage], 0)

    def along(x, role, *after):
        return spread(grid, tied(x, *after) if after else x, role)

    def deepen(x, *after):
        x = tied(x, *after) if after else x
        return swap_deep(grid, jnp.broadcast_to(x[None], (grid.size("z"),) + x.shape))

    def plane(moved):
        return stack(moved).reshape((-1,) + moved[0].shape[1:])

    def settle(stage, pieces, own, other):
        pieces = pieces + [shift(grid, p, "core", 1) for p in pieces]
        names = named(stage)
        shapes, layout = [], []
        for name in names:
            rows = [w.shape[0] for n, _, w in stage if n == name][0]
            lead = (counts_of[name],) if name in counts_of else ()
            shapes.append(lead + (devices, rows, width))
        for name, block, w in stage:
            layout.append(((names.index(name), block), w.shape[0]))
        return dict(zip(names, place(layout, shapes, own, other, pieces)))

    def gather_whole(stage):
        full = {name: [] for name in named(stage)}
        rows = lax.all_gather(load(stage), AXES, axis=0, tiled=False)
        start = 0
        for name, _, w in stage:
            full[name].append(rows[:, start : start + w.shape[0]])
            start += w.shape[0]
        return {n: jnp.stack(p) if n in counts_of else p[0] for n, p in full.items()}

    loads = [load(stage) for stage in stages]
    if fast:
        deep_0 = deepen(loads[0])
        near_0, deep_1 = join(along(deep_0, "near"), deepen(loads[1], deep_0))
        near_0 = plane(near_0)
        far_0, near_1, deep_2 = join(
            along(near_0, "far"), along(deep_1, "near", near_0), deepen(loads[2], near_0)
        )
        near_1 = plane(near_1)
        far_1, near_2 = along(near_1, "far"), along(deep_2, "near", near_1)
        deep_3 = deepen(loads[3], near_1)
        far_0 = [tied(p, near_1) for p in far_0]
        whole = settle(stages[0], far_0, own, other)
    else:
        whole = gather_whole(stages[0])
    small_full = whole["small"].reshape(width, width)
    skip_full = whole["skip"].reshape(-1, width)
    table_turned = whole["small"][:, :phone_wide, TABLE_AT:HEAD_AT].reshape(phone_width, phones)
    head_block = small_full[:, HEAD_AT:]
    gains_wide = head_block[:, mel_bins : mel_bins + 3].astype(jnp.float32).T
    tallies = whole["small"][:, 0, at_count : at_count + 3].astype(jnp.float32)
    counts = jnp.sum(
        (tallies[:, :1] == jnp.arange(SPK, dtype=jnp.float32)[None, :])
        * (16.0 * tallies[:, 1:2] + tallies[:, 2:3]),
        0,
    )
    share = jnp.sum(speaker_hot / jnp.maximum(counts, 1.0)) / SPK

    flow = flow_time[0]
    noisy_mel = (1.0 - (1.0 - SIGMA) * flow) * gauss_noise + flow * clean_mel
    context = clean_mel * (frame_valid - frame_inside)[:, None]
    target = clean_mel - (1.0 - SIGMA) * gauss_noise
    mel = jnp.concatenate([as_low(noisy_mel), as_low(context)], 1)
    mel = jnp.pad(mel, ((0, 0), (0, mel_lanes - mel.shape[1])))
    phone_hot = as_low(phone_ids[:, None] == jnp.arange(phones)[None, :])
    slopes = head_slopes(heads)
    states_turned = skip_states.T

    embedded, stream, start_turned, attn_in, attn_turned = front(
        small_full, table_turned, skip_full, skip_states, phone_hot, mel,
        time_features(flow, width)[None, :], gains_wide[0:1],
    )
    if fast:
        far_1, near_2, deep_3, embedded, stream, start_turned, attn_in, attn_turned = join(
            far_1, near_2, deep_3, embedded, stream, start_turned, attn_in, attn_turned
        )
        near_2 = plane(near_2)
        far_2, near_3 = along(near_2, "far"), along(deep_3, "near", near_2)
        far_1 = [tied(p, near_2) for p in far_1]
        whole.update(settle(stages[1], far_1, own, other))
    else:
        whole.update(gather_whole(stages[1]))
    attend_full = whole["attend"].reshape(packs, width, width)
    packed = pack(attn_in, attend_full)
    mixed, lse = attend(lengths, slopes, packed)
    if fast:
        far_2, near_3, packed, mixed, lse = join(far_2, near_3, packed, mixed, lse)
        near_3 = plane(near_3)
        far_3 = along(near_3, "far")
        far_2 = [tied(p, near_3) for p in far_2]
        whole.update(settle(stages[2], far_2, own, other))
    else:
        whole.update(gather_whole(stages[2]))
    output_full = whole["output"].reshape(width, width)
    expand_full = whole["expand"].reshape(wides, width, width)
    stream_mid, ffn_in, ffn_turned, mixed_turned = mid_step(
        mixed, output_full, stream, gains_wide[1:2]
    )
    activated, act_turned, gelu_slope = expand(ffn_in, expand_full)
    if fast:
        far_3, stream_mid, ffn_turned, mixed_turned, activated, act_turned, gelu_slope = join(
            far_3, stream_mid, ffn_turned, mixed_turned, activated, act_turned, gelu_slope
        )
        whole.update(settle(stages[3], far_3, own, other))
    else:
        whole.update(gather_whole(stages[3]))
    reduce_full = whole["reduce"].reshape(-1, width)
    d_stream_out, d_branch, grad_head, grad_gain_three, error_sum = head_step(
        share[None], activated, reduce_full, stream_mid, head_block, target,
        frame_inside[:, None], gains_wide[2:3],
    )
    if fast:
        mine, theirs = grid.owners(0, 1), grid.owners(1, 1)
    far, near, deep = (grid.size(r) for r in ("far", "near", "z"))

    def sibling(x):
        return shift(grid, x, "core", 1)

    def both(*arrays):
        return [y for x in arrays for y in (x, sibling(x))]

    def sums(plan, arrays, *others, **options):
        first = [tied(arrays[0], *others)] if others else arrays[:1]
        return grads(plan, first + arrays[1:], mine, frames, unit, width, far, **options)

    def hops(legs, role, *others):
        sent = [tied(leg, *others) if others else leg for leg in legs[1:]]
        return [shift(grid, leg, role, j + 1) for j, leg in enumerate(sent)]

    def dense(pairs):
        parts = []
        for turned, right, stride, offset in pairs:
            if right is None:
                part = turned.reshape(devices, unit, width)
            else:
                turned = turned.reshape(devices, stride, frames)[:, offset : offset + unit]
                part = dot_nn(turned.reshape(width, frames), right).reshape(devices, unit, width)
            parts.append(part)
        return lax.psum_scatter(jnp.concatenate(parts, 1), AXES, scatter_dimension=0)

    offsets = [j * unit for j in range(wides)]
    if fast:
        plan = [((0, 1), (2, 3), wides * unit, o) for o in offsets]
        legs_0 = sums(plan, both(act_turned, d_branch))
        moved_0 = hops(legs_0, "far")
        d_branch_next = tied(d_branch, legs_0[0])
    else:
        share_reduce = dense([(act_turned, d_branch, wides * unit, o) for o in offsets])
        d_branch_next = d_branch
    d_stream_mid, d_out, grad_gain_two, d_hidden = ffn_back(
        d_branch_next, d_stream_out, reduce_full, gelu_slope, expand_full, stream_mid, gains_wide[1:2]
    )
    if fast:
        turned = both(ffn_turned, mixed_turned, attn_turned)
        moved_0, turned, d_stream_mid, d_out, d_hidden = join(
            moved_0, turned, d_stream_mid, d_out, d_hidden
        )
        legs_0 = fold([legs_0[0]] + moved_0, near)
        moved_0 = hops(legs_0, "near")
        d_out, d_hidden = tied(d_out, legs_0[0]), tied(d_hidden, legs_0[0])
    d_mixed = as_low(dot_nt(d_out, output_full))
    if fast:
        plan = [((0, 1), (2, 3), unit, 0) for j in range(wides)]
        legs_1 = sums(plan, turned[:2] + both(d_hidden), d_mixed)
        d_outs = both(d_out)
        moved_0, legs_1, d_mixed, d_outs = join(moved_0, legs_1, d_mixed, d_outs)
        (sums_0,) = fold([legs_0[0]] + moved_0, 1)
        d_mixed = tied(d_mixed, sums_0)
        moved_1 = hops(legs_1, "far", sums_0)
        sums_0 = swap_deep(grid, sums_0)
    else:
        share_expand = dense([(ffn_turned, d, unit, 0) for d in d_hidden])
    d_packed = attend_back(lengths, slopes, packed, d_mixed, lse)
    if fast:
        moved_1, sums_0, d_packed = join(moved_1, sums_0, d_packed)
        legs_1 = fold([legs_1[0]] + moved_1, near)
        moved_1 = hops(legs_1, "near")
        d_packed = tied(d_packed, legs_1[0])
    d_joined_in, grad_gain_one = pack_back(
        d_packed, attend_full, d_stream_mid, stream, gains_wide[0:1]
    )
    joined_turned = jnp.concatenate([start_turned, states_turned], 0)
    if fast:
        plan = [((0, 1), (2, 3), unit, 0)] + [((4, 5), (6, 7), unit, 0) for j in range(packs)]
        legs_2 = sums(plan, turned[2:4] + d_outs + turned[4:] + both(d_packed), d_joined_in)
        joined = both(joined_turned)
        moved_1, legs_2, joined, d_joined_in = join(moved_1, legs_2, joined, d_joined_in)
        (sums_1,) = fold([legs_1[0]] + moved_1, 1)
        d_joined_in = tied(d_joined_in, sums_1)
        moved_2 = hops(legs_2, "far", sums_1)
        sums_1 = swap_deep(grid, sums_1)
    else:
        share_attend = dense(
            [(mixed_turned, d_out, unit, 0)] + [(attn_turned, d, unit, 0) for d in d_packed]
        )
    main, table = tail(d_joined_in, skip_full, small_full, embedded, mel, phone_hot)
    gain_grads = jnp.concatenate([grad_gain_one, grad_gain_two, grad_gain_three], 0).T
    edge = jnp.pad(
        jnp.concatenate([as_low(grad_head), as_low(gain_grads)], 1),
        ((0, 0), (0, width - at_count)),
    )
    if fast:
        small_grads = [main, table, edge]
        (sent,) = grads([((0, 1, 2), None, 0, 0)], small_grads, theirs, frames, unit, width, 1)
        plan = [((0, 1), (2, 3), 2 * unit, o) for o in offsets[:2]] + [((4, 5, 6), None, 0, 0)]
        legs_3 = sums(plan, joined + both(d_joined_in) + small_grads, sent, came=sibling(sent))
        moved_2, sums_1, legs_3 = join(moved_2, sums_1, legs_3)
        legs_2 = fold([legs_2[0]] + moved_2, near)
        moved_2 = hops(legs_2, "near")
        moved_3 = hops(legs_3, "far", legs_2[0])
        moved_2, moved_3 = join(moved_2, moved_3)
        (sums_2,) = fold([legs_2[0]] + moved_2, 1)
        legs_3 = fold([legs_3[0], tied(moved_3[0], sums_2)] + moved_3[1:], near)
        moved_3 = hops(legs_3, "near")
        sums_2 = swap_deep(grid, sums_2)
        (sums_3,) = fold([legs_3[0]] + moved_3, 1)
        sums_3 = swap_deep(grid, sums_3)
        share_reduce, share_expand, share_attend, share_last = [
            jnp.sum(x.astype(jnp.float32), 0) for x in (sums_0, sums_1, sums_2, sums_3)
        ]
    else:
        table = table.reshape(devices, phone_wide, phones)
        table = jnp.pad(table, ((0, 0), (0, unit - phone_wide), (0, 0))).reshape(width, phones)
        small_grads = jnp.concatenate([main, table, edge], 1).astype(jnp.float32)
        share_last = dense(
            [(joined_turned, d_joined_in, 2 * unit, o) for o in offsets[:2]]
            + [(small_grads, None, 0, 0)]
        )

    def columns(rows):
        return jnp.concatenate([rows[j : j + unit] for j in range(0, rows.shape[0], unit)], 1)

    share_small = share_last[2 * unit :]
    shares = (
        jnp.concatenate([share_small[:, phone_width:inputs], share_small[:, :phone_width]], 1).T,
        share_small[:phone_wide, TABLE_AT:HEAD_AT].T,
        share_last[: 2 * unit],
        columns(share_attend[unit:]),
        share_attend[:unit],
        columns(share_expand),
        share_reduce,
        share_small[:, HEAD_AT:at_gain],
        share_small[:, at_gain:at_count].T,
    )
    local_square = sum((jnp.sum(g * g) for g in shares))
    totals = all_sum(grid, jnp.concatenate([speaker_hot * error_sum[0, 0], local_square[None]]))
    sums, total_square = totals[:SPK], totals[SPK]
    loss_value = jnp.mean(sums / jnp.maximum(counts, 1.0))
    grad_norm = jnp.sqrt(total_square)
    clip = jnp.minimum(1.0, 1.0 / (grad_norm + 1e-06))
    results = [
        adam_step(w, g * clip, m, s, r)
        for w, g, m, s, r in zip(masters, shares, moments, squares, rates)
    ]
    next_weights = tuple((r[0] for r in results))
    next_moments = tuple((r[1] for r in results))
    next_squares = tuple((r[2] for r in results))
    return (loss_value, grad_norm) + next_weights + next_moments + next_squares


def solution(mesh):
    grid = Grid(mesh)
    in_specs = (
        P(("wide", "narrow"), None),
        P(("wide", "narrow"), None),
        P(("wide", "narrow")),
        P(("wide", "narrow")),
        P(("wide", "narrow")),
        P(("wide", "narrow")),
        P(("wide", "narrow")),
        P(("wide", "narrow")),
        P(("wide", "narrow"), None),
        P(None, ("wide", "narrow")),
        P(None, ("wide", "narrow")),
        P(("wide", "narrow"), None),
        P(("wide", "narrow"), None),
        P(("wide", "narrow"), None),
        P(("wide", "narrow"), None),
        P(("wide", "narrow"), None),
        P(("wide", "narrow"), None),
        P(None, ("wide", "narrow")),
        P(None, ("wide", "narrow")),
        P(None, ("wide", "narrow")),
        P(("wide", "narrow"), None),
        P(("wide", "narrow"), None),
        P(("wide", "narrow"), None),
        P(("wide", "narrow"), None),
        P(("wide", "narrow"), None),
        P(("wide", "narrow"), None),
        P(None, ("wide", "narrow")),
        P(None, ("wide", "narrow")),
        P(None, ("wide", "narrow")),
        P(("wide", "narrow"), None),
        P(("wide", "narrow"), None),
        P(("wide", "narrow"), None),
        P(("wide", "narrow"), None),
        P(("wide", "narrow"), None),
        P(("wide", "narrow"), None),
        P(None, ("wide", "narrow")),
    )
    out_specs = (
        P(),
        P(),
        P(None, ("wide", "narrow")),
        P(None, ("wide", "narrow")),
        P(("wide", "narrow"), None),
        P(("wide", "narrow"), None),
        P(("wide", "narrow"), None),
        P(("wide", "narrow"), None),
        P(("wide", "narrow"), None),
        P(("wide", "narrow"), None),
        P(None, ("wide", "narrow")),
        P(None, ("wide", "narrow")),
        P(None, ("wide", "narrow")),
        P(("wide", "narrow"), None),
        P(("wide", "narrow"), None),
        P(("wide", "narrow"), None),
        P(("wide", "narrow"), None),
        P(("wide", "narrow"), None),
        P(("wide", "narrow"), None),
        P(None, ("wide", "narrow")),
        P(None, ("wide", "narrow")),
        P(None, ("wide", "narrow")),
        P(("wide", "narrow"), None),
        P(("wide", "narrow"), None),
        P(("wide", "narrow"), None),
        P(("wide", "narrow"), None),
        P(("wide", "narrow"), None),
        P(("wide", "narrow"), None),
        P(None, ("wide", "narrow")),
    )

    def body(*args):
        unit = args[11].shape[1] // grid.total
        return shards(grid, unit % 32 == 0, *args)

    return jax.shard_map(body, mesh=mesh, in_specs=in_specs, out_specs=out_specs, check_vma=False)
```

time: 738 us -> 575 us (0.78)
  matrix products: 154 us -> 3.86 us
  Pallas kernels: 101 us -> 222 us
  local copies, waits for them, and re-layouts: 91 us -> 32.1 us
  other arithmetic: 96 us -> 42.5 us
  waiting for transfers between devices: 201 us -> 187 us
  starting transfers between devices: 67.7 us -> 60.2 us
    dot_general x49 -> x1, matrix products: 154 us -> 3.86 us  [dot_nt(): lax.dot_general(a, b, (((1,), (1,)), ((), ())), preferred_element_type=jn...]
    pallas_call x13 -> x31, Pallas kernels: 101 us -> 222 us  [the longest x5 40 us: grads(): pl.pallas_call(partial(grads_kernel, plan, count, rows, legs, came is not...]
    ppermute x54 -> x35, waiting for transfers between devices: 190 us -> 116 us  [shift(): return lax.ppermute(x, AXES, grid.pairs(role, step))]
    all_to_all x0 -> x8, waiting for transfers between devices: none -> 57.2 us  [swap_deep(): return lax.all_to_all(x, AXES, 0, 0, axis_index_groups=grid.lines())]
    ppermute x54 -> x35, starting transfers between devices: 64.2 us -> 22.5 us  [shift(): return lax.ppermute(x, AXES, grid.pairs(role, step))]
    all_to_all x0 -> x8, starting transfers between devices: none -> 35.1 us  [swap_deep(): return lax.all_to_all(x, AXES, 0, 0, axis_index_groups=grid.lines())]
    convert_element_type x19 -> x6, other arithmetic: 38.8 us -> 5.24 us  [as_low(): return x.astype(jnp.bfloat16)]
    unnamed x302 -> x143, local copies, waits for them, and re-layouts: 43.7 us -> 17.2 us
  transfers between devices with their start and end apart: 59 -> 48, of which waited for: 29 -> 29; matrix products, arithmetic and copies ran while one was open for 36% -> 7% of each run, Pallas kernels for 8% -> 32%
where the time goes in v2:
time: 575 us; the launch traced here: 564 us
  Pallas kernels  222 us (39%)
  waiting for transfers between devices  187 us (33%)
  starting transfers between devices  60.2 us (10%)
  other arithmetic  42.5 us (7%)
  local copies, waits for them, and re-layouts  32.1 us (6%)
  between operations  16.8 us (3%)
    ppermute x35, waiting for transfers between devices, shift(): return lax.ppermute(x, AXES, grid.pairs(role, step))  116 us
    all_to_all x8, waiting for transfers between devices, swap_deep(): return lax.all_to_all(x, AXES, 0, 0, axis_index_groups=grid.lines())  57.2 us
    pallas_call x5, Pallas kernels, grads(): pl.pallas_call(partial(grads_kernel, plan, count, rows, legs, came is not...  40 us
    all_to_all x8, starting transfers between devices, swap_deep(): return lax.all_to_all(x, AXES, 0, 0, axis_index_groups=grid.lines())  35.1 us
    pallas_call x4, Pallas kernels, place(): pl.pallas_call(partial(place_kernel, layout, len(pieces), pieces[0].shape...  28.4 us
    pallas_call x8, Pallas kernels, fold(): pl.pallas_call(partial(fold_kernel, legs), grid=(rows // tile,), in_specs...  23.5 us
    ppermute x35, starting transfers between devices, shift(): return lax.ppermute(x, AXES, grid.pairs(role, step))  22.5 us
    pallas_call x1, Pallas kernels, ffn_back(): pl.pallas_call(ffn_back_kernel, grid=(count,), in_specs=[whole(frames, wi...  18.6 us
  transfers between devices with their start and end apart: 48, of which 29 were waited for; matrix products, arithmetic and copies ran while one was open for 7% of the time, Pallas kernels for 32%

profile of v2, /device:TPU:0, one launch (start us, length us, event | category | flops | bytes accessed | tf_op | source)
XLA Modules:
  0.0 564.2 jit_solution(11970829978083913973)
XLA Ops:
  10.6 6.3 %all-to-all-start = ((bf16[4,96,1024]{2,1,0:T(8,128)(2,1)}), bf16[4,96,1024]{2,1,0:T(8,128)(2,1)S(1)}, u32[]{:S(2)}, u32[]{:S(2)}) async-start(bf16[4,96,1024]{2,1,0:T(8,128)(2,1)} %broadcast_in_dim.103), calls=%async_computation | async-start | bytes 1572864 | tf_op jit(solution)/shard_map/all_to_all | solution.py:153
  17.0 20.0 %all-to-all-done.refs_0_ = bf16[4,96,1024]{2,1,0:T(8,128)(2,1)S(1)} async-done(((bf16[4,96,1024]{2,1,0:T(8,128)(2,1)}), bf16[4,96,1024]{2,1,0:T(8,128)(2,1)S(1)}, u32[]{:S(2)}, u32[]{:S(2)}) %all-to-all-start) | async-done | bytes 786464 | tf_op jit(solution)/shard_map/all_to_all | solution.py:153
  38.1 3.5 all-to-all-start.1
  44.1 9.7 %collective-permute-done.refs_1_ = bf16[4,96,1024]{2,1,0:T(8,128)(2,1)S(1)} collective-permute-done((bf16[4,96,1024]{2,1,0:T(8,128)(2,1)S(1)}, bf16[4,96,1024]{2,1,0:T(8,128)(2,1)S(1)}, u32[]{:S(2)}, u32[]{:S(2)}) %collective-permute-start) | collective-permute-done | bytes 786464 | tf_op jit(solution)/shard_map/ppermute | solution.py:145
  53.8 7.4 %all-to-all-done.1.refs_0_ = bf16[4,96,1024]{2,1,0:T(8,128)(2,1)S(1)} async-done(((bf16[4,96,1024]{2,1,0:T(8,128)(2,1)}), bf16[4,96,1024]{2,1,0:T(8,128)(2,1)S(1)}, u32[]{:S(2)}, u32[]{:S(2)}) %all-to-all-start.1) | async-done | bytes 786464 | tf_op jit(solution)/shard_map/all_to_all | solution.py:153
  61.2 2.8 stack.20
  65.3 3.5 all-to-all-start.2
  72.7 18.5 %collective-permute-done.2.refs_1_ = bf16[4,96,1024]{2,1,0:T(8,128)(2,1)} collective-permute-done((bf16[4,96,1024]{2,1,0:T(8,128)(2,1)}, bf16[4,96,1024]{2,1,0:T(8,128)(2,1)}, u32[]{:S(2)}, u32[]{:S(2)}) %collective-permute-start.2) | collective-permute-done | bytes 786464 | tf_op jit(solution)/shard_map/ppermute | solution.py:145
  91.2 6.2 %collective-permute-done.1.refs_3_ = bf16[8,96,1024]{2,1,0:T(8,128)(2,1)} collective-permute-done((bf16[8,96,1024]{2,1,0:T(8,128)(2,1)S(1)}, bf16[8,96,1024]{2,1,0:T(8,128)(2,1)}, u32[]{:S(2)}, u32[]{:S(2)}) %collective-permute-start.1) | collective-permute-done | bytes 1572896 | tf_op jit(solution)/shard_map/ppermute | solution.py:145
  99.7 3.0 stack.21
  106.0 4.4 all-to-all-start.3
  118.1 6.2 %place.4 = (bf16[32,32,1024]{2,1,0:T(8,128)(2,1)}, bf16[32,64,1024]{2,1,0:T(8,128)(2,1)}) custom-call(s32[16]{0:T(128)} %get-tuple-element.437.refs_0_, s32[16]{0:T(128)} %get-tuple-element.436.refs_1_, bf16[8,96,1024]{2,1,0:T(8,128)(2,1)} %bitcast.91, bf16[8,96,1024]{2,1,0:T(8,128)(2,1)} %collective-permute-done.1.refs_3_, ...), custom_call_target="tpu_custom_call" | custom-call | tf_op jit(solution)/shard_map/place/pallas_call | solution.py:744
  128.9 9.2 %front.1 = (bf16[512,512]{1,0:T(8,128)(2,1)}, f32[512,1024]{1,0:T(8,128)}, bf16[1024,512]{1,0:T(8,128)(2,1)}, bf16[512,1024]{1,0:T(8,128)(2,1)}, bf16[1024,512]{1,0:T(8,128)(2,1)}) custom-call(bf16[1024,1024]{1,0:T(8,128)(2,1)} %bitcast.79, bf16[512,128]{1,0:T(8,128)(2,1)} %bitcast.98, bf16[2048,1024]{1,0:T(8,128)(2,1)} %bitcast.76, ...), custom_call_target="tpu_custom_call" | custom-call | tf_op jit(solution)/shard_map/front/pallas_call | solution.py:352
  138.1 3.3 stack.22
  144.7 2.9 collective-permute-done.10.refs_5_
  149.9 6.1 %place.5 = bf16[3,32,32,1024]{3,2,1,0:T(8,128)(2,1)} custom-call(s32[16]{0:T(128)} %get-tuple-element.437.refs_0_, s32[16]{0:T(128)} %get-tuple-element.436.refs_1_, bf16[8,96,1024]{2,1,0:T(8,128)(2,1)} %bitcast.89, bf16[8,96,1024]{2,1,0:T(8,128)(2,1)} %collective-permute-done.5.refs_3_, bf16[8,96,1024]{2,1,0:T(8,128)(2,1)} %copy-done.20, ...), custom_call_target="tpu_custom_call" | custom-call | tf_op jit(solution)/shard_map/place/pallas_call | solution.py:744
  156.0 7.3 %pack.1.packed_ref = bf16[3,512,1024]{2,1,0:T(8,128)(2,1)} custom-call(bf16[512,1024]{1,0:T(8,128)(2,1)} %get-tuple-element.191.x_ref, bf16[3,1024,1024]{2,1,0:T(8,128)(2,1)} %bitcast.72), custom_call_target="tpu_custom_call" | custom-call | tf_op jit(solution)/shard_map/pack/pallas_call | solution.py:372
  163.3 12.9 %attend.1 = (bf16[512,1024]{1,0:T(8,128)(2,1)}, f32[8,2,512]{2,1,0:T(2,128)}) custom-call(s32[1]{0:T(128)} %copy.185.length_ref, f32[16]{0:T(128)} %multiply_power_fusion.slope_ref, bf16[3,512,1024]{2,1,0:T(8,128)(2,1)} %pack.1.packed_ref), custom_call_target="tpu_custom_call" | custom-call | tf_op jit(solution)/shard_map/attend/pallas_call | solution.py:222
  176.2 8.5 %collective-permute-done.7.refs_3_ = bf16[8,160,1024]{2,1,0:T(8,128)(2,1)} collective-permute-done((bf16[8,160,1024]{2,1,0:T(8,128)(2,1)}, bf16[8,160,1024]{2,1,0:T(8,128)(2,1)}, u32[]{:S(2)}, u32[]{:S(2)}) %collective-permute-start.7) | collective-permute-done | bytes 2621472 | tf_op jit(solution)/shard_map/ppermute | solution.py:145
  184.7 3.1 stack.23
  190.9 5.1 collective-permute-done.13.refs_5_
  196.6 8.8 %place.6 = (bf16[32,32,1024]{2,1,0:T(8,128)(2,1)}, bf16[4,32,32,1024]{3,2,1,0:T(8,128)(2,1)}) custom-call(s32[16]{0:T(128)} %get-tuple-element.437.refs_0_, s32[16]{0:T(128)} %get-tuple-element.436.refs_1_, bf16[8,160,1024]{2,1,0:T(8,128)(2,1)} %bitcast.83, bf16[8,160,1024]{2,1,0:T(8,128)(2,1)} %collective-permute-done.7.refs_3_, ...), custom_call_target="tpu_custom_call" | custom-call | tf_op jit(solution)/shard_map/place/pallas_call | solution.py:744
  205.4 6.1 %mid.1 = (f32[512,1024]{1,0:T(8,128)}, bf16[512,1024]{1,0:T(8,128)(2,1)}, bf16[1024,512]{1,0:T(8,128)(2,1)}, bf16[1024,512]{1,0:T(8,128)(2,1)}) custom-call(bf16[512,1024]{1,0:T(8,128)(2,1)} %get-tuple-element.200.mixed_ref, bf16[1024,1024]{1,0:T(8,128)(2,1)} %bitcast.95, f32[512,1024]{1,0:T(8,128)} %get-tuple-element.206.stream_ref, f32[1,1024]{1,0:T(1,128)} %copy.168.gain_ref), custom_call_target="tpu_custom_call" | custom-call | tf_op jit(solution)/shard_map/mid/pallas_call | solution.py:399
  211.6 16.3 %expand.1 = (bf16[512,4096]{1,0:T(8,128)(2,1)}, bf16[4096,512]{1,0:T(8,128)(2,1)}, bf16[512,4096]{1,0:T(8,128)(2,1)}) custom-call(bf16[512,1024]{1,0:T(8,128)(2,1)} %get-tuple-element.210.x_ref, bf16[4,1024,1024]{2,1,0:T(8,128)(2,1)} %bitcast.74), custom_call_target="tpu_custom_call" | custom-call | tf_op jit(solution)/shard_map/expand/pallas_call | solution.py:307
  234.2 4.5 collective-permute-done.14.refs_4_
  238.7 2.7 collective-permute-done.15.refs_5_
  241.4 7.4 %place.7 = bf16[32,128,1024]{2,1,0:T(8,128)(2,1)} custom-call(s32[16]{0:T(128)} %get-tuple-element.437.refs_0_, s32[16]{0:T(128)} %get-tuple-element.436.refs_1_, bf16[8,128,1024]{2,1,0:T(8,128)(2,1)} %bitcast.86, bf16[8,128,1024]{2,1,0:T(8,128)(2,1)} %collective-permute-done.11.refs_3_, bf16[8,128,1024]{2,1,0:T(8,128)(2,1)} %collective-permute-done.14.refs_4_, ...), custom_call_target="tpu_custom_call" | custom-call | tf_op jit(solution)/shard_map/place/pallas_call | solution.py:744
  248.8 13.4 %head.1 = (f32[512,1024]{1,0:T(8,128)}, bf16[512,1024]{1,0:T(8,128)(2,1)}, f32[1024,80]{1,0:T(8,128)}, f32[1,1024]{1,0:T(1,128)}, f32[1,1]{1,0:T(1,128)}) custom-call(f32[1]{0:T(128)} %bitcast.16.share_ref, bf16[512,4096]{1,0:T(8,128)(2,1)} %get-tuple-element.215.act_ref, bf16[4096,1024]{1,0:T(8,128)(2,1)} %bitcast.70, ...), custom_call_target="tpu_custom_call" | custom-call | tf_op jit(solution)/shard_map/head/pallas_call | solution.py:450
  262.4 2.7 collective-permute-done.17.refs_3_
  266.1 9.3 %grads.5 = (bf16[8,128,1024]{2,1,0:T(8,128)(2,1)}, bf16[8,128,1024]{2,1,0:T(8,128)(2,1)}) custom-call(s32[16]{0:T(128)} %get-tuple-element.435.idx_ref, bf16[4096,512]{1,0:T(8,128)(2,1)} %get-tuple-element.220.refs_0_, bf16[4096,512]{1,0:T(8,128)(2,1)} %collective-permute-done.16.refs_1_, bf16[512,1024]{1,0:T(8,128)(2,1)} %get-tuple-element.227.refs_2_.low_ref, ...), custom_call_target="tpu_custom_call" | custom-call | tf_op jit(solution)/shard_map/grads/pallas_call | solution.py:658
  276.8 18.6 %ffn_back.1 = (f32[512,1024]{1,0:T(8,128)}, bf16[512,1024]{1,0:T(8,128)(2,1)}, f32[1,1024]{1,0:T(1,128)}, bf16[4,512,1024]{2,1,0:T(8,128)(2,1)}) custom-call(bf16[512,1024]{1,0:T(8,128)(2,1)} %get-tuple-element.227.refs_2_.low_ref, f32[512,1024]{1,0:T(8,128)} %get-tuple-element.228.d_ref, bf16[4096,1024]{1,0:T(8,128)(2,1)} %bitcast.71, ...), custom_call_target="tpu_custom_call" | custom-call | tf_op jit(solution)/shard_map/ffn_back/pallas_call | solution.py:506
  295.5 6.3 %collective-permute-done.18.refs_1_.refs_3_ = bf16[8,128,1024]{2,1,0:T(8,128)(2,1)S(1)} collective-permute-done((bf16[8,128,1024]{2,1,0:T(8,128)(2,1)}, bf16[8,128,1024]{2,1,0:T(8,128)(2,1)S(1)}, u32[]{:S(2)}, u32[]{:S(2)}) %collective-permute-start.18) | collective-permute-done | bytes 2097184 | tf_op jit(solution)/shard_map/ppermute | solution.py:145
  303.0 3.5 fold.8
  308.5 3.9 convolution_convert_fusion.d_ref
  312.3 3.7 collective-permute-done.23.refs_3_
  316.0 9.9 %grads.6 = (bf16[8,128,1024]{2,1,0:T(8,128)(2,1)}, bf16[8,128,1024]{2,1,0:T(8,128)(2,1)}) custom-call(s32[16]{0:T(128)} %get-tuple-element.435.idx_ref, bf16[1024,512]{1,0:T(8,128)(2,1)} %get-tuple-element.239.refs_0_, bf16[1024,512]{1,0:T(8,128)(2,1)} %collective-permute-done.19.refs_1_, bf16[4,512,1024]{2,1,0:T(8,128)(2,1)} %get-tuple-element.242.refs_2_, ...), custom_call_target="tpu_custom_call" | custom-call | tf_op jit(solution)/shard_map/grads/pallas_call | solution.py:658
  327.9 2.4 fold.9
  331.0 5.1 all-to-all-start.4
  336.1 17.0 %attend_back.1.packed_ref.refs_6_ = bf16[3,512,1024]{2,1,0:T(8,128)(2,1)} custom-call(s32[1]{0:T(128)} %copy.185.length_ref, f32[16]{0:T(128)} %multiply_power_fusion.slope_ref, bf16[3,512,1024]{2,1,0:T(8,128)(2,1)} %pack.1.packed_ref, bf16[512,1024]{1,0:T(8,128)(2,1)} %convolution_convert_fusion.d_ref, f32[8,2,512]{2,1,0:T(2,128)} %get-tuple-element.252.lse_ref), custom_call_target="tpu_custom_call" | custom-call | tf_op jit(solution)/shard_map/attend_back/pallas_call | solution.py:269
  353.1 8.8 %all-to-all-done.4 = bf16[4,128,1024]{2,1,0:T(8,128)(2,1)} async-done(((bf16[4,128,1024]{2,1,0:T(8,128)(2,1)}), bf16[4,128,1024]{2,1,0:T(8,128)(2,1)}, u32[]{:S(2)}, u32[]{:S(2)}) %all-to-all-start.4) | async-done | bytes 1048608 | tf_op jit(solution)/shard_map/all_to_all | solution.py:153
  361.9 3.4 fold.10
  365.4 2.3 copy.175
  371.5 10.1 %pack_back.1 = (bf16[512,1024]{1,0:T(8,128)(2,1)}, f32[1,1024]{1,0:T(1,128)}) custom-call(bf16[3,512,1024]{2,1,0:T(8,128)(2,1)} %attend_back.1.packed_ref.refs_6_, bf16[3,1024,1024]{2,1,0:T(8,128)(2,1)} %bitcast.73, f32[512,1024]{1,0:T(8,128)} %get-tuple-element.259.d_ref, f32[512,1024]{1,0:T(8,128)} %get-tuple-element.206.stream_ref, f32[1,1024]{1,0:T(1,128)} %copy.167.gain_ref), custom_call_target="tpu_custom_call" | custom-call | tf_op jit(solution)/shard_map/pack_back/pallas_call | solution.py:539
  381.6 10.5 %grads.7 = (bf16[8,128,1024]{2,1,0:T(8,128)(2,1)}, bf16[8,128,1024]{2,1,0:T(8,128)(2,1)}) custom-call(s32[16]{0:T(128)} %get-tuple-element.435.idx_ref, bf16[1024,512]{1,0:T(8,128)(2,1)} %get-tuple-element.261.refs_0_, bf16[1024,512]{1,0:T(8,128)(2,1)} %copy-done.28, bf16[512,1024]{1,0:T(8,128)(2,1)} %get-tuple-element.263.refs_2_, ...), custom_call_target="tpu_custom_call" | custom-call | tf_op jit(solution)/shard_map/grads/pallas_call | solution.py:658
  393.4 2.5 fold.11
  396.4 3.8 all-to-all-start.5
  404.1 6.7 %tail.1 = (bf16[1024,768]{1,0:T(8,128)(2,1)}, bf16[512,128]{1,0:T(8,128)(2,1)}) custom-call(bf16[512,1024]{1,0:T(8,128)(2,1)} %get-tuple-element.275.d_ref.refs_2_, bf16[2048,1024]{1,0:T(8,128)(2,1)} %bitcast.77, bf16[1024,1024]{1,0:T(8,128)(2,1)} %bitcast.81, bf16[512,512]{1,0:T(8,128)(2,1)} %get-tuple-element.276.embed_ref, ...), custom_call_target="tpu_custom_call" | custom-call | tf_op jit(solution)/shard_map/tail/pallas_call | solution.py:563
  410.8 2.7 grads.8
  414.1 3.0 collective-permute-done.31.refs_7_
  419.0 7.6 %grads.9 = (bf16[8,96,1024]{2,1,0:T(8,128)(2,1)}, bf16[8,96,1024]{2,1,0:T(8,128)(2,1)}) custom-call(s32[16]{0:T(128)} %get-tuple-element.435.idx_ref, bf16[2048,512]{1,0:T(8,128)(2,1)} %copy-done.3, bf16[2048,512]{1,0:T(8,128)(2,1)} %copy-done.18, bf16[512,1024]{1,0:T(8,128)(2,1)} %get-tuple-element.275.d_ref.refs_2_, bf16[512,1024]{1,0:T(8,128)(2,1)} %copy-done.33, ...), custom_call_target="tpu_custom_call" | custom-call | tf_op jit(solution)/shard_map/grads/pallas_call | solution.py:658
  428.0 3.5 fold.12
  433.5 25.8 %collective-permute-done.32.refs_1_ = bf16[4,128,1024]{2,1,0:T(8,128)(2,1)S(1)} collective-permute-done((bf16[4,128,1024]{2,1,0:T(8,128)(2,1)}, bf16[4,128,1024]{2,1,0:T(8,128)(2,1)S(1)}, u32[]{:S(2)}, u32[]{:S(2)}) %collective-permute-start.32) | collective-permute-done | bytes 1048608 | tf_op jit(solution)/shard_map/ppermute | solution.py:145
  459.3 3.8 collective-permute-done.33.refs_1_.refs_3_
  463.1 3.0 fold.13
  466.2 5.1 all-to-all-start.7
  471.3 3.0 fold.14
  475.4 11.1 %collective-permute-done.34.refs_1_ = bf16[4,96,1024]{2,1,0:T(8,128)(2,1)S(1)} collective-permute-done((bf16[4,96,1024]{2,1,0:T(8,128)(2,1)}, bf16[4,96,1024]{2,1,0:T(8,128)(2,1)S(1)}, u32[]{:S(2)}, u32[]{:S(2)}) %collective-permute-start.34) | collective-permute-done | bytes 786464 | tf_op jit(solution)/shard_map/ppermute | solution.py:145
  489.5 7.0 %all-to-all-done.7 = bf16[4,128,1024]{2,1,0:T(8,128)(2,1)} async-done(((bf16[4,128,1024]{2,1,0:T(8,128)(2,1)}), bf16[4,128,1024]{2,1,0:T(8,128)(2,1)}, u32[]{:S(2)}, u32[]{:S(2)}) %all-to-all-start.7) | async-done | bytes 1048608 | tf_op jit(solution)/shard_map/all_to_all | solution.py:153
  496.5 3.5 all-to-all-start.6
  507.9 11.7 %all-to-all-done.6 = bf16[4,96,1024]{2,1,0:T(8,128)(2,1)S(1)} async-done(((bf16[4,96,1024]{2,1,0:T(8,128)(2,1)}), bf16[4,96,1024]{2,1,0:T(8,128)(2,1)S(1)}, u32[]{:S(2)}, u32[]{:S(2)}) %all-to-all-start.6) | async-done | bytes 786464 | tf_op jit(solution)/shard_map/all_to_all | solution.py:153
  536.2 2.4 collective-permute-done.37
  538.6 3.5 collective-permute-done.38
  542.1 4.4 collective-permute-done.39
  552.6 2.6 multiply_subtract_fusion
  (314 shorter events, 104.0 us)
Async XLA Ops:
  0.7 16.3 %copy-start.21 = (f32[32,3072]{1,0:T(8,128)S(1)}, f32[32,3072]{1,0:T(8,128)}, u32[]{:S(2)}) copy-start(f32[32,3072]{1,0:T(8,128)} %param.48) | copy-start | bytes 1179652
  10.6 26.4 %all-to-all-start = ((bf16[4,96,1024]{2,1,0:T(8,128)(2,1)}), bf16[4,96,1024]{2,1,0:T(8,128)(2,1)S(1)}, u32[]{:S(2)}, u32[]{:S(2)}) async-start(bf16[4,96,1024]{2,1,0:T(8,128)(2,1)} %broadcast_in_dim.103), calls=%async_computation | async-start | bytes 1572864 | tf_op jit(solution)/shard_map/all_to_all | solution.py:153
  16.9 24.7 %copy-start.16 = (f32[32,4096]{1,0:T(8,128)S(1)}, f32[32,4096]{1,0:T(8,128)}, u32[]{:S(2)}) copy-start(f32[32,4096]{1,0:T(8,128)} %param.50) | copy-start | bytes 1572868
  17.0 24.7 %copy-start.42 = (f32[32,1024]{1,0:T(8,128)S(1)}, f32[32,1024]{1,0:T(8,128)}, u32[]{:S(2)}) copy-start(f32[32,1024]{1,0:T(8,128)} %param.49) | copy-start | bytes 393220
  37.0 24.2 %copy-start.13 = (bf16[4,96,1024]{2,1,0:T(8,128)(2,1)}, bf16[4,96,1024]{2,1,0:T(8,128)(2,1)S(1)}, u32[]{:S(2)}) copy-start(bf16[4,96,1024]{2,1,0:T(8,128)(2,1)S(1)} %all-to-all-done.refs_0_) | copy-start | bytes 2359300
  38.1 23.1 %all-to-all-start.1 = ((bf16[4,96,1024]{2,1,0:T(8,128)(2,1)}), bf16[4,96,1024]{2,1,0:T(8,128)(2,1)S(1)}, u32[]{:S(2)}, u32[]{:S(2)}) async-start(bf16[4,96,1024]{2,1,0:T(8,128)(2,1)} %broadcast_in_dim.104), calls=%async_computation.1 | async-start | bytes 1572864 | tf_op jit(solution)/shard_map/all_to_all | solution.py:153
  41.7 12.1 %collective-permute-start = (bf16[4,96,1024]{2,1,0:T(8,128)(2,1)S(1)}, bf16[4,96,1024]{2,1,0:T(8,128)(2,1)S(1)}, u32[]{:S(2)}, u32[]{:S(2)}) collective-permute-start(bf16[4,96,1024]{2,1,0:T(8,128)(2,1)S(1)} %all-to-all-done.refs_0_), channel_id=1, source_target_pairs={{0,4},{1,3},{2,6},{3,1},{4,0},{5,7},{6,2},{7,5},{8,12},{9,11},{10,... | collective-permute-start | bytes 2359304 | tf_op jit(solution)/shard_map/ppermute | solution.py:145
  65.3 34.3 %all-to-all-start.2 = ((bf16[4,160,1024]{2,1,0:T(8,128)(2,1)}), bf16[4,160,1024]{2,1,0:T(8,128)(2,1)S(1)}, u32[]{:S(2)}, u32[]{:S(2)}) async-start(bf16[4,160,1024]{2,1,0:T(8,128)(2,1)} %broadcast_in_dim.105), calls=%async_computation.2 | async-start | bytes 2621440 | tf_op jit(solution)/shard_map/all_to_all | solution.py:153
  68.9 28.5 %collective-permute-start.1 = (bf16[8,96,1024]{2,1,0:T(8,128)(2,1)S(1)}, bf16[8,96,1024]{2,1,0:T(8,128)(2,1)}, u32[]{:S(2)}, u32[]{:S(2)}) collective-permute-start(bf16[8,96,1024]{2,1,0:T(8,128)(2,1)S(1)} %bitcast.92), channel_id=1, source_target_pairs={{0,2},{1,5},{2,0},{3,7},{4,6},{5,1},{6,4},{7,3},{8,10},{9,13},{10,... | collective-permute-start | bytes 4718600 | tf_op jit(solution)/shard_map/ppermute | solution.py:145
  70.4 20.8 %collective-permute-start.2 = (bf16[4,96,1024]{2,1,0:T(8,128)(2,1)}, bf16[4,96,1024]{2,1,0:T(8,128)(2,1)}, u32[]{:S(2)}, u32[]{:S(2)}) collective-permute-start(bf16[4,96,1024]{2,1,0:T(8,128)(2,1)} %copy-done.12), channel_id=1, source_target_pairs={{0,4},{1,3},{2,6},{3,1},{4,0},{5,7},{6,2},{7,5},{8,12},{9,11},{10,... | collective-permute-start | bytes 2359304 | tf_op jit(solution)/shard_map/ppermute | solution.py:145
  72.7 32.2 %copy-start.35 = (bf16[128,1024]{1,0:T(8,128)(2,1)S(1)}, bf16[128,1024]{1,0:T(8,128)(2,1)}, u32[]{:S(2)}) copy-start(bf16[128,1024]{1,0:T(8,128)(2,1)} %convert_element_type.117) | copy-start | bytes 786436
  99.7 14.0 %copy-start.9 = (bf16[4,160,1024]{2,1,0:T(8,128)(2,1)}, bf16[4,160,1024]{2,1,0:T(8,128)(2,1)S(1)}, u32[]{:S(2)}) copy-start(bf16[4,160,1024]{2,1,0:T(8,128)(2,1)S(1)} %all-to-all-done.2.refs_0_) | copy-start | bytes 3932164
  102.7 15.5 %collective-permute-start.4 = (bf16[8,96,1024]{2,1,0:T(8,128)(2,1)}, bf16[8,96,1024]{2,1,0:T(8,128)(2,1)}, u32[]{:S(2)}, u32[]{:S(2)}) collective-permute-start(bf16[8,96,1024]{2,1,0:T(8,128)(2,1)} %collective-permute-done.1.refs_3_), channel_id=1, source_target_pairs={{0,1},{1,0},{2,3},{3,2},{4,5},{5,4},{6,7},{7,6},{8,9},{9,8},{10,11... | collective-permute-start | bytes 4718600 | tf_op jit(solution)/shard_map/ppermute | solution.py:145
  102.8 15.4 %collective-permute-start.3 = (bf16[8,96,1024]{2,1,0:T(8,128)(2,1)S(1)}, bf16[8,96,1024]{2,1,0:T(8,128)(2,1)}, u32[]{:S(2)}, u32[]{:S(2)}) collective-permute-start(bf16[8,96,1024]{2,1,0:T(8,128)(2,1)S(1)} %bitcast.93), channel_id=1, source_target_pairs={{0,1},{1,0},{2,3},{3,2},{4,5},{5,4},{6,7},{7,6},{8,9},{9,8},{10,11... | collective-permute-start | bytes 4718600 | tf_op jit(solution)/shard_map/ppermute | solution.py:145
  103.4 34.7 %collective-permute-start.5 = (bf16[8,96,1024]{2,1,0:T(8,128)(2,1)}, bf16[8,96,1024]{2,1,0:T(8,128)(2,1)}, u32[]{:S(2)}, u32[]{:S(2)}) collective-permute-start(bf16[8,96,1024]{2,1,0:T(8,128)(2,1)} %bitcast.88), channel_id=1, source_target_pairs={{0,2},{1,5},{2,0},{3,7},{4,6},{5,1},{6,4},{7,3},{8,10},{9,13},{10,... | collective-permute-start | bytes 4718600 | tf_op jit(solution)/shard_map/ppermute | solution.py:145
  106.0 11.3 %copy-start.65 = (s32[512]{0:T(512)S(1)}, s32[512]{0:T(512)}, u32[]{:S(2)}) copy-start(s32[512]{0:T(512)} %param.39) | copy-start | bytes 6148
  106.0 32.1 %all-to-all-start.3 = ((bf16[4,128,1024]{2,1,0:T(8,128)(2,1)}), bf16[4,128,1024]{2,1,0:T(8,128)(2,1)}, u32[]{:S(2)}, u32[]{:S(2)}) async-start(bf16[4,128,1024]{2,1,0:T(8,128)(2,1)} %broadcast_in_dim.107), calls=%async_computation.3 | async-start | bytes 2097152 | tf_op jit(solution)/shard_map/all_to_all | solution.py:153
  113.7 24.4 %collective-permute-start.6 = (bf16[4,160,1024]{2,1,0:T(8,128)(2,1)S(1)}, bf16[4,160,1024]{2,1,0:T(8,128)(2,1)}, u32[]{:S(2)}, u32[]{:S(2)}) collective-permute-start(bf16[4,160,1024]{2,1,0:T(8,128)(2,1)S(1)} %all-to-all-done.2.refs_0_), channel_id=1, source_target_pairs={{0,4},{1,3},{2,6},{3,1},{4,0},{5,7},{6,2},{7,5},{8,12},{9,11},{10,... | collective-permute-start | bytes 3932168 | tf_op jit(solution)/shard_map/ppermute | solution.py:145
  141.4 43.3 %collective-permute-start.7 = (bf16[8,160,1024]{2,1,0:T(8,128)(2,1)}, bf16[8,160,1024]{2,1,0:T(8,128)(2,1)}, u32[]{:S(2)}, u32[]{:S(2)}) collective-permute-start(bf16[8,160,1024]{2,1,0:T(8,128)(2,1)} %bitcast.82), channel_id=1, source_target_pairs={{0,2},{1,5},{2,0},{3,7},{4,6},{5,1},{6,4},{7,3},{8,10},{9,13},{10,... | collective-permute-start | bytes 7864328 | tf_op jit(solution)/shard_map/ppermute | solution.py:145
  142.2 5.4 collective-permute-start.10
  142.7 5.3 collective-permute-start.9
  142.7 33.5 %collective-permute-start.8 = (bf16[4,128,1024]{2,1,0:T(8,128)(2,1)}, bf16[4,128,1024]{2,1,0:T(8,128)(2,1)S(1)}, u32[]{:S(2)}, u32[]{:S(2)}) collective-permute-start(bf16[4,128,1024]{2,1,0:T(8,128)(2,1)} %all-to-all-done.3.refs_0_), channel_id=1, source_target_pairs={{0,4},{1,3},{2,6},{3,1},{4,0},{5,7},{6,2},{7,5},{8,12},{9,11},{10,... | collective-permute-start | bytes 3145736 | tf_op jit(solution)/shard_map/ppermute | solution.py:145
  187.8 8.2 %collective-permute-start.13 = (bf16[8,160,1024]{2,1,0:T(8,128)(2,1)}, bf16[8,160,1024]{2,1,0:T(8,128)(2,1)}, u32[]{:S(2)}, u32[]{:S(2)}) collective-permute-start(bf16[8,160,1024]{2,1,0:T(8,128)(2,1)} %collective-permute-done.7.refs_3_), channel_id=1, source_target_pairs={{0,1},{1,0},{2,3},{3,2},{4,5},{5,4},{6,7},{7,6},{8,9},{9,8},{10,11... | collective-permute-start | bytes 7864328 | tf_op jit(solution)/shard_map/ppermute | solution.py:145
  187.9 8.8 %collective-permute-start.12 = (bf16[8,160,1024]{2,1,0:T(8,128)(2,1)S(1)}, bf16[8,160,1024]{2,1,0:T(8,128)(2,1)}, u32[]{:S(2)}, u32[]{:S(2)}) collective-permute-start(bf16[8,160,1024]{2,1,0:T(8,128)(2,1)S(1)} %bitcast.84), channel_id=1, source_target_pairs={{0,1},{1,0},{2,3},{3,2},{4,5},{5,4},{6,7},{7,6},{8,9},{9,8},{10,11... | collective-permute-start | bytes 7864328 | tf_op jit(solution)/shard_map/ppermute | solution.py:145
  188.4 39.6 %collective-permute-start.11 = (bf16[8,128,1024]{2,1,0:T(8,128)(2,1)}, bf16[8,128,1024]{2,1,0:T(8,128)(2,1)}, u32[]{:S(2)}, u32[]{:S(2)}) collective-permute-start(bf16[8,128,1024]{2,1,0:T(8,128)(2,1)} %bitcast.85), channel_id=1, source_target_pairs={{0,2},{1,5},{2,0},{3,7},{4,6},{5,1},{6,4},{7,3},{8,10},{9,13},{10,... | collective-permute-start | bytes 6291464 | tf_op jit(solution)/shard_map/ppermute | solution.py:145
  211.6 16.5 %copy-start.2 = (bf16[2,4,128,1024]{3,2,1,0:T(8,128)(2,1)S(1)}, bf16[2,4,128,1024]{3,2,1,0:T(8,128)(2,1)}, u32[]{:S(2)}) copy-start(bf16[2,4,128,1024]{3,2,1,0:T(8,128)(2,1)} %stack.23) | copy-start | bytes 6291460
  227.9 37.2 %collective-permute-start.16 = (bf16[4096,512]{1,0:T(8,128)(2,1)}, bf16[4096,512]{1,0:T(8,128)(2,1)}, u32[]{:S(2)}, u32[]{:S(2)}) collective-permute-start(bf16[4096,512]{1,0:T(8,128)(2,1)} %get-tuple-element.220.refs_0_), channel_id=1, source_target_pairs={{0,1},{1,0},{2,3},{3,2},{4,5},{5,4},{6,7},{7,6},{8,9},{9,8},{10,11... | collective-permute-start | bytes 12582920 | tf_op jit(solution)/shard_map/ppermute | solution.py:145
  228.1 10.7 %collective-permute-start.14 = (bf16[8,128,1024]{2,1,0:T(8,128)(2,1)S(1)}, bf16[8,128,1024]{2,1,0:T(8,128)(2,1)}, u32[]{:S(2)}, u32[]{:S(2)}) collective-permute-start(bf16[8,128,1024]{2,1,0:T(8,128)(2,1)S(1)} %bitcast.87), channel_id=1, source_target_pairs={{0,1},{1,0},{2,3},{3,2},{4,5},{5,4},{6,7},{7,6},{8,9},{9,8},{10,11... | collective-permute-start | bytes 6291464 | tf_op jit(solution)/shard_map/ppermute | solution.py:145
  228.5 13.0 %collective-permute-start.15 = (bf16[8,128,1024]{2,1,0:T(8,128)(2,1)}, bf16[8,128,1024]{2,1,0:T(8,128)(2,1)}, u32[]{:S(2)}, u32[]{:S(2)}) collective-permute-start(bf16[8,128,1024]{2,1,0:T(8,128)(2,1)} %collective-permute-done.11.refs_3_), channel_id=1, source_target_pairs={{0,1},{1,0},{2,3},{3,2},{4,5},{5,4},{6,7},{7,6},{8,9},{9,8},{10,11... | collective-permute-start | bytes 6291464 | tf_op jit(solution)/shard_map/ppermute | solution.py:145
  232.2 16.6 %copy-start.67 = (f32[16]{0:T(128)}, f32[16]{0:T(128)S(1)}, u32[]{:S(2)}) copy-start(f32[16]{0:T(128)S(1)} %select_reduce_fusion) | copy-start | bytes 196
  262.2 2.9 collective-permute-start.17
  266.1 10.6 %copy-start.26 = (bf16[1024,512]{1,0:T(8,128)(2,1)S(1)}, bf16[1024,512]{1,0:T(8,128)(2,1)}, u32[]{:S(2)}) copy-start(bf16[1024,512]{1,0:T(8,128)(2,1)} %get-tuple-element.261.refs_0_) | copy-start | bytes 3145732
  275.4 26.3 %collective-permute-start.18 = (bf16[8,128,1024]{2,1,0:T(8,128)(2,1)}, bf16[8,128,1024]{2,1,0:T(8,128)(2,1)S(1)}, u32[]{:S(2)}, u32[]{:S(2)}) collective-permute-start(bf16[8,128,1024]{2,1,0:T(8,128)(2,1)} %get-tuple-element.223), channel_id=1, source_target_pairs={{0,2},{1,5},{2,0},{3,7},{4,6},{5,1},{6,4},{7,3},{8,10},{9,13},{10,... | collective-permute-start | bytes 6291464 | tf_op jit(solution)/shard_map/ppermute | solution.py:145
  276.2 19.2 %collective-permute-start.21 = (bf16[1024,512]{1,0:T(8,128)(2,1)S(1)}, bf16[1024,512]{1,0:T(8,128)(2,1)S(1)}, u32[]{:S(2)}, u32[]{:S(2)}) collective-permute-start(bf16[1024,512]{1,0:T(8,128)(2,1)S(1)} %copy-done.25), channel_id=1, source_target_pairs={{0,1},{1,0},{2,3},{3,2},{4,5},{5,4},{6,7},{7,6},{8,9},{9,8},{10,11... | collective-permute-start | bytes 3145736 | tf_op jit(solution)/shard_map/ppermute | solution.py:145
  276.2 19.2 %collective-permute-start.19 = (bf16[1024,512]{1,0:T(8,128)(2,1)S(1)}, bf16[1024,512]{1,0:T(8,128)(2,1)}, u32[]{:S(2)}, u32[]{:S(2)}) collective-permute-start(bf16[1024,512]{1,0:T(8,128)(2,1)S(1)} %copy-done.38), channel_id=1, source_target_pairs={{0,1},{1,0},{2,3},{3,2},{4,5},{5,4},{6,7},{7,6},{8,9},{9,8},{10,11... | collective-permute-start | bytes 3145736 | tf_op jit(solution)/shard_map/ppermute | solution.py:145
  276.7 18.8 %collective-permute-start.20 = (bf16[1024,512]{1,0:T(8,128)(2,1)S(1)}, bf16[1024,512]{1,0:T(8,128)(2,1)S(1)}, u32[]{:S(2)}, u32[]{:S(2)}) collective-permute-start(bf16[1024,512]{1,0:T(8,128)(2,1)S(1)} %copy-done.26), channel_id=1, source_target_pairs={{0,1},{1,0},{2,3},{3,2},{4,5},{5,4},{6,7},{7,6},{8,9},{9,8},{10,11... | collective-permute-start | bytes 3145736 | tf_op jit(solution)/shard_map/ppermute | solution.py:145
  307.2 8.8 %collective-permute-start.23 = (bf16[4,512,1024]{2,1,0:T(8,128)(2,1)S(1)}, bf16[4,512,1024]{2,1,0:T(8,128)(2,1)}, u32[]{:S(2)}, u32[]{:S(2)}) collective-permute-start(bf16[4,512,1024]{2,1,0:T(8,128)(2,1)S(1)} %copy-done.10), channel_id=1, source_target_pairs={{0,1},{1,0},{2,3},{3,2},{4,5},{5,4},{6,7},{7,6},{8,9},{9,8},{10,11... | collective-permute-start | bytes 12582920 | tf_op jit(solution)/shard_map/ppermute | solution.py:145
  307.5 18.4 %collective-permute-start.24 = (bf16[512,1024]{1,0:T(8,128)(2,1)S(1)}, bf16[512,1024]{1,0:T(8,128)(2,1)S(1)}, u32[]{:S(2)}, u32[]{:S(2)}) collective-permute-start(bf16[512,1024]{1,0:T(8,128)(2,1)S(1)} %copy-done.29), channel_id=1, source_target_pairs={{0,1},{1,0},{2,3},{3,2},{4,5},{5,4},{6,7},{7,6},{8,9},{9,8},{10,11... | collective-permute-start | bytes 3145736 | tf_op jit(solution)/shard_map/ppermute | solution.py:145
  307.8 19.2 %collective-permute-start.22 = (bf16[4,128,1024]{2,1,0:T(8,128)(2,1)}, bf16[4,128,1024]{2,1,0:T(8,128)(2,1)S(1)}, u32[]{:S(2)}, u32[]{:S(2)}) collective-permute-start(bf16[4,128,1024]{2,1,0:T(8,128)(2,1)} %get-tuple-element.234), channel_id=1, source_target_pairs={{0,4},{1,3},{2,6},{3,1},{4,0},{5,7},{6,2},{7,5},{8,12},{9,11},{10,... | collective-permute-start | bytes 3145736 | tf_op jit(solution)/shard_map/ppermute | solution.py:145
  330.3 31.6 %collective-permute-start.25 = (bf16[8,128,1024]{2,1,0:T(8,128)(2,1)}, bf16[8,128,1024]{2,1,0:T(8,128)(2,1)}, u32[]{:S(2)}, u32[]{:S(2)}) collective-permute-start(bf16[8,128,1024]{2,1,0:T(8,128)(2,1)} %get-tuple-element.248), channel_id=1, source_target_pairs={{0,2},{1,5},{2,0},{3,7},{4,6},{5,1},{6,4},{7,3},{8,10},{9,13},{10,... | collective-permute-start | bytes 6291464 | tf_op jit(solution)/shard_map/ppermute | solution.py:145
  331.0 30.9 %all-to-all-start.4 = ((bf16[4,128,1024]{2,1,0:T(8,128)(2,1)}), bf16[4,128,1024]{2,1,0:T(8,128)(2,1)}, u32[]{:S(2)}, u32[]{:S(2)}) async-start(bf16[4,128,1024]{2,1,0:T(8,128)(2,1)} %fold.9), calls=%async_computation.4 | async-start | bytes 2097152 | tf_op jit(solution)/shard_map/all_to_all | solution.py:153
  353.1 12.2 %copy-start = (bf16[3,512,1024]{2,1,0:T(8,128)(2,1)S(1)}, bf16[3,512,1024]{2,1,0:T(8,128)(2,1)}, u32[]{:S(2)}) copy-start(bf16[3,512,1024]{2,1,0:T(8,128)(2,1)} %attend_back.1.packed_ref.refs_6_) | copy-start | bytes 9437188
  365.3 16.2 %collective-permute-start.27 = (bf16[3,512,1024]{2,1,0:T(8,128)(2,1)S(1)}, bf16[3,512,1024]{2,1,0:T(8,128)(2,1)}, u32[]{:S(2)}, u32[]{:S(2)}) collective-permute-start(bf16[3,512,1024]{2,1,0:T(8,128)(2,1)S(1)} %copy-done), channel_id=1, source_target_pairs={{0,1},{1,0},{2,3},{3,2},{4,5},{5,4},{6,7},{7,6},{8,9},{9,8},{10,11... | collective-permute-start | bytes 9437192 | tf_op jit(solution)/shard_map/ppermute | solution.py:145
  369.4 12.2 %copy-start.3 = (bf16[2048,512]{1,0:T(8,128)(2,1)}, bf16[2048,512]{1,0:T(8,128)(2,1)S(1)}, u32[]{:S(2)}) copy-start(bf16[2048,512]{1,0:T(8,128)(2,1)S(1)} %pad_maximum_fusion.refs_0_) | copy-start | bytes 6291460
  369.4 22.7 %collective-permute-start.28 = (bf16[2048,512]{1,0:T(8,128)(2,1)S(1)}, bf16[2048,512]{1,0:T(8,128)(2,1)S(1)}, u32[]{:S(2)}, u32[]{:S(2)}) collective-permute-start(bf16[2048,512]{1,0:T(8,128)(2,1)S(1)} %pad_maximum_fusion.refs_0_), channel_id=1, source_target_pairs={{0,1},{1,0},{2,3},{3,2},{4,5},{5,4},{6,7},{7,6},{8,9},{9,8},{10,11... | collective-permute-start | bytes 6291464 | tf_op jit(solution)/shard_map/ppermute | solution.py:145
  369.9 22.2 %collective-permute-start.26 = (bf16[4,128,1024]{2,1,0:T(8,128)(2,1)}, bf16[4,128,1024]{2,1,0:T(8,128)(2,1)}, u32[]{:S(2)}, u32[]{:S(2)}) collective-permute-start(bf16[4,128,1024]{2,1,0:T(8,128)(2,1)} %get-tuple-element.254), channel_id=1, source_target_pairs={{0,4},{1,3},{2,6},{3,1},{4,0},{5,7},{6,2},{7,5},{8,12},{9,11},{10,... | collective-permute-start | bytes 3145736 | tf_op jit(solution)/shard_map/ppermute | solution.py:145
  395.9 30.8 %collective-permute-start.29 = (bf16[8,128,1024]{2,1,0:T(8,128)(2,1)}, bf16[8,128,1024]{2,1,0:T(8,128)(2,1)S(1)}, u32[]{:S(2)}, u32[]{:S(2)}) collective-permute-start(bf16[8,128,1024]{2,1,0:T(8,128)(2,1)} %get-tuple-element.272), channel_id=1, source_target_pairs={{0,2},{1,5},{2,0},{3,7},{4,6},{5,1},{6,4},{7,3},{8,10},{9,13},{10,... | collective-permute-start | bytes 6291464 | tf_op jit(solution)/shard_map/ppermute | solution.py:145
  396.4 30.2 %all-to-all-start.5 = ((bf16[4,128,1024]{2,1,0:T(8,128)(2,1)}), bf16[4,128,1024]{2,1,0:T(8,128)(2,1)S(1)}, u32[]{:S(2)}, u32[]{:S(2)}) async-start(bf16[4,128,1024]{2,1,0:T(8,128)(2,1)} %fold.11), calls=%async_computation.5 | async-start | bytes 2097152 | tf_op jit(solution)/shard_map/all_to_all | solution.py:153
  413.5 3.6 collective-permute-start.31
  413.6 4.1 collective-permute-start.30
  431.5 31.7 %collective-permute-start.33 = (bf16[8,96,1024]{2,1,0:T(8,128)(2,1)S(1)}, bf16[8,96,1024]{2,1,0:T(8,128)(2,1)S(1)}, u32[]{:S(2)}, u32[]{:S(2)}) collective-permute-start(bf16[8,96,1024]{2,1,0:T(8,128)(2,1)S(1)} %copy-done.66), channel_id=1, source_target_pairs={{0,2},{1,5},{2,0},{3,7},{4,6},{5,1},{6,4},{7,3},{8,10},{9,13},{10,... | collective-permute-start | bytes 4718600 | tf_op jit(solution)/shard_map/ppermute | solution.py:145
  433.0 26.3 %collective-permute-start.32 = (bf16[4,128,1024]{2,1,0:T(8,128)(2,1)}, bf16[4,128,1024]{2,1,0:T(8,128)(2,1)S(1)}, u32[]{:S(2)}, u32[]{:S(2)}) collective-permute-start(bf16[4,128,1024]{2,1,0:T(8,128)(2,1)} %get-tuple-element.290), channel_id=1, source_target_pairs={{0,4},{1,3},{2,6},{3,1},{4,0},{5,7},{6,2},{7,5},{8,12},{9,11},{10,... | collective-permute-start | bytes 3145736 | tf_op jit(solution)/shard_map/ppermute | solution.py:145
  466.2 30.3 %all-to-all-start.7 = ((bf16[4,128,1024]{2,1,0:T(8,128)(2,1)}), bf16[4,128,1024]{2,1,0:T(8,128)(2,1)}, u32[]{:S(2)}, u32[]{:S(2)}) async-start(bf16[4,128,1024]{2,1,0:T(8,128)(2,1)} %fold.13), calls=%async_computation.7 | async-start | bytes 2097152 | tf_op jit(solution)/shard_map/all_to_all | solution.py:153
  474.2 12.2 %collective-permute-start.34 = (bf16[4,96,1024]{2,1,0:T(8,128)(2,1)}, bf16[4,96,1024]{2,1,0:T(8,128)(2,1)S(1)}, u32[]{:S(2)}, u32[]{:S(2)}) collective-permute-start(bf16[4,96,1024]{2,1,0:T(8,128)(2,1)} %get-tuple-element.298), channel_id=1, source_target_pairs={{0,4},{1,3},{2,6},{3,1},{4,0},{5,7},{6,2},{7,5},{8,12},{9,11},{10,... | collective-permute-start | bytes 2359304 | tf_op jit(solution)/shard_map/ppermute | solution.py:145
  496.5 23.1 %all-to-all-start.6 = ((bf16[4,96,1024]{2,1,0:T(8,128)(2,1)}), bf16[4,96,1024]{2,1,0:T(8,128)(2,1)S(1)}, u32[]{:S(2)}, u32[]{:S(2)}) async-start(bf16[4,96,1024]{2,1,0:T(8,128)(2,1)} %fold.15), calls=%async_computation.6 | async-start | bytes 1572864 | tf_op jit(solution)/shard_map/all_to_all | solution.py:153
  505.0 46.2 %copy-start.58 = (f32[32,80]{1,0:T(8,128)S(1)}, f32[32,80]{1,0:T(8,128)}, u32[]{:S(2)}) copy-start(f32[32,80]{1,0:T(8,128)} %param.52) | copy-start | bytes 30724
  505.0 47.6 %copy-start.15 = (f32[128,1024]{1,0:T(8,128)S(1)}, f32[128,1024]{1,0:T(8,128)}, u32[]{:S(2)}) copy-start(f32[128,1024]{1,0:T(8,128)} %param.51) | copy-start | bytes 1572868
  520.4 34.9 %copy-start.17 = (f32[32,4096]{1,0:T(8,128)S(1)}, f32[32,4096]{1,0:T(8,128)}, u32[]{:S(2)}) copy-start(f32[32,4096]{1,0:T(8,128)} %param.50) | copy-start | bytes 1572868
  520.4 34.9 %copy-start.24 = (f32[32,1024]{1,0:T(8,128)S(1)}, f32[32,1024]{1,0:T(8,128)}, u32[]{:S(2)}) copy-start(f32[32,1024]{1,0:T(8,128)} %copy-done.23) | copy-start | bytes 393220
  529.7 1.1 collective-permute-start.35
  531.5 3.5 collective-permute-start.36
  535.1 3.5 collective-permute-start.37
  538.6 3.5 collective-permute-start.38
  542.1 4.4 collective-permute-start.39
  (52 other events, 182.7 us)

commit v3 on v2

--- a/solution.py
+++ b/solution.py
@@ -22,9 +22,10 @@
 DECAY = 0.01
 ADAM_EPS = 1e-08
 FAR_AWAY = -1e30
-VMEM = 56 * 1024 * 1024
+VMEM = 62 * 1024 * 1024
 TABLE_AT = 768
 HEAD_AT = 896
+BANDS = 32
 
 
 def as_low(x):
@@ -127,11 +128,13 @@
         deep = self.total // self.sizes[0]
         return [[z * deep + rest for z in range(self.sizes[0])] for rest in range(deep)]
 
-    def owners(self, core_step, direction):
+    def owners(self, core_step, direction, deep_first=False):
         me = self.coords(lax.axis_index(AXES))
         core = (me[3] + core_step) % 2
         far, near, deep = (self.size(r) for r in ("far", "near", "z"))
         f, n, z = jnp.meshgrid(jnp.arange(far), jnp.arange(near), jnp.arange(deep), indexing="ij")
+        if deep_first:
+            f, n, z = (t.swapaxes(1, 2) for t in (f, n, z))
         if self.mixed():
             y = jnp.where(core == 0, me[1] + direction * n, me[1] + direction * f) % self.sizes[1]
             x = jnp.where(core == 0, me[2] + direction * f, me[2] + direction * n) % self.sizes[2]
@@ -162,11 +165,7 @@
 
 
 def all_sum(grid, x):
-    step = 1
-    while step < grid.total:
-        x = x + lax.ppermute(x, AXES, [(i, i ^ step) for i in range(grid.total)])
-        step *= 2
-    return x
+    return jnp.sum(lax.all_to_all(jnp.broadcast_to(x[None], (grid.total,) + x.shape), AXES, 0, 0), 0)
 
 
 def dot_nn(a, b):
@@ -235,7 +234,9 @@
     )(length, slopes, packed)
 
 
-def attend_back_kernel(length_ref, slope_ref, packed_ref, d_ref, lse_ref, out_ref, bias_ref):
+def attend_back_kernel(
+    length_ref, slope_ref, packed_ref, d_ref, lse_ref, dq_ref, dk_ref, dv_ref, bias_ref
+):
     step = pl.program_id(0)
     q_ref, k_ref, v_ref = (packed_ref.at[j] for j in range(3))
     frames = q_ref.shape[0]
@@ -257,9 +258,9 @@
         d_values.append(dot_nn(as_low(probs), d_mixed))
         d_keys.append(dot_nn(d_scores, query))
         d_query.append(dot_tn(keys, d_scores))
-    out_ref[0] = as_low((jnp.concatenate(d_query, 0) * HD**-0.5).T)
-    out_ref[1] = as_low(jnp.concatenate(d_keys, 1))
-    out_ref[2] = as_low(jnp.concatenate(d_values, 1))
+    dq_ref[...] = as_low((jnp.concatenate(d_query, 0) * HD**-0.5).T)
+    dk_ref[...] = as_low(jnp.concatenate(d_keys, 1))
+    dv_ref[...] = as_low(jnp.concatenate(d_values, 1))
 
 
 def attend_back(length, slopes, packed, d_mixed, lse):
@@ -272,8 +273,8 @@
         in_specs=[pl.BlockSpec(memory_space=pltpu.SMEM)] * 2
         + [stacked, pl.BlockSpec((frames, 2 * HD), lambda i: (0, i))]
         + [pl.BlockSpec((1, 2, frames), lambda i: (i, 0, 0))],
-        out_specs=stacked,
-        out_shape=jax.ShapeDtypeStruct((3, frames, width), jnp.bfloat16),
+        out_specs=[pl.BlockSpec((frames, 2 * HD), lambda i: (0, i))] * 3,
+        out_shape=[jax.ShapeDtypeStruct((frames, width), jnp.bfloat16)] * 3,
         scratch_shapes=[pltpu.VMEM((frames, frames), jnp.float32)],
         compiler_params=params(),
         name="attend_back",
@@ -290,131 +291,301 @@
     return x * share, share + x * bell * (0.5 / math.pi) ** 0.5
 
 
-def expand_kernel(x_ref, w_ref, act_ref, turned_ref, slope_ref):
-    hidden = dot_nn(x_ref[...], w_ref[0])
-    act, slope = gelu_both(hidden)
-    act = as_low(act)
-    act_ref[...] = act
-    turned_ref[...] = act.T
-    slope_ref[...] = as_low(slope)
-
-
-def expand(x, w, tile=1024):
+def expand_kernel(count, blocks, own_ref, other_ref, *refs):
+    sources = refs[:count]
+    x_ref, w_out, act_ref, turned_ref, slope_ref, w_ref, sems, out_sems = refs[count:]
+    step = pl.program_id(0)
+    width = x_ref.shape[1]
+    unit = width // sum(source.shape[0] for source in sources)
+
+    def copies(j):
+        entry = (w_ref.at[j], (j + 1) * unit, unit, None, sems.at[j])
+        return landing((own_ref, other_ref), sources, [entry])
+
+    def kept(j):
+        return pltpu.make_async_copy(w_ref.at[j], w_out.at[j], out_sems.at[j])
+
+    def chunk(j):
+        if j == 0:
+            for n in range(blocks):
+                begin(copies(n))
+        finish(copies(j))
+        kept(j).start()
+        hidden = dot_nn(x_ref[...], w_ref[j])
+        act, slope = gelu_both(hidden)
+        act = as_low(act)
+        act_ref[...] = act
+        turned_ref[...] = act.T
+        slope_ref[...] = as_low(slope)
+        if j == blocks - 1:
+            for n in range(blocks):
+                kept(n).wait()
+
+    for j in range(blocks):
+        pl.when(step == j)(partial(chunk, j))
+
+
+def expand(own, other, pieces, x, blocks):
     frames, width = x.shape
-    count, _, wide = w.shape
-    per = wide // tile
-    total = count * wide
+    total = blocks * width
     return pl.pallas_call(
-        expand_kernel,
-        grid=(count * per,),
-        in_specs=[
-            pl.BlockSpec((frames, width), lambda i: (0, 0)),
-            pl.BlockSpec((1, width, tile), lambda i: (i // per, 0, i % per)),
-        ],
+        partial(expand_kernel, len(pieces), blocks),
+        grid=(blocks,),
+        in_specs=piece_specs(pieces) + [pl.BlockSpec((frames, width), lambda i: (0, 0))],
         out_specs=[
-            pl.BlockSpec((frames, tile), lambda i: (0, i)),
-            pl.BlockSpec((tile, frames), lambda i: (i, 0)),
-            pl.BlockSpec((frames, tile), lambda i: (0, i)),
+            pl.BlockSpec(memory_space=pl.ANY),
+            pl.BlockSpec((frames, width), lambda i: (0, i)),
+            pl.BlockSpec((width, frames), lambda i: (i, 0)),
+            pl.BlockSpec((frames, width), lambda i: (0, i)),
         ],
         out_shape=[
+            jax.ShapeDtypeStruct((blocks, width, width), jnp.bfloat16),
             jax.ShapeDtypeStruct((frames, total), jnp.bfloat16),
             jax.ShapeDtypeStruct((total, frames), jnp.bfloat16),
             jax.ShapeDtypeStruct((frames, total), jnp.bfloat16),
         ],
+        scratch_shapes=[
+            pltpu.VMEM((blocks, width, width), jnp.bfloat16),
+            pltpu.SemaphoreType.DMA((blocks,)),
+            pltpu.SemaphoreType.DMA((blocks,)),
+        ],
         compiler_params=params(),
         name="expand",
-    )(x, w)
+    )(own, other, *pieces, x)
+
+
+def landing(idx_refs, sources, entries):
+    half = len(sources) // 2
+    copies = []
+    for s, source in enumerate(sources):
+        idx_ref = idx_refs[s // half]
+        count = source.shape[0]
+        for i in range(count):
+            band = idx_ref[(s % half) * count + i]
+            for goal, start, rows, lane, sem in entries:
+                part = source.at[i, pl.ds(start, rows)]
+                if lane is not None:
+                    part = source.at[i, pl.ds(start, rows), pl.ds(lane, goal.shape[-1])]
+                place = goal.at[pl.ds(pl.multiple_of(band * rows, rows), rows)]
+                copies.append(pltpu.make_async_copy(part, place, sem))
+    return copies
+
+
+def begin(copies):
+    for copy in copies:
+        copy.start()
+
+
+def finish(copies):
+    for copy in copies:
+        copy.wait()
+
+
+def piece_specs(pieces):
+    smem = pl.BlockSpec(memory_space=pltpu.SMEM)
+    return [smem, smem] + [pl.BlockSpec(memory_space=pl.ANY)] * len(pieces)
+
+
+def gain_row(edge_ref, at):
+    return edge_ref[at : at + 1].astype(jnp.float32)
 
 
 def front_kernel(
-    small_ref, table_ref, skip_ref, states_ref, hot_ref, mel_ref, time_ref, gain_ref,
-    embed_ref, stream_ref, start_ref, normed_ref, turned_ref,
+    at_gain, count, phone_rows, own_ref, other_ref, *refs
 ):
+    sources = refs[:count]
+    states_ref, states_turned_ref, hot_ref, mel_ref, time_ref = refs[count : count + 5]
+    (
+        small_out, skip_out, embed_ref, stream_ref, joined_ref, normed_ref, turned_ref, edge_ref,
+        small_ref, skip_ref, table_ref, sems, out_sems,
+    ) = refs[count + 5 :]
+    width = stream_ref.shape[1]
+    bands = sum(source.shape[0] for source in sources)
+    unit = width // bands
+    idx = (own_ref, other_ref)
+    first = landing(
+        idx, sources,
+        [(small_ref, 0, unit, None, sems.at[0]), (table_ref, 0, phone_rows, TABLE_AT, sems.at[0])],
+    )
+    second = landing(idx, sources, [(skip_ref, unit, 2 * unit, None, sems.at[1])])
+    begin(first)
+    begin(second)
     phones = embed_ref.shape[1]
-    width = stream_ref.shape[1]
+    joined_ref[width:] = states_turned_ref[...]
+    finish(first)
+    small_copy = pltpu.make_async_copy(small_ref, small_out, out_sems.at[0])
+    small_copy.start()
+    edge_ref[...] = small_ref[:, HEAD_AT:].T
     embedded = as_low(dot_nt(hot_ref[...], table_ref[...]))
     embed_ref[...] = embedded
     start = dot_nt(embedded, small_ref[:, :phones])
     start = start + dot_nt(mel_ref[...], small_ref[:, phones:TABLE_AT]) + time_ref[...]
     start = as_low(start)
-    start_ref[...] = start.T
+    joined_ref[:width] = start.T
+    finish(second)
+    skip_copy = pltpu.make_async_copy(skip_ref, skip_out, out_sems.at[1])
+    skip_copy.start()
     stream = dot_nn(start, skip_ref[:width]) + dot_nn(states_ref[...], skip_ref[width:])
     stream_ref[...] = stream
-    normed = as_low(normalize(stream)[0] * gain_ref[...])
+    normed = as_low(normalize(stream)[0] * gain_row(edge_ref, at_gain))
     normed_ref[...] = normed
     turned_ref[...] = normed.T
-
-
-def front(small, table, skip, states, hot, mel, time, gain):
+    small_copy.wait()
+    skip_copy.wait()
+
+
+def front(own, other, pieces, states, states_turned, hot, mel, time, phones, at_gain):
     frames, width = states.shape
-    phones = table.shape[0]
     f32, low = jnp.float32, jnp.bfloat16
+    bands = sum(p.shape[0] for p in pieces)
+    vmem, anywhere = pl.BlockSpec(memory_space=pltpu.VMEM), pl.BlockSpec(memory_space=pl.ANY)
     return pl.pallas_call(
-        front_kernel,
+        partial(front_kernel, at_gain, len(pieces), phones // bands),
+        in_specs=piece_specs(pieces) + [vmem] * 5,
+        out_specs=[anywhere] * 2 + [vmem] * 6,
         out_shape=[
+            jax.ShapeDtypeStruct((width, width), low),
+            jax.ShapeDtypeStruct((2 * width, width), low),
             jax.ShapeDtypeStruct((frames, phones), low),
             jax.ShapeDtypeStruct((frames, width), f32),
-            jax.ShapeDtypeStruct((width, frames), low),
+            jax.ShapeDtypeStruct((2 * width, frames), low),
             jax.ShapeDtypeStruct((frames, width), low),
             jax.ShapeDtypeStruct((width, frames), low),
+            jax.ShapeDtypeStruct((width - HEAD_AT, width), low),
+        ],
+        scratch_shapes=[
+            pltpu.VMEM((width, width), low),
+            pltpu.VMEM((2 * width, width), low),
+            pltpu.VMEM((phones, hot.shape[1]), low),
+            pltpu.SemaphoreType.DMA((2,)),
+            pltpu.SemaphoreType.DMA((2,)),
         ],
         compiler_params=params(),
         name="front",
-    )(small, table, skip, states, hot, mel, time, gain)
-
-
-def pack_kernel(x_ref, w_ref, out_ref):
-    out_ref[0] = as_low(dot_nn(x_ref[...], w_ref[0]))
-
-
-def pack(x, w):
+    )(own, other, *pieces, states, states_turned, hot, mel, time)
+
+
+def pack_kernel(count, blocks, own_ref, other_ref, *refs):
+    sources = refs[:count]
+    x_ref, w_out, out_ref, w_ref, sems, out_sems = refs[count:]
+    step = pl.program_id(0)
+    width = x_ref.shape[1]
+    unit = width // sum(source.shape[0] for source in sources)
+
+    def copies(j):
+        entry = (w_ref.at[j], j * unit, unit, None, sems.at[j])
+        return landing((own_ref, other_ref), sources, [entry])
+
+    def kept(j):
+        return pltpu.make_async_copy(w_ref.at[j], w_out.at[j], out_sems.at[j])
+
+    def chunk(j):
+        if j == 0:
+            for n in range(blocks):
+                begin(copies(n))
+        finish(copies(j))
+        kept(j).start()
+        out_ref[0] = as_low(dot_nn(x_ref[...], w_ref[j]))
+        if j == blocks - 1:
+            for n in range(blocks):
+                kept(n).wait()
+
+    for j in range(blocks):
+        pl.when(step == j)(partial(chunk, j))
+
+
+def pack(own, other, pieces, x, blocks):
     frames, width = x.shape
     return pl.pallas_call(
-        pack_kernel,
-        grid=(w.shape[0],),
-        in_specs=[
-            pl.BlockSpec((frames, width), lambda i: (0, 0)),
-            pl.BlockSpec((1, width, width), lambda i: (i, 0, 0)),
-        ],
-        out_specs=pl.BlockSpec((1, frames, width), lambda i: (i, 0, 0)),
-        out_shape=jax.ShapeDtypeStruct((w.shape[0], frames, width), jnp.bfloat16),
+        partial(pack_kernel, len(pieces), blocks),
+        grid=(blocks,),
+        in_specs=piece_specs(pieces) + [pl.BlockSpec((frames, width), lambda i: (0, 0))],
+        out_specs=[
+            pl.BlockSpec(memory_space=pl.ANY),
+            pl.BlockSpec((1, frames, width), lambda i: (i, 0, 0)),
+        ],
+        out_shape=[
+            jax.ShapeDtypeStruct((blocks, width, width), jnp.bfloat16),
+            jax.ShapeDtypeStruct((blocks, frames, width), jnp.bfloat16),
+        ],
+        scratch_shapes=[
+            pltpu.VMEM((blocks, width, width), jnp.bfloat16),
+            pltpu.SemaphoreType.DMA((blocks,)),
+            pltpu.SemaphoreType.DMA((blocks,)),
+        ],
         compiler_params=params(),
         name="pack",
-    )(x, w)
-
-
-def mid_kernel(mixed_ref, w_ref, stream_ref, gain_ref, mid_ref, in_ref, turned_ref, mixed_turned_ref):
+    )(own, other, *pieces, x)
+
+
+def mid_kernel(at_gain, count, own_ref, other_ref, *refs):
+    sources = refs[:count]
+    (
+        mixed_ref, stream_ref, edge_ref, w_out, mid_ref, in_ref, turned_ref, mixed_turned_ref,
+        w_ref, sem, out_sem,
+    ) = refs[count:]
+    width = stream_ref.shape[1]
+    unit = width // sum(source.shape[0] for source in sources)
+    copies = landing((own_ref, other_ref), sources, [(w_ref, 0, unit, None, sem)])
+    begin(copies)
     mixed = mixed_ref[...]
+    mixed_turned_ref[...] = mixed.T
+    finish(copies)
+    kept = pltpu.make_async_copy(w_ref, w_out, out_sem)
+    kept.start()
     mid = stream_ref[...] + dot_nn(mixed, w_ref[...])
     mid_ref[...] = mid
-    normed = as_low(normalize(mid)[0] * gain_ref[...])
+    normed = as_low(normalize(mid)[0] * gain_row(edge_ref, at_gain))
     in_ref[...] = normed
     turned_ref[...] = normed.T
-    mixed_turned_ref[...] = mixed.T
-
-
-def mid_step(mixed, w, stream, gain):
+    kept.wait()
+
+
+def mid_step(own, other, pieces, mixed, stream, edge, at_gain):
     frames, width = stream.shape
     low = jnp.bfloat16
+    vmem = pl.BlockSpec(memory_space=pltpu.VMEM)
     return pl.pallas_call(
-        mid_kernel,
+        partial(mid_kernel, at_gain, len(pieces)),
+        in_specs=piece_specs(pieces) + [vmem] * 3,
+        out_specs=[pl.BlockSpec(memory_space=pl.ANY)] + [vmem] * 4,
         out_shape=[
+            jax.ShapeDtypeStruct((width, width), low),
             jax.ShapeDtypeStruct((frames, width), jnp.float32),
             jax.ShapeDtypeStruct((frames, width), low),
             jax.ShapeDtypeStruct((width, frames), low),
             jax.ShapeDtypeStruct((width, frames), low),
         ],
+        scratch_shapes=[
+            pltpu.VMEM((width, width), low),
+            pltpu.SemaphoreType.DMA,
+            pltpu.SemaphoreType.DMA,
+        ],
         compiler_params=params(),
         name="mid",
-    )(mixed, w, stream, gain)
-
-
-def head_kernel(
-    share_ref, act_ref, w_ref, mid_ref, head_ref, target_ref, inside_ref, gain_ref,
-    d_ref, low_ref, grad_ref, gain_grad_ref, error_ref, total_ref,
-):
+    )(own, other, *pieces, mixed, stream, edge)
+
+
+def head_kernel(at_gain, count, share_ref, own_ref, other_ref, *refs):
+    sources = refs[:count]
+    (
+        act_ref, mid_ref, edge_ref, target_ref, inside_ref,
+        w_out, d_ref, low_ref, grad_ref, gain_grad_ref, error_ref,
+        total_ref, w_ref, sem, out_sem,
+    ) = refs[count:]
     step = pl.program_id(0)
-    part = dot_nn(act_ref[...], w_ref[...])
+    tile = act_ref.shape[1]
+    rows = w_ref.shape[0] // sum(source.shape[0] for source in sources)
+    kept = pltpu.make_async_copy(w_ref, w_out, out_sem)
+
+    @pl.when(step == 0)
+    def _():
+        copies = landing((own_ref, other_ref), sources, [(w_ref, 0, rows, None, sem)])
+        begin(copies)
+        finish(copies)
+        kept.start()
+
+    part = dot_nn(act_ref[...], w_ref[pl.ds(pl.multiple_of(step * tile, tile), tile)])
 
     @pl.when(step == 0)
     def _():
@@ -428,57 +599,72 @@
     def _():
         bins = target_ref.shape[1]
         normed, inverse = normalize(total_ref[...])
-        gain = gain_ref[...]
+        gain = gain_row(edge_ref, at_gain)
         head_in = as_low(normed * gain)
-        head = head_ref[:, :bins]
+        head = edge_ref[:bins]
         inside = inside_ref[...]
-        error = dot_nn(head_in, head) - target_ref[...]
+        error = dot_nt(head_in, head) - target_ref[...]
         error_ref[...] = jnp.sum(jnp.sum(error * error, 1, keepdims=True) * inside, 0, keepdims=True)
         d_prediction = as_low((2.0 * share_ref[0]) * error * inside)
         grad_ref[...] = dot_tn(head_in, d_prediction)
-        d_head_in = dot_nt(d_prediction, head)
+        d_head_in = dot_nn(d_prediction, head)
         gain_grad_ref[...] = jnp.sum(d_head_in * normed, 0, keepdims=True)
         d_stream = normalize_back(d_head_in * gain, normed, inverse)
         d_ref[...] = d_stream
         low_ref[...] = as_low(d_stream)
-
-
-def head_step(share, act, w, mid, head, target, inside, gain, tile=1024):
+        kept.wait()
+
+
+def head_step(share, own, other, pieces, act, mid, edge, target, inside, at_gain, tile=1024):
     frames, width = mid.shape
     bins = target.shape[1]
+    total = act.shape[1]
     whole = lambda *shape: pl.BlockSpec(shape, lambda i: (0,) * len(shape))
     return pl.pallas_call(
-        head_kernel,
-        grid=(act.shape[1] // tile,),
-        in_specs=[
-            pl.BlockSpec(memory_space=pltpu.SMEM),
+        partial(head_kernel, at_gain, len(pieces)),
+        grid=(total // tile,),
+        in_specs=[pl.BlockSpec(memory_space=pltpu.SMEM)]
+        + piece_specs(pieces)
+        + [
             pl.BlockSpec((frames, tile), lambda i: (0, i)),
-            pl.BlockSpec((tile, width), lambda i: (i, 0)),
-            whole(frames, width), whole(*head.shape), whole(frames, bins), whole(frames, 1), whole(1, width),
+            whole(frames, width), whole(*edge.shape), whole(frames, bins), whole(frames, 1),
         ],
         out_specs=[
+            pl.BlockSpec(memory_space=pl.ANY),
             whole(frames, width), whole(frames, width), whole(width, bins), whole(1, width), whole(1, 1),
         ],
         out_shape=[
+            jax.ShapeDtypeStruct((total, width), jnp.bfloat16),
             jax.ShapeDtypeStruct((frames, width), jnp.float32),
             jax.ShapeDtypeStruct((frames, width), jnp.bfloat16),
             jax.ShapeDtypeStruct((width, bins), jnp.float32),
             jax.ShapeDtypeStruct((1, width), jnp.float32),
             jax.ShapeDtypeStruct((1, 1), jnp.float32),
         ],
-        scratch_shapes=[pltpu.VMEM((frames, width), jnp.float32)],
+        scratch_shapes=[
+            pltpu.VMEM((frames, width), jnp.float32),
+            pltpu.VMEM((total, width), jnp.bfloat16),
+            pltpu.SemaphoreType.DMA,
+            pltpu.SemaphoreType.DMA,
+        ],
         compiler_params=params(),
         name="head",
-    )(share, act, w, mid, head, target, inside, gain)
+    )(share, own, other, *pieces, act, mid, edge, target, inside)
 
 
 def ffn_back_kernel(
-    low_ref, d_ref, down_ref, slope_ref, up_ref, mid_ref, gain_ref,
-    out_ref, out_low_ref, gain_grad_ref, hidden_ref, total_ref,
+    at_gain, low_ref, d_ref, down_ref, slope_ref, up_ref, mid_ref, edge_ref,
+    out_ref, out_low_ref, gain_grad_ref, *refs,
 ):
+    hidden_refs, total_ref = refs[:-1], refs[-1]
     step = pl.program_id(0)
     d_hidden = as_low(dot_nt(low_ref[...], down_ref[...]) * slope_ref[...].astype(jnp.float32))
-    hidden_ref[0] = d_hidden
+    for j, ref in enumerate(hidden_refs):
+
+        @pl.when(step == j)
+        def _(ref=ref):
+            ref[...] = d_hidden
+
     part = dot_nt(d_hidden, up_ref[0])
 
     @pl.when(step == 0)
@@ -494,92 +680,120 @@
         normed, inverse = normalize(mid_ref[...])
         grad = total_ref[...]
         gain_grad_ref[...] = jnp.sum(grad * normed, 0, keepdims=True)
-        out = d_ref[...] + normalize_back(grad * gain_ref[...], normed, inverse)
+        out = d_ref[...] + normalize_back(grad * gain_row(edge_ref, at_gain), normed, inverse)
         out_ref[...] = out
         out_low_ref[...] = as_low(out)
 
 
-def ffn_back(low, d, down, slope, up, mid, gain):
+def ffn_back(low, d, down, slope, up, mid, edge, at_gain):
     frames, width = mid.shape
     count = up.shape[0]
     whole = lambda *shape: pl.BlockSpec(shape, lambda i: (0,) * len(shape))
     return pl.pallas_call(
-        ffn_back_kernel,
+        partial(ffn_back_kernel, at_gain),
         grid=(count,),
         in_specs=[
             whole(frames, width), whole(frames, width),
             pl.BlockSpec((width, width), lambda i: (i, 0)),
             pl.BlockSpec((frames, width), lambda i: (0, i)),
             pl.BlockSpec((1, width, width), lambda i: (i, 0, 0)),
-            whole(frames, width), whole(1, width),
+            whole(frames, width), whole(*edge.shape),
         ],
         out_specs=[whole(frames, width), whole(frames, width), whole(1, width)]
-        + [pl.BlockSpec((1, frames, width), lambda i: (i, 0, 0))],
+        + [whole(frames, width)] * count,
         out_shape=[
             jax.ShapeDtypeStruct((frames, width), jnp.float32),
             jax.ShapeDtypeStruct((frames, width), jnp.bfloat16),
             jax.ShapeDtypeStruct((1, width), jnp.float32),
         ]
-        + [jax.ShapeDtypeStruct((count, frames, width), jnp.bfloat16)],
+        + [jax.ShapeDtypeStruct((frames, width), jnp.bfloat16)] * count,
         scratch_shapes=[pltpu.VMEM((frames, width), jnp.float32)],
         compiler_params=params(),
         name="ffn_back",
-    )(low, d, down, slope, up, mid, gain)
-
-
-def pack_back_kernel(packed_ref, w_ref, d_ref, stream_ref, gain_ref, low_ref, gain_grad_ref):
-    grad = sum(dot_nt(packed_ref[j], w_ref[j]) for j in range(w_ref.shape[0]))
-    normed, inverse = normalize(stream_ref[...])
-    gain_grad_ref[...] = jnp.sum(grad * normed, 0, keepdims=True)
-    low_ref[...] = as_low(d_ref[...] + normalize_back(grad * gain_ref[...], normed, inverse))
-
-
-def pack_back(packed, w, d, stream, gain):
+    )(low, d, down, slope, up, mid, edge)
+
+
+def pack_back_kernel(at_gain, blocks, *refs):
+    w_ref, d_ref, stream_ref, edge_ref, low_ref, gain_grad_ref, total_ref = refs[blocks:]
+    step = pl.program_id(0)
+
+    def chunk(j):
+        part = dot_nt(refs[j][...], w_ref[0])
+        total_ref[...] = part if j == 0 else total_ref[...] + part
+
+    for j in range(blocks):
+        pl.when(step == j)(partial(chunk, j))
+
+    @pl.when(step == pl.num_programs(0) - 1)
+    def _():
+        grad = total_ref[...]
+        normed, inverse = normalize(stream_ref[...])
+        gain_grad_ref[...] = jnp.sum(grad * normed, 0, keepdims=True)
+        gain = gain_row(edge_ref, at_gain)
+        low_ref[...] = as_low(d_ref[...] + normalize_back(grad * gain, normed, inverse))
+
+
+def pack_back(packed, w, d, stream, edge, at_gain):
     frames, width = stream.shape
+    whole = lambda *shape: pl.BlockSpec(shape, lambda i: (0,) * len(shape))
     return pl.pallas_call(
-        pack_back_kernel,
+        partial(pack_back_kernel, at_gain, w.shape[0]),
+        grid=(w.shape[0],),
+        in_specs=[whole(frames, width)] * w.shape[0]
+        + [
+            pl.BlockSpec((1, width, width), lambda i: (i, 0, 0)),
+            whole(frames, width), whole(frames, width), whole(*edge.shape),
+        ],
+        out_specs=[whole(frames, width), whole(1, width)],
         out_shape=[
             jax.ShapeDtypeStruct((frames, width), jnp.bfloat16),
             jax.ShapeDtypeStruct((1, width), jnp.float32),
         ],
+        scratch_shapes=[pltpu.VMEM((frames, width), jnp.float32)],
         compiler_params=params(),
         name="pack_back",
-    )(packed, w, d, stream, gain)
-
-
-def tail_kernel(d_ref, skip_ref, small_ref, embed_ref, mel_ref, hot_ref, main_ref, table_ref):
+    )(*packed, w, d, stream, edge)
+
+
+def tail_kernel(
+    at_gain, d_ref, skip_ref, small_ref, embed_ref, mel_ref, hot_ref, head_ref, one_ref, two_ref, three_ref,
+    main_ref, table_ref, edge_ref,
+):
     phones = embed_ref.shape[1]
     d_start = as_low(dot_nt(d_ref[...], skip_ref[...]))
     d_phones = as_low(dot_nn(d_start, small_ref[:, :phones]))
     main_ref[:, :phones] = as_low(dot_tn(d_start, embed_ref[...]))
     main_ref[:, phones:] = as_low(dot_tn(d_start, mel_ref[...]))
     table_ref[...] = as_low(dot_tn(d_phones, hot_ref[...]))
-
-
-def tail(d, skip, small, embed, mel, hot):
+    edge = head_ref[...]
+    lanes = edge.shape[1]
+    edge = jnp.pad(edge, ((0, 0), (0, edge_ref.shape[1] - lanes)))
+    lane = lax.broadcasted_iota(jnp.int32, edge.shape, 1)
+    for j, ref in enumerate((one_ref, two_ref, three_ref)):
+        column = jnp.broadcast_to(ref[...], (8, edge.shape[0])).T[:, :1]
+        edge = jnp.where(lane == at_gain + j, column, edge)
+    edge_ref[...] = as_low(edge)
+
+
+def tail(d, skip, small, embed, mel, hot, head, gains, at_gain):
     width = d.shape[1]
     phones = embed.shape[1]
     whole = lambda x: pl.BlockSpec(x.shape, lambda i: (0, 0))
+    arrays = (small, embed, mel, hot, head, *gains)
+    shapes = [(width, TABLE_AT), (phones, hot.shape[1]), (width, width - HEAD_AT)]
     return pl.pallas_call(
-        tail_kernel,
+        partial(tail_kernel, at_gain),
         grid=(1,),
-        in_specs=[whole(d), pl.BlockSpec((width, width), lambda i: (0, 0))]
-        + [whole(x) for x in (small, embed, mel, hot)],
-        out_specs=[
-            pl.BlockSpec((width, TABLE_AT), lambda i: (0, 0)),
-            pl.BlockSpec((phones, hot.shape[1]), lambda i: (0, 0)),
-        ],
-        out_shape=[
-            jax.ShapeDtypeStruct((width, TABLE_AT), jnp.bfloat16),
-            jax.ShapeDtypeStruct((phones, hot.shape[1]), jnp.bfloat16),
-        ],
+        in_specs=[whole(d), pl.BlockSpec((width, width), lambda i: (0, 0))] + [whole(x) for x in arrays],
+        out_specs=[pl.BlockSpec(s, lambda i: (0, 0)) for s in shapes],
+        out_shape=[jax.ShapeDtypeStruct(s, jnp.bfloat16) for s in shapes],
         compiler_params=params(),
         name="tail",
-    )(d, skip, small, embed, mel, hot)
+    )(d, skip, *arrays)
 
 
 def grads_kernel(plan, count, rows, legs, came_too, idx_ref, *refs):
-    refs, picked_ref, sems = refs[:-2], refs[-2], refs[-1]
+    refs, picked_ref, right_ref, sems = refs[:-3], refs[-3], refs[-2], refs[-1]
     outs = refs[len(refs) - legs :]
     came_ref = refs[len(refs) - legs - 1] if came_too else None
     step = pl.program_id(0)
@@ -598,6 +812,9 @@
             )
             for side, left in enumerate(lefts)
             for i in range(count)
+        ] + [
+            pltpu.make_async_copy(refs[right], right_ref.at[slot, side], sems.at[slot])
+            for side, right in enumerate(rights)
         ]
 
     def chunk(c):
@@ -627,10 +844,7 @@
                 total = total + came_ref[...].astype(jnp.float32)
         else:
             wide = outs[0].shape[2]
-            total = sum(
-                dot_nn(picked_ref[c % 2, side], refs[r][0] if len(refs[r].shape) == 3 else refs[r][...])
-                for side, r in enumerate(rights)
-            )
+            total = sum(dot_nn(picked_ref[c % 2, side], right_ref[c % 2, side]) for side in range(len(rights)))
             total = total.reshape(count, rows, wide)
         for f in range(legs):
             outs[f][...] = as_low(total[f * each : (f + 1) * each])
@@ -641,14 +855,11 @@
 
 def grads(plan, arrays, idx, frames, rows, width, legs, came=None):
     count = idx.shape[0]
-    picked = [j for entry in plan if entry[1] is not None for j in entry[0]]
+    copied = [j for entry in plan if entry[1] is not None for j in entry[0] + entry[1]]
 
     def spec(j, x):
-        if j in picked:
+        if j in copied:
             return pl.BlockSpec(memory_space=pl.ANY)
-        if len(x.shape) == 3:
-            first = min(c for c, entry in enumerate(plan) if entry[1] is not None and j in entry[1])
-            return pl.BlockSpec((1,) + x.shape[1:], lambda i: (jnp.maximum(i - first, 0), 0, 0))
         return pl.BlockSpec(x.shape, lambda i, n=len(x.shape): (0,) * n)
 
     specs = [spec(j, x) for j, x in enumerate(arrays)]
@@ -663,6 +874,7 @@
         out_shape=[jax.ShapeDtypeStruct((count // legs, rows * len(plan), width), jnp.bfloat16)] * legs,
         scratch_shapes=[
             pltpu.VMEM((2, 2, count * rows, frames), jnp.bfloat16),
+            pltpu.VMEM((2, 2, frames, width), jnp.bfloat16),
             pltpu.SemaphoreType.DMA((2,)),
         ],
         compiler_params=params(),
@@ -718,39 +930,59 @@
     )(*parts)
 
 
-def place_kernel(layout, sources, count, *refs):
-    idx_refs, sources_refs = refs[:2], refs[2 : 2 + sources]
-    outs, sem = refs[2 + sources : -1], refs[-1]
-    copies = []
-    for s, source in enumerate(sources_refs):
-        idx_ref = idx_refs[s // (sources // 2)]
-        first = (s % (sources // 2)) * count
-        for i in range(count):
-            owner = idx_ref[first + i]
-            start = 0
-            for (out, block), rows in layout:
-                ref = outs[out]
-                goal = ref.at[owner] if block is None else ref.at[block, owner]
-                copy = pltpu.make_async_copy(source.at[i, pl.ds(start, rows)], goal, sem)
-                copy.start()
-                copies.append(copy)
-                start += rows
-    for copy in copies:
-        copy.wait()
-
-
-def place(layout, shapes, own, other, pieces):
-    width = pieces[0].shape[2]
-    return pl.pallas_call(
-        partial(place_kernel, layout, len(pieces), pieces[0].shape[0]),
-        in_specs=[pl.BlockSpec(memory_space=pltpu.SMEM)] * 2
-        + [pl.BlockSpec(memory_space=pl.ANY)] * len(pieces),
-        out_specs=[pl.BlockSpec(memory_space=pltpu.VMEM)] * len(shapes),
-        out_shape=[jax.ShapeDtypeStruct(s, jnp.bfloat16) for s in shapes],
-        scratch_shapes=[pltpu.SemaphoreType.DMA],
+def update(grad, rate, master_ref, moment_ref, square_ref, clip):
+    return adam_step(master_ref[...], grad * clip, moment_ref[...], square_ref[...], rate)
+
+
+def adam_kernel(at, clip_ref, *refs):
+    phone_rows, phone_width, inputs, at_gain = at
+    small, skip, attend, output, expand, reduce = refs[:6]
+    masters, moments, squares = refs[6:15], refs[15:24], refs[24:33]
+    outs = refs[33:]
+    unit = small.shape[0]
+    clip = clip_ref[0]
+    mel_lanes = inputs - phone_width
+    lanes = [small[:, phone_width : phone_width + mel_lanes], small[:, :phone_width]]
+    edge = small[:, HEAD_AT:]
+    turned_edge = edge.T
+    bins = masters[7].shape[1]
+
+    def columns(ref, first):
+        blocks = [ref[j : j + unit] for j in range(first, ref.shape[0], unit)]
+        return jnp.concatenate(blocks, 1)
+
+    grads_of = [
+        jnp.concatenate(lanes, 1),
+        small[:phone_rows, TABLE_AT:HEAD_AT],
+        skip[...],
+        columns(attend, unit),
+        attend[:unit],
+        columns(expand, 0),
+        reduce[...],
+        edge[:, :bins],
+        turned_edge[at_gain : at_gain + 3],
+    ]
+    for j, grad in enumerate(grads_of):
+        rate = GAIN_RATE if j in (1, 8) else LEARN_RATE
+        after = update(grad, rate, masters[j], moments[j], squares[j], clip)
+        for n, value in enumerate(after):
+            outs[9 * n + j][...] = value
+
+
+def adam(clip, shares, masters, moments, squares, at):
+    turned = lambda group: [x.T if j < 2 else x for j, x in enumerate(group)]
+    masters, moments, squares = turned(masters), turned(moments), turned(squares)
+    vmem = pl.BlockSpec(memory_space=pltpu.VMEM)
+    arrays = [*shares, *masters, *moments, *squares]
+    results = pl.pallas_call(
+        partial(adam_kernel, at),
+        in_specs=[pl.BlockSpec(memory_space=pltpu.SMEM)] + [vmem] * len(arrays),
+        out_specs=[vmem] * 27,
+        out_shape=[jax.ShapeDtypeStruct(x.shape, jnp.float32) for x in (*masters, *moments, *squares)],
         compiler_params=params(),
-        name="place",
-    )(own, other, *pieces)
+        name="adam",
+    )(clip, *arrays)
+    return [y for n in range(3) for y in turned(results[9 * n : 9 * n + 9])]
 
 
 def shards(
@@ -802,7 +1034,6 @@
         square_input, square_table, square_skip, square_attend, square_output,
         square_expand, square_reduce, square_head, square_gains,
     )
-    rates = (LEARN_RATE, GAIN_RATE) + (LEARN_RATE,) * 6 + (GAIN_RATE,)
     frames, mel_bins = clean_mel.shape
     width = w_skip.shape[1]
     heads = width // HD
@@ -851,15 +1082,16 @@
         [("output", None, as_low(w_output))] + [("expand", j, w) for j, w in enumerate(expand_blocks)],
         [("reduce", None, as_low(w_reduce))],
     ]
-    counts_of = {"attend": packs, "expand": wides}
     if fast:
         own, other = grid.owners(0, -1), grid.owners(1, -1)
-
-    def named(stage):
-        return list(dict.fromkeys(name for name, _, _ in stage))
+        own_turned, other_turned = grid.owners(0, -1, True), grid.owners(1, -1, True)
+        mine, theirs = grid.owners(0, 1), grid.owners(1, 1)
 
     def load(stage):
         return jnp.concatenate([w for _, _, w in stage], 0)
+
+    def sibling(x):
+        return shift(grid, x, "core", 1)
 
     def along(x, role, *after):
         return spread(grid, tied(x, *after) if after else x, role)
@@ -871,54 +1103,20 @@
     def plane(moved):
         return stack(moved).reshape((-1,) + moved[0].shape[1:])
 
-    def settle(stage, pieces, own, other):
-        pieces = pieces + [shift(grid, p, "core", 1) for p in pieces]
-        names = named(stage)
-        shapes, layout = [], []
-        for name in names:
-            rows = [w.shape[0] for n, _, w in stage if n == name][0]
-            lead = (counts_of[name],) if name in counts_of else ()
-            shapes.append(lead + (devices, rows, width))
-        for name, block, w in stage:
-            layout.append(((names.index(name), block), w.shape[0]))
-        return dict(zip(names, place(layout, shapes, own, other, pieces)))
-
     def gather_whole(stage):
-        full = {name: [] for name in named(stage)}
         rows = lax.all_gather(load(stage), AXES, axis=0, tiled=False)
-        start = 0
+        parts, start = [], 0
         for name, _, w in stage:
-            full[name].append(rows[:, start : start + w.shape[0]])
+            part = rows[:, start : start + w.shape[0]]
             start += w.shape[0]
-        return {n: jnp.stack(p) if n in counts_of else p[0] for n, p in full.items()}
-
-    loads = [load(stage) for stage in stages]
-    if fast:
-        deep_0 = deepen(loads[0])
-        near_0, deep_1 = join(along(deep_0, "near"), deepen(loads[1], deep_0))
-        near_0 = plane(near_0)
-        far_0, near_1, deep_2 = join(
-            along(near_0, "far"), along(deep_1, "near", near_0), deepen(loads[2], near_0)
-        )
-        near_1 = plane(near_1)
-        far_1, near_2 = along(near_1, "far"), along(deep_2, "near", near_1)
-        deep_3 = deepen(loads[3], near_1)
-        far_0 = [tied(p, near_1) for p in far_0]
-        whole = settle(stages[0], far_0, own, other)
-    else:
-        whole = gather_whole(stages[0])
-    small_full = whole["small"].reshape(width, width)
-    skip_full = whole["skip"].reshape(-1, width)
-    table_turned = whole["small"][:, :phone_wide, TABLE_AT:HEAD_AT].reshape(phone_width, phones)
-    head_block = small_full[:, HEAD_AT:]
-    gains_wide = head_block[:, mel_bins : mel_bins + 3].astype(jnp.float32).T
-    tallies = whole["small"][:, 0, at_count : at_count + 3].astype(jnp.float32)
-    counts = jnp.sum(
-        (tallies[:, :1] == jnp.arange(SPK, dtype=jnp.float32)[None, :])
-        * (16.0 * tallies[:, 1:2] + tallies[:, 2:3]),
-        0,
-    )
-    share = jnp.sum(speaker_hot / jnp.maximum(counts, 1.0)) / SPK
+            if name == "small":
+                table = part[:, :phone_wide, TABLE_AT:HEAD_AT].reshape(BANDS, -1, phones)
+                table = jnp.pad(table, ((0, 0), (0, width // BANDS - table.shape[1]), (0, 0)))
+                part = part.reshape(BANDS, -1, width)
+                part = jnp.concatenate([part[..., :TABLE_AT], table, part[..., HEAD_AT:]], 2)
+            parts.append(part.reshape(BANDS, -1, width))
+        rows = jnp.concatenate(parts, 1)
+        return [rows[: BANDS // 2], rows[BANDS // 2 :]]
 
     flow = flow_time[0]
     noisy_mel = (1.0 - (1.0 - SIGMA) * flow) * gauss_noise + flow * clean_mel
@@ -928,57 +1126,86 @@
     mel = jnp.pad(mel, ((0, 0), (0, mel_lanes - mel.shape[1])))
     phone_hot = as_low(phone_ids[:, None] == jnp.arange(phones)[None, :])
     slopes = head_slopes(heads)
+    times = time_features(flow, width)[None, :]
+    inside = frame_inside[:, None]
     states_turned = skip_states.T
-
-    embedded, stream, start_turned, attn_in, attn_turned = front(
-        small_full, table_turned, skip_full, skip_states, phone_hot, mel,
-        time_features(flow, width)[None, :], gains_wide[0:1],
-    )
+    loads = [load(stage) for stage in stages]
     if fast:
-        far_1, near_2, deep_3, embedded, stream, start_turned, attn_in, attn_turned = join(
-            far_1, near_2, deep_3, embedded, stream, start_turned, attn_in, attn_turned
+        deep_0, near_2 = join(deepen(loads[0]), along(loads[2], "near"))
+        pair_2 = stack(near_2)
+        near_0, deep_1, target, mel, phone_hot, slopes, times, inside, states_turned = join(
+            along(deep_0, "near"), deepen(loads[1], deep_0),
+            target, mel, phone_hot, slopes, times, inside, states_turned,
         )
-        near_2 = plane(near_2)
-        far_2, near_3 = along(near_2, "far"), along(deep_3, "near", near_2)
-        far_1 = [tied(p, near_2) for p in far_1]
-        whole.update(settle(stages[1], far_1, own, other))
+        near_0 = plane(near_0)
+        deep_2 = deepen(pair_2, near_0)
+        far_0, core_0, near_1, own, other, own_turned, other_turned, mine, theirs = join(
+            along(near_0, "far")[1], sibling(near_0), along(deep_1, "near", near_0),
+            own, other, own_turned, other_turned, mine, theirs,
+        )
+        near_1 = plane(near_1)
+        far_0 = tied(far_0, near_1)
+        pieces_0 = [near_0, far_0, core_0, sibling(far_0)]
+        far_1 = along(near_1, "far")[1]
+        core_1 = sibling(near_1)
     else:
-        whole.update(gather_whole(stages[1]))
-    attend_full = whole["attend"].reshape(packs, width, width)
-    packed = pack(attn_in, attend_full)
+        own, other = jnp.arange(BANDS // 2), jnp.arange(BANDS // 2, BANDS)
+        own_turned, other_turned = own, other
+        pieces_0 = gather_whole(stages[0])
+    small_full, skip_full, embedded, stream, joined_turned, attn_in, attn_turned, edges = front(
+        own, other, pieces_0, skip_states, states_turned, phone_hot, mel, times, phone_width, mel_bins
+    )
+    tallies = edges[at_count - HEAD_AT : at_count - HEAD_AT + 3].reshape(3, devices, unit)
+    tallies = tallies[:, :, 0].astype(jnp.float32)
+    counts = jnp.sum(
+        (tallies[0][:, None] == jnp.arange(SPK, dtype=jnp.float32)[None, :])
+        * (16.0 * tallies[1] + tallies[2])[:, None],
+        0,
+    )
+    share = jnp.sum(speaker_hot / jnp.maximum(counts, 1.0)) / SPK
+
+    if fast:
+        far_1, core_1, deep_2, embedded, stream, attn_in, attn_turned, edges = join(
+            far_1, core_1, deep_2, embedded, stream, attn_in, attn_turned, edges
+        )
+        near_2 = deep_2.reshape((-1,) + deep_2.shape[2:])
+        pieces_1 = [near_1, far_1, core_1, sibling(far_1)]
+        far_2 = along(near_2, "far")[1]
+        core_2 = sibling(near_2)
+        deep_3 = deepen(loads[3], near_2)
+    else:
+        pieces_1 = gather_whole(stages[1])
+    attend_full, packed = pack(own, other, pieces_1, attn_in, packs)
     mixed, lse = attend(lengths, slopes, packed)
     if fast:
-        far_2, near_3, packed, mixed, lse = join(far_2, near_3, packed, mixed, lse)
-        near_3 = plane(near_3)
-        far_3 = along(near_3, "far")
-        far_2 = [tied(p, near_3) for p in far_2]
-        whole.update(settle(stages[2], far_2, own, other))
+        far_2, deep_3, core_2, packed, mixed, lse, share, joined_turned = join(
+            far_2, deep_3, core_2, packed, mixed, lse, share, joined_turned
+        )
+        near_3 = along(deep_3, "near")
+        pieces_2 = [near_2, far_2, core_2, sibling(far_2)]
     else:
-        whole.update(gather_whole(stages[2]))
-    output_full = whole["output"].reshape(width, width)
-    expand_full = whole["expand"].reshape(wides, width, width)
-    stream_mid, ffn_in, ffn_turned, mixed_turned = mid_step(
-        mixed, output_full, stream, gains_wide[1:2]
-    )
-    activated, act_turned, gelu_slope = expand(ffn_in, expand_full)
+        pieces_2 = gather_whole(stages[2])
+    output_full, stream_mid, ffn_in, ffn_turned, mixed_turned = mid_step(
+        own_turned, other_turned, pieces_2, mixed, stream, edges, mel_bins + 1
+    )
     if fast:
-        far_3, stream_mid, ffn_turned, mixed_turned, activated, act_turned, gelu_slope = join(
-            far_3, stream_mid, ffn_turned, mixed_turned, activated, act_turned, gelu_slope
+        near_3 = plane([near_3[0], tied(near_3[1], ffn_in)] + near_3[2:])
+        far_3 = along(near_3, "far")[1]
+        core_3 = sibling(near_3)
+    expand_full, activated, act_turned, gelu_slope = expand(
+        own_turned, other_turned, pieces_2, ffn_in, wides
+    )
+    if fast:
+        far_3, core_3, stream_mid, ffn_turned, mixed_turned, activated, act_turned, gelu_slope = join(
+            far_3, core_3, stream_mid, ffn_turned, mixed_turned, activated, act_turned, gelu_slope
         )
-        whole.update(settle(stages[3], far_3, own, other))
+        pieces_3 = [near_3, far_3, core_3, sibling(far_3)]
     else:
-        whole.update(gather_whole(stages[3]))
-    reduce_full = whole["reduce"].reshape(-1, width)
-    d_stream_out, d_branch, grad_head, grad_gain_three, error_sum = head_step(
-        share[None], activated, reduce_full, stream_mid, head_block, target,
-        frame_inside[:, None], gains_wide[2:3],
-    )
-    if fast:
-        mine, theirs = grid.owners(0, 1), grid.owners(1, 1)
+        pieces_3 = gather_whole(stages[3])
+    reduce_full, d_stream_out, d_branch, grad_head, grad_gain_three, error_sum = head_step(
+        share[None], own, other, pieces_3, activated, stream_mid, edges, target, inside, mel_bins + 2
+    )
     far, near, deep = (grid.size(r) for r in ("far", "near", "z"))
-
-    def sibling(x):
-        return shift(grid, x, "core", 1)
 
     def both(*arrays):
         return [y for x in arrays for y in (x, sibling(x))]
@@ -1005,29 +1232,28 @@
     offsets = [j * unit for j in range(wides)]
     if fast:
         plan = [((0, 1), (2, 3), wides * unit, o) for o in offsets]
-        legs_0 = sums(plan, both(act_turned, d_branch))
+        legs_0 = sums(plan, both(tied(act_turned, pieces_3[3]), d_branch))
         moved_0 = hops(legs_0, "far")
         d_branch_next = tied(d_branch, legs_0[0])
     else:
         share_reduce = dense([(act_turned, d_branch, wides * unit, o) for o in offsets])
         d_branch_next = d_branch
-    d_stream_mid, d_out, grad_gain_two, d_hidden = ffn_back(
-        d_branch_next, d_stream_out, reduce_full, gelu_slope, expand_full, stream_mid, gains_wide[1:2]
-    )
+    d_stream_mid, d_out, grad_gain_two, *d_hidden = ffn_back(
+        d_branch_next, d_stream_out, reduce_full, gelu_slope, expand_full, stream_mid, edges, mel_bins + 1
+    )
+    d_mixed = as_low(dot_nt(d_out, output_full))
     if fast:
-        turned = both(ffn_turned, mixed_turned, attn_turned)
-        moved_0, turned, d_stream_mid, d_out, d_hidden = join(
-            moved_0, turned, d_stream_mid, d_out, d_hidden
+        turned = both(ffn_turned)
+        d_hiddens = both(*d_hidden)
+        moved_0, turned, d_hiddens, d_stream_mid, d_out, d_mixed = join(
+            moved_0, turned, d_hiddens, d_stream_mid, d_out, d_mixed
         )
         legs_0 = fold([legs_0[0]] + moved_0, near)
         moved_0 = hops(legs_0, "near")
-        d_out, d_hidden = tied(d_out, legs_0[0]), tied(d_hidden, legs_0[0])
-    d_mixed = as_low(dot_nt(d_out, output_full))
-    if fast:
-        plan = [((0, 1), (2, 3), unit, 0) for j in range(wides)]
-        legs_1 = sums(plan, turned[:2] + both(d_hidden), d_mixed)
-        d_outs = both(d_out)
-        moved_0, legs_1, d_mixed, d_outs = join(moved_0, legs_1, d_mixed, d_outs)
+        plan = [((0, 1), (2 + 2 * j, 3 + 2 * j), unit, 0) for j in range(wides)]
+        legs_1 = sums(plan, turned + d_hiddens, legs_0[0])
+        turned = both(tied(mixed_turned, legs_0[0]), attn_turned, d_out)
+        moved_0, legs_1, turned, d_mixed = join(moved_0, legs_1, turned, d_mixed)
         (sums_0,) = fold([legs_0[0]] + moved_0, 1)
         d_mixed = tied(d_mixed, sums_0)
         moved_1 = hops(legs_1, "far", sums_0)
@@ -1035,19 +1261,18 @@
     else:
         share_expand = dense([(ffn_turned, d, unit, 0) for d in d_hidden])
     d_packed = attend_back(lengths, slopes, packed, d_mixed, lse)
+    d_joined_in, grad_gain_one = pack_back(
+        d_packed, attend_full, d_stream_mid, stream, edges, mel_bins
+    )
     if fast:
-        moved_1, sums_0, d_packed = join(moved_1, sums_0, d_packed)
+        d_packs = both(*d_packed)
+        moved_1, sums_0, d_packs, d_joined_in = join(moved_1, sums_0, d_packs, d_joined_in)
         legs_1 = fold([legs_1[0]] + moved_1, near)
         moved_1 = hops(legs_1, "near")
-        d_packed = tied(d_packed, legs_1[0])
-    d_joined_in, grad_gain_one = pack_back(
-        d_packed, attend_full, d_stream_mid, stream, gains_wide[0:1]
-    )
-    joined_turned = jnp.concatenate([start_turned, states_turned], 0)
-    if fast:
-        plan = [((0, 1), (2, 3), unit, 0)] + [((4, 5), (6, 7), unit, 0) for j in range(packs)]
-        legs_2 = sums(plan, turned[2:4] + d_outs + turned[4:] + both(d_packed), d_joined_in)
-        joined = both(joined_turned)
+        plan = [((0, 1), (4, 5), unit, 0)]
+        plan = plan + [((2, 3), (6 + 2 * j, 7 + 2 * j), unit, 0) for j in range(packs)]
+        legs_2 = sums(plan, turned + d_packs, legs_1[0])
+        joined = both(tied(joined_turned, legs_1[0]), tied(d_joined_in, legs_1[0]))
         moved_1, legs_2, joined, d_joined_in = join(moved_1, legs_2, joined, d_joined_in)
         (sums_1,) = fold([legs_1[0]] + moved_1, 1)
         d_joined_in = tied(d_joined_in, sums_1)
@@ -1057,69 +1282,57 @@
         share_attend = dense(
             [(mixed_turned, d_out, unit, 0)] + [(attn_turned, d, unit, 0) for d in d_packed]
         )
-    main, table = tail(d_joined_in, skip_full, small_full, embedded, mel, phone_hot)
-    gain_grads = jnp.concatenate([grad_gain_one, grad_gain_two, grad_gain_three], 0).T
-    edge = jnp.pad(
-        jnp.concatenate([as_low(grad_head), as_low(gain_grads)], 1),
-        ((0, 0), (0, width - at_count)),
+        share_skip = dense([(joined_turned, d_joined_in, 2 * unit, o) for o in offsets[:2]])
+    gain_grads = [grad_gain_one, grad_gain_two, grad_gain_three]
+    small_grads = tail(
+        d_joined_in, skip_full, small_full, embedded, mel, phone_hot, grad_head, gain_grads, mel_bins
     )
     if fast:
-        small_grads = [main, table, edge]
-        (sent,) = grads([((0, 1, 2), None, 0, 0)], small_grads, theirs, frames, unit, width, 1)
-        plan = [((0, 1), (2, 3), 2 * unit, o) for o in offsets[:2]] + [((4, 5, 6), None, 0, 0)]
-        legs_3 = sums(plan, joined + both(d_joined_in) + small_grads, sent, came=sibling(sent))
-        moved_2, sums_1, legs_3 = join(moved_2, sums_1, legs_3)
+        plan = [((0, 1, 2), None, 0, 0)]
+        small_grads = list(small_grads)
+        (sent,) = grads(plan, small_grads, theirs, frames, unit, width, 1)
+        plan_skip = [((0, 1), (2, 3), 2 * unit, o) for o in offsets[:2]]
+        legs_3 = sums(plan_skip, joined, sent)
+        legs_4 = grads(plan, small_grads, mine, frames, unit, width, far, sibling(sent))
+        moved_2, legs_3, legs_4 = join(moved_2, legs_3, legs_4)
         legs_2 = fold([legs_2[0]] + moved_2, near)
         moved_2 = hops(legs_2, "near")
         moved_3 = hops(legs_3, "far", legs_2[0])
-        moved_2, moved_3 = join(moved_2, moved_3)
+        moved_2, moved_3, sums_1 = join(moved_2, moved_3, sums_1)
         (sums_2,) = fold([legs_2[0]] + moved_2, 1)
         legs_3 = fold([legs_3[0], tied(moved_3[0], sums_2)] + moved_3[1:], near)
+        sums_2 = swap_deep(grid, sums_2)
         moved_3 = hops(legs_3, "near")
-        sums_2 = swap_deep(grid, sums_2)
+        moved_4 = hops(legs_4, "far", legs_3[0])
+        moved_3, moved_4, sums_2 = join(moved_3, moved_4, sums_2)
         (sums_3,) = fold([legs_3[0]] + moved_3, 1)
+        legs_4 = fold([legs_4[0], tied(moved_4[0], sums_3)] + moved_4[1:], near)
+        moved_4 = hops(legs_4, "near")
         sums_3 = swap_deep(grid, sums_3)
-        share_reduce, share_expand, share_attend, share_last = [
-            jnp.sum(x.astype(jnp.float32), 0) for x in (sums_0, sums_1, sums_2, sums_3)
+        moved_4, sums_3 = join(moved_4, sums_3)
+        (sums_4,) = fold([legs_4[0]] + moved_4, 1)
+        sums_4 = swap_deep(grid, sums_4)
+        share_reduce, share_expand, share_attend, share_skip, share_small = [
+            jnp.sum(x.astype(jnp.float32), 0) for x in (sums_0, sums_1, sums_2, sums_3, sums_4)
         ]
     else:
+        main, table, edge = small_grads
         table = table.reshape(devices, phone_wide, phones)
         table = jnp.pad(table, ((0, 0), (0, unit - phone_wide), (0, 0))).reshape(width, phones)
         small_grads = jnp.concatenate([main, table, edge], 1).astype(jnp.float32)
-        share_last = dense(
-            [(joined_turned, d_joined_in, 2 * unit, o) for o in offsets[:2]]
-            + [(small_grads, None, 0, 0)]
-        )
-
-    def columns(rows):
-        return jnp.concatenate([rows[j : j + unit] for j in range(0, rows.shape[0], unit)], 1)
-
-    share_small = share_last[2 * unit :]
-    shares = (
-        jnp.concatenate([share_small[:, phone_width:inputs], share_small[:, :phone_width]], 1).T,
-        share_small[:phone_wide, TABLE_AT:HEAD_AT].T,
-        share_last[: 2 * unit],
-        columns(share_attend[unit:]),
-        share_attend[:unit],
-        columns(share_expand),
-        share_reduce,
-        share_small[:, HEAD_AT:at_gain],
-        share_small[:, at_gain:at_count].T,
-    )
+        share_small = dense([(small_grads, None, 0, 0)])
+
+    shares = (share_small, share_skip, share_attend, share_expand, share_reduce)
     local_square = sum((jnp.sum(g * g) for g in shares))
     totals = all_sum(grid, jnp.concatenate([speaker_hot * error_sum[0, 0], local_square[None]]))
     sums, total_square = totals[:SPK], totals[SPK]
     loss_value = jnp.mean(sums / jnp.maximum(counts, 1.0))
     grad_norm = jnp.sqrt(total_square)
     clip = jnp.minimum(1.0, 1.0 / (grad_norm + 1e-06))
-    results = [
-        adam_step(w, g * clip, m, s, r)
-        for w, g, m, s, r in zip(masters, shares, moments, squares, rates)
-    ]
-    next_weights = tuple((r[0] for r in results))
-    next_moments = tuple((r[1] for r in results))
-    next_squares = tuple((r[2] for r in results))
-    return (loss_value, grad_norm) + next_weights + next_moments + next_squares
+    shares = (share_small, share_skip, share_attend, share_attend, share_expand, share_reduce)
+    at = (phone_wide, phone_width, inputs, mel_bins)
+    results = adam(clip[None], shares, masters, moments, squares, at)
+    return (loss_value, grad_norm, *results)
 
 
 def solution(mesh):

time: 575 us -> 504 us (0.88)
  waiting for transfers between devices: 187 us -> 152 us
  other arithmetic: 42.5 us -> 20 us
  local copies, waits for them, and re-layouts: 32.1 us -> 16 us
  blocking collectives: 0 us -> 9.74 us
  Pallas kernels: 222 us -> 215 us
  starting transfers between devices: 60.2 us -> 66 us
    ppermute x35 -> x42, waiting for transfers between devices: 116 us -> 98.9 us  [shift(): return lax.ppermute(x, AXES, grid.pairs(role, step))]
    ppermute x5 -> x0, waiting for transfers between devices: 13.5 us -> none  [all_sum(): x = x + lax.ppermute(x, AXES, [(i, i ^ step) for i in range(grid.total)])]
    sub x10 -> x0, other arithmetic: 12.1 us -> none  [the longest x9 11.4 us: adam_step(): master - rate * (moment_hat / (jnp.sqrt(square_hat) + ADAM_EPS) + DECAY *...]
    pallas_call x12 -> x9, Pallas kernels: 116 us -> 106 us  [the longest x1 20.6 us: ffn_back(): pl.pallas_call(partial(ffn_back_kernel, at_gain), grid=(count,), in_specs...]
    all_to_all x0 -> x1, blocking collectives: none -> 9.74 us  [all_sum(): lax.all_to_all(jnp.broadcast_to(x[None], (grid.total,) + x.shape), AXES,...]
    unnamed x143 -> x67, local copies, waits for them, and re-layouts: 17.2 us -> 8.05 us
    slice x10 -> x1, local copies, waits for them, and re-layouts: 7.87 us -> 0.73 us  [shards(): edges[at_count - HEAD_AT:at_count - HEAD_AT + 3].reshape(3, devices, unit)]
    all_to_all x8 -> x9, waiting for transfers between devices: 57.2 us -> 52.8 us  [swap_deep(): return lax.all_to_all(x, AXES, 0, 0, axis_index_groups=grid.lines())]
  transfers between devices with their start and end apart: 48 -> 51, of which waited for: 29 -> 25; matrix products, arithmetic and copies ran while one was open for 7% -> 5% of each run, Pallas kernels for 32% -> 38%
where the time goes in v3:
time: 504 us; the launch traced here: 496 us
  Pallas kernels  215 us (43%)
  waiting for transfers between devices  152 us (30%)
  starting transfers between devices  66 us (13%)
  other arithmetic  20 us (4%)
  local copies, waits for them, and re-layouts  16 us (3%)
  between operations  13.8 us (3%)
  blocking collectives  9.74 us (2%)
    ppermute x42, waiting for transfers between devices, shift(): return lax.ppermute(x, AXES, grid.pairs(role, step))  98.9 us
    all_to_all x9, waiting for transfers between devices, swap_deep(): return lax.all_to_all(x, AXES, 0, 0, axis_index_groups=grid.lines())  52.8 us
    pallas_call x6, Pallas kernels, grads(): pl.pallas_call(partial(grads_kernel, plan, count, rows, legs, came is not...  42 us
    all_to_all x9, starting transfers between devices, swap_deep(): return lax.all_to_all(x, AXES, 0, 0, axis_index_groups=grid.lines())  39.3 us
    ppermute x42, starting transfers between devices, shift(): return lax.ppermute(x, AXES, grid.pairs(role, step))  26.7 us
    pallas_call x10, Pallas kernels, fold(): pl.pallas_call(partial(fold_kernel, legs), grid=(rows // tile,), in_specs...  26.2 us
    pallas_call x1, Pallas kernels, ffn_back(): pl.pallas_call(partial(ffn_back_kernel, at_gain), grid=(count,), in_specs...  20.6 us
    pallas_call x1, Pallas kernels, expand(): pl.pallas_call(partial(expand_kernel, len(pieces), blocks), grid=(blocks,...  17.4 us
  transfers between devices with their start and end apart: 51, of which 25 were waited for; matrix products, arithmetic and copies ran while one was open for 5% of the time, Pallas kernels for 38%

profile of v3, /device:TPU:0, one launch (start us, length us, event | category | flops | bytes accessed | tf_op | source)
XLA Modules:
  0.0 496.2 jit_solution(13355768298971540966)
XLA Ops:
  10.7 6.3 %all-to-all-start = ((bf16[4,96,1024]{2,1,0:T(8,128)(2,1)}), bf16[4,96,1024]{2,1,0:T(8,128)(2,1)}, u32[]{:S(2)}, u32[]{:S(2)}) async-start(bf16[4,96,1024]{2,1,0:T(8,128)(2,1)} %broadcast_in_dim.113), calls=%async_computation | async-start | bytes 1572864 | tf_op jit(solution)/shard_map/all_to_all | solution.py:156
  18.8 5.5 %collective-permute-done.refs_1_ = bf16[160,1024]{1,0:T(8,128)(2,1)S(1)} collective-permute-done((bf16[160,1024]{1,0:T(8,128)(2,1)S(1)}, bf16[160,1024]{1,0:T(8,128)(2,1)S(1)}, u32[]{:S(2)}, u32[]{:S(2)}) %collective-permute-start) | collective-permute-done | bytes 327712 | tf_op jit(solution)/shard_map/ppermute | solution.py:148
  24.3 12.9 %all-to-all-done.refs_0_ = bf16[4,96,1024]{2,1,0:T(8,128)(2,1)} async-done(((bf16[4,96,1024]{2,1,0:T(8,128)(2,1)}), bf16[4,96,1024]{2,1,0:T(8,128)(2,1)}, u32[]{:S(2)}, u32[]{:S(2)}) %all-to-all-start) | async-done | bytes 786464 | tf_op jit(solution)/shard_map/all_to_all | solution.py:156
  38.3 3.5 all-to-all-start.1
  51.8 1.9 stack.22
  53.7 5.1 %collective-permute-done.1.refs_1_ = bf16[4,96,1024]{2,1,0:T(8,128)(2,1)} collective-permute-done((bf16[4,96,1024]{2,1,0:T(8,128)(2,1)}, bf16[4,96,1024]{2,1,0:T(8,128)(2,1)}, u32[]{:S(2)}, u32[]{:S(2)}) %collective-permute-start.1) | collective-permute-done | bytes 786464 | tf_op jit(solution)/shard_map/ppermute | solution.py:148
  58.8 2.5 all-to-all-done.1.refs_0_
  61.3 2.8 stack.20
  66.1 4.7 all-to-all-start.2
  76.1 17.8 %collective-permute-done.4.refs_1_ = bf16[4,96,1024]{2,1,0:T(8,128)(2,1)S(1)} collective-permute-done((bf16[4,96,1024]{2,1,0:T(8,128)(2,1)S(1)}, bf16[4,96,1024]{2,1,0:T(8,128)(2,1)S(1)}, u32[]{:S(2)}, u32[]{:S(2)}) %collective-permute-start.4) | collective-permute-done | bytes 786464 | tf_op jit(solution)/shard_map/ppermute | solution.py:148
  93.9 6.1 %collective-permute-done.2.refs_1_ = bf16[8,96,1024]{2,1,0:T(8,128)(2,1)} collective-permute-done((bf16[8,96,1024]{2,1,0:T(8,128)(2,1)S(1)}, bf16[8,96,1024]{2,1,0:T(8,128)(2,1)}, u32[]{:S(2)}, u32[]{:S(2)}) %collective-permute-start.2) | collective-permute-done | bytes 1572896 | tf_op jit(solution)/shard_map/ppermute | solution.py:148
  100.0 2.5 stack.21
  104.3 2.0 collective-permute-done.7.refs_3_
  106.3 11.4 %front.1 = (bf16[1024,1024]{1,0:T(8,128)(2,1)}, bf16[2048,1024]{1,0:T(8,128)(2,1)}, bf16[512,512]{1,0:T(8,128)(2,1)}, f32[512,1024]{1,0:T(8,128)}, bf16[2048,512...) custom-call(s32[16]{0:T(128)} %get-tuple-element.252.own_ref, ...), custom_call_target="tpu_custom_call" | custom-call | tf_op jit(solution)/shard_map/front/pallas_call | solution.py:442
  117.7 5.7 %collective-permute-done.5.refs_1_ = bf16[8,96,1024]{2,1,0:T(8,128)(2,1)} collective-permute-done((bf16[8,96,1024]{2,1,0:T(8,128)(2,1)}, bf16[8,96,1024]{2,1,0:T(8,128)(2,1)}, u32[]{:S(2)}, u32[]{:S(2)}) %collective-permute-start.5) | collective-permute-done | bytes 1572896 | tf_op jit(solution)/shard_map/ppermute | solution.py:148
  123.4 6.4 %all-to-all-done.2 = bf16[4,2,160,1024]{3,2,1,0:T(8,128)(2,1)} async-done(((bf16[4,2,160,1024]{3,2,1,0:T(8,128)(2,1)}), bf16[4,2,160,1024]{3,2,1,0:T(8,128)(2,1)}, u32[]{:S(2)}, u32[]{:S(2)}) %all-to-all-start.2) | async-done | bytes 2621472 | tf_op jit(solution)/shard_map/all_to_all | solution.py:156
  132.9 3.7 all-to-all-start.3
  139.0 8.2 %pack.1 = (bf16[3,1024,1024]{2,1,0:T(8,128)(2,1)}, bf16[3,512,1024]{2,1,0:T(8,128)(2,1)}) custom-call(s32[16]{0:T(128)} %get-tuple-element.252.own_ref, s32[16]{0:T(128)} %get-tuple-element.253.other_ref, bf16[8,96,1024]{2,1,0:T(8,128)(2,1)} %bitcast.66, bf16[8,96,1024]{2,1,0:T(8,128)(2,1)} %collective-permute-done.5.refs_1_, ...), custom_call_target="tpu_custom_call" | custom-call | tf_op jit(solution)/shard_map/pack/pallas_call | solution.py:499
  147.1 12.9 %attend.1 = (bf16[512,1024]{1,0:T(8,128)(2,1)}, f32[8,2,512]{2,1,0:T(2,128)}) custom-call(s32[1]{0:T(128)} %copy.127.length_ref, f32[16]{0:T(128)} %multiply_power_fusion.slope_ref, bf16[3,512,1024]{2,1,0:T(8,128)(2,1)} %get-tuple-element.344.packed_ref), custom_call_target="tpu_custom_call" | custom-call | tf_op jit(solution)/shard_map/attend/pallas_call | solution.py:221
  160.1 2.7 all-to-all-done.3.refs_0_
  164.4 3.7 collective-permute-done.12.refs_3_
  168.1 7.8 %mid.1 = (bf16[1024,1024]{1,0:T(8,128)(2,1)}, f32[512,1024]{1,0:T(8,128)}, bf16[512,1024]{1,0:T(8,128)(2,1)}, bf16[1024,512]{1,0:T(8,128)(2,1)}, bf16[1024,512]{1,0:T(8,128)(2,1)}) custom-call(s32[16]{0:T(128)} %get-tuple-element.278.own_ref, s32[16]{0:T(128)} %get-tuple-element.279.other_ref, bf16[8,160,1024]{2,1,0:T(8,128)(2,1)} %bitcast.16.refs_0_, ...), custom_call_target="tpu_custom_call" | custom-call | tf_op jit(solution)/shard_map/mid/pallas_call | solution.py:548
  177.8 2.9 stack.23
  181.6 17.4 %expand.1 = (bf16[4,1024,1024]{2,1,0:T(8,128)(2,1)}, bf16[512,4096]{1,0:T(8,128)(2,1)}, bf16[4096,512]{1,0:T(8,128)(2,1)}, bf16[512,4096]{1,0:T(8,128)(2,1)}) custom-call(s32[16]{0:T(128)} %get-tuple-element.278.own_ref, s32[16]{0:T(128)} %get-tuple-element.279.other_ref, bf16[8,160,1024]{2,1,0:T(8,128)(2,1)} %bitcast.16.refs_0_, ...), custom_call_target="tpu_custom_call" | custom-call | tf_op jit(solution)/shard_map/expand/pallas_call | solution.py:331
  199.0 8.1 %collective-permute-done.13.refs_1_ = bf16[8,128,1024]{2,1,0:T(8,128)(2,1)} collective-permute-done((bf16[8,128,1024]{2,1,0:T(8,128)(2,1)}, bf16[8,128,1024]{2,1,0:T(8,128)(2,1)}, u32[]{:S(2)}, u32[]{:S(2)}) %collective-permute-start.13) | collective-permute-done | bytes 2097184 | tf_op jit(solution)/shard_map/ppermute | solution.py:148
  207.1 4.5 collective-permute-done.15.refs_3_
  211.7 16.6 %head.1 = (bf16[4096,1024]{1,0:T(8,128)(2,1)}, f32[512,1024]{1,0:T(8,128)}, bf16[512,1024]{1,0:T(8,128)(2,1)}, f32[1024,80]{1,0:T(8,128)}, f32[1,1024]{1,0:T(1,128)}, /*index=5*/f32[1,1]{1,0:T(1,128)}) custom-call(f32[1]{0:T(128)} %bitcast.19.share_ref, s32[16]{0:T(128)} %get-tuple-element.252.own_ref, s32[16]{0:T(128)} %get-tuple-element.253.other_ref, ...), custom_call_target="tpu_custom_call" | custom-call | tf_op jit(solution)/shard_map/head/pallas_call | solution.py:623
  229.0 2.6 collective-permute-done.17.refs_3_
  231.6 10.1 %grads.6 = (bf16[8,128,1024]{2,1,0:T(8,128)(2,1)}, bf16[8,128,1024]{2,1,0:T(8,128)(2,1)}) custom-call(s32[16]{0:T(128)} %get-tuple-element.300.idx_ref, bf16[4096,512]{1,0:T(8,128)(2,1)} %get-tuple-element.302.refs_0_, bf16[4096,512]{1,0:T(8,128)(2,1)} %collective-permute-done.16.refs_1_, bf16[512,1024]{1,0:T(8,128)(2,1)} %get-tuple-element.307.refs_2_.low_ref, ...), custom_call_target="tpu_custom_call" | custom-call | tf_op jit(solution)/shard_map/grads/pallas_call | solution.py:869
  242.3 20.6 %ffn_back.1 = (f32[512,1024]{1,0:T(8,128)}, bf16[512,1024]{1,0:T(8,128)(2,1)}, f32[1,1024]{1,0:T(1,128)}, bf16[512,1024]{1,0:T(8,128)(2,1)}, bf16[512,1024]{1,0:...) custom-call(bf16[512,1024]{1,0:T(8,128)(2,1)} %get-tuple-element.307.refs_2_.low_ref, ...), custom_call_target="tpu_custom_call" | custom-call | tf_op jit(solution)/shard_map/ffn_back/pallas_call | solution.py:692
  264.6 4.3 convolution_convert_fusion.d_ref
  272.8 3.5 fold.10
  277.4 10.1 %grads.7 = (bf16[8,128,1024]{2,1,0:T(8,128)(2,1)}, bf16[8,128,1024]{2,1,0:T(8,128)(2,1)}) custom-call(s32[16]{0:T(128)} %get-tuple-element.300.idx_ref, bf16[1024,512]{1,0:T(8,128)(2,1)} %get-tuple-element.323.refs_0_, bf16[1024,512]{1,0:T(8,128)(2,1)} %collective-permute-done.19.refs_1_, bf16[512,1024]{1,0:T(8,128)(2,1)} %get-tuple-element.325.refs_2_, ...), custom_call_target="tpu_custom_call" | custom-call | tf_op jit(solution)/shard_map/grads/pallas_call | solution.py:869
  287.5 4.4 collective-permute-done.24.refs_1_
  291.9 2.4 fold.11
  294.8 3.5 all-to-all-start.4
  298.4 17.0 %attend_back.1 = (bf16[512,1024]{1,0:T(8,128)(2,1)}, bf16[512,1024]{1,0:T(8,128)(2,1)}, bf16[512,1024]{1,0:T(8,128)(2,1)}) custom-call(s32[1]{0:T(128)} %copy.127.length_ref, f32[16]{0:T(128)} %multiply_power_fusion.slope_ref, bf16[3,512,1024]{2,1,0:T(8,128)(2,1)} %get-tuple-element.344.packed_ref, bf16[512,1024]{1,0:T(8,128)(2,1)} %convolution_convert_fusion.d_ref, ...), custom_call_target="tpu_custom_call" | custom-call | tf_op jit(solution)/shard_map/attend_back/pallas_call | solution.py:270
  315.9 9.8 %pack_back.1 = (bf16[512,1024]{1,0:T(8,128)(2,1)}, f32[1,1024]{1,0:T(1,128)}) custom-call(bf16[512,1024]{1,0:T(8,128)(2,1)} %get-tuple-element.364.refs_0_.refs_6_, bf16[512,1024]{1,0:T(8,128)(2,1)} %get-tuple-element.366.refs_1_.refs_8_, bf16[512,1024]{1,0:T(8,128)(2,1)} %get-tuple-element.368.refs_2_.refs_10_, ...), custom_call_target="tpu_custom_call" | custom-call | tf_op jit(solution)/shard_map/pack_back/pallas_call | solution.py:739
  326.7 3.5 fold.12
  332.2 10.1 %grads.8 = (bf16[8,128,1024]{2,1,0:T(8,128)(2,1)}, bf16[8,128,1024]{2,1,0:T(8,128)(2,1)}) custom-call(s32[16]{0:T(128)} %get-tuple-element.300.idx_ref, bf16[1024,512]{1,0:T(8,128)(2,1)} %get-tuple-element.358.refs_0_, bf16[1024,512]{1,0:T(8,128)(2,1)} %collective-permute-done.25.refs_1_, bf16[1024,512]{1,0:T(8,128)(2,1)} %get-tuple-element.360.refs_2_, ...), custom_call_target="tpu_custom_call" | custom-call | tf_op jit(solution)/shard_map/grads/pallas_call | solution.py:869
  342.3 3.6 collective-permute-done.32.refs_1_
  345.9 2.6 fold.13
  350.1 7.1 %tail.1 = (bf16[1024,768]{1,0:T(8,128)(2,1)}, bf16[512,128]{1,0:T(8,128)(2,1)}, bf16[1024,128]{1,0:T(8,128)(2,1)}) custom-call(bf16[512,1024]{1,0:T(8,128)(2,1)} %get-tuple-element.395.d_ref.refs_2_, bf16[2048,1024]{1,0:T(8,128)(2,1)} %get-tuple-element.383.skip_ref, bf16[1024,1024]{1,0:T(8,128)(2,1)} %get-tuple-element.384.small_ref, ...), custom_call_target="tpu_custom_call" | custom-call | tf_op jit(solution)/shard_map/tail/pallas_call | solution.py:784
  357.2 2.6 grads.9
  359.8 5.1 %all-to-all-start.5 = ((bf16[4,128,1024]{2,1,0:T(8,128)(2,1)}), bf16[4,128,1024]{2,1,0:T(8,128)(2,1)S(1)}, u32[]{:S(2)}, u32[]{:S(2)}) async-start(bf16[4,128,1024]{2,1,0:T(8,128)(2,1)} %fold.13), calls=%async_computation.5 | async-start | bytes 2097152 | tf_op jit(solution)/shard_map/all_to_all | solution.py:156
  364.9 6.3 %grads.10 = (bf16[8,64,1024]{2,1,0:T(8,128)(2,1)}, bf16[8,64,1024]{2,1,0:T(8,128)(2,1)}) custom-call(s32[16]{0:T(128)} %get-tuple-element.300.idx_ref, bf16[2048,512]{1,0:T(8,128)(2,1)} %get-tuple-element.393.refs_0_, bf16[2048,512]{1,0:T(8,128)(2,1)} %collective-permute-done.33.refs_1_, bf16[512,1024]{1,0:T(8,128)(2,1)} %get-tuple-element.395.d_ref.refs_2_, ...), custom_call_target="tpu_custom_call" | custom-call | tf_op jit(solution)/shard_map/grads/pallas_call | solution.py:869
  371.2 3.0 grads.11
  374.9 3.4 fold.14
  380.3 10.9 %all-to-all-done.5 = bf16[4,128,1024]{2,1,0:T(8,128)(2,1)S(1)} async-done(((bf16[4,128,1024]{2,1,0:T(8,128)(2,1)}), bf16[4,128,1024]{2,1,0:T(8,128)(2,1)S(1)}, u32[]{:S(2)}, u32[]{:S(2)}) %all-to-all-start.5) | async-done | bytes 1048608 | tf_op jit(solution)/shard_map/all_to_all | solution.py:156
  391.3 12.3 %collective-permute-done.38.refs_1_.refs_3_ = bf16[8,64,1024]{2,1,0:T(8,128)(2,1)} collective-permute-done((bf16[8,64,1024]{2,1,0:T(8,128)(2,1)}, bf16[8,64,1024]{2,1,0:T(8,128)(2,1)}, u32[]{:S(2)}, u32[]{:S(2)}) %collective-permute-start.38) | collective-permute-done | bytes 1048608 | tf_op jit(solution)/shard_map/ppermute | solution.py:148
  403.6 2.5 fold.15
  406.1 5.0 %all-to-all-start.6 = ((bf16[4,128,1024]{2,1,0:T(8,128)(2,1)}), bf16[4,128,1024]{2,1,0:T(8,128)(2,1)}, u32[]{:S(2)}, u32[]{:S(2)}) async-start(bf16[4,128,1024]{2,1,0:T(8,128)(2,1)} %fold.15), calls=%async_computation.6 | async-start | bytes 2097152 | tf_op jit(solution)/shard_map/all_to_all | solution.py:156
  411.2 2.4 fold.16
  415.7 11.3 %collective-permute-done.40.refs_1_.refs_3_ = bf16[8,32,1024]{2,1,0:T(8,128)(2,1)} collective-permute-done((bf16[8,32,1024]{2,1,0:T(8,128)(2,1)}, bf16[8,32,1024]{2,1,0:T(8,128)(2,1)}, u32[]{:S(2)}, u32[]{:S(2)}) %collective-permute-start.40) | collective-permute-done | bytes 524320 | tf_op jit(solution)/shard_map/ppermute | solution.py:148
  427.0 9.2 %all-to-all-done.6 = bf16[4,128,1024]{2,1,0:T(8,128)(2,1)} async-done(((bf16[4,128,1024]{2,1,0:T(8,128)(2,1)}), bf16[4,128,1024]{2,1,0:T(8,128)(2,1)}, u32[]{:S(2)}, u32[]{:S(2)}) %all-to-all-start.6) | async-done | bytes 1048608 | tf_op jit(solution)/shard_map/all_to_all | solution.py:156
  436.2 2.0 fold.17
  438.2 4.1 all-to-all-start.7
  443.9 2.1 fold.18
  448.9 3.7 collective-permute-done.41.refs_1_
  452.5 3.8 all-to-all-done.7
  458.1 3.4 all-to-all-start.8
  465.6 4.3 all-to-all-done.8
  473.9 9.7 %all_to_all.51 = f32[32,1,17]{2,1,0:T(1,128)S(1)} all-to-all(f32[32,1,17]{2,1,0:T(1,128)S(1)} %broadcast_in_dim.130), channel_id=1, replica_groups=mesh['wide'=8,'narrow'=4] {'wide','narrow'}, dimensions={0} | all-to-all | bytes 4352 | tf_op jit(solution)/shard_map/all_to_all | solution.py:168
  486.3 7.5 %adam.1 = (f32[32,672]{1,0:T(8,128)}, f32[16,128]{1,0:T(8,128)}, f32[64,1024]{1,0:T(8,128)}, f32[32,3072]{1,0:T(8,128)}, f32[32,1024]{1,0:T(8,128)}, /*index=5*/...) custom-call(f32[1]{0:T(128)} %bitcast.24.clip_ref, ...), custom_call_target="tpu_custom_call" | custom-call | tf_op jit(solution)/shard_map/adam/pallas_call | solution.py:977
  (224 shorter events, 67.2 us)
Async XLA Ops:
  0.7 16.4 %copy-start.14 = (f32[32,4096]{1,0:T(8,128)S(1)}, f32[32,4096]{1,0:T(8,128)}, u32[]{:S(2)}) copy-start(f32[32,4096]{1,0:T(8,128)} %refs_11_.1) | copy-start | bytes 1572868
  10.7 26.5 %all-to-all-start = ((bf16[4,96,1024]{2,1,0:T(8,128)(2,1)}), bf16[4,96,1024]{2,1,0:T(8,128)(2,1)}, u32[]{:S(2)}, u32[]{:S(2)}) async-start(bf16[4,96,1024]{2,1,0:T(8,128)(2,1)} %broadcast_in_dim.113), calls=%async_computation | async-start | bytes 1572864 | tf_op jit(solution)/shard_map/all_to_all | solution.py:156
  17.2 24.6 %copy-start.26 = (bf16[160,1024]{1,0:T(8,128)(2,1)}, bf16[160,1024]{1,0:T(8,128)(2,1)S(1)}, u32[]{:S(2)}) copy-start(bf16[160,1024]{1,0:T(8,128)(2,1)S(1)} %slice_dynamic-update-slice_fusion.refs_0_) | copy-start | bytes 983044
  17.2 7.1 %collective-permute-start = (bf16[160,1024]{1,0:T(8,128)(2,1)S(1)}, bf16[160,1024]{1,0:T(8,128)(2,1)S(1)}, u32[]{:S(2)}, u32[]{:S(2)}) collective-permute-start(bf16[160,1024]{1,0:T(8,128)(2,1)S(1)} %slice_dynamic-update-slice_fusion.refs_0_), channel_id=1, source_target_pairs={{0,4},{1,3},{2,6},{3,1},{4,0},{5,7},{6,2},{7,5},{8,12},{9,11},{10,... | collective-permute-start | bytes 983048 | tf_op jit(solution)/shard_map/ppermute | solution.py:148
  18.8 25.7 %copy-start.9 = (bf16[512,1024]{1,0:T(8,128)(2,1)S(1)}, bf16[512,1024]{1,0:T(8,128)(2,1)}, u32[]{:S(2)}) copy-start(bf16[512,1024]{1,0:T(8,128)(2,1)} %refs_4_.1) | copy-start | bytes 3145732
  24.3 21.6 %copy-start.27 = (bf16[160,1024]{1,0:T(8,128)(2,1)}, bf16[160,1024]{1,0:T(8,128)(2,1)S(1)}, u32[]{:S(2)}) copy-start(bf16[160,1024]{1,0:T(8,128)(2,1)S(1)} %collective-permute-done.refs_1_) | copy-start | bytes 983044
  38.3 23.1 %all-to-all-start.1 = ((bf16[4,96,1024]{2,1,0:T(8,128)(2,1)}), bf16[4,96,1024]{2,1,0:T(8,128)(2,1)S(1)}, u32[]{:S(2)}, u32[]{:S(2)}) async-start(bf16[4,96,1024]{2,1,0:T(8,128)(2,1)} %broadcast_in_dim.114), calls=%async_computation.1 | async-start | bytes 1572864 | tf_op jit(solution)/shard_map/all_to_all | solution.py:156
  46.5 12.3 %collective-permute-start.1 = (bf16[4,96,1024]{2,1,0:T(8,128)(2,1)}, bf16[4,96,1024]{2,1,0:T(8,128)(2,1)}, u32[]{:S(2)}, u32[]{:S(2)}) collective-permute-start(bf16[4,96,1024]{2,1,0:T(8,128)(2,1)} %all-to-all-done.refs_0_), channel_id=1, source_target_pairs={{0,4},{1,3},{2,6},{3,1},{4,0},{5,7},{6,2},{7,5},{8,12},{9,11},{10,... | collective-permute-start | bytes 2359304 | tf_op jit(solution)/shard_map/ppermute | solution.py:148
  66.1 63.7 %all-to-all-start.2 = ((bf16[4,2,160,1024]{3,2,1,0:T(8,128)(2,1)}), bf16[4,2,160,1024]{3,2,1,0:T(8,128)(2,1)}, u32[]{:S(2)}, u32[]{:S(2)}) async-start(bf16[4,2,160,1024]{3,2,1,0:T(8,128)(2,1)} %broadcast_in_dim.126), calls=%async_computation.2 | async-start | bytes 5242880 | tf_op jit(solution)/shard_map/all_to_all | solution.py:156
  71.0 29.0 %collective-permute-start.2 = (bf16[8,96,1024]{2,1,0:T(8,128)(2,1)S(1)}, bf16[8,96,1024]{2,1,0:T(8,128)(2,1)}, u32[]{:S(2)}, u32[]{:S(2)}) collective-permute-start(bf16[8,96,1024]{2,1,0:T(8,128)(2,1)S(1)} %bitcast.62), channel_id=1, source_target_pairs={{0,2},{1,5},{2,0},{3,7},{4,6},{5,1},{6,4},{7,3},{8,10},{9,13},{10,... | collective-permute-start | bytes 4718600 | tf_op jit(solution)/shard_map/ppermute | solution.py:148
  72.5 27.5 %collective-permute-start.3 = (bf16[8,96,1024]{2,1,0:T(8,128)(2,1)S(1)}, bf16[8,96,1024]{2,1,0:T(8,128)(2,1)}, u32[]{:S(2)}, u32[]{:S(2)}) collective-permute-start(bf16[8,96,1024]{2,1,0:T(8,128)(2,1)S(1)} %bitcast.63), channel_id=1, source_target_pairs={{0,1},{1,0},{2,3},{3,2},{4,5},{5,4},{6,7},{7,6},{8,9},{9,8},{10,11... | collective-permute-start | bytes 4718600 | tf_op jit(solution)/shard_map/ppermute | solution.py:148
  73.3 20.5 %collective-permute-start.4 = (bf16[4,96,1024]{2,1,0:T(8,128)(2,1)S(1)}, bf16[4,96,1024]{2,1,0:T(8,128)(2,1)S(1)}, u32[]{:S(2)}, u32[]{:S(2)}) collective-permute-start(bf16[4,96,1024]{2,1,0:T(8,128)(2,1)S(1)} %all-to-all-done.1.refs_0_), channel_id=1, source_target_pairs={{0,4},{1,3},{2,6},{3,1},{4,0},{5,7},{6,2},{7,5},{8,12},{9,11},{10,... | collective-permute-start | bytes 2359304 | tf_op jit(solution)/shard_map/ppermute | solution.py:148
  102.5 29.3 %copy-start.13 = (f32[128,1024]{1,0:T(8,128)S(1)}, f32[128,1024]{1,0:T(8,128)}, u32[]{:S(2)}) copy-start(f32[128,1024]{1,0:T(8,128)} %refs_12_.1) | copy-start | bytes 1572868
  102.5 3.8 collective-permute-start.7
  102.6 20.8 %collective-permute-start.5 = (bf16[8,96,1024]{2,1,0:T(8,128)(2,1)}, bf16[8,96,1024]{2,1,0:T(8,128)(2,1)}, u32[]{:S(2)}, u32[]{:S(2)}) collective-permute-start(bf16[8,96,1024]{2,1,0:T(8,128)(2,1)} %bitcast.64), channel_id=1, source_target_pairs={{0,2},{1,5},{2,0},{3,7},{4,6},{5,1},{6,4},{7,3},{8,10},{9,13},{10,... | collective-permute-start | bytes 4718600 | tf_op jit(solution)/shard_map/ppermute | solution.py:148
  104.1 19.2 %collective-permute-start.6 = (bf16[8,96,1024]{2,1,0:T(8,128)(2,1)}, bf16[8,96,1024]{2,1,0:T(8,128)(2,1)}, u32[]{:S(2)}, u32[]{:S(2)}) collective-permute-start(bf16[8,96,1024]{2,1,0:T(8,128)(2,1)} %bitcast.65), channel_id=1, source_target_pairs={{0,1},{1,0},{2,3},{3,2},{4,5},{5,4},{6,7},{7,6},{8,9},{9,8},{10,11... | collective-permute-start | bytes 4718600 | tf_op jit(solution)/shard_map/ppermute | solution.py:148
  129.8 33.0 %collective-permute-start.8 = (bf16[8,160,1024]{2,1,0:T(8,128)(2,1)}, bf16[8,160,1024]{2,1,0:T(8,128)(2,1)}, u32[]{:S(2)}, u32[]{:S(2)}) collective-permute-start(bf16[8,160,1024]{2,1,0:T(8,128)(2,1)} %bitcast.16.refs_0_), channel_id=1, source_target_pairs={{0,2},{1,5},{2,0},{3,7},{4,6},{5,1},{6,4},{7,3},{8,10},{9,13},{10,... | collective-permute-start | bytes 7864328 | tf_op jit(solution)/shard_map/ppermute | solution.py:148
  131.3 31.5 %collective-permute-start.9 = (bf16[8,160,1024]{2,1,0:T(8,128)(2,1)}, bf16[8,160,1024]{2,1,0:T(8,128)(2,1)}, u32[]{:S(2)}, u32[]{:S(2)}) collective-permute-start(bf16[8,160,1024]{2,1,0:T(8,128)(2,1)} %bitcast.16.refs_0_), channel_id=1, source_target_pairs={{0,1},{1,0},{2,3},{3,2},{4,5},{5,4},{6,7},{7,6},{8,9},{9,8},{10,11... | collective-permute-start | bytes 7864328 | tf_op jit(solution)/shard_map/ppermute | solution.py:148
  131.3 7.7 %collective-permute-start.10 = (bf16[8,96,1024]{2,1,0:T(8,128)(2,1)}, bf16[8,96,1024]{2,1,0:T(8,128)(2,1)}, u32[]{:S(2)}, u32[]{:S(2)}) collective-permute-start(bf16[8,96,1024]{2,1,0:T(8,128)(2,1)} %collective-permute-done.5.refs_1_), channel_id=1, source_target_pairs={{0,1},{1,0},{2,3},{3,2},{4,5},{5,4},{6,7},{7,6},{8,9},{9,8},{10,11... | collective-permute-start | bytes 4718600 | tf_op jit(solution)/shard_map/ppermute | solution.py:148
  132.9 29.8 %all-to-all-start.3 = ((bf16[4,128,1024]{2,1,0:T(8,128)(2,1)}), bf16[4,128,1024]{2,1,0:T(8,128)(2,1)S(1)}, u32[]{:S(2)}, u32[]{:S(2)}) async-start(bf16[4,128,1024]{2,1,0:T(8,128)(2,1)} %broadcast_in_dim.127), calls=%async_computation.3 | async-start | bytes 2097152 | tf_op jit(solution)/shard_map/all_to_all | solution.py:156
  162.7 13.2 %copy-start.8 = (bf16[4,128,1024]{2,1,0:T(8,128)(2,1)}, bf16[4,128,1024]{2,1,0:T(8,128)(2,1)S(1)}, u32[]{:S(2)}) copy-start(bf16[4,128,1024]{2,1,0:T(8,128)(2,1)S(1)} %all-to-all-done.3.refs_0_) | copy-start | bytes 3145732
  162.8 5.3 %collective-permute-start.12 = (bf16[8,160,1024]{2,1,0:T(8,128)(2,1)}, bf16[8,160,1024]{2,1,0:T(8,128)(2,1)}, u32[]{:S(2)}, u32[]{:S(2)}) collective-permute-start(bf16[8,160,1024]{2,1,0:T(8,128)(2,1)} %collective-permute-done.8.refs_1_), channel_id=1, source_target_pairs={{0,1},{1,0},{2,3},{3,2},{4,5},{5,4},{6,7},{7,6},{8,9},{9,8},{10,11... | collective-permute-start | bytes 7864328 | tf_op jit(solution)/shard_map/ppermute | solution.py:148
  162.8 15.0 %collective-permute-start.11 = (bf16[4,128,1024]{2,1,0:T(8,128)(2,1)S(1)}, bf16[4,128,1024]{2,1,0:T(8,128)(2,1)}, u32[]{:S(2)}, u32[]{:S(2)}) collective-permute-start(bf16[4,128,1024]{2,1,0:T(8,128)(2,1)S(1)} %all-to-all-done.3.refs_0_), channel_id=1, source_target_pairs={{0,4},{1,3},{2,6},{3,1},{4,0},{5,7},{6,2},{7,5},{8,12},{9,11},{10,... | collective-permute-start | bytes 3145736 | tf_op jit(solution)/shard_map/ppermute | solution.py:148
  180.7 26.4 %collective-permute-start.13 = (bf16[8,128,1024]{2,1,0:T(8,128)(2,1)}, bf16[8,128,1024]{2,1,0:T(8,128)(2,1)}, u32[]{:S(2)}, u32[]{:S(2)}) collective-permute-start(bf16[8,128,1024]{2,1,0:T(8,128)(2,1)} %bitcast.58), channel_id=1, source_target_pairs={{0,2},{1,5},{2,0},{3,7},{4,6},{5,1},{6,4},{7,3},{8,10},{9,13},{10,... | collective-permute-start | bytes 6291464 | tf_op jit(solution)/shard_map/ppermute | solution.py:148
  181.3 25.8 %collective-permute-start.14 = (bf16[8,128,1024]{2,1,0:T(8,128)(2,1)}, bf16[8,128,1024]{2,1,0:T(8,128)(2,1)}, u32[]{:S(2)}, u32[]{:S(2)}) collective-permute-start(bf16[8,128,1024]{2,1,0:T(8,128)(2,1)} %bitcast.59), channel_id=1, source_target_pairs={{0,1},{1,0},{2,3},{3,2},{4,5},{5,4},{6,7},{7,6},{8,9},{9,8},{10,11... | collective-permute-start | bytes 6291464 | tf_op jit(solution)/shard_map/ppermute | solution.py:148
  207.1 4.5 collective-permute-start.15
  211.6 20.0 %collective-permute-start.16 = (bf16[4096,512]{1,0:T(8,128)(2,1)}, bf16[4096,512]{1,0:T(8,128)(2,1)}, u32[]{:S(2)}, u32[]{:S(2)}) collective-permute-start(bf16[4096,512]{1,0:T(8,128)(2,1)} %get-tuple-element.302.refs_0_), channel_id=1, source_target_pairs={{0,1},{1,0},{2,3},{3,2},{4,5},{5,4},{6,7},{7,6},{8,9},{9,8},{10,11... | collective-permute-start | bytes 12582920 | tf_op jit(solution)/shard_map/ppermute | solution.py:148
  211.7 17.1 %copy-start.18 = (bf16[1024,512]{1,0:T(8,128)(2,1)S(1)}, bf16[1024,512]{1,0:T(8,128)(2,1)}, u32[]{:S(2)}) copy-start(bf16[1024,512]{1,0:T(8,128)(2,1)} %get-tuple-element.323.refs_0_) | copy-start | bytes 3145732
  228.4 3.2 collective-permute-start.17
  228.8 35.6 %collective-permute-start.19 = (bf16[1024,512]{1,0:T(8,128)(2,1)S(1)}, bf16[1024,512]{1,0:T(8,128)(2,1)}, u32[]{:S(2)}, u32[]{:S(2)}) collective-permute-start(bf16[1024,512]{1,0:T(8,128)(2,1)S(1)} %copy-done.18), channel_id=1, source_target_pairs={{0,1},{1,0},{2,3},{3,2},{4,5},{5,4},{6,7},{7,6},{8,9},{9,8},{10,11... | collective-permute-start | bytes 3145736 | tf_op jit(solution)/shard_map/ppermute | solution.py:148
  241.7 31.2 %collective-permute-start.18 = (bf16[8,128,1024]{2,1,0:T(8,128)(2,1)}, bf16[8,128,1024]{2,1,0:T(8,128)(2,1)}, u32[]{:S(2)}, u32[]{:S(2)}) collective-permute-start(bf16[8,128,1024]{2,1,0:T(8,128)(2,1)} %get-tuple-element.305), channel_id=1, source_target_pairs={{0,2},{1,5},{2,0},{3,7},{4,6},{5,1},{6,4},{7,3},{8,10},{9,13},{10,... | collective-permute-start | bytes 6291464 | tf_op jit(solution)/shard_map/ppermute | solution.py:148
  262.8 6.1 %collective-permute-start.20 = (bf16[512,1024]{1,0:T(8,128)(2,1)}, bf16[512,1024]{1,0:T(8,128)(2,1)S(1)}, u32[]{:S(2)}, u32[]{:S(2)}) collective-permute-start(bf16[512,1024]{1,0:T(8,128)(2,1)} %get-tuple-element.325.refs_2_), channel_id=1, source_target_pairs={{0,1},{1,0},{2,3},{3,2},{4,5},{5,4},{6,7},{7,6},{8,9},{9,8},{10,11... | collective-permute-start | bytes 3145736 | tf_op jit(solution)/shard_map/ppermute | solution.py:148
  264.0 5.9 %collective-permute-start.21 = (bf16[512,1024]{1,0:T(8,128)(2,1)}, bf16[512,1024]{1,0:T(8,128)(2,1)S(1)}, u32[]{:S(2)}, u32[]{:S(2)}) collective-permute-start(bf16[512,1024]{1,0:T(8,128)(2,1)} %get-tuple-element.327.refs_4_), channel_id=1, source_target_pairs={{0,1},{1,0},{2,3},{3,2},{4,5},{5,4},{6,7},{7,6},{8,9},{9,8},{10,11... | collective-permute-start | bytes 3145736 | tf_op jit(solution)/shard_map/ppermute | solution.py:148
  264.0 6.8 %collective-permute-start.22 = (bf16[512,1024]{1,0:T(8,128)(2,1)}, bf16[512,1024]{1,0:T(8,128)(2,1)S(1)}, u32[]{:S(2)}, u32[]{:S(2)}) collective-permute-start(bf16[512,1024]{1,0:T(8,128)(2,1)} %get-tuple-element.329.refs_6_), channel_id=1, source_target_pairs={{0,1},{1,0},{2,3},{3,2},{4,5},{5,4},{6,7},{7,6},{8,9},{9,8},{10,11... | collective-permute-start | bytes 3145736 | tf_op jit(solution)/shard_map/ppermute | solution.py:148
  264.5 7.4 %collective-permute-start.23 = (bf16[512,1024]{1,0:T(8,128)(2,1)}, bf16[512,1024]{1,0:T(8,128)(2,1)S(1)}, u32[]{:S(2)}, u32[]{:S(2)}) collective-permute-start(bf16[512,1024]{1,0:T(8,128)(2,1)} %get-tuple-element.331.refs_8_), channel_id=1, source_target_pairs={{0,1},{1,0},{2,3},{3,2},{4,5},{5,4},{6,7},{7,6},{8,9},{9,8},{10,11... | collective-permute-start | bytes 3145736 | tf_op jit(solution)/shard_map/ppermute | solution.py:148
  268.9 18.6 %collective-permute-start.26 = (bf16[1024,512]{1,0:T(8,128)(2,1)S(1)}, bf16[1024,512]{1,0:T(8,128)(2,1)}, u32[]{:S(2)}, u32[]{:S(2)}) collective-permute-start(bf16[1024,512]{1,0:T(8,128)(2,1)S(1)} %copy-done.17), channel_id=1, source_target_pairs={{0,1},{1,0},{2,3},{3,2},{4,5},{5,4},{6,7},{7,6},{8,9},{9,8},{10,11... | collective-permute-start | bytes 3145736 | tf_op jit(solution)/shard_map/ppermute | solution.py:148
  276.3 11.2 %collective-permute-start.25 = (bf16[1024,512]{1,0:T(8,128)(2,1)}, bf16[1024,512]{1,0:T(8,128)(2,1)}, u32[]{:S(2)}, u32[]{:S(2)}) collective-permute-start(bf16[1024,512]{1,0:T(8,128)(2,1)} %get-tuple-element.358.refs_0_), channel_id=1, source_target_pairs={{0,1},{1,0},{2,3},{3,2},{4,5},{5,4},{6,7},{7,6},{8,9},{9,8},{10,11... | collective-permute-start | bytes 3145736 | tf_op jit(solution)/shard_map/ppermute | solution.py:148
  276.7 15.1 %collective-permute-start.24 = (bf16[4,128,1024]{2,1,0:T(8,128)(2,1)}, bf16[4,128,1024]{2,1,0:T(8,128)(2,1)}, u32[]{:S(2)}, u32[]{:S(2)}) collective-permute-start(bf16[4,128,1024]{2,1,0:T(8,128)(2,1)} %get-tuple-element.320), channel_id=1, source_target_pairs={{0,4},{1,3},{2,6},{3,1},{4,0},{5,7},{6,2},{7,5},{8,12},{9,11},{10,... | collective-permute-start | bytes 3145736 | tf_op jit(solution)/shard_map/ppermute | solution.py:148
  277.3 14.6 %collective-permute-start.27 = (bf16[512,1024]{1,0:T(8,128)(2,1)}, bf16[512,1024]{1,0:T(8,128)(2,1)}, u32[]{:S(2)}, u32[]{:S(2)}) collective-permute-start(bf16[512,1024]{1,0:T(8,128)(2,1)} %get-tuple-element.362.refs_4_), channel_id=1, source_target_pairs={{0,1},{1,0},{2,3},{3,2},{4,5},{5,4},{6,7},{7,6},{8,9},{9,8},{10,11... | collective-permute-start | bytes 3145736 | tf_op jit(solution)/shard_map/ppermute | solution.py:148
  294.3 31.4 %collective-permute-start.28 = (bf16[8,128,1024]{2,1,0:T(8,128)(2,1)}, bf16[8,128,1024]{2,1,0:T(8,128)(2,1)}, u32[]{:S(2)}, u32[]{:S(2)}) collective-permute-start(bf16[8,128,1024]{2,1,0:T(8,128)(2,1)} %get-tuple-element.343), channel_id=1, source_target_pairs={{0,2},{1,5},{2,0},{3,7},{4,6},{5,1},{6,4},{7,3},{8,10},{9,13},{10,... | collective-permute-start | bytes 6291464 | tf_op jit(solution)/shard_map/ppermute | solution.py:148
  294.8 30.8 %all-to-all-start.4 = ((bf16[4,128,1024]{2,1,0:T(8,128)(2,1)}), bf16[4,128,1024]{2,1,0:T(8,128)(2,1)S(1)}, u32[]{:S(2)}, u32[]{:S(2)}) async-start(bf16[4,128,1024]{2,1,0:T(8,128)(2,1)} %fold.11), calls=%async_computation.4 | async-start | bytes 2097152 | tf_op jit(solution)/shard_map/all_to_all | solution.py:156
  315.3 10.3 %collective-permute-start.29 = (bf16[512,1024]{1,0:T(8,128)(2,1)}, bf16[512,1024]{1,0:T(8,128)(2,1)}, u32[]{:S(2)}, u32[]{:S(2)}) collective-permute-start(bf16[512,1024]{1,0:T(8,128)(2,1)} %get-tuple-element.364.refs_0_.refs_6_), channel_id=1, source_target_pairs={{0,1},{1,0},{2,3},{3,2},{4,5},{5,4},{6,7},{7,6},{8,9},{9,8},{10,11... | collective-permute-start | bytes 3145736 | tf_op jit(solution)/shard_map/ppermute | solution.py:148
  315.3 10.3 %collective-permute-start.30 = (bf16[512,1024]{1,0:T(8,128)(2,1)}, bf16[512,1024]{1,0:T(8,128)(2,1)}, u32[]{:S(2)}, u32[]{:S(2)}) collective-permute-start(bf16[512,1024]{1,0:T(8,128)(2,1)} %get-tuple-element.366.refs_1_.refs_8_), channel_id=1, source_target_pairs={{0,1},{1,0},{2,3},{3,2},{4,5},{5,4},{6,7},{7,6},{8,9},{9,8},{10,11... | collective-permute-start | bytes 3145736 | tf_op jit(solution)/shard_map/ppermute | solution.py:148
  315.8 9.8 %collective-permute-start.31 = (bf16[512,1024]{1,0:T(8,128)(2,1)}, bf16[512,1024]{1,0:T(8,128)(2,1)}, u32[]{:S(2)}, u32[]{:S(2)}) collective-permute-start(bf16[512,1024]{1,0:T(8,128)(2,1)} %get-tuple-element.368.refs_2_.refs_10_), channel_id=1, source_target_pairs={{0,1},{1,0},{2,3},{3,2},{4,5},{5,4},{6,7},{7,6},{8,9},{9,8},{10,11... | collective-permute-start | bytes 3145736 | tf_op jit(solution)/shard_map/ppermute | solution.py:148
  330.2 15.6 %collective-permute-start.33 = (bf16[2048,512]{1,0:T(8,128)(2,1)}, bf16[2048,512]{1,0:T(8,128)(2,1)}, u32[]{:S(2)}, u32[]{:S(2)}) collective-permute-start(bf16[2048,512]{1,0:T(8,128)(2,1)} %get-tuple-element.393.refs_0_), channel_id=1, source_target_pairs={{0,1},{1,0},{2,3},{3,2},{4,5},{5,4},{6,7},{7,6},{8,9},{9,8},{10,11... | collective-permute-start | bytes 6291464 | tf_op jit(solution)/shard_map/ppermute | solution.py:148
  330.7 11.6 %collective-permute-start.34 = (bf16[512,1024]{1,0:T(8,128)(2,1)S(1)}, bf16[512,1024]{1,0:T(8,128)(2,1)}, u32[]{:S(2)}, u32[]{:S(2)}) collective-permute-start(bf16[512,1024]{1,0:T(8,128)(2,1)S(1)} %copy-done.4), channel_id=1, source_target_pairs={{0,1},{1,0},{2,3},{3,2},{4,5},{5,4},{6,7},{7,6},{8,9},{9,8},{10,11... | collective-permute-start | bytes 3145736 | tf_op jit(solution)/shard_map/ppermute | solution.py:148
  330.7 15.1 %collective-permute-start.32 = (bf16[4,128,1024]{2,1,0:T(8,128)(2,1)}, bf16[4,128,1024]{2,1,0:T(8,128)(2,1)}, u32[]{:S(2)}, u32[]{:S(2)}) collective-permute-start(bf16[4,128,1024]{2,1,0:T(8,128)(2,1)} %get-tuple-element.355), channel_id=1, source_target_pairs={{0,4},{1,3},{2,6},{3,1},{4,0},{5,7},{6,2},{7,5},{8,12},{9,11},{10,... | collective-permute-start | bytes 3145736 | tf_op jit(solution)/shard_map/ppermute | solution.py:148
  348.5 26.4 %collective-permute-start.35 = (bf16[8,128,1024]{2,1,0:T(8,128)(2,1)}, bf16[8,128,1024]{2,1,0:T(8,128)(2,1)}, u32[]{:S(2)}, u32[]{:S(2)}) collective-permute-start(bf16[8,128,1024]{2,1,0:T(8,128)(2,1)} %get-tuple-element.378), channel_id=1, source_target_pairs={{0,2},{1,5},{2,0},{3,7},{4,6},{5,1},{6,4},{7,3},{8,10},{9,13},{10,... | collective-permute-start | bytes 6291464 | tf_op jit(solution)/shard_map/ppermute | solution.py:148
  359.8 11.4 %collective-permute-start.36 = (bf16[16,32,1024]{2,1,0:T(8,128)(2,1)}, bf16[16,32,1024]{2,1,0:T(8,128)(2,1)}, u32[]{:S(2)}, u32[]{:S(2)}) collective-permute-start(bf16[16,32,1024]{2,1,0:T(8,128)(2,1)} %grads.9), channel_id=1, source_target_pairs={{0,1},{1,0},{2,3},{3,2},{4,5},{5,4},{6,7},{7,6},{8,9},{9,8},{10,11... | collective-permute-start | bytes 3145736 | tf_op jit(solution)/shard_map/ppermute | solution.py:148
  359.8 31.4 %all-to-all-start.5 = ((bf16[4,128,1024]{2,1,0:T(8,128)(2,1)}), bf16[4,128,1024]{2,1,0:T(8,128)(2,1)S(1)}, u32[]{:S(2)}, u32[]{:S(2)}) async-start(bf16[4,128,1024]{2,1,0:T(8,128)(2,1)} %fold.13), calls=%async_computation.5 | async-start | bytes 2097152 | tf_op jit(solution)/shard_map/all_to_all | solution.py:156
  378.3 25.3 %collective-permute-start.38 = (bf16[8,64,1024]{2,1,0:T(8,128)(2,1)}, bf16[8,64,1024]{2,1,0:T(8,128)(2,1)}, u32[]{:S(2)}, u32[]{:S(2)}) collective-permute-start(bf16[8,64,1024]{2,1,0:T(8,128)(2,1)} %get-tuple-element.408), channel_id=1, source_target_pairs={{0,2},{1,5},{2,0},{3,7},{4,6},{5,1},{6,4},{7,3},{8,10},{9,13},{10,... | collective-permute-start | bytes 3145736 | tf_op jit(solution)/shard_map/ppermute | solution.py:148
  379.8 23.8 %collective-permute-start.37 = (bf16[4,128,1024]{2,1,0:T(8,128)(2,1)}, bf16[4,128,1024]{2,1,0:T(8,128)(2,1)}, u32[]{:S(2)}, u32[]{:S(2)}) collective-permute-start(bf16[4,128,1024]{2,1,0:T(8,128)(2,1)} %get-tuple-element.405), channel_id=1, source_target_pairs={{0,4},{1,3},{2,6},{3,1},{4,0},{5,7},{6,2},{7,5},{8,12},{9,11},{10,... | collective-permute-start | bytes 3145736 | tf_op jit(solution)/shard_map/ppermute | solution.py:148
  391.3 14.9 %copy-start.7 = (bf16[4,128,1024]{2,1,0:T(8,128)(2,1)}, bf16[4,128,1024]{2,1,0:T(8,128)(2,1)S(1)}, u32[]{:S(2)}) copy-start(bf16[4,128,1024]{2,1,0:T(8,128)(2,1)S(1)} %all-to-all-done.5) | copy-start | bytes 3145732
  406.1 30.1 %all-to-all-start.6 = ((bf16[4,128,1024]{2,1,0:T(8,128)(2,1)}), bf16[4,128,1024]{2,1,0:T(8,128)(2,1)}, u32[]{:S(2)}, u32[]{:S(2)}) async-start(bf16[4,128,1024]{2,1,0:T(8,128)(2,1)} %fold.15), calls=%async_computation.6 | async-start | bytes 2097152 | tf_op jit(solution)/shard_map/all_to_all | solution.py:156
  413.6 29.4 %copy-start.6 = (bf16[4,128,1024]{2,1,0:T(8,128)(2,1)S(1)}, bf16[4,128,1024]{2,1,0:T(8,128)(2,1)}, u32[]{:S(2)}) copy-start(bf16[4,128,1024]{2,1,0:T(8,128)(2,1)} %copy-done.5) | copy-start | bytes 3145732
  413.6 13.3 %collective-permute-start.40 = (bf16[8,32,1024]{2,1,0:T(8,128)(2,1)}, bf16[8,32,1024]{2,1,0:T(8,128)(2,1)}, u32[]{:S(2)}, u32[]{:S(2)}) collective-permute-start(bf16[8,32,1024]{2,1,0:T(8,128)(2,1)} %get-tuple-element.415), channel_id=1, source_target_pairs={{0,2},{1,5},{2,0},{3,7},{4,6},{5,1},{6,4},{7,3},{8,10},{9,13},{10,... | collective-permute-start | bytes 1572872 | tf_op jit(solution)/shard_map/ppermute | solution.py:148
  414.7 12.2 %collective-permute-start.39 = (bf16[4,64,1024]{2,1,0:T(8,128)(2,1)}, bf16[4,64,1024]{2,1,0:T(8,128)(2,1)S(1)}, u32[]{:S(2)}, u32[]{:S(2)}) collective-permute-start(bf16[4,64,1024]{2,1,0:T(8,128)(2,1)} %get-tuple-element.412), channel_id=1, source_target_pairs={{0,4},{1,3},{2,6},{3,1},{4,0},{5,7},{6,2},{7,5},{8,12},{9,11},{10,... | collective-permute-start | bytes 1572872 | tf_op jit(solution)/shard_map/ppermute | solution.py:148
  438.2 18.2 %all-to-all-start.7 = ((bf16[4,64,1024]{2,1,0:T(8,128)(2,1)}), bf16[4,64,1024]{2,1,0:T(8,128)(2,1)}, u32[]{:S(2)}, u32[]{:S(2)}) async-start(bf16[4,64,1024]{2,1,0:T(8,128)(2,1)} %fold.17), calls=%async_computation.7 | async-start | bytes 1048576 | tf_op jit(solution)/shard_map/all_to_all | solution.py:156
  446.0 6.6 %collective-permute-start.41 = (bf16[4,32,1024]{2,1,0:T(8,128)(2,1)}, bf16[4,32,1024]{2,1,0:T(8,128)(2,1)S(1)}, u32[]{:S(2)}, u32[]{:S(2)}) collective-permute-start(bf16[4,32,1024]{2,1,0:T(8,128)(2,1)} %get-tuple-element.420), channel_id=1, source_target_pairs={{0,4},{1,3},{2,6},{3,1},{4,0},{5,7},{6,2},{7,5},{8,12},{9,11},{10,... | collective-permute-start | bytes 786440 | tf_op jit(solution)/shard_map/ppermute | solution.py:148
  448.1 16.8 %copy-start.3 = (f32[128,1024]{1,0:T(8,128)}, f32[128,1024]{1,0:T(8,128)S(1)}, u32[]{:S(2)}) copy-start(f32[128,1024]{1,0:T(8,128)S(1)} %convert_reduce_fusion.1.refs_4_) | copy-start | bytes 1572868
  458.1 11.7 %all-to-all-start.8 = ((bf16[4,32,1024]{2,1,0:T(8,128)(2,1)}), bf16[4,32,1024]{2,1,0:T(8,128)(2,1)S(1)}, u32[]{:S(2)}, u32[]{:S(2)}) async-start(bf16[4,32,1024]{2,1,0:T(8,128)(2,1)} %fold.19), calls=%async_computation.8 | async-start | bytes 524288 | tf_op jit(solution)/shard_map/all_to_all | solution.py:156
  463.0 23.2 %copy-start = (f32[128,1024]{1,0:T(8,128)}, f32[128,1024]{1,0:T(8,128)S(1)}, u32[]{:S(2)}) copy-start(f32[128,1024]{1,0:T(8,128)S(1)} %convert_reduce_fusion.2.refs_2_.refs_3_) | copy-start | bytes 1572868
  464.9 21.3 %copy-start.12 = (f32[64,1024]{1,0:T(8,128)}, f32[64,1024]{1,0:T(8,128)S(1)}, u32[]{:S(2)}) copy-start(f32[64,1024]{1,0:T(8,128)S(1)} %convert_reduce_fusion.3.refs_1_) | copy-start | bytes 786436
  469.9 16.4 %copy-start.16 = (f32[32,1024]{1,0:T(8,128)}, f32[32,1024]{1,0:T(8,128)S(1)}, u32[]{:S(2)}) copy-start(f32[32,1024]{1,0:T(8,128)S(1)} %convert_reduce_fusion.4.refs_0_) | copy-start | bytes 393220
  (17 other events, 89.9 us)

commit v4 on v3

--- a/solution.py
+++ b/solution.py
@@ -22,10 +22,11 @@
 DECAY = 0.01
 ADAM_EPS = 1e-08
 FAR_AWAY = -1e30
-VMEM = 62 * 1024 * 1024
+VMEM = 64 * 1024 * 1024
 TABLE_AT = 768
 HEAD_AT = 896
 BANDS = 32
+HEADS_AT_ONCE = 4
 
 
 def as_low(x):
@@ -194,17 +195,18 @@
 def attend_kernel(length_ref, slope_ref, packed_ref, mixed_ref, lse_ref, bias_ref):
     step = pl.program_id(0)
     q_ref, k_ref, v_ref = (packed_ref.at[j] for j in range(3))
-    frames = q_ref.shape[0]
+    frames, lanes_here = mixed_ref.shape
+    here = lanes_here // HD
 
     @pl.when(step == 0)
     def _():
         bias_ref[...] = key_bias(length_ref[0], frames)
 
     parts = []
-    for h in range(2):
+    for h in range(here):
         lanes = slice(h * HD, (h + 1) * HD)
         scores = dot_nt(k_ref[:, lanes], q_ref[:, lanes] * jnp.bfloat16(HD**-0.5))
-        scores = scores + slope_ref[2 * step + h] * bias_ref[...]
+        scores = scores + slope_ref[here * step + h] * bias_ref[...]
         top = jnp.max(scores, 0, keepdims=True)
         expo = jnp.exp(scores - top)
         total = jnp.sum(expo, 0, keepdims=True)
@@ -216,17 +218,17 @@
 
 def attend(length, slopes, packed):
     _, frames, width = packed.shape
-    pairs = width // (2 * HD)
-    block = pl.BlockSpec((frames, 2 * HD), lambda i: (0, i))
+    steps = width // (HEADS_AT_ONCE * HD)
+    block = pl.BlockSpec((frames, HEADS_AT_ONCE * HD), lambda i: (0, i))
     return pl.pallas_call(
         attend_kernel,
-        grid=(pairs,),
+        grid=(steps,),
         in_specs=[pl.BlockSpec(memory_space=pltpu.SMEM)] * 2
-        + [pl.BlockSpec((3, frames, 2 * HD), lambda i: (0, 0, i))],
-        out_specs=[block, pl.BlockSpec((1, 2, frames), lambda i: (i, 0, 0))],
+        + [pl.BlockSpec((3, frames, HEADS_AT_ONCE * HD), lambda i: (0, 0, i))],
+        out_specs=[block, pl.BlockSpec((1, HEADS_AT_ONCE, frames), lambda i: (i, 0, 0))],
         out_shape=[
             jax.ShapeDtypeStruct((frames, width), jnp.bfloat16),
-            jax.ShapeDtypeStruct((pairs, 2, frames), jnp.float32),
+            jax.ShapeDtypeStruct((steps, HEADS_AT_ONCE, frames), jnp.float32),
         ],
         scratch_shapes=[pltpu.VMEM((frames, frames), jnp.float32)],
         compiler_params=params(),
@@ -235,22 +237,24 @@
 
 
 def attend_back_kernel(
-    length_ref, slope_ref, packed_ref, d_ref, lse_ref, dq_ref, dk_ref, dv_ref, bias_ref
+    length_ref, slope_ref, packed_ref, d_out_ref, w_ref, lse_ref, dq_ref, dk_ref, dv_ref, bias_ref
 ):
     step = pl.program_id(0)
     q_ref, k_ref, v_ref = (packed_ref.at[j] for j in range(3))
-    frames = q_ref.shape[0]
+    frames, lanes_here = dq_ref.shape
+    here = lanes_here // HD
 
     @pl.when(step == 0)
     def _():
         bias_ref[...] = key_bias(length_ref[0], frames)
 
+    d_mixed_here = as_low(dot_nt(d_out_ref[...], w_ref[...]))
     d_query, d_keys, d_values = [], [], []
-    for h in range(2):
+    for h in range(here):
         lanes = slice(h * HD, (h + 1) * HD)
         query = q_ref[:, lanes] * jnp.bfloat16(HD**-0.5)
-        keys, values, d_mixed = k_ref[:, lanes], v_ref[:, lanes], d_ref[:, lanes]
-        scores = dot_nt(keys, query) + slope_ref[2 * step + h] * bias_ref[...]
+        keys, values, d_mixed = k_ref[:, lanes], v_ref[:, lanes], d_mixed_here[:, lanes]
+        scores = dot_nt(keys, query) + slope_ref[here * step + h] * bias_ref[...]
         probs = jnp.exp(scores - lse_ref[0, h : h + 1])
         d_probs = dot_nt(values, d_mixed)
         row_dot = jnp.sum(d_probs * probs, 0, keepdims=True)
@@ -263,22 +267,26 @@
     dv_ref[...] = as_low(jnp.concatenate(d_values, 1))
 
 
-def attend_back(length, slopes, packed, d_mixed, lse):
+def attend_back(length, slopes, packed, d_out, w, lse):
     _, frames, width = packed.shape
-    pairs = width // (2 * HD)
-    stacked = pl.BlockSpec((3, frames, 2 * HD), lambda i: (0, 0, i))
+    wide = HEADS_AT_ONCE * HD
+    block = pl.BlockSpec((frames, wide), lambda i: (0, i))
     return pl.pallas_call(
         attend_back_kernel,
-        grid=(pairs,),
+        grid=(width // wide,),
         in_specs=[pl.BlockSpec(memory_space=pltpu.SMEM)] * 2
-        + [stacked, pl.BlockSpec((frames, 2 * HD), lambda i: (0, i))]
-        + [pl.BlockSpec((1, 2, frames), lambda i: (i, 0, 0))],
-        out_specs=[pl.BlockSpec((frames, 2 * HD), lambda i: (0, i))] * 3,
+        + [
+            pl.BlockSpec((3, frames, wide), lambda i: (0, 0, i)),
+            pl.BlockSpec((frames, width), lambda i: (0, 0)),
+            pl.BlockSpec((wide, width), lambda i: (i, 0)),
+            pl.BlockSpec((1, HEADS_AT_ONCE, frames), lambda i: (i, 0, 0)),
+        ],
+        out_specs=[block] * 3,
         out_shape=[jax.ShapeDtypeStruct((frames, width), jnp.bfloat16)] * 3,
         scratch_shapes=[pltpu.VMEM((frames, frames), jnp.float32)],
         compiler_params=params(),
         name="attend_back",
-    )(length, slopes, packed, d_mixed, lse)
+    )(length, slopes, packed, d_out, w, lse)
 
 
 def gelu_both(x):
@@ -859,7 +867,7 @@
 
     def spec(j, x):
         if j in copied:
-            return pl.BlockSpec(memory_space=pl.ANY)
+            return pl.BlockSpec(memory_space=pltpu.HBM)
         return pl.BlockSpec(x.shape, lambda i, n=len(x.shape): (0,) * n)
 
     specs = [spec(j, x) for j, x in enumerate(arrays)]
@@ -936,10 +944,11 @@
 
 def adam_kernel(at, clip_ref, *refs):
     phone_rows, phone_width, inputs, at_gain = at
-    small, skip, attend, output, expand, reduce = refs[:6]
-    masters, moments, squares = refs[6:15], refs[15:24], refs[24:33]
-    outs = refs[33:]
-    unit = small.shape[0]
+    last, attend, expand, reduce = refs[:4]
+    masters, moments, squares = refs[4:13], refs[13:22], refs[22:31]
+    outs = refs[31:]
+    unit = last.shape[0] // 3
+    small = last[2 * unit :]
     clip = clip_ref[0]
     mel_lanes = inputs - phone_width
     lanes = [small[:, phone_width : phone_width + mel_lanes], small[:, :phone_width]]
@@ -954,7 +963,7 @@
     grads_of = [
         jnp.concatenate(lanes, 1),
         small[:phone_rows, TABLE_AT:HEAD_AT],
-        skip[...],
+        last[: 2 * unit],
         columns(attend, unit),
         attend[:unit],
         columns(expand, 0),
@@ -983,6 +992,45 @@
         name="adam",
     )(clip, *arrays)
     return [y for n in range(3) for y in turned(results[9 * n : 9 * n + 9])]
+
+
+def prepare_kernel(at_mel, at_count, frames, facts_ref, input_ref, table_ref, head_ref, gains_ref, skip_ref, out_ref):
+    unit, inputs = input_ref.shape
+    phones = inputs - at_mel
+    turned = as_low(input_ref[...])
+    out_ref[0, :unit, :phones] = turned[:, at_mel:]
+    out_ref[0, :unit, phones:TABLE_AT] = jnp.pad(turned[:, :at_mel], ((0, 0), (0, TABLE_AT - inputs)))
+    table = as_low(table_ref[...])
+    rest = jnp.zeros((unit - table.shape[0], table.shape[1]), jnp.bfloat16)
+    out_ref[0, :unit, TABLE_AT:HEAD_AT] = jnp.concatenate([table, rest], 0)
+    bins = head_ref.shape[1]
+    edge = jnp.pad(head_ref[...], ((0, 0), (0, out_ref.shape[2] - HEAD_AT - bins)))
+    lane = lax.broadcasted_iota(jnp.int32, edge.shape, 1)
+    spot = (gains_ref.shape[0], edge.shape[1])
+    row = lax.broadcasted_iota(jnp.int32, spot, 0)
+    here = lax.broadcasted_iota(jnp.int32, spot, 1) == row + bins
+    edge = as_low(edge).astype(jnp.float32) + dot_tn(as_low(gains_ref[...]), as_low(here))
+    end = jnp.minimum(jnp.minimum(facts_ref[2], facts_ref[3]), frames)
+    count = jnp.maximum(end - jnp.maximum(facts_ref[1], 0), 0)
+    for j, fact in enumerate((facts_ref[0], lax.div(count, 16), lax.rem(count, 16))):
+        edge = jnp.where(lane == at_count - HEAD_AT + j, fact.astype(jnp.float32), edge)
+    out_ref[0, :unit, HEAD_AT:] = as_low(edge)
+    out_ref[0, unit:] = as_low(skip_ref[...])
+    for z in range(1, out_ref.shape[0]):
+        out_ref[z] = out_ref[0]
+
+
+def prepare(facts, turned, table, head, gains, skip, deep, frames, at_mel, at_count):
+    vmem = pl.BlockSpec(memory_space=pltpu.VMEM)
+    rows, width = turned.shape[0] + skip.shape[0], skip.shape[1]
+    return pl.pallas_call(
+        partial(prepare_kernel, at_mel, at_count, frames),
+        in_specs=[pl.BlockSpec(memory_space=pltpu.SMEM)] + [vmem] * 5,
+        out_specs=vmem,
+        out_shape=jax.ShapeDtypeStruct((deep, rows, width), jnp.bfloat16),
+        compiler_params=params(),
+        name="prepare",
+    )(facts, turned, table, head, gains, skip)
 
 
 def shards(
@@ -1096,9 +1144,11 @@
     def along(x, role, *after):
         return spread(grid, tied(x, *after) if after else x, role)
 
+    def copies(x):
+        return jnp.broadcast_to(x[None], (grid.size("z"),) + x.shape)
+
     def deepen(x, *after):
-        x = tied(x, *after) if after else x
-        return swap_deep(grid, jnp.broadcast_to(x[None], (grid.size("z"),) + x.shape))
+        return swap_deep(grid, tied(x, *after) if after else x)
 
     def plane(moved):
         return stack(moved).reshape((-1,) + moved[0].shape[1:])
@@ -1131,10 +1181,19 @@
     states_turned = skip_states.T
     loads = [load(stage) for stage in stages]
     if fast:
-        deep_0, near_2 = join(deepen(loads[0]), along(loads[2], "near"))
-        pair_2 = stack(near_2)
-        near_0, deep_1, target, mel, phone_hot, slopes, times, inside, states_turned = join(
-            along(deep_0, "near"), deepen(loads[1], deep_0),
+        if unit % 16 == 0 and inputs % 16 == 0:
+            first = prepare(
+                jnp.stack([speaker[0], span_start[0], span_end[0], lengths[0]]), w_input.T, phone_table.T,
+                w_head, norm_gains, w_skip, grid.size("z"), frames, 2 * mel_bins, at_count,
+            )
+        else:
+            first = copies(loads[0])
+        deep_0, near_2, load_1, load_3 = join(
+            deepen(first), along(loads[2], "near"), copies(loads[1]), copies(loads[3])
+        )
+        pair_2 = copies(stack(near_2))
+        near_0, deep_1, pair_2, target, mel, phone_hot, slopes, times, inside, states_turned = join(
+            along(deep_0, "near", pair_2), deepen(load_1, deep_0), pair_2,
             target, mel, phone_hot, slopes, times, inside, states_turned,
         )
         near_0 = plane(near_0)
@@ -1165,21 +1224,21 @@
     share = jnp.sum(speaker_hot / jnp.maximum(counts, 1.0)) / SPK
 
     if fast:
-        far_1, core_1, deep_2, embedded, stream, attn_in, attn_turned, edges = join(
-            far_1, core_1, deep_2, embedded, stream, attn_in, attn_turned, edges
+        far_1, core_1, deep_2, embedded, stream, attn_in, attn_turned, edges, share, counts = join(
+            far_1, core_1, deep_2, embedded, stream, attn_in, attn_turned, edges, share, counts
         )
         near_2 = deep_2.reshape((-1,) + deep_2.shape[2:])
         pieces_1 = [near_1, far_1, core_1, sibling(far_1)]
         far_2 = along(near_2, "far")[1]
         core_2 = sibling(near_2)
-        deep_3 = deepen(loads[3], near_2)
+        deep_3 = deepen(load_3, near_2)
     else:
         pieces_1 = gather_whole(stages[1])
     attend_full, packed = pack(own, other, pieces_1, attn_in, packs)
     mixed, lse = attend(lengths, slopes, packed)
     if fast:
-        far_2, deep_3, core_2, packed, mixed, lse, share, joined_turned = join(
-            far_2, deep_3, core_2, packed, mixed, lse, share, joined_turned
+        far_2, deep_3, core_2, packed, mixed, lse, joined_turned = join(
+            far_2, deep_3, core_2, packed, mixed, lse, joined_turned
         )
         near_3 = along(deep_3, "near")
         pieces_2 = [near_2, far_2, core_2, sibling(far_2)]
@@ -1241,26 +1300,25 @@
     d_stream_mid, d_out, grad_gain_two, *d_hidden = ffn_back(
         d_branch_next, d_stream_out, reduce_full, gelu_slope, expand_full, stream_mid, edges, mel_bins + 1
     )
-    d_mixed = as_low(dot_nt(d_out, output_full))
     if fast:
         turned = both(ffn_turned)
         d_hiddens = both(*d_hidden)
-        moved_0, turned, d_hiddens, d_stream_mid, d_out, d_mixed = join(
-            moved_0, turned, d_hiddens, d_stream_mid, d_out, d_mixed
+        moved_0, turned, d_hiddens, d_stream_mid, d_out = join(
+            moved_0, turned, d_hiddens, d_stream_mid, d_out
         )
         legs_0 = fold([legs_0[0]] + moved_0, near)
         moved_0 = hops(legs_0, "near")
         plan = [((0, 1), (2 + 2 * j, 3 + 2 * j), unit, 0) for j in range(wides)]
         legs_1 = sums(plan, turned + d_hiddens, legs_0[0])
         turned = both(tied(mixed_turned, legs_0[0]), attn_turned, d_out)
-        moved_0, legs_1, turned, d_mixed = join(moved_0, legs_1, turned, d_mixed)
+        moved_0, legs_1, turned, d_out = join(moved_0, legs_1, turned, d_out)
         (sums_0,) = fold([legs_0[0]] + moved_0, 1)
-        d_mixed = tied(d_mixed, sums_0)
+        d_out = tied(d_out, sums_0)
         moved_1 = hops(legs_1, "far", sums_0)
         sums_0 = swap_deep(grid, sums_0)
     else:
         share_expand = dense([(ffn_turned, d, unit, 0) for d in d_hidden])
-    d_packed = attend_back(lengths, slopes, packed, d_mixed, lse)
+    d_packed = attend_back(lengths, slopes, packed, d_out, output_full, lse)
     d_joined_in, grad_gain_one = pack_back(
         d_packed, attend_full, d_stream_mid, stream, edges, mel_bins
     )
@@ -1282,54 +1340,45 @@
         share_attend = dense(
             [(mixed_turned, d_out, unit, 0)] + [(attn_turned, d, unit, 0) for d in d_packed]
         )
-        share_skip = dense([(joined_turned, d_joined_in, 2 * unit, o) for o in offsets[:2]])
     gain_grads = [grad_gain_one, grad_gain_two, grad_gain_three]
     small_grads = tail(
         d_joined_in, skip_full, small_full, embedded, mel, phone_hot, grad_head, gain_grads, mel_bins
     )
     if fast:
-        plan = [((0, 1, 2), None, 0, 0)]
         small_grads = list(small_grads)
-        (sent,) = grads(plan, small_grads, theirs, frames, unit, width, 1)
-        plan_skip = [((0, 1), (2, 3), 2 * unit, o) for o in offsets[:2]]
-        legs_3 = sums(plan_skip, joined, sent)
-        legs_4 = grads(plan, small_grads, mine, frames, unit, width, far, sibling(sent))
-        moved_2, legs_3, legs_4 = join(moved_2, legs_3, legs_4)
+        (sent,) = grads([((0, 1, 2), None, 0, 0)], small_grads, theirs, frames, unit, width, 1)
+        plan = [((0, 1), (2, 3), 2 * unit, o) for o in offsets[:2]] + [((4, 5, 6), None, 0, 0)]
+        legs_3 = sums(plan, joined + small_grads, sent, came=sibling(sent))
+        moved_2, legs_3 = join(moved_2, legs_3)
         legs_2 = fold([legs_2[0]] + moved_2, near)
-        moved_2 = hops(legs_2, "near")
         moved_3 = hops(legs_3, "far", legs_2[0])
-        moved_2, moved_3, sums_1 = join(moved_2, moved_3, sums_1)
+        moved_2, sums_1 = join(hops(legs_2, "near"), sums_1)
         (sums_2,) = fold([legs_2[0]] + moved_2, 1)
-        legs_3 = fold([legs_3[0], tied(moved_3[0], sums_2)] + moved_3[1:], near)
-        sums_2 = swap_deep(grid, sums_2)
-        moved_3 = hops(legs_3, "near")
-        moved_4 = hops(legs_4, "far", legs_3[0])
-        moved_3, moved_4, sums_2 = join(moved_3, moved_4, sums_2)
+        moved_3 = [tied(moved_3[0], sums_2)] + moved_3[1:]
+        legs_3 = fold([legs_3[0]] + moved_3, near)
+        moved_3, sums_2 = join(hops(legs_3, "near"), swap_deep(grid, sums_2))
         (sums_3,) = fold([legs_3[0]] + moved_3, 1)
-        legs_4 = fold([legs_4[0], tied(moved_4[0], sums_3)] + moved_4[1:], near)
-        moved_4 = hops(legs_4, "near")
         sums_3 = swap_deep(grid, sums_3)
-        moved_4, sums_3 = join(moved_4, sums_3)
-        (sums_4,) = fold([legs_4[0]] + moved_4, 1)
-        sums_4 = swap_deep(grid, sums_4)
-        share_reduce, share_expand, share_attend, share_skip, share_small = [
-            jnp.sum(x.astype(jnp.float32), 0) for x in (sums_0, sums_1, sums_2, sums_3, sums_4)
+        share_reduce, share_expand, share_attend, share_last = [
+            jnp.sum(x.astype(jnp.float32), 0) for x in (sums_0, sums_1, sums_2, sums_3)
         ]
     else:
         main, table, edge = small_grads
         table = table.reshape(devices, phone_wide, phones)
         table = jnp.pad(table, ((0, 0), (0, unit - phone_wide), (0, 0))).reshape(width, phones)
         small_grads = jnp.concatenate([main, table, edge], 1).astype(jnp.float32)
-        share_small = dense([(small_grads, None, 0, 0)])
-
-    shares = (share_small, share_skip, share_attend, share_expand, share_reduce)
+        share_last = dense(
+            [(joined_turned, d_joined_in, 2 * unit, o) for o in offsets[:2]]
+            + [(small_grads, None, 0, 0)]
+        )
+
+    shares = (share_last, share_attend, share_expand, share_reduce)
     local_square = sum((jnp.sum(g * g) for g in shares))
     totals = all_sum(grid, jnp.concatenate([speaker_hot * error_sum[0, 0], local_square[None]]))
     sums, total_square = totals[:SPK], totals[SPK]
     loss_value = jnp.mean(sums / jnp.maximum(counts, 1.0))
     grad_norm = jnp.sqrt(total_square)
     clip = jnp.minimum(1.0, 1.0 / (grad_norm + 1e-06))
-    shares = (share_small, share_skip, share_attend, share_attend, share_expand, share_reduce)
     at = (phone_wide, phone_width, inputs, mel_bins)
     results = adam(clip[None], shares, masters, moments, squares, at)
     return (loss_value, grad_norm, *results)

time: 504 us -> 486 us (0.964)
    all_to_all x9 -> x8, waiting for transfers between devices: 52.8 us -> 42.7 us  [swap_deep(): return lax.all_to_all(x, AXES, 0, 0, axis_index_groups=grid.lines())]
    ppermute x42 -> x40, waiting for transfers between devices: 98.9 us -> 105 us  [shift(): return lax.ppermute(x, AXES, grid.pairs(role, step))]
    pallas_call x10 -> x8, Pallas kernels: 26.2 us -> 23.2 us  [fold(): pl.pallas_call(partial(fold_kernel, legs), grid=(rows // tile,), in_specs...]
    pallas_call x2 -> x3, Pallas kernels: 29.9 us -> 32.6 us  [the longest x1 18.3 us: attend_back(): pl.pallas_call(attend_back_kernel, grid=(width // wide,), in_specs=[pl.Bl...]
    ppermute x42 -> x40, starting transfers between devices: 26.7 us -> 25 us  [shift(): return lax.ppermute(x, AXES, grid.pairs(role, step))]
    pallas_call x6 -> x5, Pallas kernels: 42 us -> 40.7 us  [grads(): pl.pallas_call(partial(grads_kernel, plan, count, rows, legs, came is not...]
    all_to_all x9 -> x8, starting transfers between devices: 39.3 us -> 38.1 us  [swap_deep(): return lax.all_to_all(x, AXES, 0, 0, axis_index_groups=grid.lines())]
  transfers between devices with their start and end apart: 51 -> 48, of which waited for: 25 -> 27; matrix products, arithmetic and copies ran while one was open for 5% -> 5% of each run, Pallas kernels for 38% -> 39%
where the time goes in v4:
time: 486 us; the launch traced here: 479 us
  Pallas kernels  212 us (44%)
  waiting for transfers between devices  147 us (30%)
  starting transfers between devices  63.1 us (13%)
  other arithmetic  18.3 us (4%)
  local copies, waits for them, and re-layouts  15.9 us (3%)
  between operations  11.6 us (2%)
  blocking collectives  10.4 us (2%)
    ppermute x40, waiting for transfers between devices, shift(): return lax.ppermute(x, AXES, grid.pairs(role, step))  105 us
    all_to_all x8, waiting for transfers between devices, swap_deep(): return lax.all_to_all(x, AXES, 0, 0, axis_index_groups=grid.lines())  42.7 us
    pallas_call x5, Pallas kernels, grads(): pl.pallas_call(partial(grads_kernel, plan, count, rows, legs, came is not...  40.7 us
    all_to_all x8, starting transfers between devices, swap_deep(): return lax.all_to_all(x, AXES, 0, 0, axis_index_groups=grid.lines())  38.1 us
    ppermute x40, starting transfers between devices, shift(): return lax.ppermute(x, AXES, grid.pairs(role, step))  25 us
    pallas_call x8, Pallas kernels, fold(): pl.pallas_call(partial(fold_kernel, legs), grid=(rows // tile,), in_specs...  23.2 us
    pallas_call x1, Pallas kernels, ffn_back(): pl.pallas_call(partial(ffn_back_kernel, at_gain), grid=(count,), in_specs...  20.4 us
    pallas_call x1, Pallas kernels, attend_back(): pl.pallas_call(attend_back_kernel, grid=(width // wide,), in_specs=[pl.Bl...  18.3 us
  transfers between devices with their start and end apart: 48, of which 27 were waited for; matrix products, arithmetic and copies ran while one was open for 5% of the time, Pallas kernels for 39%

profile of v4, /device:TPU:0, one launch (start us, length us, event | category | flops | bytes accessed | tf_op | source)
XLA Modules:
  0.0 478.7 jit_solution(17906767681490275517)
XLA Ops:
  3.8 2.2 prepare.1
  6.0 6.5 %all-to-all-start = ((bf16[4,96,1024]{2,1,0:T(8,128)(2,1)}), bf16[4,96,1024]{2,1,0:T(8,128)(2,1)S(1)}, u32[]{:S(2)}, u32[]{:S(2)}) async-start(bf16[4,96,1024]{2,1,0:T(8,128)(2,1)} %prepare.1), calls=%async_computation | async-start | bytes 1572864 | tf_op jit(solution)/shard_map/all_to_all | solution.py:157
  13.6 1.6 collective-permute-start
  16.0 4.8 %collective-permute-done.refs_1_ = bf16[160,1024]{1,0:T(8,128)(2,1)S(1)} collective-permute-done((bf16[160,1024]{1,0:T(8,128)(2,1)S(1)}, bf16[160,1024]{1,0:T(8,128)(2,1)S(1)}, u32[]{:S(2)}, u32[]{:S(2)}) %collective-permute-start) | collective-permute-done | bytes 327712 | tf_op jit(solution)/shard_map/ppermute | solution.py:149
  20.8 11.8 %all-to-all-done.refs_0_ = bf16[4,96,1024]{2,1,0:T(8,128)(2,1)S(1)} async-done(((bf16[4,96,1024]{2,1,0:T(8,128)(2,1)}), bf16[4,96,1024]{2,1,0:T(8,128)(2,1)S(1)}, u32[]{:S(2)}, u32[]{:S(2)}) %all-to-all-start) | async-done | bytes 786464 | tf_op jit(solution)/shard_map/all_to_all | solution.py:157
  35.6 4.2 all-to-all-start.1
  45.3 1.9 stack.8
  47.3 3.1 broadcast_in_dim.94
  55.6 6.9 %collective-permute-done.1.refs_1_ = bf16[4,96,1024]{2,1,0:T(8,128)(2,1)} collective-permute-done((bf16[4,96,1024]{2,1,0:T(8,128)(2,1)S(1)}, bf16[4,96,1024]{2,1,0:T(8,128)(2,1)}, u32[]{:S(2)}, u32[]{:S(2)}) %collective-permute-start.1) | collective-permute-done | bytes 786464 | tf_op jit(solution)/shard_map/ppermute | solution.py:149
  62.5 2.5 stack.9
  65.0 5.2 %all-to-all-start.2 = ((bf16[4,2,160,1024]{3,2,1,0:T(8,128)(2,1)}), bf16[4,2,160,1024]{3,2,1,0:T(8,128)(2,1)}, u32[]{:S(2)}, u32[]{:S(2)}) async-start(bf16[4,2,160,1024]{3,2,1,0:T(8,128)(2,1)} %broadcast_in_dim.94), calls=%async_computation.2 | async-start | bytes 5242880 | tf_op jit(solution)/shard_map/all_to_all | solution.py:157
  75.4 18.1 %collective-permute-done.4.refs_1_ = bf16[4,96,1024]{2,1,0:T(8,128)(2,1)} collective-permute-done((bf16[4,96,1024]{2,1,0:T(8,128)(2,1)}, bf16[4,96,1024]{2,1,0:T(8,128)(2,1)}, u32[]{:S(2)}, u32[]{:S(2)}) %collective-permute-start.4) | collective-permute-done | bytes 786464 | tf_op jit(solution)/shard_map/ppermute | solution.py:149
  93.5 5.7 %collective-permute-done.2.refs_1_ = bf16[8,96,1024]{2,1,0:T(8,128)(2,1)S(1)} collective-permute-done((bf16[8,96,1024]{2,1,0:T(8,128)(2,1)S(1)}, bf16[8,96,1024]{2,1,0:T(8,128)(2,1)S(1)}, u32[]{:S(2)}, u32[]{:S(2)}) %collective-permute-start.2) | collective-permute-done | bytes 1572896 | tf_op jit(solution)/shard_map/ppermute | solution.py:149
  100.3 2.5 stack.10
  104.7 2.0 collective-permute-done.7.refs_3_
  106.7 11.4 %front.1 = (bf16[1024,1024]{1,0:T(8,128)(2,1)}, bf16[2048,1024]{1,0:T(8,128)(2,1)}, bf16[512,512]{1,0:T(8,128)(2,1)}, f32[512,1024]{1,0:T(8,128)}, bf16[2048,512...) custom-call(s32[16]{0:T(128)} %get-tuple-element.247.own_ref, ...), custom_call_target="tpu_custom_call" | custom-call | tf_op jit(solution)/shard_map/front/pallas_call | solution.py:450
  120.9 2.8 collective-permute-done.5.refs_1_
  123.7 4.2 all-to-all-done.2
  129.9 4.4 all-to-all-start.3
  134.3 2.6 collective-permute-done.10.refs_3_
  136.9 8.1 %pack.1 = (bf16[3,1024,1024]{2,1,0:T(8,128)(2,1)}, bf16[3,512,1024]{2,1,0:T(8,128)(2,1)}) custom-call(s32[16]{0:T(128)} %get-tuple-element.247.own_ref, s32[16]{0:T(128)} %get-tuple-element.248.other_ref, bf16[8,96,1024]{2,1,0:T(8,128)(2,1)} %bitcast.52, bf16[8,96,1024]{2,1,0:T(8,128)(2,1)} %collective-permute-done.5.refs_1_, ...), custom_call_target="tpu_custom_call" | custom-call | tf_op jit(solution)/shard_map/pack/pallas_call | solution.py:507
  145.0 12.1 %attend.1 = (bf16[512,1024]{1,0:T(8,128)(2,1)}, f32[4,4,512]{2,1,0:T(4,128)}) custom-call(s32[1]{0:T(128)} %copy.121.length_ref, f32[16]{0:T(128)} %multiply_power_fusion.slope_ref, bf16[3,512,1024]{2,1,0:T(8,128)(2,1)} %get-tuple-element.338.packed_ref), custom_call_target="tpu_custom_call" | custom-call | tf_op jit(solution)/shard_map/attend/pallas_call | solution.py:223
  157.1 3.5 all-to-all-done.3.refs_0_
  162.2 3.7 collective-permute-done.12.refs_3_
  165.8 7.8 %mid.1 = (bf16[1024,1024]{1,0:T(8,128)(2,1)}, f32[512,1024]{1,0:T(8,128)}, bf16[512,1024]{1,0:T(8,128)(2,1)}, bf16[1024,512]{1,0:T(8,128)(2,1)}, bf16[1024,512]{1,0:T(8,128)(2,1)}) custom-call(s32[16]{0:T(128)} %get-tuple-element.274.own_ref, s32[16]{0:T(128)} %get-tuple-element.275.other_ref, bf16[8,160,1024]{2,1,0:T(8,128)(2,1)} %bitcast.14.refs_0_, ...), custom_call_target="tpu_custom_call" | custom-call | tf_op jit(solution)/shard_map/mid/pallas_call | solution.py:556
  173.6 2.1 collective-permute-done.11.refs_1_
  175.8 2.9 stack.11
  179.5 17.4 %expand.1 = (bf16[4,1024,1024]{2,1,0:T(8,128)(2,1)}, bf16[512,4096]{1,0:T(8,128)(2,1)}, bf16[4096,512]{1,0:T(8,128)(2,1)}, bf16[512,4096]{1,0:T(8,128)(2,1)}) custom-call(s32[16]{0:T(128)} %get-tuple-element.274.own_ref, s32[16]{0:T(128)} %get-tuple-element.275.other_ref, bf16[8,160,1024]{2,1,0:T(8,128)(2,1)} %bitcast.14.refs_0_, ...), custom_call_target="tpu_custom_call" | custom-call | tf_op jit(solution)/shard_map/expand/pallas_call | solution.py:339
  196.9 8.1 %collective-permute-done.13.refs_1_ = bf16[8,128,1024]{2,1,0:T(8,128)(2,1)} collective-permute-done((bf16[8,128,1024]{2,1,0:T(8,128)(2,1)}, bf16[8,128,1024]{2,1,0:T(8,128)(2,1)}, u32[]{:S(2)}, u32[]{:S(2)}) %collective-permute-start.13) | collective-permute-done | bytes 2097184 | tf_op jit(solution)/shard_map/ppermute | solution.py:149
  205.1 4.5 collective-permute-done.15.refs_3_
  209.7 16.6 %head.1 = (bf16[4096,1024]{1,0:T(8,128)(2,1)}, f32[512,1024]{1,0:T(8,128)}, bf16[512,1024]{1,0:T(8,128)(2,1)}, f32[1024,80]{1,0:T(8,128)}, f32[1,1024]{1,0:T(1,128)}, /*index=5*/f32[1,1]{1,0:T(1,128)}) custom-call(f32[1]{0:T(128)} %bitcast.13.share_ref, s32[16]{0:T(128)} %get-tuple-element.247.own_ref, s32[16]{0:T(128)} %get-tuple-element.248.other_ref, ...), custom_call_target="tpu_custom_call" | custom-call | tf_op jit(solution)/shard_map/head/pallas_call | solution.py:631
  226.9 2.5 collective-permute-done.17.refs_3_
  229.4 10.1 %grads.5 = (bf16[8,128,1024]{2,1,0:T(8,128)(2,1)}, bf16[8,128,1024]{2,1,0:T(8,128)(2,1)}) custom-call(s32[16]{0:T(128)} %get-tuple-element.296.idx_ref, bf16[4096,512]{1,0:T(8,128)(2,1)} %get-tuple-element.298.refs_0_, bf16[4096,512]{1,0:T(8,128)(2,1)} %collective-permute-done.16.refs_1_, bf16[512,1024]{1,0:T(8,128)(2,1)} %get-tuple-element.303.refs_2_.low_ref, ...), custom_call_target="tpu_custom_call" | custom-call | tf_op jit(solution)/shard_map/grads/pallas_call | solution.py:877
  240.3 20.4 %ffn_back.1 = (f32[512,1024]{1,0:T(8,128)}, bf16[512,1024]{1,0:T(8,128)(2,1)}, f32[1,1024]{1,0:T(1,128)}, bf16[512,1024]{1,0:T(8,128)(2,1)}, bf16[512,1024]{1,0:...) custom-call(bf16[512,1024]{1,0:T(8,128)(2,1)} %get-tuple-element.303.refs_2_.low_ref, ...), custom_call_target="tpu_custom_call" | custom-call | tf_op jit(solution)/shard_map/ffn_back/pallas_call | solution.py:700
  262.1 2.0 collective-permute-done.20.refs_3_
  268.7 3.6 fold.8
  273.5 10.1 %grads.6 = (bf16[8,128,1024]{2,1,0:T(8,128)(2,1)}, bf16[8,128,1024]{2,1,0:T(8,128)(2,1)}) custom-call(s32[16]{0:T(128)} %get-tuple-element.296.idx_ref, bf16[1024,512]{1,0:T(8,128)(2,1)} %get-tuple-element.318.refs_0_, bf16[1024,512]{1,0:T(8,128)(2,1)} %collective-permute-done.19.refs_1_, bf16[512,1024]{1,0:T(8,128)(2,1)} %get-tuple-element.320.refs_2_, ...), custom_call_target="tpu_custom_call" | custom-call | tf_op jit(solution)/shard_map/grads/pallas_call | solution.py:877
  283.6 4.2 collective-permute-done.24.refs_1_
  287.8 2.4 fold.9
  291.0 4.2 all-to-all-start.4
  295.2 18.3 %attend_back.1 = (bf16[512,1024]{1,0:T(8,128)(2,1)}, bf16[512,1024]{1,0:T(8,128)(2,1)}, bf16[512,1024]{1,0:T(8,128)(2,1)}) custom-call(s32[1]{0:T(128)} %copy.121.length_ref, f32[16]{0:T(128)} %multiply_power_fusion.slope_ref, bf16[3,512,1024]{2,1,0:T(8,128)(2,1)} %get-tuple-element.338.packed_ref, bf16[512,1024]{1,0:T(8,128)(2,1)} %get-tuple-element.357.d_out_ref.refs_4_, ...), custom_call_target="tpu_custom_call" | custom-call | tf_op jit(solution)/shard_map/attend_back/pallas_call | solution.py:274
  314.1 9.7 %pack_back.1 = (bf16[512,1024]{1,0:T(8,128)(2,1)}, f32[1,1024]{1,0:T(1,128)}) custom-call(bf16[512,1024]{1,0:T(8,128)(2,1)} %get-tuple-element.359.refs_0_.refs_6_, bf16[512,1024]{1,0:T(8,128)(2,1)} %get-tuple-element.361.refs_1_.refs_8_, bf16[512,1024]{1,0:T(8,128)(2,1)} %get-tuple-element.363.refs_2_.refs_10_, ...), custom_call_target="tpu_custom_call" | custom-call | tf_op jit(solution)/shard_map/pack_back/pallas_call | solution.py:747
  323.8 3.5 fold.10
  329.1 10.1 %grads.7 = (bf16[8,128,1024]{2,1,0:T(8,128)(2,1)}, bf16[8,128,1024]{2,1,0:T(8,128)(2,1)}) custom-call(s32[16]{0:T(128)} %get-tuple-element.296.idx_ref, bf16[1024,512]{1,0:T(8,128)(2,1)} %get-tuple-element.353.refs_0_, bf16[1024,512]{1,0:T(8,128)(2,1)} %collective-permute-done.25.refs_1_, bf16[1024,512]{1,0:T(8,128)(2,1)} %get-tuple-element.355.refs_2_, ...), custom_call_target="tpu_custom_call" | custom-call | tf_op jit(solution)/shard_map/grads/pallas_call | solution.py:877
  339.2 3.7 collective-permute-done.32.refs_1_
  342.9 2.7 fold.11
  346.9 7.1 %tail.1 = (bf16[1024,768]{1,0:T(8,128)(2,1)}, bf16[512,128]{1,0:T(8,128)(2,1)}, bf16[1024,128]{1,0:T(8,128)(2,1)}) custom-call(bf16[512,1024]{1,0:T(8,128)(2,1)} %get-tuple-element.390.d_ref.refs_2_, bf16[2048,1024]{1,0:T(8,128)(2,1)} %get-tuple-element.378.skip_ref, bf16[1024,1024]{1,0:T(8,128)(2,1)} %get-tuple-element.379.small_ref, ...), custom_call_target="tpu_custom_call" | custom-call | tf_op jit(solution)/shard_map/tail/pallas_call | solution.py:792
  354.0 2.7 grads.8
  356.8 5.0 %all-to-all-start.5 = ((bf16[4,128,1024]{2,1,0:T(8,128)(2,1)}), bf16[4,128,1024]{2,1,0:T(8,128)(2,1)}, u32[]{:S(2)}, u32[]{:S(2)}) async-start(bf16[4,128,1024]{2,1,0:T(8,128)(2,1)} %fold.11), calls=%async_computation.5 | async-start | bytes 2097152 | tf_op jit(solution)/shard_map/all_to_all | solution.py:157
  361.8 7.8 %grads.9 = (bf16[8,96,1024]{2,1,0:T(8,128)(2,1)}, bf16[8,96,1024]{2,1,0:T(8,128)(2,1)}) custom-call(s32[16]{0:T(128)} %get-tuple-element.296.idx_ref, bf16[2048,512]{1,0:T(8,128)(2,1)} %get-tuple-element.388.refs_0_, bf16[2048,512]{1,0:T(8,128)(2,1)} %collective-permute-done.33.refs_1_, bf16[512,1024]{1,0:T(8,128)(2,1)} %get-tuple-element.390.d_ref.refs_2_, ...), custom_call_target="tpu_custom_call" | custom-call | tf_op jit(solution)/shard_map/grads/pallas_call | solution.py:877
  369.6 2.3 collective-permute-done.35.refs_1_.refs_3_
  372.0 3.4 fold.12
  377.5 10.8 %all-to-all-done.5 = bf16[4,128,1024]{2,1,0:T(8,128)(2,1)} async-done(((bf16[4,128,1024]{2,1,0:T(8,128)(2,1)}), bf16[4,128,1024]{2,1,0:T(8,128)(2,1)}, u32[]{:S(2)}, u32[]{:S(2)}) %all-to-all-start.5) | async-done | bytes 1048608 | tf_op jit(solution)/shard_map/all_to_all | solution.py:157
  388.3 13.5 %collective-permute-done.38.refs_1_ = bf16[4,128,1024]{2,1,0:T(8,128)(2,1)} collective-permute-done((bf16[4,128,1024]{2,1,0:T(8,128)(2,1)}, bf16[4,128,1024]{2,1,0:T(8,128)(2,1)}, u32[]{:S(2)}, u32[]{:S(2)}) %collective-permute-start.38) | collective-permute-done | bytes 1048608 | tf_op jit(solution)/shard_map/ppermute | solution.py:149
  401.8 2.4 fold.13
  404.2 5.0 %all-to-all-start.6 = ((bf16[4,128,1024]{2,1,0:T(8,128)(2,1)}), bf16[4,128,1024]{2,1,0:T(8,128)(2,1)}, u32[]{:S(2)}, u32[]{:S(2)}) async-start(bf16[4,128,1024]{2,1,0:T(8,128)(2,1)} %fold.13), calls=%async_computation.6 | async-start | bytes 2097152 | tf_op jit(solution)/shard_map/all_to_all | solution.py:157
  409.2 3.0 fold.14
  413.6 10.9 %collective-permute-done.39.refs_1_ = bf16[4,96,1024]{2,1,0:T(8,128)(2,1)} collective-permute-done((bf16[4,96,1024]{2,1,0:T(8,128)(2,1)}, bf16[4,96,1024]{2,1,0:T(8,128)(2,1)}, u32[]{:S(2)}, u32[]{:S(2)}) %collective-permute-start.39) | collective-permute-done | bytes 786464 | tf_op jit(solution)/shard_map/ppermute | solution.py:149
  424.5 4.9 %all-to-all-done.6 = bf16[4,128,1024]{2,1,0:T(8,128)(2,1)} async-done(((bf16[4,128,1024]{2,1,0:T(8,128)(2,1)}), bf16[4,128,1024]{2,1,0:T(8,128)(2,1)}, u32[]{:S(2)}, u32[]{:S(2)}) %all-to-all-start.6) | async-done | bytes 1048608 | tf_op jit(solution)/shard_map/all_to_all | solution.py:157
  429.4 2.2 fold.15
  431.7 3.5 all-to-all-start.7
  444.0 7.6 %all-to-all-done.7 = bf16[4,96,1024]{2,1,0:T(8,128)(2,1)S(1)} async-done(((bf16[4,96,1024]{2,1,0:T(8,128)(2,1)}), bf16[4,96,1024]{2,1,0:T(8,128)(2,1)S(1)}, u32[]{:S(2)}, u32[]{:S(2)}) %all-to-all-start.7) | async-done | bytes 786464 | tf_op jit(solution)/shard_map/all_to_all | solution.py:157
  455.9 10.4 %all_to_all.46 = f32[32,1,17]{2,1,0:T(1,128)S(1)} all-to-all(f32[32,1,17]{2,1,0:T(1,128)S(1)} %broadcast_in_dim.108), channel_id=1, replica_groups=mesh['wide'=8,'narrow'=4] {'wide','narrow'}, dimensions={0} | all-to-all | bytes 4352 | tf_op jit(solution)/shard_map/all_to_all | solution.py:169
  468.9 7.3 %adam.1 = (f32[32,672]{1,0:T(8,128)}, f32[16,128]{1,0:T(8,128)}, f32[64,1024]{1,0:T(8,128)}, f32[32,3072]{1,0:T(8,128)}, f32[32,1024]{1,0:T(8,128)}, /*index=5*/...) custom-call(f32[1]{0:T(128)} %bitcast.19.clip_ref, ...), custom_call_target="tpu_custom_call" | custom-call | tf_op jit(solution)/shard_map/adam/pallas_call | solution.py:986
  (186 shorter events, 58.7 us)
Async XLA Ops:
  6.0 7.5 %copy-start.13 = (f32[32,1024]{1,0:T(8,128)S(1)}, f32[32,1024]{1,0:T(8,128)}, u32[]{:S(2)}) copy-start(f32[32,1024]{1,0:T(8,128)} %refs_8_.1) | copy-start | bytes 393220
  6.0 9.2 %copy-start.9 = (f32[32,3072]{1,0:T(8,128)S(1)}, f32[32,3072]{1,0:T(8,128)}, u32[]{:S(2)}) copy-start(f32[32,3072]{1,0:T(8,128)} %refs_7_.1) | copy-start | bytes 1179652
  6.0 9.3 %copy-start.8 = (f32[128,1024]{1,0:T(8,128)S(1)}, f32[128,1024]{1,0:T(8,128)}, u32[]{:S(2)}) copy-start(f32[128,1024]{1,0:T(8,128)} %refs_10_.1) | copy-start | bytes 1572868
  6.0 26.6 %all-to-all-start = ((bf16[4,96,1024]{2,1,0:T(8,128)(2,1)}), bf16[4,96,1024]{2,1,0:T(8,128)(2,1)S(1)}, u32[]{:S(2)}, u32[]{:S(2)}) async-start(bf16[4,96,1024]{2,1,0:T(8,128)(2,1)} %prepare.1), calls=%async_computation | async-start | bytes 1572864 | tf_op jit(solution)/shard_map/all_to_all | solution.py:157
  13.6 21.9 %copy-start.14 = (bf16[160,1024]{1,0:T(8,128)(2,1)}, bf16[160,1024]{1,0:T(8,128)(2,1)S(1)}, u32[]{:S(2)}) copy-start(bf16[160,1024]{1,0:T(8,128)(2,1)S(1)} %slice_dynamic-update-slice_fusion.refs_0_) | copy-start | bytes 983044
  13.6 7.1 %collective-permute-start = (bf16[160,1024]{1,0:T(8,128)(2,1)S(1)}, bf16[160,1024]{1,0:T(8,128)(2,1)S(1)}, u32[]{:S(2)}, u32[]{:S(2)}) collective-permute-start(bf16[160,1024]{1,0:T(8,128)(2,1)S(1)} %slice_dynamic-update-slice_fusion.refs_0_), channel_id=1, source_target_pairs={{0,4},{1,3},{2,6},{3,1},{4,0},{5,7},{6,2},{7,5},{8,12},{9,11},{10,... | collective-permute-start | bytes 983048 | tf_op jit(solution)/shard_map/ppermute | solution.py:149
  15.9 25.1 %copy-start.16 = (f32[512,80]{0,1:T(8,128)S(1)}, f32[512,80]{0,1:T(8,128)}, u32[]{:S(2)}) copy-start(f32[512,80]{0,1:T(8,128)} %param.37) | copy-start | bytes 491524
  16.0 25.9 %copy-start.17 = (f32[512,80]{0,1:T(8,128)S(1)}, f32[512,80]{0,1:T(8,128)}, u32[]{:S(2)}) copy-start(f32[512,80]{0,1:T(8,128)} %param.36) | copy-start | bytes 491524
  20.8 23.2 %copy-start.15 = (bf16[160,1024]{1,0:T(8,128)(2,1)}, bf16[160,1024]{1,0:T(8,128)(2,1)S(1)}, u32[]{:S(2)}) copy-start(bf16[160,1024]{1,0:T(8,128)(2,1)S(1)} %collective-permute-done.refs_1_) | copy-start | bytes 983044
  34.5 8.2 %copy-start.4 = (bf16[512,1024]{1,0:T(8,128)(2,1)S(1)}, bf16[512,1024]{1,0:T(8,128)(2,1)}, u32[]{:S(2)}) copy-start(bf16[512,1024]{1,0:T(8,128)(2,1)} %refs_4_.1) | copy-start | bytes 3145732
  35.6 26.9 %all-to-all-start.1 = ((bf16[4,96,1024]{2,1,0:T(8,128)(2,1)}), bf16[4,96,1024]{2,1,0:T(8,128)(2,1)}, u32[]{:S(2)}, u32[]{:S(2)}) async-start(bf16[4,96,1024]{2,1,0:T(8,128)(2,1)} %broadcast_in_dim.92), calls=%async_computation.1 | async-start | bytes 1572864 | tf_op jit(solution)/shard_map/all_to_all | solution.py:157
  47.2 5.2 %copy-start.11 = (f32[512,80]{1,0:T(8,128)S(1)}, f32[512,80]{1,0:T(8,128)}, u32[]{:S(2)}) copy-start(f32[512,80]{1,0:T(8,128)} %copy.102) | copy-start | bytes 491524
  47.2 5.2 %copy-start.12 = (f32[512,80]{1,0:T(8,128)S(1)}, f32[512,80]{1,0:T(8,128)}, u32[]{:S(2)}) copy-start(f32[512,80]{1,0:T(8,128)} %copy.103) | copy-start | bytes 491524
  47.2 7.6 %copy-start.21 = (s32[512]{0:T(512)S(1)}, s32[512]{0:T(512)}, u32[]{:S(2)}) copy-start(s32[512]{0:T(512)} %param.39) | copy-start | bytes 6148
  50.4 12.1 %collective-permute-start.1 = (bf16[4,96,1024]{2,1,0:T(8,128)(2,1)S(1)}, bf16[4,96,1024]{2,1,0:T(8,128)(2,1)}, u32[]{:S(2)}, u32[]{:S(2)}) collective-permute-start(bf16[4,96,1024]{2,1,0:T(8,128)(2,1)S(1)} %copy-done.7), channel_id=1, source_target_pairs={{0,4},{1,3},{2,6},{3,1},{4,0},{5,7},{6,2},{7,5},{8,12},{9,11},{10,... | collective-permute-start | bytes 2359304 | tf_op jit(solution)/shard_map/ppermute | solution.py:149
  65.0 5.3 %copy-start = (bf16[2,4,96,1024]{3,2,1,0:T(8,128)(2,1)S(1)}, bf16[2,4,96,1024]{3,2,1,0:T(8,128)(2,1)}, u32[]{:S(2)}) copy-start(bf16[2,4,96,1024]{3,2,1,0:T(8,128)(2,1)} %stack.9) | copy-start | bytes 4718596
  65.0 6.8 %copy-start.18 = (s32[2,4,2]{2,1,0:T(4,128)S(1)}, s32[2,4,2]{2,1,0:T(4,128)}, u32[]{:S(2)}) copy-start(s32[2,4,2]{2,1,0:T(4,128)} %fusion.7) | copy-start | bytes 196
  65.0 6.9 %copy-start.19 = (s32[2,4,2]{2,1,0:T(4,128)S(1)}, s32[2,4,2]{2,1,0:T(4,128)}, u32[]{:S(2)}) copy-start(s32[2,4,2]{2,1,0:T(4,128)} %fusion.8) | copy-start | bytes 196
  65.0 62.9 %all-to-all-start.2 = ((bf16[4,2,160,1024]{3,2,1,0:T(8,128)(2,1)}), bf16[4,2,160,1024]{3,2,1,0:T(8,128)(2,1)}, u32[]{:S(2)}, u32[]{:S(2)}) async-start(bf16[4,2,160,1024]{3,2,1,0:T(8,128)(2,1)} %broadcast_in_dim.94), calls=%async_computation.2 | async-start | bytes 5242880 | tf_op jit(solution)/shard_map/all_to_all | solution.py:157
  70.3 28.8 %collective-permute-start.2 = (bf16[8,96,1024]{2,1,0:T(8,128)(2,1)S(1)}, bf16[8,96,1024]{2,1,0:T(8,128)(2,1)S(1)}, u32[]{:S(2)}, u32[]{:S(2)}) collective-permute-start(bf16[8,96,1024]{2,1,0:T(8,128)(2,1)S(1)} %bitcast.48), channel_id=1, source_target_pairs={{0,2},{1,5},{2,0},{3,7},{4,6},{5,1},{6,4},{7,3},{8,10},{9,13},{10,... | collective-permute-start | bytes 4718600 | tf_op jit(solution)/shard_map/ppermute | solution.py:149
  71.8 27.4 %collective-permute-start.3 = (bf16[8,96,1024]{2,1,0:T(8,128)(2,1)S(1)}, bf16[8,96,1024]{2,1,0:T(8,128)(2,1)}, u32[]{:S(2)}, u32[]{:S(2)}) collective-permute-start(bf16[8,96,1024]{2,1,0:T(8,128)(2,1)S(1)} %bitcast.49), channel_id=1, source_target_pairs={{0,1},{1,0},{2,3},{3,2},{4,5},{5,4},{6,7},{7,6},{8,9},{9,8},{10,11... | collective-permute-start | bytes 4718600 | tf_op jit(solution)/shard_map/ppermute | solution.py:149
  72.6 20.8 %collective-permute-start.4 = (bf16[4,96,1024]{2,1,0:T(8,128)(2,1)}, bf16[4,96,1024]{2,1,0:T(8,128)(2,1)}, u32[]{:S(2)}, u32[]{:S(2)}) collective-permute-start(bf16[4,96,1024]{2,1,0:T(8,128)(2,1)} %all-to-all-done.1.refs_0_), channel_id=1, source_target_pairs={{0,4},{1,3},{2,6},{3,1},{4,0},{5,7},{6,2},{7,5},{8,12},{9,11},{10,... | collective-permute-start | bytes 2359304 | tf_op jit(solution)/shard_map/ppermute | solution.py:149
  102.9 3.8 collective-permute-start.7
  102.9 20.8 %collective-permute-start.5 = (bf16[8,96,1024]{2,1,0:T(8,128)(2,1)}, bf16[8,96,1024]{2,1,0:T(8,128)(2,1)}, u32[]{:S(2)}, u32[]{:S(2)}) collective-permute-start(bf16[8,96,1024]{2,1,0:T(8,128)(2,1)} %bitcast.50), channel_id=1, source_target_pairs={{0,2},{1,5},{2,0},{3,7},{4,6},{5,1},{6,4},{7,3},{8,10},{9,13},{10,... | collective-permute-start | bytes 4718600 | tf_op jit(solution)/shard_map/ppermute | solution.py:149
  104.5 19.2 %collective-permute-start.6 = (bf16[8,96,1024]{2,1,0:T(8,128)(2,1)}, bf16[8,96,1024]{2,1,0:T(8,128)(2,1)}, u32[]{:S(2)}, u32[]{:S(2)}) collective-permute-start(bf16[8,96,1024]{2,1,0:T(8,128)(2,1)} %bitcast.51), channel_id=1, source_target_pairs={{0,1},{1,0},{2,3},{3,2},{4,5},{5,4},{6,7},{7,6},{8,9},{9,8},{10,11... | collective-permute-start | bytes 4718600 | tf_op jit(solution)/shard_map/ppermute | solution.py:149
  127.9 32.7 %collective-permute-start.8 = (bf16[8,160,1024]{2,1,0:T(8,128)(2,1)}, bf16[8,160,1024]{2,1,0:T(8,128)(2,1)}, u32[]{:S(2)}, u32[]{:S(2)}) collective-permute-start(bf16[8,160,1024]{2,1,0:T(8,128)(2,1)} %bitcast.14.refs_0_), channel_id=1, source_target_pairs={{0,2},{1,5},{2,0},{3,7},{4,6},{5,1},{6,4},{7,3},{8,10},{9,13},{10,... | collective-permute-start | bytes 7864328 | tf_op jit(solution)/shard_map/ppermute | solution.py:149
  129.4 31.2 %collective-permute-start.9 = (bf16[8,160,1024]{2,1,0:T(8,128)(2,1)}, bf16[8,160,1024]{2,1,0:T(8,128)(2,1)}, u32[]{:S(2)}, u32[]{:S(2)}) collective-permute-start(bf16[8,160,1024]{2,1,0:T(8,128)(2,1)} %bitcast.14.refs_0_), channel_id=1, source_target_pairs={{0,1},{1,0},{2,3},{3,2},{4,5},{5,4},{6,7},{7,6},{8,9},{9,8},{10,11... | collective-permute-start | bytes 7864328 | tf_op jit(solution)/shard_map/ppermute | solution.py:149
  129.4 7.5 %collective-permute-start.10 = (bf16[8,96,1024]{2,1,0:T(8,128)(2,1)}, bf16[8,96,1024]{2,1,0:T(8,128)(2,1)}, u32[]{:S(2)}, u32[]{:S(2)}) collective-permute-start(bf16[8,96,1024]{2,1,0:T(8,128)(2,1)} %collective-permute-done.5.refs_1_), channel_id=1, source_target_pairs={{0,1},{1,0},{2,3},{3,2},{4,5},{5,4},{6,7},{7,6},{8,9},{9,8},{10,11... | collective-permute-start | bytes 4718600 | tf_op jit(solution)/shard_map/ppermute | solution.py:149
  129.9 30.7 %all-to-all-start.3 = ((bf16[4,128,1024]{2,1,0:T(8,128)(2,1)}), bf16[4,128,1024]{2,1,0:T(8,128)(2,1)}, u32[]{:S(2)}, u32[]{:S(2)}) async-start(bf16[4,128,1024]{2,1,0:T(8,128)(2,1)} %broadcast_in_dim.93), calls=%async_computation.3 | async-start | bytes 2097152 | tf_op jit(solution)/shard_map/all_to_all | solution.py:157
  160.6 5.3 %collective-permute-start.12 = (bf16[8,160,1024]{2,1,0:T(8,128)(2,1)}, bf16[8,160,1024]{2,1,0:T(8,128)(2,1)}, u32[]{:S(2)}, u32[]{:S(2)}) collective-permute-start(bf16[8,160,1024]{2,1,0:T(8,128)(2,1)} %collective-permute-done.8.refs_1_), channel_id=1, source_target_pairs={{0,1},{1,0},{2,3},{3,2},{4,5},{5,4},{6,7},{7,6},{8,9},{9,8},{10,11... | collective-permute-start | bytes 7864328 | tf_op jit(solution)/shard_map/ppermute | solution.py:149
  160.6 15.2 %collective-permute-start.11 = (bf16[4,128,1024]{2,1,0:T(8,128)(2,1)}, bf16[4,128,1024]{2,1,0:T(8,128)(2,1)}, u32[]{:S(2)}, u32[]{:S(2)}) collective-permute-start(bf16[4,128,1024]{2,1,0:T(8,128)(2,1)} %all-to-all-done.3.refs_0_), channel_id=1, source_target_pairs={{0,4},{1,3},{2,6},{3,1},{4,0},{5,7},{6,2},{7,5},{8,12},{9,11},{10,... | collective-permute-start | bytes 3145736 | tf_op jit(solution)/shard_map/ppermute | solution.py:149
  178.6 26.4 %collective-permute-start.13 = (bf16[8,128,1024]{2,1,0:T(8,128)(2,1)}, bf16[8,128,1024]{2,1,0:T(8,128)(2,1)}, u32[]{:S(2)}, u32[]{:S(2)}) collective-permute-start(bf16[8,128,1024]{2,1,0:T(8,128)(2,1)} %bitcast.44), channel_id=1, source_target_pairs={{0,2},{1,5},{2,0},{3,7},{4,6},{5,1},{6,4},{7,3},{8,10},{9,13},{10,... | collective-permute-start | bytes 6291464 | tf_op jit(solution)/shard_map/ppermute | solution.py:149
  179.4 25.6 %collective-permute-start.14 = (bf16[8,128,1024]{2,1,0:T(8,128)(2,1)}, bf16[8,128,1024]{2,1,0:T(8,128)(2,1)}, u32[]{:S(2)}, u32[]{:S(2)}) collective-permute-start(bf16[8,128,1024]{2,1,0:T(8,128)(2,1)} %bitcast.45), channel_id=1, source_target_pairs={{0,1},{1,0},{2,3},{3,2},{4,5},{5,4},{6,7},{7,6},{8,9},{9,8},{10,11... | collective-permute-start | bytes 6291464 | tf_op jit(solution)/shard_map/ppermute | solution.py:149
  205.0 4.5 collective-permute-start.15
  209.6 19.9 %collective-permute-start.16 = (bf16[4096,512]{1,0:T(8,128)(2,1)}, bf16[4096,512]{1,0:T(8,128)(2,1)}, u32[]{:S(2)}, u32[]{:S(2)}) collective-permute-start(bf16[4096,512]{1,0:T(8,128)(2,1)} %get-tuple-element.298.refs_0_), channel_id=1, source_target_pairs={{0,1},{1,0},{2,3},{3,2},{4,5},{5,4},{6,7},{7,6},{8,9},{9,8},{10,11... | collective-permute-start | bytes 12582920 | tf_op jit(solution)/shard_map/ppermute | solution.py:149
  226.3 3.1 collective-permute-start.17
  226.8 35.3 %collective-permute-start.19 = (bf16[1024,512]{1,0:T(8,128)(2,1)}, bf16[1024,512]{1,0:T(8,128)(2,1)}, u32[]{:S(2)}, u32[]{:S(2)}) collective-permute-start(bf16[1024,512]{1,0:T(8,128)(2,1)} %get-tuple-element.318.refs_0_), channel_id=1, source_target_pairs={{0,1},{1,0},{2,3},{3,2},{4,5},{5,4},{6,7},{7,6},{8,9},{9,8},{10,11... | collective-permute-start | bytes 3145736 | tf_op jit(solution)/shard_map/ppermute | solution.py:149
  239.5 29.2 %collective-permute-start.18 = (bf16[8,128,1024]{2,1,0:T(8,128)(2,1)}, bf16[8,128,1024]{2,1,0:T(8,128)(2,1)}, u32[]{:S(2)}, u32[]{:S(2)}) collective-permute-start(bf16[8,128,1024]{2,1,0:T(8,128)(2,1)} %get-tuple-element.301), channel_id=1, source_target_pairs={{0,2},{1,5},{2,0},{3,7},{4,6},{5,1},{6,4},{7,3},{8,10},{9,13},{10,... | collective-permute-start | bytes 6291464 | tf_op jit(solution)/shard_map/ppermute | solution.py:149
  260.6 3.5 collective-permute-start.20
  261.5 4.1 collective-permute-start.21
  261.6 5.6 %collective-permute-start.22 = (bf16[512,1024]{1,0:T(8,128)(2,1)}, bf16[512,1024]{1,0:T(8,128)(2,1)}, u32[]{:S(2)}, u32[]{:S(2)}) collective-permute-start(bf16[512,1024]{1,0:T(8,128)(2,1)} %get-tuple-element.324.refs_6_), channel_id=1, source_target_pairs={{0,1},{1,0},{2,3},{3,2},{4,5},{5,4},{6,7},{7,6},{8,9},{9,8},{10,11... | collective-permute-start | bytes 3145736 | tf_op jit(solution)/shard_map/ppermute | solution.py:149
  262.1 6.6 %collective-permute-start.23 = (bf16[512,1024]{1,0:T(8,128)(2,1)}, bf16[512,1024]{1,0:T(8,128)(2,1)}, u32[]{:S(2)}, u32[]{:S(2)}) collective-permute-start(bf16[512,1024]{1,0:T(8,128)(2,1)} %get-tuple-element.326.refs_8_), channel_id=1, source_target_pairs={{0,1},{1,0},{2,3},{3,2},{4,5},{5,4},{6,7},{7,6},{8,9},{9,8},{10,11... | collective-permute-start | bytes 3145736 | tf_op jit(solution)/shard_map/ppermute | solution.py:149
  264.2 19.4 %collective-permute-start.26 = (bf16[1024,512]{1,0:T(8,128)(2,1)}, bf16[1024,512]{1,0:T(8,128)(2,1)}, u32[]{:S(2)}, u32[]{:S(2)}) collective-permute-start(bf16[1024,512]{1,0:T(8,128)(2,1)} %get-tuple-element.355.refs_2_), channel_id=1, source_target_pairs={{0,1},{1,0},{2,3},{3,2},{4,5},{5,4},{6,7},{7,6},{8,9},{9,8},{10,11... | collective-permute-start | bytes 3145736 | tf_op jit(solution)/shard_map/ppermute | solution.py:149
  272.2 11.3 %collective-permute-start.25 = (bf16[1024,512]{1,0:T(8,128)(2,1)}, bf16[1024,512]{1,0:T(8,128)(2,1)}, u32[]{:S(2)}, u32[]{:S(2)}) collective-permute-start(bf16[1024,512]{1,0:T(8,128)(2,1)} %get-tuple-element.353.refs_0_), channel_id=1, source_target_pairs={{0,1},{1,0},{2,3},{3,2},{4,5},{5,4},{6,7},{7,6},{8,9},{9,8},{10,11... | collective-permute-start | bytes 3145736 | tf_op jit(solution)/shard_map/ppermute | solution.py:149
  272.7 15.1 %collective-permute-start.24 = (bf16[4,128,1024]{2,1,0:T(8,128)(2,1)}, bf16[4,128,1024]{2,1,0:T(8,128)(2,1)}, u32[]{:S(2)}, u32[]{:S(2)}) collective-permute-start(bf16[4,128,1024]{2,1,0:T(8,128)(2,1)} %get-tuple-element.315), channel_id=1, source_target_pairs={{0,4},{1,3},{2,6},{3,1},{4,0},{5,7},{6,2},{7,5},{8,12},{9,11},{10,... | collective-permute-start | bytes 3145736 | tf_op jit(solution)/shard_map/ppermute | solution.py:149
  273.5 14.4 %collective-permute-start.27 = (bf16[512,1024]{1,0:T(8,128)(2,1)}, bf16[512,1024]{1,0:T(8,128)(2,1)}, u32[]{:S(2)}, u32[]{:S(2)}) collective-permute-start(bf16[512,1024]{1,0:T(8,128)(2,1)} %get-tuple-element.357.d_out_ref.refs_4_), channel_id=1, source_target_pairs={{0,1},{1,0},{2,3},{3,2},{4,5},{5,4},{6,7},{7,6},{8,9},{9,8},{10,11... | collective-permute-start | bytes 3145736 | tf_op jit(solution)/shard_map/ppermute | solution.py:149
  290.2 33.5 %collective-permute-start.28 = (bf16[8,128,1024]{2,1,0:T(8,128)(2,1)}, bf16[8,128,1024]{2,1,0:T(8,128)(2,1)}, u32[]{:S(2)}, u32[]{:S(2)}) collective-permute-start(bf16[8,128,1024]{2,1,0:T(8,128)(2,1)} %get-tuple-element.337), channel_id=1, source_target_pairs={{0,2},{1,5},{2,0},{3,7},{4,6},{5,1},{6,4},{7,3},{8,10},{9,13},{10,... | collective-permute-start | bytes 6291464 | tf_op jit(solution)/shard_map/ppermute | solution.py:149
  291.0 32.8 %all-to-all-start.4 = ((bf16[4,128,1024]{2,1,0:T(8,128)(2,1)}), bf16[4,128,1024]{2,1,0:T(8,128)(2,1)}, u32[]{:S(2)}, u32[]{:S(2)}) async-start(bf16[4,128,1024]{2,1,0:T(8,128)(2,1)} %fold.9), calls=%async_computation.4 | async-start | bytes 2097152 | tf_op jit(solution)/shard_map/all_to_all | solution.py:157
  313.5 10.2 %collective-permute-start.29 = (bf16[512,1024]{1,0:T(8,128)(2,1)}, bf16[512,1024]{1,0:T(8,128)(2,1)}, u32[]{:S(2)}, u32[]{:S(2)}) collective-permute-start(bf16[512,1024]{1,0:T(8,128)(2,1)} %get-tuple-element.359.refs_0_.refs_6_), channel_id=1, source_target_pairs={{0,1},{1,0},{2,3},{3,2},{4,5},{5,4},{6,7},{7,6},{8,9},{9,8},{10,11... | collective-permute-start | bytes 3145736 | tf_op jit(solution)/shard_map/ppermute | solution.py:149
  313.5 10.2 %collective-permute-start.30 = (bf16[512,1024]{1,0:T(8,128)(2,1)}, bf16[512,1024]{1,0:T(8,128)(2,1)}, u32[]{:S(2)}, u32[]{:S(2)}) collective-permute-start(bf16[512,1024]{1,0:T(8,128)(2,1)} %get-tuple-element.361.refs_1_.refs_8_), channel_id=1, source_target_pairs={{0,1},{1,0},{2,3},{3,2},{4,5},{5,4},{6,7},{7,6},{8,9},{9,8},{10,11... | collective-permute-start | bytes 3145736 | tf_op jit(solution)/shard_map/ppermute | solution.py:149
  314.0 9.7 %collective-permute-start.31 = (bf16[512,1024]{1,0:T(8,128)(2,1)}, bf16[512,1024]{1,0:T(8,128)(2,1)}, u32[]{:S(2)}, u32[]{:S(2)}) collective-permute-start(bf16[512,1024]{1,0:T(8,128)(2,1)} %get-tuple-element.363.refs_2_.refs_10_), channel_id=1, source_target_pairs={{0,1},{1,0},{2,3},{3,2},{4,5},{5,4},{6,7},{7,6},{8,9},{9,8},{10,11... | collective-permute-start | bytes 3145736 | tf_op jit(solution)/shard_map/ppermute | solution.py:149
  327.3 15.6 %collective-permute-start.33 = (bf16[2048,512]{1,0:T(8,128)(2,1)}, bf16[2048,512]{1,0:T(8,128)(2,1)}, u32[]{:S(2)}, u32[]{:S(2)}) collective-permute-start(bf16[2048,512]{1,0:T(8,128)(2,1)} %get-tuple-element.388.refs_0_), channel_id=1, source_target_pairs={{0,1},{1,0},{2,3},{3,2},{4,5},{5,4},{6,7},{7,6},{8,9},{9,8},{10,11... | collective-permute-start | bytes 6291464 | tf_op jit(solution)/shard_map/ppermute | solution.py:149
  327.7 11.5 %collective-permute-start.34 = (bf16[512,1024]{1,0:T(8,128)(2,1)}, bf16[512,1024]{1,0:T(8,128)(2,1)}, u32[]{:S(2)}, u32[]{:S(2)}) collective-permute-start(bf16[512,1024]{1,0:T(8,128)(2,1)} %get-tuple-element.390.d_ref.refs_2_), channel_id=1, source_target_pairs={{0,1},{1,0},{2,3},{3,2},{4,5},{5,4},{6,7},{7,6},{8,9},{9,8},{10,11... | collective-permute-start | bytes 3145736 | tf_op jit(solution)/shard_map/ppermute | solution.py:149
  327.8 15.1 %collective-permute-start.32 = (bf16[4,128,1024]{2,1,0:T(8,128)(2,1)}, bf16[4,128,1024]{2,1,0:T(8,128)(2,1)}, u32[]{:S(2)}, u32[]{:S(2)}) collective-permute-start(bf16[4,128,1024]{2,1,0:T(8,128)(2,1)} %get-tuple-element.350), channel_id=1, source_target_pairs={{0,4},{1,3},{2,6},{3,1},{4,0},{5,7},{6,2},{7,5},{8,12},{9,11},{10,... | collective-permute-start | bytes 3145736 | tf_op jit(solution)/shard_map/ppermute | solution.py:149
  345.6 26.4 %collective-permute-start.35 = (bf16[8,128,1024]{2,1,0:T(8,128)(2,1)}, bf16[8,128,1024]{2,1,0:T(8,128)(2,1)}, u32[]{:S(2)}, u32[]{:S(2)}) collective-permute-start(bf16[8,128,1024]{2,1,0:T(8,128)(2,1)} %get-tuple-element.373), channel_id=1, source_target_pairs={{0,2},{1,5},{2,0},{3,7},{4,6},{5,1},{6,4},{7,3},{8,10},{9,13},{10,... | collective-permute-start | bytes 6291464 | tf_op jit(solution)/shard_map/ppermute | solution.py:149
  356.7 5.1 %collective-permute-start.36 = (bf16[16,32,1024]{2,1,0:T(8,128)(2,1)}, bf16[16,32,1024]{2,1,0:T(8,128)(2,1)}, u32[]{:S(2)}, u32[]{:S(2)}) collective-permute-start(bf16[16,32,1024]{2,1,0:T(8,128)(2,1)} %grads.8), channel_id=1, source_target_pairs={{0,1},{1,0},{2,3},{3,2},{4,5},{5,4},{6,7},{7,6},{8,9},{9,8},{10,11... | collective-permute-start | bytes 3145736 | tf_op jit(solution)/shard_map/ppermute | solution.py:149
  356.8 31.5 %all-to-all-start.5 = ((bf16[4,128,1024]{2,1,0:T(8,128)(2,1)}), bf16[4,128,1024]{2,1,0:T(8,128)(2,1)}, u32[]{:S(2)}, u32[]{:S(2)}) async-start(bf16[4,128,1024]{2,1,0:T(8,128)(2,1)} %fold.11), calls=%async_computation.5 | async-start | bytes 2097152 | tf_op jit(solution)/shard_map/all_to_all | solution.py:157
  375.4 26.4 %collective-permute-start.38 = (bf16[4,128,1024]{2,1,0:T(8,128)(2,1)}, bf16[4,128,1024]{2,1,0:T(8,128)(2,1)}, u32[]{:S(2)}, u32[]{:S(2)}) collective-permute-start(bf16[4,128,1024]{2,1,0:T(8,128)(2,1)} %get-tuple-element.400), channel_id=1, source_target_pairs={{0,4},{1,3},{2,6},{3,1},{4,0},{5,7},{6,2},{7,5},{8,12},{9,11},{10,... | collective-permute-start | bytes 3145736 | tf_op jit(solution)/shard_map/ppermute | solution.py:149
  376.7 32.5 %collective-permute-start.37 = (bf16[8,96,1024]{2,1,0:T(8,128)(2,1)}, bf16[8,96,1024]{2,1,0:T(8,128)(2,1)}, u32[]{:S(2)}, u32[]{:S(2)}) collective-permute-start(bf16[8,96,1024]{2,1,0:T(8,128)(2,1)} %get-tuple-element.399), channel_id=1, source_target_pairs={{0,2},{1,5},{2,0},{3,7},{4,6},{5,1},{6,4},{7,3},{8,10},{9,13},{10,... | collective-permute-start | bytes 4718600 | tf_op jit(solution)/shard_map/ppermute | solution.py:149
  404.2 25.2 %all-to-all-start.6 = ((bf16[4,128,1024]{2,1,0:T(8,128)(2,1)}), bf16[4,128,1024]{2,1,0:T(8,128)(2,1)}, u32[]{:S(2)}, u32[]{:S(2)}) async-start(bf16[4,128,1024]{2,1,0:T(8,128)(2,1)} %fold.13), calls=%async_computation.6 | async-start | bytes 2097152 | tf_op jit(solution)/shard_map/all_to_all | solution.py:157
  412.2 12.3 %collective-permute-start.39 = (bf16[4,96,1024]{2,1,0:T(8,128)(2,1)}, bf16[4,96,1024]{2,1,0:T(8,128)(2,1)}, u32[]{:S(2)}, u32[]{:S(2)}) collective-permute-start(bf16[4,96,1024]{2,1,0:T(8,128)(2,1)} %get-tuple-element.404), channel_id=1, source_target_pairs={{0,4},{1,3},{2,6},{3,1},{4,0},{5,7},{6,2},{7,5},{8,12},{9,11},{10,... | collective-permute-start | bytes 2359304 | tf_op jit(solution)/shard_map/ppermute | solution.py:149
  431.7 19.9 %all-to-all-start.7 = ((bf16[4,96,1024]{2,1,0:T(8,128)(2,1)}), bf16[4,96,1024]{2,1,0:T(8,128)(2,1)S(1)}, u32[]{:S(2)}, u32[]{:S(2)}) async-start(bf16[4,96,1024]{2,1,0:T(8,128)(2,1)} %fold.15), calls=%async_computation.7 | async-start | bytes 1572864 | tf_op jit(solution)/shard_map/all_to_all | solution.py:157
  437.3 5.2 %copy-start.1 = (f32[128,1024]{1,0:T(8,128)}, f32[128,1024]{1,0:T(8,128)S(1)}, u32[]{:S(2)}) copy-start(f32[128,1024]{1,0:T(8,128)S(1)} %convert_reduce_fusion.refs_3_) | copy-start | bytes 1572868
  440.3 27.4 %copy-start.23 = (f32[16]{0:T(128)S(1)}, f32[16]{0:T(128)}, u32[]{:S(2)}) copy-start(f32[16]{0:T(128)} %copy-done.22) | copy-start | bytes 196
  (8 other events, 13.3 us)

commit v5 on v4

--- a/solution.py
+++ b/solution.py
@@ -375,7 +375,7 @@
                 if lane is not None:
                     part = source.at[i, pl.ds(start, rows), pl.ds(lane, goal.shape[-1])]
                 place = goal.at[pl.ds(pl.multiple_of(band * rows, rows), rows)]
-                copies.append(pltpu.make_async_copy(part, place, sem))
+                copies.append(pltpu.make_async_copy(part, place, sem(band) if callable(sem) else sem))
     return copies
 
 
@@ -399,12 +399,12 @@
 
 
 def front_kernel(
-    at_gain, count, phone_rows, own_ref, other_ref, *refs
+    at_gain, at_count, spacing, count, phone_rows, speaker_ref, own_ref, other_ref, *refs
 ):
     sources = refs[:count]
     states_ref, states_turned_ref, hot_ref, mel_ref, time_ref = refs[count : count + 5]
     (
-        small_out, skip_out, embed_ref, stream_ref, joined_ref, normed_ref, turned_ref, edge_ref,
+        small_out, skip_out, embed_ref, stream_ref, joined_ref, normed_ref, turned_ref, edge_ref, share_ref,
         small_ref, skip_ref, table_ref, sems, out_sems,
     ) = refs[count + 5 :]
     width = stream_ref.shape[1]
@@ -424,6 +424,11 @@
     small_copy = pltpu.make_async_copy(small_ref, small_out, out_sems.at[0])
     small_copy.start()
     edge_ref[...] = small_ref[:, HEAD_AT:].T
+    facts = edge_ref[at_count - HEAD_AT : at_count - HEAD_AT + 3].astype(jnp.float32)
+    lane = lax.broadcasted_iota(jnp.int32, (1, width), 1)
+    hit = (facts[:1] == speaker_ref[0].astype(jnp.float32)) & (lax.rem(lane, spacing) == 0)
+    masked = jnp.sum(jnp.where(hit, 16.0 * facts[1:2] + facts[2:3], 0.0), 1, keepdims=True)
+    share_ref[...] = (1.0 / SPK) / jnp.maximum(masked, 1.0)
     embedded = as_low(dot_nt(hot_ref[...], table_ref[...]))
     embed_ref[...] = embedded
     start = dot_nt(embedded, small_ref[:, :phones])
@@ -442,15 +447,15 @@
     skip_copy.wait()
 
 
-def front(own, other, pieces, states, states_turned, hot, mel, time, phones, at_gain):
+def front(speaker, own, other, pieces, states, states_turned, hot, mel, time, phones, at_gain, at_count, spacing):
     frames, width = states.shape
     f32, low = jnp.float32, jnp.bfloat16
     bands = sum(p.shape[0] for p in pieces)
     vmem, anywhere = pl.BlockSpec(memory_space=pltpu.VMEM), pl.BlockSpec(memory_space=pl.ANY)
     return pl.pallas_call(
-        partial(front_kernel, at_gain, len(pieces), phones // bands),
-        in_specs=piece_specs(pieces) + [vmem] * 5,
-        out_specs=[anywhere] * 2 + [vmem] * 6,
+        partial(front_kernel, at_gain, at_count, spacing, len(pieces), phones // bands),
+        in_specs=[pl.BlockSpec(memory_space=pltpu.SMEM)] + piece_specs(pieces) + [vmem] * 5,
+        out_specs=[anywhere] * 2 + [vmem] * 7,
         out_shape=[
             jax.ShapeDtypeStruct((width, width), low),
             jax.ShapeDtypeStruct((2 * width, width), low),
@@ -460,6 +465,7 @@
             jax.ShapeDtypeStruct((frames, width), low),
             jax.ShapeDtypeStruct((width, frames), low),
             jax.ShapeDtypeStruct((width - HEAD_AT, width), low),
+            jax.ShapeDtypeStruct((1, 1), f32),
         ],
         scratch_shapes=[
             pltpu.VMEM((width, width), low),
@@ -470,7 +476,7 @@
         ],
         compiler_params=params(),
         name="front",
-    )(own, other, *pieces, states, states_turned, hot, mel, time)
+    )(speaker, own, other, *pieces, states, states_turned, hot, mel, time)
 
 
 def pack_kernel(count, blocks, own_ref, other_ref, *refs):
@@ -481,7 +487,7 @@
     unit = width // sum(source.shape[0] for source in sources)
 
     def copies(j):
-        entry = (w_ref.at[j], j * unit, unit, None, sems.at[j])
+        entry = (w_ref.at[j], (3 + j) * unit, unit, None, sems.at[j])
         return landing((own_ref, other_ref), sources, [entry])
 
     def kept(j):
@@ -585,12 +591,18 @@
     tile = act_ref.shape[1]
     rows = w_ref.shape[0] // sum(source.shape[0] for source in sources)
     kept = pltpu.make_async_copy(w_ref, w_out, out_sem)
+    each = tile // rows
 
     @pl.when(step == 0)
     def _():
-        copies = landing((own_ref, other_ref), sources, [(w_ref, 0, rows, None, sem)])
-        begin(copies)
-        finish(copies)
+        by_step = lambda band: sem.at[lax.div(band, each)]
+        begin(landing((own_ref, other_ref), sources, [(w_ref, 0, rows, None, by_step)]))
+
+    for _ in range(each):
+        pltpu.make_async_copy(sources[0].at[0, pl.ds(0, rows)], w_ref.at[pl.ds(0, rows)], sem.at[step]).wait()
+
+    @pl.when(step == pl.num_programs(0) - 1)
+    def _():
         kept.start()
 
     part = dot_nn(act_ref[...], w_ref[pl.ds(pl.multiple_of(step * tile, tile), tile)])
@@ -613,7 +625,7 @@
         inside = inside_ref[...]
         error = dot_nt(head_in, head) - target_ref[...]
         error_ref[...] = jnp.sum(jnp.sum(error * error, 1, keepdims=True) * inside, 0, keepdims=True)
-        d_prediction = as_low((2.0 * share_ref[0]) * error * inside)
+        d_prediction = as_low((2.0 * share_ref[...]) * error * inside)
         grad_ref[...] = dot_tn(head_in, d_prediction)
         d_head_in = dot_nn(d_prediction, head)
         gain_grad_ref[...] = jnp.sum(d_head_in * normed, 0, keepdims=True)
@@ -631,7 +643,7 @@
     return pl.pallas_call(
         partial(head_kernel, at_gain, len(pieces)),
         grid=(total // tile,),
-        in_specs=[pl.BlockSpec(memory_space=pltpu.SMEM)]
+        in_specs=[whole(1, 1)]
         + piece_specs(pieces)
         + [
             pl.BlockSpec((frames, tile), lambda i: (0, i)),
@@ -652,7 +664,7 @@
         scratch_shapes=[
             pltpu.VMEM((frames, width), jnp.float32),
             pltpu.VMEM((total, width), jnp.bfloat16),
-            pltpu.SemaphoreType.DMA,
+            pltpu.SemaphoreType.DMA((total // tile,)),
             pltpu.SemaphoreType.DMA,
         ],
         compiler_params=params(),
@@ -802,6 +814,7 @@
 
 def grads_kernel(plan, count, rows, legs, came_too, idx_ref, *refs):
     refs, picked_ref, right_ref, sems = refs[:-3], refs[-3], refs[-2], refs[-1]
+    frames = right_ref.shape[1] // 2
     outs = refs[len(refs) - legs :]
     came_ref = refs[len(refs) - legs - 1] if came_too else None
     step = pl.program_id(0)
@@ -815,13 +828,13 @@
         return [
             pltpu.make_async_copy(
                 refs[left].at[pl.ds(pl.multiple_of(idx_ref[i] * stride + offset, rows), rows)],
-                picked_ref.at[slot, side, pl.ds(i * rows, rows)],
+                picked_ref.at[slot, pl.ds(i * rows, rows), pl.ds(side * frames, frames)],
                 sems.at[slot],
             )
             for side, left in enumerate(lefts)
             for i in range(count)
         ] + [
-            pltpu.make_async_copy(refs[right], right_ref.at[slot, side], sems.at[slot])
+            pltpu.make_async_copy(refs[right], right_ref.at[slot, pl.ds(side * frames, frames)], sems.at[slot])
             for side, right in enumerate(rights)
         ]
 
@@ -852,7 +865,7 @@
                 total = total + came_ref[...].astype(jnp.float32)
         else:
             wide = outs[0].shape[2]
-            total = sum(dot_nn(picked_ref[c % 2, side], right_ref[c % 2, side]) for side in range(len(rights)))
+            total = dot_nn(picked_ref[c % 2], right_ref[c % 2])
             total = total.reshape(count, rows, wide)
         for f in range(legs):
             outs[f][...] = as_low(total[f * each : (f + 1) * each])
@@ -881,8 +894,8 @@
         out_specs=[pl.BlockSpec((count // legs, rows, width), lambda i: (0, i, 0))] * legs,
         out_shape=[jax.ShapeDtypeStruct((count // legs, rows * len(plan), width), jnp.bfloat16)] * legs,
         scratch_shapes=[
-            pltpu.VMEM((2, 2, count * rows, frames), jnp.bfloat16),
-            pltpu.VMEM((2, 2, frames, width), jnp.bfloat16),
+            pltpu.VMEM((2, count * rows, 2 * frames), jnp.bfloat16),
+            pltpu.VMEM((2, 2 * frames, width), jnp.bfloat16),
             pltpu.SemaphoreType.DMA((2,)),
         ],
         compiler_params=params(),
@@ -919,19 +932,21 @@
 
 def stack_kernel(*refs):
     ins, out, sem = refs[:-2], refs[-2], refs[-1]
-    copies = [pltpu.make_async_copy(ref, out.at[i], sem) for i, ref in enumerate(ins)]
+    copies = [
+        pltpu.make_async_copy(ref, out.at[n, i], sem) for n in range(out.shape[0]) for i, ref in enumerate(ins)
+    ]
     for copy in copies:
         copy.start()
     for copy in copies:
         copy.wait()
 
 
-def stack(parts):
+def stack(parts, times):
     return pl.pallas_call(
         stack_kernel,
         in_specs=[pl.BlockSpec(memory_space=pl.ANY)] * len(parts),
         out_specs=pl.BlockSpec(memory_space=pltpu.VMEM),
-        out_shape=jax.ShapeDtypeStruct((len(parts),) + parts[0].shape, parts[0].dtype),
+        out_shape=jax.ShapeDtypeStruct((times, len(parts)) + parts[0].shape, parts[0].dtype),
         scratch_shapes=[pltpu.SemaphoreType.DMA],
         compiler_params=params(),
         name="stack",
@@ -994,7 +1009,10 @@
     return [y for n in range(3) for y in turned(results[9 * n : 9 * n + 9])]
 
 
-def prepare_kernel(at_mel, at_count, frames, facts_ref, input_ref, table_ref, head_ref, gains_ref, skip_ref, out_ref):
+def prepare_kernel(
+    at_mel, at_count, frames,
+    facts_ref, input_ref, table_ref, head_ref, gains_ref, skip_ref, attend_ref, out_ref,
+):
     unit, inputs = input_ref.shape
     phones = inputs - at_mel
     turned = as_low(input_ref[...])
@@ -1015,22 +1033,28 @@
     for j, fact in enumerate((facts_ref[0], lax.div(count, 16), lax.rem(count, 16))):
         edge = jnp.where(lane == at_count - HEAD_AT + j, fact.astype(jnp.float32), edge)
     out_ref[0, :unit, HEAD_AT:] = as_low(edge)
-    out_ref[0, unit:] = as_low(skip_ref[...])
+    width = out_ref.shape[2]
+    start = unit + skip_ref.shape[0]
+    out_ref[0, unit:start] = as_low(skip_ref[...])
+    for j in range(attend_ref.shape[1] // width):
+        here = slice(start + j * unit, start + (j + 1) * unit)
+        out_ref[0, here] = as_low(attend_ref[:, j * width : (j + 1) * width])
     for z in range(1, out_ref.shape[0]):
         out_ref[z] = out_ref[0]
 
 
-def prepare(facts, turned, table, head, gains, skip, deep, frames, at_mel, at_count):
+def prepare(facts, turned, table, head, gains, skip, attend, deep, frames, at_mel, at_count):
     vmem = pl.BlockSpec(memory_space=pltpu.VMEM)
-    rows, width = turned.shape[0] + skip.shape[0], skip.shape[1]
+    width = skip.shape[1]
+    rows = turned.shape[0] + skip.shape[0] + attend.size // width
     return pl.pallas_call(
         partial(prepare_kernel, at_mel, at_count, frames),
-        in_specs=[pl.BlockSpec(memory_space=pltpu.SMEM)] + [vmem] * 5,
+        in_specs=[pl.BlockSpec(memory_space=pltpu.SMEM)] + [vmem] * 6,
         out_specs=vmem,
         out_shape=jax.ShapeDtypeStruct((deep, rows, width), jnp.bfloat16),
         compiler_params=params(),
         name="prepare",
-    )(facts, turned, table, head, gains, skip)
+    )(facts, turned, table, head, gains, skip, attend)
 
 
 def shards(
@@ -1125,8 +1149,8 @@
     attend_blocks, expand_blocks = blocks(w_attend), blocks(w_expand)
     packs, wides = len(attend_blocks), len(expand_blocks)
     stages = [
-        [("small", None, small), ("skip", None, as_low(w_skip))],
-        [("attend", j, w) for j, w in enumerate(attend_blocks)],
+        [("small", None, small), ("skip", None, as_low(w_skip))]
+        + [("attend", j, w) for j, w in enumerate(attend_blocks)],
         [("output", None, as_low(w_output))] + [("expand", j, w) for j, w in enumerate(expand_blocks)],
         [("reduce", None, as_low(w_reduce))],
     ]
@@ -1144,14 +1168,11 @@
     def along(x, role, *after):
         return spread(grid, tied(x, *after) if after else x, role)
 
-    def copies(x):
-        return jnp.broadcast_to(x[None], (grid.size("z"),) + x.shape)
-
     def deepen(x, *after):
         return swap_deep(grid, tied(x, *after) if after else x)
 
-    def plane(moved):
-        return stack(moved).reshape((-1,) + moved[0].shape[1:])
+    def hop_far(pieces):
+        return [shift(grid, p, "far", f) for f in range(1, grid.size("far")) for p in pieces]
 
     def gather_whole(stage):
         rows = lax.all_gather(load(stage), AXES, axis=0, tiled=False)
@@ -1181,88 +1202,64 @@
     states_turned = skip_states.T
     loads = [load(stage) for stage in stages]
     if fast:
-        if unit % 16 == 0 and inputs % 16 == 0:
-            first = prepare(
-                jnp.stack([speaker[0], span_start[0], span_end[0], lengths[0]]), w_input.T, phone_table.T,
-                w_head, norm_gains, w_skip, grid.size("z"), frames, 2 * mel_bins, at_count,
-            )
-        else:
-            first = copies(loads[0])
-        deep_0, near_2, load_1, load_3 = join(
-            deepen(first), along(loads[2], "near"), copies(loads[1]), copies(loads[3])
+        first = prepare(
+            jnp.stack([speaker[0], span_start[0], span_end[0], lengths[0]]), w_input.T, phone_table.T,
+            w_head, norm_gains, w_skip, w_attend, grid.size("z"), frames, 2 * mel_bins, at_count,
         )
-        pair_2 = copies(stack(near_2))
-        near_0, deep_1, pair_2, target, mel, phone_hot, slopes, times, inside, states_turned = join(
-            along(deep_0, "near", pair_2), deepen(load_1, deep_0), pair_2,
+        pair_1 = stack(along(loads[1], "near"), grid.size("z"))
+        load_2 = stack([loads[2]], grid.size("z"))[:, 0]
+        deep_0, pair_1, load_2 = join(deepen(first), pair_1, load_2)
+        deep_1 = deepen(pair_1)
+        near_0 = along(deep_0, "near")
+        near_0 = [tied(near_0[0], near_0[-1])] + near_0[1:]
+        (
+            near_0, far_0, core_0, deep_1, own, other, own_turned, other_turned, mine, theirs,
+            target, mel, phone_hot, slopes, times, inside, states_turned,
+        ) = join(
+            near_0, hop_far(near_0), [sibling(p) for p in near_0], deep_1,
+            own, other, own_turned, other_turned, mine, theirs,
             target, mel, phone_hot, slopes, times, inside, states_turned,
         )
-        near_0 = plane(near_0)
-        deep_2 = deepen(pair_2, near_0)
-        far_0, core_0, near_1, own, other, own_turned, other_turned, mine, theirs = join(
-            along(near_0, "far")[1], sibling(near_0), along(deep_1, "near", near_0),
-            own, other, own_turned, other_turned, mine, theirs,
-        )
-        near_1 = plane(near_1)
-        far_0 = tied(far_0, near_1)
-        pieces_0 = [near_0, far_0, core_0, sibling(far_0)]
+        pieces_0 = near_0 + far_0 + core_0 + [sibling(p) for p in far_0]
+        near_1 = deep_1.reshape((-1,) + deep_1.shape[2:])
         far_1 = along(near_1, "far")[1]
         core_1 = sibling(near_1)
+        deep_2 = deepen(load_2, near_1)
     else:
         own, other = jnp.arange(BANDS // 2), jnp.arange(BANDS // 2, BANDS)
         own_turned, other_turned = own, other
         pieces_0 = gather_whole(stages[0])
-    small_full, skip_full, embedded, stream, joined_turned, attn_in, attn_turned, edges = front(
-        own, other, pieces_0, skip_states, states_turned, phone_hot, mel, times, phone_width, mel_bins
-    )
-    tallies = edges[at_count - HEAD_AT : at_count - HEAD_AT + 3].reshape(3, devices, unit)
-    tallies = tallies[:, :, 0].astype(jnp.float32)
-    counts = jnp.sum(
-        (tallies[0][:, None] == jnp.arange(SPK, dtype=jnp.float32)[None, :])
-        * (16.0 * tallies[1] + tallies[2])[:, None],
-        0,
-    )
-    share = jnp.sum(speaker_hot / jnp.maximum(counts, 1.0)) / SPK
-
+    small_full, skip_full, embedded, stream, joined_turned, attn_in, attn_turned, edges, share = front(
+        speaker, own, other, pieces_0, skip_states, states_turned, phone_hot, mel, times, phone_width, mel_bins, at_count, unit
+    )
+    attend_full, packed = pack(own, other, pieces_0, attn_in, packs)
     if fast:
-        far_1, core_1, deep_2, embedded, stream, attn_in, attn_turned, edges, share, counts = join(
-            far_1, core_1, deep_2, embedded, stream, attn_in, attn_turned, edges, share, counts
+        near_2 = along(tied(deep_2, packed), "near")
+    mixed, lse = attend(lengths, slopes, packed)
+    if fast:
+        far_1, near_2, core_1, stream, packed, mixed, lse, joined_turned, edges, share = join(
+            far_1, near_2, core_1, stream, packed, mixed, lse, joined_turned, edges, share
         )
-        near_2 = deep_2.reshape((-1,) + deep_2.shape[2:])
         pieces_1 = [near_1, far_1, core_1, sibling(far_1)]
-        far_2 = along(near_2, "far")[1]
-        core_2 = sibling(near_2)
-        deep_3 = deepen(load_3, near_2)
+        far_2 = hop_far(near_2)
+        core_2 = [sibling(p) for p in near_2]
     else:
         pieces_1 = gather_whole(stages[1])
-    attend_full, packed = pack(own, other, pieces_1, attn_in, packs)
-    mixed, lse = attend(lengths, slopes, packed)
+    output_full, stream_mid, ffn_in, ffn_turned, mixed_turned = mid_step(
+        own_turned, other_turned, pieces_1, mixed, stream, edges, mel_bins + 1
+    )
+    expand_full, activated, act_turned, gelu_slope = expand(
+        own_turned, other_turned, pieces_1, ffn_in, wides
+    )
     if fast:
-        far_2, deep_3, core_2, packed, mixed, lse, joined_turned = join(
-            far_2, deep_3, core_2, packed, mixed, lse, joined_turned
+        far_2, core_2, stream_mid, ffn_turned, mixed_turned, activated, act_turned, gelu_slope = join(
+            far_2, core_2, stream_mid, ffn_turned, mixed_turned, activated, act_turned, gelu_slope
         )
-        near_3 = along(deep_3, "near")
-        pieces_2 = [near_2, far_2, core_2, sibling(far_2)]
+        pieces_2 = near_2 + far_2 + core_2 + [sibling(p) for p in far_2]
     else:
         pieces_2 = gather_whole(stages[2])
-    output_full, stream_mid, ffn_in, ffn_turned, mixed_turned = mid_step(
-        own_turned, other_turned, pieces_2, mixed, stream, edges, mel_bins + 1
-    )
-    if fast:
-        near_3 = plane([near_3[0], tied(near_3[1], ffn_in)] + near_3[2:])
-        far_3 = along(near_3, "far")[1]
-        core_3 = sibling(near_3)
-    expand_full, activated, act_turned, gelu_slope = expand(
-        own_turned, other_turned, pieces_2, ffn_in, wides
-    )
-    if fast:
-        far_3, core_3, stream_mid, ffn_turned, mixed_turned, activated, act_turned, gelu_slope = join(
-            far_3, core_3, stream_mid, ffn_turned, mixed_turned, activated, act_turned, gelu_slope
-        )
-        pieces_3 = [near_3, far_3, core_3, sibling(far_3)]
-    else:
-        pieces_3 = gather_whole(stages[3])
     reduce_full, d_stream_out, d_branch, grad_head, grad_gain_three, error_sum = head_step(
-        share[None], own, other, pieces_3, activated, stream_mid, edges, target, inside, mel_bins + 2
+        share, own, other, pieces_2, activated, stream_mid, edges, target, inside, mel_bins + 2
     )
     far, near, deep = (grid.size(r) for r in ("far", "near", "z"))
 
@@ -1291,7 +1288,7 @@
     offsets = [j * unit for j in range(wides)]
     if fast:
         plan = [((0, 1), (2, 3), wides * unit, o) for o in offsets]
-        legs_0 = sums(plan, both(tied(act_turned, pieces_3[3]), d_branch))
+        legs_0 = sums(plan, both(tied(act_turned, *pieces_2), d_branch))
         moved_0 = hops(legs_0, "far")
         d_branch_next = tied(d_branch, legs_0[0])
     else:
@@ -1340,6 +1337,13 @@
         share_attend = dense(
             [(mixed_turned, d_out, unit, 0)] + [(attn_turned, d, unit, 0) for d in d_packed]
         )
+    tallies = edges[at_count - HEAD_AT : at_count - HEAD_AT + 3].reshape(3, devices, unit)
+    tallies = tallies[:, :, 0].astype(jnp.float32)
+    counts = jnp.sum(
+        (tallies[0][:, None] == jnp.arange(SPK, dtype=jnp.float32)[None, :])
+        * (16.0 * tallies[1] + tallies[2])[:, None],
+        0,
+    )
     gain_grads = [grad_gain_one, grad_gain_two, grad_gain_three]
     small_grads = tail(
         d_joined_in, skip_full, small_full, embedded, mel, phone_hot, grad_head, gain_grads, mel_bins
@@ -1352,7 +1356,7 @@
         moved_2, legs_3 = join(moved_2, legs_3)
         legs_2 = fold([legs_2[0]] + moved_2, near)
         moved_3 = hops(legs_3, "far", legs_2[0])
-        moved_2, sums_1 = join(hops(legs_2, "near"), sums_1)
+        moved_2, sums_1, counts = join(hops(legs_2, "near"), sums_1, counts)
         (sums_2,) = fold([legs_2[0]] + moved_2, 1)
         moved_3 = [tied(moved_3[0], sums_2)] + moved_3[1:]
         legs_3 = fold([legs_3[0]] + moved_3, near)

time: 486 us -> 472 us (0.971)
    ppermute x40 -> x42, waiting for transfers between devices: 105 us -> 97.3 us  [shift(): return lax.ppermute(x, AXES, grid.pairs(role, step))]
    all_to_all x8 -> x7, waiting for transfers between devices: 42.7 us -> 49 us  [swap_deep(): return lax.all_to_all(x, AXES, 0, 0, axis_index_groups=grid.lines())]
    broadcast_in_dim x3 -> x0, local copies, waits for them, and re-layouts: 5.19 us -> none  [copies(): return jnp.broadcast_to(x[None], (grid.size('z'),) + x.shape)]
    pallas_call x4 -> x2, Pallas kernels: 9.83 us -> 5.98 us  [stack(): pl.pallas_call(stack_kernel, in_specs=[pl.BlockSpec(memory_space=pl.ANY)]...]
    all_to_all x8 -> x7, starting transfers between devices: 38.1 us -> 34.7 us  [swap_deep(): return lax.all_to_all(x, AXES, 0, 0, axis_index_groups=grid.lines())]
    unnamed x55 -> x31, local copies, waits for them, and re-layouts: 8.14 us -> 10.6 us
    ppermute x40 -> x42, starting transfers between devices: 25 us -> 25.8 us  [shift(): return lax.ppermute(x, AXES, grid.pairs(role, step))]
  transfers between devices with their start and end apart: 48 -> 49, of which waited for: 27 -> 24; matrix products, arithmetic and copies ran while one was open for 5% -> 5% of each run, Pallas kernels for 39% -> 40%
where the time goes in v5:
time: 472 us; the launch traced here: 468 us
  Pallas kernels  208 us (44%)
  waiting for transfers between devices  146 us (31%)
  starting transfers between devices  60.5 us (13%)
  other arithmetic  17.6 us (4%)
  local copies, waits for them, and re-layouts  13.9 us (3%)
  between operations  10.9 us (2%)
  blocking collectives  10.5 us (2%)
    ppermute x42, waiting for transfers between devices, shift(): return lax.ppermute(x, AXES, grid.pairs(role, step))  97.3 us
    all_to_all x7, waiting for transfers between devices, swap_deep(): return lax.all_to_all(x, AXES, 0, 0, axis_index_groups=grid.lines())  49 us
    pallas_call x5, Pallas kernels, grads(): pl.pallas_call(partial(grads_kernel, plan, count, rows, legs, came is not...  40.8 us
    all_to_all x7, starting transfers between devices, swap_deep(): return lax.all_to_all(x, AXES, 0, 0, axis_index_groups=grid.lines())  34.7 us
    ppermute x42, starting transfers between devices, shift(): return lax.ppermute(x, AXES, grid.pairs(role, step))  25.8 us
    pallas_call x8, Pallas kernels, fold(): pl.pallas_call(partial(fold_kernel, legs), grid=(rows // tile,), in_specs...  23 us
    pallas_call x1, Pallas kernels, ffn_back(): pl.pallas_call(partial(ffn_back_kernel, at_gain), grid=(count,), in_specs...  20.4 us
    pallas_call x1, Pallas kernels, attend_back(): pl.pallas_call(attend_back_kernel, grid=(width // wide,), in_specs=[pl.Bl...  18.3 us
  transfers between devices with their start and end apart: 49, of which 24 were waited for; matrix products, arithmetic and copies ran while one was open for 5% of the time, Pallas kernels for 40%

profile of v5, /device:TPU:0, one launch (start us, length us, event | category | flops | bytes accessed | tf_op | source)
XLA Modules:
  0.0 468.0 jit_solution(2407339914409446650)
XLA Ops:
  3.8 2.5 prepare.1
  6.4 6.5 %all-to-all-start = ((bf16[4,192,1024]{2,1,0:T(8,128)(2,1)}), bf16[4,192,1024]{2,1,0:T(8,128)(2,1)}, u32[]{:S(2)}, u32[]{:S(2)}) async-start(bf16[4,192,1024]{2,1,0:T(8,128)(2,1)} %prepare.1), calls=%async_computation | async-start | bytes 3145728 | tf_op jit(solution)/shard_map/all_to_all | solution.py:157
  16.1 1.5 collective-permute-start
  18.3 2.6 stack.7
  20.9 2.5 collective-permute-done.refs_1_
  23.5 3.4 stack.6
  26.9 23.0 %all-to-all-done.refs_0_ = bf16[4,192,1024]{2,1,0:T(8,128)(2,1)} async-done(((bf16[4,192,1024]{2,1,0:T(8,128)(2,1)}), bf16[4,192,1024]{2,1,0:T(8,128)(2,1)}, u32[]{:S(2)}, u32[]{:S(2)}) %all-to-all-start) | async-done | bytes 1572896 | tf_op jit(solution)/shard_map/all_to_all | solution.py:157
  49.9 4.5 all-to-all-start.1
  54.6 1.6 collective-permute-start.1
  57.5 17.7 %collective-permute-done.1.refs_1_ = bf16[4,192,1024]{2,1,0:T(8,128)(2,1)S(1)} collective-permute-done((bf16[4,192,1024]{2,1,0:T(8,128)(2,1)}, bf16[4,192,1024]{2,1,0:T(8,128)(2,1)S(1)}, u32[]{:S(2)}, u32[]{:S(2)}) %collective-permute-start.1) | collective-permute-done | bytes 1572896 | tf_op jit(solution)/shard_map/ppermute | solution.py:149
  80.4 1.8 copy.103
  82.2 2.3 copy.109
  85.6 1.7 add_convert_fusion
  90.3 5.6 %collective-permute-done.2.refs_2_ = bf16[4,192,1024]{2,1,0:T(8,128)(2,1)S(1)} collective-permute-done((bf16[4,192,1024]{2,1,0:T(8,128)(2,1)}, bf16[4,192,1024]{2,1,0:T(8,128)(2,1)S(1)}, u32[]{:S(2)}, u32[]{:S(2)}) %collective-permute-start.2) | collective-permute-done | bytes 1572896 | tf_op jit(solution)/shard_map/ppermute | solution.py:149
  95.9 17.0 %collective-permute-done.3.refs_3_ = bf16[4,192,1024]{2,1,0:T(8,128)(2,1)} collective-permute-done((bf16[4,192,1024]{2,1,0:T(8,128)(2,1)S(1)}, bf16[4,192,1024]{2,1,0:T(8,128)(2,1)}, u32[]{:S(2)}, u32[]{:S(2)}) %collective-permute-start.3) | collective-permute-done | bytes 1572896 | tf_op jit(solution)/shard_map/ppermute | solution.py:149
  114.0 4.5 all-to-all-start.2
  118.6 1.6 collective-permute-start.6
  121.4 11.4 %front.1 = (bf16[1024,1024]{1,0:T(8,128)(2,1)}, bf16[2048,1024]{1,0:T(8,128)(2,1)}, bf16[512,512]{1,0:T(8,128)(2,1)}, f32[512,1024]{1,0:T(8,128)}, bf16[2048,512...) custom-call(s32[1]{0:T(128)} %copy.124.speaker_ref, ...), custom_call_target="tpu_custom_call" | custom-call | tf_op jit(solution)/shard_map/front/pallas_call | solution.py:455
  132.8 8.2 %pack.1 = (bf16[3,1024,1024]{2,1,0:T(8,128)(2,1)}, bf16[3,512,1024]{2,1,0:T(8,128)(2,1)}) custom-call(s32[16]{0:T(128)} %get-tuple-element.230.own_ref, s32[16]{0:T(128)} %get-tuple-element.231.other_ref, bf16[4,192,1024]{2,1,0:T(8,128)(2,1)} %all-to-all-done.refs_0_, bf16[4,192,1024]{2,1,0:T(8,128)(2,1)} %copy-done, bf16[4,192,1024]{2,1,0:T(8,128)(2,1)} %copy-done.1, ...), custom_call_target="tpu_custom_call" | custom-call | tf_op jit(solution)/shard_map/pack/pallas_call | solution.py:513
  141.0 3.7 all-to-all-done.2.refs_0_
  144.6 1.5 collective-permute-start.9
  146.2 12.1 %attend.1 = (bf16[512,1024]{1,0:T(8,128)(2,1)}, f32[4,4,512]{2,1,0:T(4,128)}) custom-call(s32[1]{0:T(128)} %copy.121.length_ref, f32[16]{0:T(128)} %multiply_power_fusion.slope_ref, bf16[3,512,1024]{2,1,0:T(8,128)(2,1)} %get-tuple-element.320.packed_ref), custom_call_target="tpu_custom_call" | custom-call | tf_op jit(solution)/shard_map/attend/pallas_call | solution.py:223
  158.2 3.1 collective-permute-done.9.refs_1_
  164.2 2.4 collective-permute-done.15.refs_3_
  166.6 7.9 %mid.1 = (bf16[1024,1024]{1,0:T(8,128)(2,1)}, f32[512,1024]{1,0:T(8,128)}, bf16[512,1024]{1,0:T(8,128)(2,1)}, bf16[1024,512]{1,0:T(8,128)(2,1)}, bf16[1024,512]{1,0:T(8,128)(2,1)}) custom-call(s32[16]{0:T(128)} %get-tuple-element.255.own_ref, s32[16]{0:T(128)} %get-tuple-element.256.other_ref, bf16[8,160,1024]{2,1,0:T(8,128)(2,1)} %bitcast.10.refs_0_, ...), custom_call_target="tpu_custom_call" | custom-call | tf_op jit(solution)/shard_map/mid/pallas_call | solution.py:562
  174.4 17.4 %expand.1 = (bf16[4,1024,1024]{2,1,0:T(8,128)(2,1)}, bf16[512,4096]{1,0:T(8,128)(2,1)}, bf16[4096,512]{1,0:T(8,128)(2,1)}, bf16[512,4096]{1,0:T(8,128)(2,1)}) custom-call(s32[16]{0:T(128)} %get-tuple-element.255.own_ref, s32[16]{0:T(128)} %get-tuple-element.256.other_ref, bf16[8,160,1024]{2,1,0:T(8,128)(2,1)} %bitcast.10.refs_0_, ...), custom_call_target="tpu_custom_call" | custom-call | tf_op jit(solution)/shard_map/expand/pallas_call | solution.py:339
  192.5 2.5 collective-permute-done.16.refs_6_
  196.8 16.3 %head.1 = (bf16[4096,1024]{1,0:T(8,128)(2,1)}, f32[512,1024]{1,0:T(8,128)}, bf16[512,1024]{1,0:T(8,128)(2,1)}, f32[1024,80]{1,0:T(8,128)}, f32[1,1024]{1,0:T(1,128)}, /*index=5*/f32[1,1]{1,0:T(1,128)}) custom-call(f32[1,1]{1,0:T(1,128)} %get-tuple-element.252.share_ref, s32[16]{0:T(128)} %get-tuple-element.230.own_ref, s32[16]{0:T(128)} %get-tuple-element.231.other_ref, ...), custom_call_target="tpu_custom_call" | custom-call | tf_op jit(solution)/shard_map/head/pallas_call | solution.py:643
  213.7 2.5 collective-permute-done.19.refs_3_
  216.2 10.1 %grads.5 = (bf16[8,128,1024]{2,1,0:T(8,128)(2,1)}, bf16[8,128,1024]{2,1,0:T(8,128)(2,1)}) custom-call(s32[16]{0:T(128)} %get-tuple-element.278.idx_ref, bf16[4096,512]{1,0:T(8,128)(2,1)} %get-tuple-element.280.refs_0_, bf16[4096,512]{1,0:T(8,128)(2,1)} %collective-permute-done.18.refs_1_, bf16[512,1024]{1,0:T(8,128)(2,1)} %get-tuple-element.285.refs_2_.low_ref, ...), custom_call_target="tpu_custom_call" | custom-call | tf_op jit(solution)/shard_map/grads/pallas_call | solution.py:890
  226.4 1.6 collective-permute-start.20
  227.9 20.4 %ffn_back.1 = (f32[512,1024]{1,0:T(8,128)}, bf16[512,1024]{1,0:T(8,128)(2,1)}, f32[1,1024]{1,0:T(1,128)}, bf16[512,1024]{1,0:T(8,128)(2,1)}, bf16[512,1024]{1,0:...) custom-call(bf16[512,1024]{1,0:T(8,128)(2,1)} %get-tuple-element.285.refs_2_.low_ref, ...), custom_call_target="tpu_custom_call" | custom-call | tf_op jit(solution)/shard_map/ffn_back/pallas_call | solution.py:712
  249.3 2.0 collective-permute-done.22.refs_3_
  252.8 1.5 collective-permute-done.24.refs_7_
  255.8 3.4 fold.8
  259.4 1.5 collective-permute-start.26
  260.9 10.1 %grads.6 = (bf16[8,128,1024]{2,1,0:T(8,128)(2,1)}, bf16[8,128,1024]{2,1,0:T(8,128)(2,1)}) custom-call(s32[16]{0:T(128)} %get-tuple-element.278.idx_ref, bf16[1024,512]{1,0:T(8,128)(2,1)} %get-tuple-element.300.refs_0_, bf16[1024,512]{1,0:T(8,128)(2,1)} %collective-permute-done.21.refs_1_, bf16[512,1024]{1,0:T(8,128)(2,1)} %get-tuple-element.302.refs_2_, ...), custom_call_target="tpu_custom_call" | custom-call | tf_op jit(solution)/shard_map/grads/pallas_call | solution.py:890
  271.0 3.5 collective-permute-done.26.refs_1_
  274.5 2.5 fold.9
  278.3 5.5 %all-to-all-start.3 = ((bf16[4,128,1024]{2,1,0:T(8,128)(2,1)}), bf16[4,128,1024]{2,1,0:T(8,128)(2,1)}, u32[]{:S(2)}, u32[]{:S(2)}) async-start(bf16[4,128,1024]{2,1,0:T(8,128)(2,1)} %fold.9), calls=%async_computation.3 | async-start | bytes 2097152 | tf_op jit(solution)/shard_map/all_to_all | solution.py:157
  283.8 18.3 %attend_back.1 = (bf16[512,1024]{1,0:T(8,128)(2,1)}, bf16[512,1024]{1,0:T(8,128)(2,1)}, bf16[512,1024]{1,0:T(8,128)(2,1)}) custom-call(s32[1]{0:T(128)} %copy.121.length_ref, f32[16]{0:T(128)} %multiply_power_fusion.slope_ref, bf16[3,512,1024]{2,1,0:T(8,128)(2,1)} %get-tuple-element.320.packed_ref, bf16[512,1024]{1,0:T(8,128)(2,1)} %get-tuple-element.339.d_out_ref.refs_4_, ...), custom_call_target="tpu_custom_call" | custom-call | tf_op jit(solution)/shard_map/attend_back/pallas_call | solution.py:274
  302.7 9.7 %pack_back.1 = (bf16[512,1024]{1,0:T(8,128)(2,1)}, f32[1,1024]{1,0:T(1,128)}) custom-call(bf16[512,1024]{1,0:T(8,128)(2,1)} %get-tuple-element.341.refs_0_.refs_6_, bf16[512,1024]{1,0:T(8,128)(2,1)} %get-tuple-element.343.refs_1_.refs_8_, bf16[512,1024]{1,0:T(8,128)(2,1)} %get-tuple-element.345.refs_2_.refs_10_, ...), custom_call_target="tpu_custom_call" | custom-call | tf_op jit(solution)/shard_map/pack_back/pallas_call | solution.py:759
  312.4 3.4 fold.10
  317.2 10.1 %grads.7 = (bf16[8,128,1024]{2,1,0:T(8,128)(2,1)}, bf16[8,128,1024]{2,1,0:T(8,128)(2,1)}) custom-call(s32[16]{0:T(128)} %get-tuple-element.278.idx_ref, bf16[1024,512]{1,0:T(8,128)(2,1)} %get-tuple-element.335.refs_0_, bf16[1024,512]{1,0:T(8,128)(2,1)} %collective-permute-done.27.refs_1_, bf16[1024,512]{1,0:T(8,128)(2,1)} %get-tuple-element.337.refs_2_, ...), custom_call_target="tpu_custom_call" | custom-call | tf_op jit(solution)/shard_map/grads/pallas_call | solution.py:890
  327.3 4.2 collective-permute-done.34.refs_1_
  331.5 2.6 fold.11
  334.9 7.1 %tail.1 = (bf16[1024,768]{1,0:T(8,128)(2,1)}, bf16[512,128]{1,0:T(8,128)(2,1)}, bf16[1024,128]{1,0:T(8,128)(2,1)}) custom-call(bf16[512,1024]{1,0:T(8,128)(2,1)} %get-tuple-element.372.d_ref.refs_2_, bf16[2048,1024]{1,0:T(8,128)(2,1)} %get-tuple-element.360.skip_ref, bf16[1024,1024]{1,0:T(8,128)(2,1)} %get-tuple-element.361.small_ref, ...), custom_call_target="tpu_custom_call" | custom-call | tf_op jit(solution)/shard_map/tail/pallas_call | solution.py:804
  342.0 2.6 grads.8
  344.7 5.1 %all-to-all-start.4 = ((bf16[4,128,1024]{2,1,0:T(8,128)(2,1)}), bf16[4,128,1024]{2,1,0:T(8,128)(2,1)}, u32[]{:S(2)}, u32[]{:S(2)}) async-start(bf16[4,128,1024]{2,1,0:T(8,128)(2,1)} %fold.11), calls=%async_computation.4 | async-start | bytes 2097152 | tf_op jit(solution)/shard_map/all_to_all | solution.py:157
  349.8 7.9 %grads.9 = (bf16[8,96,1024]{2,1,0:T(8,128)(2,1)}, bf16[8,96,1024]{2,1,0:T(8,128)(2,1)}) custom-call(s32[16]{0:T(128)} %get-tuple-element.278.idx_ref, bf16[2048,512]{1,0:T(8,128)(2,1)} %get-tuple-element.370.refs_0_, bf16[2048,512]{1,0:T(8,128)(2,1)} %collective-permute-done.35.refs_1_, bf16[512,1024]{1,0:T(8,128)(2,1)} %get-tuple-element.372.d_ref.refs_2_, ...), custom_call_target="tpu_custom_call" | custom-call | tf_op jit(solution)/shard_map/grads/pallas_call | solution.py:890
  357.6 2.8 collective-permute-done.37.refs_1_.refs_3_
  360.5 3.4 fold.12
  367.7 8.5 %all-to-all-done.4 = bf16[4,128,1024]{2,1,0:T(8,128)(2,1)} async-done(((bf16[4,128,1024]{2,1,0:T(8,128)(2,1)}), bf16[4,128,1024]{2,1,0:T(8,128)(2,1)}, u32[]{:S(2)}, u32[]{:S(2)}) %all-to-all-start.4) | async-done | bytes 1048608 | tf_op jit(solution)/shard_map/all_to_all | solution.py:157
  376.2 14.0 %collective-permute-done.40.refs_1_ = bf16[4,128,1024]{2,1,0:T(8,128)(2,1)} collective-permute-done((bf16[4,128,1024]{2,1,0:T(8,128)(2,1)}, bf16[4,128,1024]{2,1,0:T(8,128)(2,1)}, u32[]{:S(2)}, u32[]{:S(2)}) %collective-permute-start.40) | collective-permute-done | bytes 1048608 | tf_op jit(solution)/shard_map/ppermute | solution.py:149
  390.3 2.4 fold.13
  392.7 5.1 %all-to-all-start.5 = ((bf16[4,128,1024]{2,1,0:T(8,128)(2,1)}), bf16[4,128,1024]{2,1,0:T(8,128)(2,1)}, u32[]{:S(2)}, u32[]{:S(2)}) async-start(bf16[4,128,1024]{2,1,0:T(8,128)(2,1)} %fold.13), calls=%async_computation.5 | async-start | bytes 2097152 | tf_op jit(solution)/shard_map/all_to_all | solution.py:157
  397.8 2.9 fold.14
  401.5 11.6 %collective-permute-done.41.refs_1_ = bf16[4,96,1024]{2,1,0:T(8,128)(2,1)} collective-permute-done((bf16[4,96,1024]{2,1,0:T(8,128)(2,1)}, bf16[4,96,1024]{2,1,0:T(8,128)(2,1)}, u32[]{:S(2)}, u32[]{:S(2)}) %collective-permute-start.41) | collective-permute-done | bytes 786464 | tf_op jit(solution)/shard_map/ppermute | solution.py:149
  413.1 5.5 %all-to-all-done.5 = bf16[4,128,1024]{2,1,0:T(8,128)(2,1)} async-done(((bf16[4,128,1024]{2,1,0:T(8,128)(2,1)}), bf16[4,128,1024]{2,1,0:T(8,128)(2,1)}, u32[]{:S(2)}, u32[]{:S(2)}) %all-to-all-start.5) | async-done | bytes 1048608 | tf_op jit(solution)/shard_map/all_to_all | solution.py:157
  418.5 2.2 fold.15
  420.7 3.5 all-to-all-start.6
  433.1 7.7 %all-to-all-done.6 = bf16[4,96,1024]{2,1,0:T(8,128)(2,1)S(1)} async-done(((bf16[4,96,1024]{2,1,0:T(8,128)(2,1)}), bf16[4,96,1024]{2,1,0:T(8,128)(2,1)S(1)}, u32[]{:S(2)}, u32[]{:S(2)}) %all-to-all-start.6) | async-done | bytes 786464 | tf_op jit(solution)/shard_map/all_to_all | solution.py:157
  445.0 10.5 %all_to_all.41 = f32[32,1,17]{2,1,0:T(1,128)S(1)} all-to-all(f32[32,1,17]{2,1,0:T(1,128)S(1)} %broadcast_in_dim.83), channel_id=1, replica_groups=mesh['wide'=8,'narrow'=4] {'wide','narrow'}, dimensions={0} | all-to-all | bytes 4352 | tf_op jit(solution)/shard_map/all_to_all | solution.py:169
  458.2 7.3 %adam.1 = (f32[32,672]{1,0:T(8,128)}, f32[16,128]{1,0:T(8,128)}, f32[64,1024]{1,0:T(8,128)}, f32[32,3072]{1,0:T(8,128)}, f32[32,1024]{1,0:T(8,128)}, /*index=5*/...) custom-call(f32[1]{0:T(128)} %bitcast.16.clip_ref, ...), custom_call_target="tpu_custom_call" | custom-call | tf_op jit(solution)/shard_map/adam/pallas_call | solution.py:1001
  (155 shorter events, 47.3 us)
Async XLA Ops:
  6.4 6.5 %copy-start.8 = (f32[32,4096]{1,0:T(8,128)S(1)}, f32[32,4096]{1,0:T(8,128)}, u32[]{:S(2)}) copy-start(f32[32,4096]{1,0:T(8,128)} %refs_9_.1) | copy-start | bytes 1572868
  6.4 6.5 %copy-start.9 = (f32[32,1024]{1,0:T(8,128)S(1)}, f32[32,1024]{1,0:T(8,128)}, u32[]{:S(2)}) copy-start(f32[32,1024]{1,0:T(8,128)} %refs_8_.3) | copy-start | bytes 393220
  6.4 11.2 %copy-start.7 = (f32[128,1024]{1,0:T(8,128)S(1)}, f32[128,1024]{1,0:T(8,128)}, u32[]{:S(2)}) copy-start(f32[128,1024]{1,0:T(8,128)} %refs_10_.1) | copy-start | bytes 1572868
  6.4 43.5 %all-to-all-start = ((bf16[4,192,1024]{2,1,0:T(8,128)(2,1)}), bf16[4,192,1024]{2,1,0:T(8,128)(2,1)}, u32[]{:S(2)}, u32[]{:S(2)}) async-start(bf16[4,192,1024]{2,1,0:T(8,128)(2,1)} %prepare.1), calls=%async_computation | async-start | bytes 3145728 | tf_op jit(solution)/shard_map/all_to_all | solution.py:157
  16.1 7.4 %collective-permute-start = (bf16[160,1024]{1,0:T(8,128)(2,1)}, bf16[160,1024]{1,0:T(8,128)(2,1)}, u32[]{:S(2)}, u32[]{:S(2)}) collective-permute-start(bf16[160,1024]{1,0:T(8,128)(2,1)} %slice_dynamic-update-slice_fusion.refs_0_), channel_id=1, source_target_pairs={{0,4},{1,3},{2,6},{3,1},{4,0},{5,7},{6,2},{7,5},{8,12},{9,11},{10,... | collective-permute-start | bytes 983048 | tf_op jit(solution)/shard_map/ppermute | solution.py:149
  49.9 63.5 %all-to-all-start.1 = ((bf16[4,2,160,1024]{3,2,1,0:T(8,128)(2,1)}), bf16[4,2,160,1024]{3,2,1,0:T(8,128)(2,1)}, u32[]{:S(2)}, u32[]{:S(2)}) async-start(bf16[4,2,160,1024]{3,2,1,0:T(8,128)(2,1)} %stack.6), calls=%async_computation.1 | async-start | bytes 5242880 | tf_op jit(solution)/shard_map/all_to_all | solution.py:157
  54.6 20.7 %collective-permute-start.1 = (bf16[4,192,1024]{2,1,0:T(8,128)(2,1)}, bf16[4,192,1024]{2,1,0:T(8,128)(2,1)S(1)}, u32[]{:S(2)}, u32[]{:S(2)}) collective-permute-start(bf16[4,192,1024]{2,1,0:T(8,128)(2,1)} %all-to-all-done.refs_0_), channel_id=1, source_target_pairs={{0,4},{1,3},{2,6},{3,1},{4,0},{5,7},{6,2},{7,5},{8,12},{9,11},{10,... | collective-permute-start | bytes 4718600 | tf_op jit(solution)/shard_map/ppermute | solution.py:149
  75.3 12.9 %copy-start = (bf16[4,192,1024]{2,1,0:T(8,128)(2,1)}, bf16[4,192,1024]{2,1,0:T(8,128)(2,1)S(1)}, u32[]{:S(2)}) copy-start(bf16[4,192,1024]{2,1,0:T(8,128)(2,1)S(1)} %collective-permute-done.1.refs_1_) | copy-start | bytes 4718596
  75.3 20.6 %collective-permute-start.2 = (bf16[4,192,1024]{2,1,0:T(8,128)(2,1)}, bf16[4,192,1024]{2,1,0:T(8,128)(2,1)S(1)}, u32[]{:S(2)}, u32[]{:S(2)}) collective-permute-start(bf16[4,192,1024]{2,1,0:T(8,128)(2,1)} %all-to-all-done.refs_0_), channel_id=1, source_target_pairs={{0,2},{1,5},{2,0},{3,7},{4,6},{5,1},{6,4},{7,3},{8,10},{9,13},{10,... | collective-permute-start | bytes 4718600 | tf_op jit(solution)/shard_map/ppermute | solution.py:149
  76.8 19.1 %collective-permute-start.4 = (bf16[4,192,1024]{2,1,0:T(8,128)(2,1)}, bf16[4,192,1024]{2,1,0:T(8,128)(2,1)}, u32[]{:S(2)}, u32[]{:S(2)}) collective-permute-start(bf16[4,192,1024]{2,1,0:T(8,128)(2,1)} %all-to-all-done.refs_0_), channel_id=1, source_target_pairs={{0,1},{1,0},{2,3},{3,2},{4,5},{5,4},{6,7},{7,6},{8,9},{9,8},{10,11... | collective-permute-start | bytes 4718600 | tf_op jit(solution)/shard_map/ppermute | solution.py:149
  76.8 36.1 %collective-permute-start.3 = (bf16[4,192,1024]{2,1,0:T(8,128)(2,1)S(1)}, bf16[4,192,1024]{2,1,0:T(8,128)(2,1)}, u32[]{:S(2)}, u32[]{:S(2)}) collective-permute-start(bf16[4,192,1024]{2,1,0:T(8,128)(2,1)S(1)} %collective-permute-done.1.refs_1_), channel_id=1, source_target_pairs={{0,2},{1,5},{2,0},{3,7},{4,6},{5,1},{6,4},{7,3},{8,10},{9,13},{10,... | collective-permute-start | bytes 4718600 | tf_op jit(solution)/shard_map/ppermute | solution.py:149
  77.3 35.6 %collective-permute-start.5 = (bf16[4,192,1024]{2,1,0:T(8,128)(2,1)S(1)}, bf16[4,192,1024]{2,1,0:T(8,128)(2,1)}, u32[]{:S(2)}, u32[]{:S(2)}) collective-permute-start(bf16[4,192,1024]{2,1,0:T(8,128)(2,1)S(1)} %collective-permute-done.1.refs_1_), channel_id=1, source_target_pairs={{0,1},{1,0},{2,3},{3,2},{4,5},{5,4},{6,7},{7,6},{8,9},{9,8},{10,11... | collective-permute-start | bytes 4718600 | tf_op jit(solution)/shard_map/ppermute | solution.py:149
  82.2 7.3 %copy-start.10 = (s32[512]{0:T(512)S(1)}, s32[512]{0:T(512)}, u32[]{:S(2)}) copy-start(s32[512]{0:T(512)} %param.39) | copy-start | bytes 6148
  95.9 17.6 %copy-start.1 = (bf16[4,192,1024]{2,1,0:T(8,128)(2,1)}, bf16[4,192,1024]{2,1,0:T(8,128)(2,1)S(1)}, u32[]{:S(2)}) copy-start(bf16[4,192,1024]{2,1,0:T(8,128)(2,1)S(1)} %collective-permute-done.2.refs_2_) | copy-start | bytes 4718596
  113.5 6.7 %collective-permute-start.7 = (bf16[4,192,1024]{2,1,0:T(8,128)(2,1)S(1)}, bf16[4,192,1024]{2,1,0:T(8,128)(2,1)S(1)}, u32[]{:S(2)}, u32[]{:S(2)}) collective-permute-start(bf16[4,192,1024]{2,1,0:T(8,128)(2,1)S(1)} %collective-permute-done.2.refs_2_), channel_id=1, source_target_pairs={{0,1},{1,0},{2,3},{3,2},{4,5},{5,4},{6,7},{7,6},{8,9},{9,8},{10,11... | collective-permute-start | bytes 4718600 | tf_op jit(solution)/shard_map/ppermute | solution.py:149
  113.5 7.9 %collective-permute-start.8 = (bf16[4,192,1024]{2,1,0:T(8,128)(2,1)}, bf16[4,192,1024]{2,1,0:T(8,128)(2,1)}, u32[]{:S(2)}, u32[]{:S(2)}) collective-permute-start(bf16[4,192,1024]{2,1,0:T(8,128)(2,1)} %collective-permute-done.3.refs_3_), channel_id=1, source_target_pairs={{0,1},{1,0},{2,3},{3,2},{4,5},{5,4},{6,7},{7,6},{8,9},{9,8},{10,11... | collective-permute-start | bytes 4718600 | tf_op jit(solution)/shard_map/ppermute | solution.py:149
  114.0 30.7 %all-to-all-start.2 = ((bf16[4,128,1024]{2,1,0:T(8,128)(2,1)}), bf16[4,128,1024]{2,1,0:T(8,128)(2,1)}, u32[]{:S(2)}, u32[]{:S(2)}) async-start(bf16[4,128,1024]{2,1,0:T(8,128)(2,1)} %bitcast.41), calls=%async_computation.2 | async-start | bytes 2097152 | tf_op jit(solution)/shard_map/all_to_all | solution.py:157
  118.5 42.8 %collective-permute-start.10 = (bf16[8,160,1024]{2,1,0:T(8,128)(2,1)}, bf16[8,160,1024]{2,1,0:T(8,128)(2,1)}, u32[]{:S(2)}, u32[]{:S(2)}) collective-permute-start(bf16[8,160,1024]{2,1,0:T(8,128)(2,1)} %bitcast.10.refs_0_), channel_id=1, source_target_pairs={{0,1},{1,0},{2,3},{3,2},{4,5},{5,4},{6,7},{7,6},{8,9},{9,8},{10,11... | collective-permute-start | bytes 7864328 | tf_op jit(solution)/shard_map/ppermute | solution.py:149
  118.6 42.7 %collective-permute-start.6 = (bf16[8,160,1024]{2,1,0:T(8,128)(2,1)}, bf16[8,160,1024]{2,1,0:T(8,128)(2,1)}, u32[]{:S(2)}, u32[]{:S(2)}) collective-permute-start(bf16[8,160,1024]{2,1,0:T(8,128)(2,1)} %bitcast.10.refs_0_), channel_id=1, source_target_pairs={{0,2},{1,5},{2,0},{3,7},{4,6},{5,1},{6,4},{7,3},{8,10},{9,13},{10,... | collective-permute-start | bytes 7864328 | tf_op jit(solution)/shard_map/ppermute | solution.py:149
  120.2 1.2 copy-start.2
  144.6 16.7 %collective-permute-start.9 = (bf16[4,128,1024]{2,1,0:T(8,128)(2,1)}, bf16[4,128,1024]{2,1,0:T(8,128)(2,1)}, u32[]{:S(2)}, u32[]{:S(2)}) collective-permute-start(bf16[4,128,1024]{2,1,0:T(8,128)(2,1)} %all-to-all-done.2.refs_0_), channel_id=1, source_target_pairs={{0,4},{1,3},{2,6},{3,1},{4,0},{5,7},{6,2},{7,5},{8,12},{9,11},{10,... | collective-permute-start | bytes 3145736 | tf_op jit(solution)/shard_map/ppermute | solution.py:149
  161.3 5.3 %collective-permute-start.15 = (bf16[8,160,1024]{2,1,0:T(8,128)(2,1)}, bf16[8,160,1024]{2,1,0:T(8,128)(2,1)}, u32[]{:S(2)}, u32[]{:S(2)}) collective-permute-start(bf16[8,160,1024]{2,1,0:T(8,128)(2,1)} %collective-permute-done.6.refs_1_), channel_id=1, source_target_pairs={{0,1},{1,0},{2,3},{3,2},{4,5},{5,4},{6,7},{7,6},{8,9},{9,8},{10,11... | collective-permute-start | bytes 7864328 | tf_op jit(solution)/shard_map/ppermute | solution.py:149
  161.7 30.2 %collective-permute-start.11 = (bf16[4,128,1024]{2,1,0:T(8,128)(2,1)}, bf16[4,128,1024]{2,1,0:T(8,128)(2,1)}, u32[]{:S(2)}, u32[]{:S(2)}) collective-permute-start(bf16[4,128,1024]{2,1,0:T(8,128)(2,1)} %all-to-all-done.2.refs_0_), channel_id=1, source_target_pairs={{0,2},{1,5},{2,0},{3,7},{4,6},{5,1},{6,4},{7,3},{8,10},{9,13},{10,... | collective-permute-start | bytes 3145736 | tf_op jit(solution)/shard_map/ppermute | solution.py:149
  163.2 28.7 %collective-permute-start.12 = (bf16[4,128,1024]{2,1,0:T(8,128)(2,1)}, bf16[4,128,1024]{2,1,0:T(8,128)(2,1)}, u32[]{:S(2)}, u32[]{:S(2)}) collective-permute-start(bf16[4,128,1024]{2,1,0:T(8,128)(2,1)} %collective-permute-done.9.refs_1_), channel_id=1, source_target_pairs={{0,2},{1,5},{2,0},{3,7},{4,6},{5,1},{6,4},{7,3},{8,10},{9,13},{10,... | collective-permute-start | bytes 3145736 | tf_op jit(solution)/shard_map/ppermute | solution.py:149
  163.7 28.2 %collective-permute-start.13 = (bf16[4,128,1024]{2,1,0:T(8,128)(2,1)}, bf16[4,128,1024]{2,1,0:T(8,128)(2,1)}, u32[]{:S(2)}, u32[]{:S(2)}) collective-permute-start(bf16[4,128,1024]{2,1,0:T(8,128)(2,1)} %all-to-all-done.2.refs_0_), channel_id=1, source_target_pairs={{0,1},{1,0},{2,3},{3,2},{4,5},{5,4},{6,7},{7,6},{8,9},{9,8},{10,11... | collective-permute-start | bytes 3145736 | tf_op jit(solution)/shard_map/ppermute | solution.py:149
  163.7 28.2 %collective-permute-start.14 = (bf16[4,128,1024]{2,1,0:T(8,128)(2,1)}, bf16[4,128,1024]{2,1,0:T(8,128)(2,1)}, u32[]{:S(2)}, u32[]{:S(2)}) collective-permute-start(bf16[4,128,1024]{2,1,0:T(8,128)(2,1)} %collective-permute-done.9.refs_1_), channel_id=1, source_target_pairs={{0,1},{1,0},{2,3},{3,2},{4,5},{5,4},{6,7},{7,6},{8,9},{9,8},{10,11... | collective-permute-start | bytes 3145736 | tf_op jit(solution)/shard_map/ppermute | solution.py:149
  191.9 3.1 collective-permute-start.16
  192.3 4.1 collective-permute-start.17
  196.5 19.8 %collective-permute-start.18 = (bf16[4096,512]{1,0:T(8,128)(2,1)}, bf16[4096,512]{1,0:T(8,128)(2,1)}, u32[]{:S(2)}, u32[]{:S(2)}) collective-permute-start(bf16[4096,512]{1,0:T(8,128)(2,1)} %get-tuple-element.280.refs_0_), channel_id=1, source_target_pairs={{0,1},{1,0},{2,3},{3,2},{4,5},{5,4},{6,7},{7,6},{8,9},{9,8},{10,11... | collective-permute-start | bytes 12582920 | tf_op jit(solution)/shard_map/ppermute | solution.py:149
  213.2 3.1 collective-permute-start.19
  213.4 35.5 %collective-permute-start.21 = (bf16[1024,512]{1,0:T(8,128)(2,1)}, bf16[1024,512]{1,0:T(8,128)(2,1)}, u32[]{:S(2)}, u32[]{:S(2)}) collective-permute-start(bf16[1024,512]{1,0:T(8,128)(2,1)} %get-tuple-element.300.refs_0_), channel_id=1, source_target_pairs={{0,1},{1,0},{2,3},{3,2},{4,5},{5,4},{6,7},{7,6},{8,9},{9,8},{10,11... | collective-permute-start | bytes 3145736 | tf_op jit(solution)/shard_map/ppermute | solution.py:149
  226.4 29.4 %collective-permute-start.20 = (bf16[8,128,1024]{2,1,0:T(8,128)(2,1)}, bf16[8,128,1024]{2,1,0:T(8,128)(2,1)}, u32[]{:S(2)}, u32[]{:S(2)}) collective-permute-start(bf16[8,128,1024]{2,1,0:T(8,128)(2,1)} %get-tuple-element.283), channel_id=1, source_target_pairs={{0,2},{1,5},{2,0},{3,7},{4,6},{5,1},{6,4},{7,3},{8,10},{9,13},{10,... | collective-permute-start | bytes 6291464 | tf_op jit(solution)/shard_map/ppermute | solution.py:149
  248.3 3.0 collective-permute-start.22
  248.3 4.5 collective-permute-start.23
  248.8 5.5 %collective-permute-start.24 = (bf16[512,1024]{1,0:T(8,128)(2,1)}, bf16[512,1024]{1,0:T(8,128)(2,1)}, u32[]{:S(2)}, u32[]{:S(2)}) collective-permute-start(bf16[512,1024]{1,0:T(8,128)(2,1)} %get-tuple-element.306.refs_6_), channel_id=1, source_target_pairs={{0,1},{1,0},{2,3},{3,2},{4,5},{5,4},{6,7},{7,6},{8,9},{9,8},{10,11... | collective-permute-start | bytes 3145736 | tf_op jit(solution)/shard_map/ppermute | solution.py:149
  248.9 6.9 %collective-permute-start.25 = (bf16[512,1024]{1,0:T(8,128)(2,1)}, bf16[512,1024]{1,0:T(8,128)(2,1)}, u32[]{:S(2)}, u32[]{:S(2)}) collective-permute-start(bf16[512,1024]{1,0:T(8,128)(2,1)} %get-tuple-element.308.refs_8_), channel_id=1, source_target_pairs={{0,1},{1,0},{2,3},{3,2},{4,5},{5,4},{6,7},{7,6},{8,9},{9,8},{10,11... | collective-permute-start | bytes 3145736 | tf_op jit(solution)/shard_map/ppermute | solution.py:149
  251.3 19.7 %collective-permute-start.28 = (bf16[1024,512]{1,0:T(8,128)(2,1)}, bf16[1024,512]{1,0:T(8,128)(2,1)}, u32[]{:S(2)}, u32[]{:S(2)}) collective-permute-start(bf16[1024,512]{1,0:T(8,128)(2,1)} %get-tuple-element.337.refs_2_), channel_id=1, source_target_pairs={{0,1},{1,0},{2,3},{3,2},{4,5},{5,4},{6,7},{7,6},{8,9},{9,8},{10,11... | collective-permute-start | bytes 3145736 | tf_op jit(solution)/shard_map/ppermute | solution.py:149
  259.2 11.8 %collective-permute-start.27 = (bf16[1024,512]{1,0:T(8,128)(2,1)}, bf16[1024,512]{1,0:T(8,128)(2,1)}, u32[]{:S(2)}, u32[]{:S(2)}) collective-permute-start(bf16[1024,512]{1,0:T(8,128)(2,1)} %get-tuple-element.335.refs_0_), channel_id=1, source_target_pairs={{0,1},{1,0},{2,3},{3,2},{4,5},{5,4},{6,7},{7,6},{8,9},{9,8},{10,11... | collective-permute-start | bytes 3145736 | tf_op jit(solution)/shard_map/ppermute | solution.py:149
  259.4 15.1 %collective-permute-start.26 = (bf16[4,128,1024]{2,1,0:T(8,128)(2,1)}, bf16[4,128,1024]{2,1,0:T(8,128)(2,1)}, u32[]{:S(2)}, u32[]{:S(2)}) collective-permute-start(bf16[4,128,1024]{2,1,0:T(8,128)(2,1)} %get-tuple-element.297), channel_id=1, source_target_pairs={{0,4},{1,3},{2,6},{3,1},{4,0},{5,7},{6,2},{7,5},{8,12},{9,11},{10,... | collective-permute-start | bytes 3145736 | tf_op jit(solution)/shard_map/ppermute | solution.py:149
  260.9 13.6 %collective-permute-start.29 = (bf16[512,1024]{1,0:T(8,128)(2,1)}, bf16[512,1024]{1,0:T(8,128)(2,1)}, u32[]{:S(2)}, u32[]{:S(2)}) collective-permute-start(bf16[512,1024]{1,0:T(8,128)(2,1)} %get-tuple-element.339.d_out_ref.refs_4_), channel_id=1, source_target_pairs={{0,1},{1,0},{2,3},{3,2},{4,5},{5,4},{6,7},{7,6},{8,9},{9,8},{10,11... | collective-permute-start | bytes 3145736 | tf_op jit(solution)/shard_map/ppermute | solution.py:149
  277.0 35.4 %collective-permute-start.30 = (bf16[8,128,1024]{2,1,0:T(8,128)(2,1)}, bf16[8,128,1024]{2,1,0:T(8,128)(2,1)}, u32[]{:S(2)}, u32[]{:S(2)}) collective-permute-start(bf16[8,128,1024]{2,1,0:T(8,128)(2,1)} %get-tuple-element.319), channel_id=1, source_target_pairs={{0,2},{1,5},{2,0},{3,7},{4,6},{5,1},{6,4},{7,3},{8,10},{9,13},{10,... | collective-permute-start | bytes 6291464 | tf_op jit(solution)/shard_map/ppermute | solution.py:149
  278.3 34.1 %all-to-all-start.3 = ((bf16[4,128,1024]{2,1,0:T(8,128)(2,1)}), bf16[4,128,1024]{2,1,0:T(8,128)(2,1)}, u32[]{:S(2)}, u32[]{:S(2)}) async-start(bf16[4,128,1024]{2,1,0:T(8,128)(2,1)} %fold.9), calls=%async_computation.3 | async-start | bytes 2097152 | tf_op jit(solution)/shard_map/all_to_all | solution.py:157
  302.1 10.3 %collective-permute-start.31 = (bf16[512,1024]{1,0:T(8,128)(2,1)}, bf16[512,1024]{1,0:T(8,128)(2,1)}, u32[]{:S(2)}, u32[]{:S(2)}) collective-permute-start(bf16[512,1024]{1,0:T(8,128)(2,1)} %get-tuple-element.341.refs_0_.refs_6_), channel_id=1, source_target_pairs={{0,1},{1,0},{2,3},{3,2},{4,5},{5,4},{6,7},{7,6},{8,9},{9,8},{10,11... | collective-permute-start | bytes 3145736 | tf_op jit(solution)/shard_map/ppermute | solution.py:149
  302.1 10.3 %collective-permute-start.32 = (bf16[512,1024]{1,0:T(8,128)(2,1)}, bf16[512,1024]{1,0:T(8,128)(2,1)}, u32[]{:S(2)}, u32[]{:S(2)}) collective-permute-start(bf16[512,1024]{1,0:T(8,128)(2,1)} %get-tuple-element.343.refs_1_.refs_8_), channel_id=1, source_target_pairs={{0,1},{1,0},{2,3},{3,2},{4,5},{5,4},{6,7},{7,6},{8,9},{9,8},{10,11... | collective-permute-start | bytes 3145736 | tf_op jit(solution)/shard_map/ppermute | solution.py:149
  302.6 9.8 %collective-permute-start.33 = (bf16[512,1024]{1,0:T(8,128)(2,1)}, bf16[512,1024]{1,0:T(8,128)(2,1)}, u32[]{:S(2)}, u32[]{:S(2)}) collective-permute-start(bf16[512,1024]{1,0:T(8,128)(2,1)} %get-tuple-element.345.refs_2_.refs_10_), channel_id=1, source_target_pairs={{0,1},{1,0},{2,3},{3,2},{4,5},{5,4},{6,7},{7,6},{8,9},{9,8},{10,11... | collective-permute-start | bytes 3145736 | tf_op jit(solution)/shard_map/ppermute | solution.py:149
  315.8 15.6 %collective-permute-start.35 = (bf16[2048,512]{1,0:T(8,128)(2,1)}, bf16[2048,512]{1,0:T(8,128)(2,1)}, u32[]{:S(2)}, u32[]{:S(2)}) collective-permute-start(bf16[2048,512]{1,0:T(8,128)(2,1)} %get-tuple-element.370.refs_0_), channel_id=1, source_target_pairs={{0,1},{1,0},{2,3},{3,2},{4,5},{5,4},{6,7},{7,6},{8,9},{9,8},{10,11... | collective-permute-start | bytes 6291464 | tf_op jit(solution)/shard_map/ppermute | solution.py:149
  316.3 11.0 %collective-permute-start.36 = (bf16[512,1024]{1,0:T(8,128)(2,1)}, bf16[512,1024]{1,0:T(8,128)(2,1)}, u32[]{:S(2)}, u32[]{:S(2)}) collective-permute-start(bf16[512,1024]{1,0:T(8,128)(2,1)} %get-tuple-element.372.d_ref.refs_2_), channel_id=1, source_target_pairs={{0,1},{1,0},{2,3},{3,2},{4,5},{5,4},{6,7},{7,6},{8,9},{9,8},{10,11... | collective-permute-start | bytes 3145736 | tf_op jit(solution)/shard_map/ppermute | solution.py:149
  316.4 15.1 %collective-permute-start.34 = (bf16[4,128,1024]{2,1,0:T(8,128)(2,1)}, bf16[4,128,1024]{2,1,0:T(8,128)(2,1)}, u32[]{:S(2)}, u32[]{:S(2)}) collective-permute-start(bf16[4,128,1024]{2,1,0:T(8,128)(2,1)} %get-tuple-element.332), channel_id=1, source_target_pairs={{0,4},{1,3},{2,6},{3,1},{4,0},{5,7},{6,2},{7,5},{8,12},{9,11},{10,... | collective-permute-start | bytes 3145736 | tf_op jit(solution)/shard_map/ppermute | solution.py:149
  334.1 26.4 %collective-permute-start.37 = (bf16[8,128,1024]{2,1,0:T(8,128)(2,1)}, bf16[8,128,1024]{2,1,0:T(8,128)(2,1)}, u32[]{:S(2)}, u32[]{:S(2)}) collective-permute-start(bf16[8,128,1024]{2,1,0:T(8,128)(2,1)} %get-tuple-element.355), channel_id=1, source_target_pairs={{0,2},{1,5},{2,0},{3,7},{4,6},{5,1},{6,4},{7,3},{8,10},{9,13},{10,... | collective-permute-start | bytes 6291464 | tf_op jit(solution)/shard_map/ppermute | solution.py:149
  344.6 5.2 %collective-permute-start.38 = (bf16[16,32,1024]{2,1,0:T(8,128)(2,1)}, bf16[16,32,1024]{2,1,0:T(8,128)(2,1)}, u32[]{:S(2)}, u32[]{:S(2)}) collective-permute-start(bf16[16,32,1024]{2,1,0:T(8,128)(2,1)} %grads.8), channel_id=1, source_target_pairs={{0,1},{1,0},{2,3},{3,2},{4,5},{5,4},{6,7},{7,6},{8,9},{9,8},{10,11... | collective-permute-start | bytes 3145736 | tf_op jit(solution)/shard_map/ppermute | solution.py:149
  344.7 31.6 %all-to-all-start.4 = ((bf16[4,128,1024]{2,1,0:T(8,128)(2,1)}), bf16[4,128,1024]{2,1,0:T(8,128)(2,1)}, u32[]{:S(2)}, u32[]{:S(2)}) async-start(bf16[4,128,1024]{2,1,0:T(8,128)(2,1)} %fold.11), calls=%async_computation.4 | async-start | bytes 2097152 | tf_op jit(solution)/shard_map/all_to_all | solution.py:157
  363.9 26.4 %collective-permute-start.40 = (bf16[4,128,1024]{2,1,0:T(8,128)(2,1)}, bf16[4,128,1024]{2,1,0:T(8,128)(2,1)}, u32[]{:S(2)}, u32[]{:S(2)}) collective-permute-start(bf16[4,128,1024]{2,1,0:T(8,128)(2,1)} %get-tuple-element.382), channel_id=1, source_target_pairs={{0,4},{1,3},{2,6},{3,1},{4,0},{5,7},{6,2},{7,5},{8,12},{9,11},{10,... | collective-permute-start | bytes 3145736 | tf_op jit(solution)/shard_map/ppermute | solution.py:149
  364.7 33.2 %collective-permute-start.39 = (bf16[8,96,1024]{2,1,0:T(8,128)(2,1)}, bf16[8,96,1024]{2,1,0:T(8,128)(2,1)}, u32[]{:S(2)}, u32[]{:S(2)}) collective-permute-start(bf16[8,96,1024]{2,1,0:T(8,128)(2,1)} %get-tuple-element.381), channel_id=1, source_target_pairs={{0,2},{1,5},{2,0},{3,7},{4,6},{5,1},{6,4},{7,3},{8,10},{9,13},{10,... | collective-permute-start | bytes 4718600 | tf_op jit(solution)/shard_map/ppermute | solution.py:149
  392.7 25.8 %all-to-all-start.5 = ((bf16[4,128,1024]{2,1,0:T(8,128)(2,1)}), bf16[4,128,1024]{2,1,0:T(8,128)(2,1)}, u32[]{:S(2)}, u32[]{:S(2)}) async-start(bf16[4,128,1024]{2,1,0:T(8,128)(2,1)} %fold.13), calls=%async_computation.5 | async-start | bytes 2097152 | tf_op jit(solution)/shard_map/all_to_all | solution.py:157
  400.8 12.3 %collective-permute-start.41 = (bf16[4,96,1024]{2,1,0:T(8,128)(2,1)}, bf16[4,96,1024]{2,1,0:T(8,128)(2,1)}, u32[]{:S(2)}, u32[]{:S(2)}) collective-permute-start(bf16[4,96,1024]{2,1,0:T(8,128)(2,1)} %get-tuple-element.386), channel_id=1, source_target_pairs={{0,4},{1,3},{2,6},{3,1},{4,0},{5,7},{6,2},{7,5},{8,12},{9,11},{10,... | collective-permute-start | bytes 2359304 | tf_op jit(solution)/shard_map/ppermute | solution.py:149
  420.7 20.0 %all-to-all-start.6 = ((bf16[4,96,1024]{2,1,0:T(8,128)(2,1)}), bf16[4,96,1024]{2,1,0:T(8,128)(2,1)S(1)}, u32[]{:S(2)}, u32[]{:S(2)}) async-start(bf16[4,96,1024]{2,1,0:T(8,128)(2,1)} %fold.15), calls=%async_computation.6 | async-start | bytes 1572864 | tf_op jit(solution)/shard_map/all_to_all | solution.py:157
  426.4 5.2 %copy-start.3 = (f32[128,1024]{1,0:T(8,128)}, f32[128,1024]{1,0:T(8,128)S(1)}, u32[]{:S(2)}) copy-start(f32[128,1024]{1,0:T(8,128)S(1)} %convert_reduce_fusion.refs_3_) | copy-start | bytes 1572868
  428.6 0.8 copy-start.4
  429.4 27.6 %copy-start.11 = (f32[16]{0:T(128)S(1)}, f32[16]{0:T(128)}, u32[]{:S(2)}) copy-start(f32[16]{0:T(128)} %select_reduce_fusion) | copy-start | bytes 196
  431.6 0.8 copy-start.5
  440.9 0.8 copy-start.6

commit v6 on v5

--- a/solution.py
+++ b/solution.py
@@ -26,7 +26,7 @@
 TABLE_AT = 768
 HEAD_AT = 896
 BANDS = 32
-HEADS_AT_ONCE = 4
+HEADS_AT_ONCE = 8
 
 
 def as_low(x):
@@ -1300,8 +1300,8 @@
     if fast:
         turned = both(ffn_turned)
         d_hiddens = both(*d_hidden)
-        moved_0, turned, d_hiddens, d_stream_mid, d_out = join(
-            moved_0, turned, d_hiddens, d_stream_mid, d_out
+        moved_0, turned, d_hiddens[:4], d_stream_mid, d_out = join(
+            moved_0, turned, d_hiddens[:4], d_stream_mid, d_out
         )
         legs_0 = fold([legs_0[0]] + moved_0, near)
         moved_0 = hops(legs_0, "near")

time: 472 us -> 469 us (level)
  waiting for transfers between devices: 146 us -> 141 us
    ppermute x42, waiting for transfers between devices: 97.3 us -> 92.4 us  [shift(): return lax.ppermute(x, AXES, grid.pairs(role, step))]
  transfers between devices with their start and end apart: 49 -> 49, of which waited for: 24 -> 22; matrix products, arithmetic and copies ran while one was open for 5% -> 5% of each run, Pallas kernels for 40% -> 38%
where the time goes in v6:
time: 469 us; the launch traced here: 464 us
  Pallas kernels  207 us (44%)
  waiting for transfers between devices  141 us (30%)
  starting transfers between devices  62 us (13%)
  other arithmetic  17.6 us (4%)
  local copies, waits for them, and re-layouts  13.9 us (3%)
  blocking collectives  11.8 us (3%)
  between operations  10.9 us (2%)
    ppermute x42, waiting for transfers between devices, shift(): return lax.ppermute(x, AXES, grid.pairs(role, step))  92.4 us
    all_to_all x7, waiting for transfers between devices, swap_deep(): return lax.all_to_all(x, AXES, 0, 0, axis_index_groups=grid.lines())  48.1 us
    pallas_call x5, Pallas kernels, grads(): pl.pallas_call(partial(grads_kernel, plan, count, rows, legs, came is not...  41 us
    all_to_all x7, starting transfers between devices, swap_deep(): return lax.all_to_all(x, AXES, 0, 0, axis_index_groups=grid.lines())  34.3 us
    ppermute x42, starting transfers between devices, shift(): return lax.ppermute(x, AXES, grid.pairs(role, step))  27.7 us
    pallas_call x8, Pallas kernels, fold(): pl.pallas_call(partial(fold_kernel, legs), grid=(rows // tile,), in_specs...  23.2 us
    pallas_call x1, Pallas kernels, ffn_back(): pl.pallas_call(partial(ffn_back_kernel, at_gain), grid=(count,), in_specs...  20.4 us
    pallas_call x1, Pallas kernels, expand(): pl.pallas_call(partial(expand_kernel, len(pieces), blocks), grid=(blocks,...  17.4 us
  transfers between devices with their start and end apart: 49, of which 22 were waited for; matrix products, arithmetic and copies ran while one was open for 5% of the time, Pallas kernels for 38%

profile of v6, /device:TPU:0, one launch (start us, length us, event | category | flops | bytes accessed | tf_op | source)
XLA Modules:
  0.0 464.2 jit_solution(14295777637261215867)
XLA Ops:
  3.8 2.5 prepare.1
  6.4 6.5 %all-to-all-start = ((bf16[4,192,1024]{2,1,0:T(8,128)(2,1)}), bf16[4,192,1024]{2,1,0:T(8,128)(2,1)}, u32[]{:S(2)}, u32[]{:S(2)}) async-start(bf16[4,192,1024]{2,1,0:T(8,128)(2,1)} %prepare.1), calls=%async_computation | async-start | bytes 3145728 | tf_op jit(solution)/shard_map/all_to_all | solution.py:157
  16.1 1.5 collective-permute-start
  18.3 2.6 stack.7
  20.9 2.5 collective-permute-done.refs_1_
  23.5 3.4 stack.6
  26.9 23.0 %all-to-all-done.refs_0_ = bf16[4,192,1024]{2,1,0:T(8,128)(2,1)} async-done(((bf16[4,192,1024]{2,1,0:T(8,128)(2,1)}), bf16[4,192,1024]{2,1,0:T(8,128)(2,1)}, u32[]{:S(2)}, u32[]{:S(2)}) %all-to-all-start) | async-done | bytes 1572896 | tf_op jit(solution)/shard_map/all_to_all | solution.py:157
  49.9 4.5 all-to-all-start.1
  54.6 1.6 collective-permute-start.1
  57.5 17.7 %collective-permute-done.1.refs_1_ = bf16[4,192,1024]{2,1,0:T(8,128)(2,1)S(1)} collective-permute-done((bf16[4,192,1024]{2,1,0:T(8,128)(2,1)}, bf16[4,192,1024]{2,1,0:T(8,128)(2,1)S(1)}, u32[]{:S(2)}, u32[]{:S(2)}) %collective-permute-start.1) | collective-permute-done | bytes 1572896 | tf_op jit(solution)/shard_map/ppermute | solution.py:149
  80.4 1.8 copy.103
  82.2 2.3 copy.109
  85.6 1.7 add_convert_fusion
  90.3 5.6 %collective-permute-done.2.refs_2_ = bf16[4,192,1024]{2,1,0:T(8,128)(2,1)S(1)} collective-permute-done((bf16[4,192,1024]{2,1,0:T(8,128)(2,1)}, bf16[4,192,1024]{2,1,0:T(8,128)(2,1)S(1)}, u32[]{:S(2)}, u32[]{:S(2)}) %collective-permute-start.2) | collective-permute-done | bytes 1572896 | tf_op jit(solution)/shard_map/ppermute | solution.py:149
  95.9 17.0 %collective-permute-done.3.refs_3_ = bf16[4,192,1024]{2,1,0:T(8,128)(2,1)} collective-permute-done((bf16[4,192,1024]{2,1,0:T(8,128)(2,1)S(1)}, bf16[4,192,1024]{2,1,0:T(8,128)(2,1)}, u32[]{:S(2)}, u32[]{:S(2)}) %collective-permute-start.3) | collective-permute-done | bytes 1572896 | tf_op jit(solution)/shard_map/ppermute | solution.py:149
  114.0 4.5 all-to-all-start.2
  118.6 1.6 collective-permute-start.6
  121.4 11.4 %front.1 = (bf16[1024,1024]{1,0:T(8,128)(2,1)}, bf16[2048,1024]{1,0:T(8,128)(2,1)}, bf16[512,512]{1,0:T(8,128)(2,1)}, f32[512,1024]{1,0:T(8,128)}, bf16[2048,512...) custom-call(s32[1]{0:T(128)} %copy.124.speaker_ref, ...), custom_call_target="tpu_custom_call" | custom-call | tf_op jit(solution)/shard_map/front/pallas_call | solution.py:455
  132.8 8.2 %pack.1 = (bf16[3,1024,1024]{2,1,0:T(8,128)(2,1)}, bf16[3,512,1024]{2,1,0:T(8,128)(2,1)}) custom-call(s32[16]{0:T(128)} %get-tuple-element.226.own_ref, s32[16]{0:T(128)} %get-tuple-element.227.other_ref, bf16[4,192,1024]{2,1,0:T(8,128)(2,1)} %all-to-all-done.refs_0_, bf16[4,192,1024]{2,1,0:T(8,128)(2,1)} %copy-done, bf16[4,192,1024]{2,1,0:T(8,128)(2,1)} %copy-done.1, ...), custom_call_target="tpu_custom_call" | custom-call | tf_op jit(solution)/shard_map/pack/pallas_call | solution.py:513
  141.0 3.7 all-to-all-done.2.refs_0_
  144.6 1.5 collective-permute-start.9
  146.2 11.9 %attend.1 = (bf16[512,1024]{1,0:T(8,128)(2,1)}, f32[2,8,512]{2,1,0:T(8,128)}) custom-call(s32[1]{0:T(128)} %copy.121.length_ref, f32[16]{0:T(128)} %multiply_power_fusion.slope_ref, bf16[3,512,1024]{2,1,0:T(8,128)(2,1)} %get-tuple-element.312.packed_ref), custom_call_target="tpu_custom_call" | custom-call | tf_op jit(solution)/shard_map/attend/pallas_call | solution.py:223
  158.1 3.2 collective-permute-done.9.refs_1_
  164.2 2.4 collective-permute-done.15.refs_3_
  166.6 7.9 %mid.1 = (bf16[1024,1024]{1,0:T(8,128)(2,1)}, f32[512,1024]{1,0:T(8,128)}, bf16[512,1024]{1,0:T(8,128)(2,1)}, bf16[1024,512]{1,0:T(8,128)(2,1)}, bf16[1024,512]{1,0:T(8,128)(2,1)}) custom-call(s32[16]{0:T(128)} %get-tuple-element.251.own_ref, s32[16]{0:T(128)} %get-tuple-element.252.other_ref, bf16[8,160,1024]{2,1,0:T(8,128)(2,1)} %bitcast.10.refs_0_, ...), custom_call_target="tpu_custom_call" | custom-call | tf_op jit(solution)/shard_map/mid/pallas_call | solution.py:562
  174.4 17.4 %expand.1 = (bf16[4,1024,1024]{2,1,0:T(8,128)(2,1)}, bf16[512,4096]{1,0:T(8,128)(2,1)}, bf16[4096,512]{1,0:T(8,128)(2,1)}, bf16[512,4096]{1,0:T(8,128)(2,1)}) custom-call(s32[16]{0:T(128)} %get-tuple-element.251.own_ref, s32[16]{0:T(128)} %get-tuple-element.252.other_ref, bf16[8,160,1024]{2,1,0:T(8,128)(2,1)} %bitcast.10.refs_0_, ...), custom_call_target="tpu_custom_call" | custom-call | tf_op jit(solution)/shard_map/expand/pallas_call | solution.py:339
  192.5 2.5 collective-permute-done.16.refs_6_
  196.8 16.3 %head.1 = (bf16[4096,1024]{1,0:T(8,128)(2,1)}, f32[512,1024]{1,0:T(8,128)}, bf16[512,1024]{1,0:T(8,128)(2,1)}, f32[1024,80]{1,0:T(8,128)}, f32[1,1024]{1,0:T(1,128)}, /*index=5*/f32[1,1]{1,0:T(1,128)}) custom-call(f32[1,1]{1,0:T(1,128)} %get-tuple-element.248.share_ref, s32[16]{0:T(128)} %get-tuple-element.226.own_ref, s32[16]{0:T(128)} %get-tuple-element.227.other_ref, ...), custom_call_target="tpu_custom_call" | custom-call | tf_op jit(solution)/shard_map/head/pallas_call | solution.py:643
  213.4 2.9 collective-permute-done.19.refs_3_
  216.2 10.1 %grads.5 = (bf16[8,128,1024]{2,1,0:T(8,128)(2,1)}, bf16[8,128,1024]{2,1,0:T(8,128)(2,1)}) custom-call(s32[16]{0:T(128)} %get-tuple-element.274.idx_ref, bf16[4096,512]{1,0:T(8,128)(2,1)} %get-tuple-element.276.refs_0_, bf16[4096,512]{1,0:T(8,128)(2,1)} %collective-permute-done.18.refs_1_, bf16[512,1024]{1,0:T(8,128)(2,1)} %get-tuple-element.281.refs_2_.low_ref, ...), custom_call_target="tpu_custom_call" | custom-call | tf_op jit(solution)/shard_map/grads/pallas_call | solution.py:890
  226.4 1.6 collective-permute-start.20
  227.9 20.4 %ffn_back.1 = (f32[512,1024]{1,0:T(8,128)}, bf16[512,1024]{1,0:T(8,128)(2,1)}, f32[1,1024]{1,0:T(1,128)}, bf16[512,1024]{1,0:T(8,128)(2,1)}, bf16[512,1024]{1,0:...) custom-call(bf16[512,1024]{1,0:T(8,128)(2,1)} %get-tuple-element.281.refs_2_.low_ref, ...), custom_call_target="tpu_custom_call" | custom-call | tf_op jit(solution)/shard_map/ffn_back/pallas_call | solution.py:712
  249.4 2.0 collective-permute-done.22.refs_3_
  253.0 3.8 fold.8
  258.7 10.1 %grads.6 = (bf16[8,128,1024]{2,1,0:T(8,128)(2,1)}, bf16[8,128,1024]{2,1,0:T(8,128)(2,1)}) custom-call(s32[16]{0:T(128)} %get-tuple-element.274.idx_ref, bf16[1024,512]{1,0:T(8,128)(2,1)} %get-tuple-element.294.refs_0_, bf16[1024,512]{1,0:T(8,128)(2,1)} %collective-permute-done.21.refs_1_, bf16[512,1024]{1,0:T(8,128)(2,1)} %get-tuple-element.296.refs_2_, ...), custom_call_target="tpu_custom_call" | custom-call | tf_op jit(solution)/shard_map/grads/pallas_call | solution.py:890
  268.9 3.4 collective-permute-done.24.refs_1_
  272.3 2.5 fold.9
  275.8 5.1 %all-to-all-start.3 = ((bf16[4,128,1024]{2,1,0:T(8,128)(2,1)}), bf16[4,128,1024]{2,1,0:T(8,128)(2,1)}, u32[]{:S(2)}, u32[]{:S(2)}) async-start(bf16[4,128,1024]{2,1,0:T(8,128)(2,1)} %fold.9), calls=%async_computation.3 | async-start | bytes 2097152 | tf_op jit(solution)/shard_map/all_to_all | solution.py:157
  280.9 17.0 %attend_back.1 = (bf16[512,1024]{1,0:T(8,128)(2,1)}, bf16[512,1024]{1,0:T(8,128)(2,1)}, bf16[512,1024]{1,0:T(8,128)(2,1)}) custom-call(s32[1]{0:T(128)} %copy.121.length_ref, f32[16]{0:T(128)} %multiply_power_fusion.slope_ref, bf16[3,512,1024]{2,1,0:T(8,128)(2,1)} %get-tuple-element.312.packed_ref, bf16[512,1024]{1,0:T(8,128)(2,1)} %get-tuple-element.331.d_out_ref.refs_4_, ...), custom_call_target="tpu_custom_call" | custom-call | tf_op jit(solution)/shard_map/attend_back/pallas_call | solution.py:274
  298.5 9.7 %pack_back.1 = (bf16[512,1024]{1,0:T(8,128)(2,1)}, f32[1,1024]{1,0:T(1,128)}) custom-call(bf16[512,1024]{1,0:T(8,128)(2,1)} %get-tuple-element.333.refs_0_.refs_6_, bf16[512,1024]{1,0:T(8,128)(2,1)} %get-tuple-element.335.refs_1_.refs_8_, bf16[512,1024]{1,0:T(8,128)(2,1)} %get-tuple-element.337.refs_2_.refs_10_, ...), custom_call_target="tpu_custom_call" | custom-call | tf_op jit(solution)/shard_map/pack_back/pallas_call | solution.py:759
  308.2 3.4 fold.10
  312.2 1.5 collective-permute-start.34
  313.7 10.3 %grads.7 = (bf16[8,128,1024]{2,1,0:T(8,128)(2,1)}, bf16[8,128,1024]{2,1,0:T(8,128)(2,1)}) custom-call(s32[16]{0:T(128)} %get-tuple-element.274.idx_ref, bf16[1024,512]{1,0:T(8,128)(2,1)} %get-tuple-element.327.refs_0_, bf16[1024,512]{1,0:T(8,128)(2,1)} %collective-permute-done.27.refs_1_, bf16[1024,512]{1,0:T(8,128)(2,1)} %get-tuple-element.329.refs_2_, ...), custom_call_target="tpu_custom_call" | custom-call | tf_op jit(solution)/shard_map/grads/pallas_call | solution.py:890
  324.0 3.3 collective-permute-done.34.refs_1_
  327.3 2.5 fold.11
  330.8 7.1 %tail.1 = (bf16[1024,768]{1,0:T(8,128)(2,1)}, bf16[512,128]{1,0:T(8,128)(2,1)}, bf16[1024,128]{1,0:T(8,128)(2,1)}) custom-call(bf16[512,1024]{1,0:T(8,128)(2,1)} %get-tuple-element.364.d_ref.refs_2_, bf16[2048,1024]{1,0:T(8,128)(2,1)} %get-tuple-element.352.skip_ref, bf16[1024,1024]{1,0:T(8,128)(2,1)} %get-tuple-element.353.small_ref, ...), custom_call_target="tpu_custom_call" | custom-call | tf_op jit(solution)/shard_map/tail/pallas_call | solution.py:804
  337.9 2.6 grads.8
  340.6 5.1 %all-to-all-start.4 = ((bf16[4,128,1024]{2,1,0:T(8,128)(2,1)}), bf16[4,128,1024]{2,1,0:T(8,128)(2,1)}, u32[]{:S(2)}, u32[]{:S(2)}) async-start(bf16[4,128,1024]{2,1,0:T(8,128)(2,1)} %fold.11), calls=%async_computation.4 | async-start | bytes 2097152 | tf_op jit(solution)/shard_map/all_to_all | solution.py:157
  345.7 7.9 %grads.9 = (bf16[8,96,1024]{2,1,0:T(8,128)(2,1)}, bf16[8,96,1024]{2,1,0:T(8,128)(2,1)}) custom-call(s32[16]{0:T(128)} %get-tuple-element.274.idx_ref, bf16[2048,512]{1,0:T(8,128)(2,1)} %get-tuple-element.362.refs_0_, bf16[2048,512]{1,0:T(8,128)(2,1)} %collective-permute-done.35.refs_1_, bf16[512,1024]{1,0:T(8,128)(2,1)} %get-tuple-element.364.d_ref.refs_2_, ...), custom_call_target="tpu_custom_call" | custom-call | tf_op jit(solution)/shard_map/grads/pallas_call | solution.py:890
  353.5 2.6 collective-permute-done.37.refs_1_.refs_3_
  356.1 3.4 fold.12
  359.5 1.5 collective-permute-start.40
  363.6 8.5 %all-to-all-done.4 = bf16[4,128,1024]{2,1,0:T(8,128)(2,1)} async-done(((bf16[4,128,1024]{2,1,0:T(8,128)(2,1)}), bf16[4,128,1024]{2,1,0:T(8,128)(2,1)}, u32[]{:S(2)}, u32[]{:S(2)}) %all-to-all-start.4) | async-done | bytes 1048608 | tf_op jit(solution)/shard_map/all_to_all | solution.py:157
  372.1 13.8 %collective-permute-done.40.refs_1_ = bf16[4,128,1024]{2,1,0:T(8,128)(2,1)} collective-permute-done((bf16[4,128,1024]{2,1,0:T(8,128)(2,1)}, bf16[4,128,1024]{2,1,0:T(8,128)(2,1)}, u32[]{:S(2)}, u32[]{:S(2)}) %collective-permute-start.40) | collective-permute-done | bytes 1048608 | tf_op jit(solution)/shard_map/ppermute | solution.py:149
  385.9 2.4 fold.13
  388.4 5.1 %all-to-all-start.5 = ((bf16[4,128,1024]{2,1,0:T(8,128)(2,1)}), bf16[4,128,1024]{2,1,0:T(8,128)(2,1)}, u32[]{:S(2)}, u32[]{:S(2)}) async-start(bf16[4,128,1024]{2,1,0:T(8,128)(2,1)} %fold.13), calls=%async_computation.5 | async-start | bytes 2097152 | tf_op jit(solution)/shard_map/all_to_all | solution.py:157
  393.5 2.9 fold.14
  397.9 10.8 %collective-permute-done.41.refs_1_ = bf16[4,96,1024]{2,1,0:T(8,128)(2,1)} collective-permute-done((bf16[4,96,1024]{2,1,0:T(8,128)(2,1)}, bf16[4,96,1024]{2,1,0:T(8,128)(2,1)}, u32[]{:S(2)}, u32[]{:S(2)}) %collective-permute-start.41) | collective-permute-done | bytes 786464 | tf_op jit(solution)/shard_map/ppermute | solution.py:149
  408.7 4.8 %all-to-all-done.5 = bf16[4,128,1024]{2,1,0:T(8,128)(2,1)} async-done(((bf16[4,128,1024]{2,1,0:T(8,128)(2,1)}), bf16[4,128,1024]{2,1,0:T(8,128)(2,1)}, u32[]{:S(2)}, u32[]{:S(2)}) %all-to-all-start.5) | async-done | bytes 1048608 | tf_op jit(solution)/shard_map/all_to_all | solution.py:157
  413.5 2.2 fold.15
  415.7 3.5 all-to-all-start.6
  428.1 7.5 %all-to-all-done.6 = bf16[4,96,1024]{2,1,0:T(8,128)(2,1)S(1)} async-done(((bf16[4,96,1024]{2,1,0:T(8,128)(2,1)}), bf16[4,96,1024]{2,1,0:T(8,128)(2,1)S(1)}, u32[]{:S(2)}, u32[]{:S(2)}) %all-to-all-start.6) | async-done | bytes 786464 | tf_op jit(solution)/shard_map/all_to_all | solution.py:157
  439.9 11.8 %all_to_all.41 = f32[32,1,17]{2,1,0:T(1,128)S(1)} all-to-all(f32[32,1,17]{2,1,0:T(1,128)S(1)} %broadcast_in_dim.83), channel_id=1, replica_groups=mesh['wide'=8,'narrow'=4] {'wide','narrow'}, dimensions={0} | all-to-all | bytes 4352 | tf_op jit(solution)/shard_map/all_to_all | solution.py:169
  454.4 7.3 %adam.1 = (f32[32,672]{1,0:T(8,128)}, f32[16,128]{1,0:T(8,128)}, f32[64,1024]{1,0:T(8,128)}, f32[32,3072]{1,0:T(8,128)}, f32[32,1024]{1,0:T(8,128)}, /*index=5*/...) custom-call(f32[1]{0:T(128)} %bitcast.16.clip_ref, ...), custom_call_target="tpu_custom_call" | custom-call | tf_op jit(solution)/shard_map/adam/pallas_call | solution.py:1001
  (155 shorter events, 46.0 us)
Async XLA Ops:
  6.4 6.5 %copy-start.8 = (f32[32,4096]{1,0:T(8,128)S(1)}, f32[32,4096]{1,0:T(8,128)}, u32[]{:S(2)}) copy-start(f32[32,4096]{1,0:T(8,128)} %refs_9_.1) | copy-start | bytes 1572868
  6.4 6.5 %copy-start.9 = (f32[32,1024]{1,0:T(8,128)S(1)}, f32[32,1024]{1,0:T(8,128)}, u32[]{:S(2)}) copy-start(f32[32,1024]{1,0:T(8,128)} %refs_8_.3) | copy-start | bytes 393220
  6.4 11.2 %copy-start.7 = (f32[128,1024]{1,0:T(8,128)S(1)}, f32[128,1024]{1,0:T(8,128)}, u32[]{:S(2)}) copy-start(f32[128,1024]{1,0:T(8,128)} %refs_10_.1) | copy-start | bytes 1572868
  6.4 43.5 %all-to-all-start = ((bf16[4,192,1024]{2,1,0:T(8,128)(2,1)}), bf16[4,192,1024]{2,1,0:T(8,128)(2,1)}, u32[]{:S(2)}, u32[]{:S(2)}) async-start(bf16[4,192,1024]{2,1,0:T(8,128)(2,1)} %prepare.1), calls=%async_computation | async-start | bytes 3145728 | tf_op jit(solution)/shard_map/all_to_all | solution.py:157
  16.1 7.4 %collective-permute-start = (bf16[160,1024]{1,0:T(8,128)(2,1)}, bf16[160,1024]{1,0:T(8,128)(2,1)}, u32[]{:S(2)}, u32[]{:S(2)}) collective-permute-start(bf16[160,1024]{1,0:T(8,128)(2,1)} %slice_dynamic-update-slice_fusion.refs_0_), channel_id=1, source_target_pairs={{0,4},{1,3},{2,6},{3,1},{4,0},{5,7},{6,2},{7,5},{8,12},{9,11},{10,... | collective-permute-start | bytes 983048 | tf_op jit(solution)/shard_map/ppermute | solution.py:149
  49.9 63.5 %all-to-all-start.1 = ((bf16[4,2,160,1024]{3,2,1,0:T(8,128)(2,1)}), bf16[4,2,160,1024]{3,2,1,0:T(8,128)(2,1)}, u32[]{:S(2)}, u32[]{:S(2)}) async-start(bf16[4,2,160,1024]{3,2,1,0:T(8,128)(2,1)} %stack.6), calls=%async_computation.1 | async-start | bytes 5242880 | tf_op jit(solution)/shard_map/all_to_all | solution.py:157
  54.6 20.7 %collective-permute-start.1 = (bf16[4,192,1024]{2,1,0:T(8,128)(2,1)}, bf16[4,192,1024]{2,1,0:T(8,128)(2,1)S(1)}, u32[]{:S(2)}, u32[]{:S(2)}) collective-permute-start(bf16[4,192,1024]{2,1,0:T(8,128)(2,1)} %all-to-all-done.refs_0_), channel_id=1, source_target_pairs={{0,4},{1,3},{2,6},{3,1},{4,0},{5,7},{6,2},{7,5},{8,12},{9,11},{10,... | collective-permute-start | bytes 4718600 | tf_op jit(solution)/shard_map/ppermute | solution.py:149
  75.3 12.9 %copy-start = (bf16[4,192,1024]{2,1,0:T(8,128)(2,1)}, bf16[4,192,1024]{2,1,0:T(8,128)(2,1)S(1)}, u32[]{:S(2)}) copy-start(bf16[4,192,1024]{2,1,0:T(8,128)(2,1)S(1)} %collective-permute-done.1.refs_1_) | copy-start | bytes 4718596
  75.3 20.6 %collective-permute-start.2 = (bf16[4,192,1024]{2,1,0:T(8,128)(2,1)}, bf16[4,192,1024]{2,1,0:T(8,128)(2,1)S(1)}, u32[]{:S(2)}, u32[]{:S(2)}) collective-permute-start(bf16[4,192,1024]{2,1,0:T(8,128)(2,1)} %all-to-all-done.refs_0_), channel_id=1, source_target_pairs={{0,2},{1,5},{2,0},{3,7},{4,6},{5,1},{6,4},{7,3},{8,10},{9,13},{10,... | collective-permute-start | bytes 4718600 | tf_op jit(solution)/shard_map/ppermute | solution.py:149
  76.8 19.1 %collective-permute-start.4 = (bf16[4,192,1024]{2,1,0:T(8,128)(2,1)}, bf16[4,192,1024]{2,1,0:T(8,128)(2,1)}, u32[]{:S(2)}, u32[]{:S(2)}) collective-permute-start(bf16[4,192,1024]{2,1,0:T(8,128)(2,1)} %all-to-all-done.refs_0_), channel_id=1, source_target_pairs={{0,1},{1,0},{2,3},{3,2},{4,5},{5,4},{6,7},{7,6},{8,9},{9,8},{10,11... | collective-permute-start | bytes 4718600 | tf_op jit(solution)/shard_map/ppermute | solution.py:149
  76.8 36.1 %collective-permute-start.3 = (bf16[4,192,1024]{2,1,0:T(8,128)(2,1)S(1)}, bf16[4,192,1024]{2,1,0:T(8,128)(2,1)}, u32[]{:S(2)}, u32[]{:S(2)}) collective-permute-start(bf16[4,192,1024]{2,1,0:T(8,128)(2,1)S(1)} %collective-permute-done.1.refs_1_), channel_id=1, source_target_pairs={{0,2},{1,5},{2,0},{3,7},{4,6},{5,1},{6,4},{7,3},{8,10},{9,13},{10,... | collective-permute-start | bytes 4718600 | tf_op jit(solution)/shard_map/ppermute | solution.py:149
  77.3 35.6 %collective-permute-start.5 = (bf16[4,192,1024]{2,1,0:T(8,128)(2,1)S(1)}, bf16[4,192,1024]{2,1,0:T(8,128)(2,1)}, u32[]{:S(2)}, u32[]{:S(2)}) collective-permute-start(bf16[4,192,1024]{2,1,0:T(8,128)(2,1)S(1)} %collective-permute-done.1.refs_1_), channel_id=1, source_target_pairs={{0,1},{1,0},{2,3},{3,2},{4,5},{5,4},{6,7},{7,6},{8,9},{9,8},{10,11... | collective-permute-start | bytes 4718600 | tf_op jit(solution)/shard_map/ppermute | solution.py:149
  82.2 7.3 %copy-start.10 = (s32[512]{0:T(512)S(1)}, s32[512]{0:T(512)}, u32[]{:S(2)}) copy-start(s32[512]{0:T(512)} %param.39) | copy-start | bytes 6148
  95.9 17.6 %copy-start.1 = (bf16[4,192,1024]{2,1,0:T(8,128)(2,1)}, bf16[4,192,1024]{2,1,0:T(8,128)(2,1)S(1)}, u32[]{:S(2)}) copy-start(bf16[4,192,1024]{2,1,0:T(8,128)(2,1)S(1)} %collective-permute-done.2.refs_2_) | copy-start | bytes 4718596
  113.5 6.7 %collective-permute-start.7 = (bf16[4,192,1024]{2,1,0:T(8,128)(2,1)S(1)}, bf16[4,192,1024]{2,1,0:T(8,128)(2,1)S(1)}, u32[]{:S(2)}, u32[]{:S(2)}) collective-permute-start(bf16[4,192,1024]{2,1,0:T(8,128)(2,1)S(1)} %collective-permute-done.2.refs_2_), channel_id=1, source_target_pairs={{0,1},{1,0},{2,3},{3,2},{4,5},{5,4},{6,7},{7,6},{8,9},{9,8},{10,11... | collective-permute-start | bytes 4718600 | tf_op jit(solution)/shard_map/ppermute | solution.py:149
  113.5 7.9 %collective-permute-start.8 = (bf16[4,192,1024]{2,1,0:T(8,128)(2,1)}, bf16[4,192,1024]{2,1,0:T(8,128)(2,1)}, u32[]{:S(2)}, u32[]{:S(2)}) collective-permute-start(bf16[4,192,1024]{2,1,0:T(8,128)(2,1)} %collective-permute-done.3.refs_3_), channel_id=1, source_target_pairs={{0,1},{1,0},{2,3},{3,2},{4,5},{5,4},{6,7},{7,6},{8,9},{9,8},{10,11... | collective-permute-start | bytes 4718600 | tf_op jit(solution)/shard_map/ppermute | solution.py:149
  114.0 30.7 %all-to-all-start.2 = ((bf16[4,128,1024]{2,1,0:T(8,128)(2,1)}), bf16[4,128,1024]{2,1,0:T(8,128)(2,1)}, u32[]{:S(2)}, u32[]{:S(2)}) async-start(bf16[4,128,1024]{2,1,0:T(8,128)(2,1)} %bitcast.41), calls=%async_computation.2 | async-start | bytes 2097152 | tf_op jit(solution)/shard_map/all_to_all | solution.py:157
  118.5 42.8 %collective-permute-start.10 = (bf16[8,160,1024]{2,1,0:T(8,128)(2,1)}, bf16[8,160,1024]{2,1,0:T(8,128)(2,1)}, u32[]{:S(2)}, u32[]{:S(2)}) collective-permute-start(bf16[8,160,1024]{2,1,0:T(8,128)(2,1)} %bitcast.10.refs_0_), channel_id=1, source_target_pairs={{0,1},{1,0},{2,3},{3,2},{4,5},{5,4},{6,7},{7,6},{8,9},{9,8},{10,11... | collective-permute-start | bytes 7864328 | tf_op jit(solution)/shard_map/ppermute | solution.py:149
  118.6 42.7 %collective-permute-start.6 = (bf16[8,160,1024]{2,1,0:T(8,128)(2,1)}, bf16[8,160,1024]{2,1,0:T(8,128)(2,1)}, u32[]{:S(2)}, u32[]{:S(2)}) collective-permute-start(bf16[8,160,1024]{2,1,0:T(8,128)(2,1)} %bitcast.10.refs_0_), channel_id=1, source_target_pairs={{0,2},{1,5},{2,0},{3,7},{4,6},{5,1},{6,4},{7,3},{8,10},{9,13},{10,... | collective-permute-start | bytes 7864328 | tf_op jit(solution)/shard_map/ppermute | solution.py:149
  120.2 1.2 copy-start.2
  144.6 16.7 %collective-permute-start.9 = (bf16[4,128,1024]{2,1,0:T(8,128)(2,1)}, bf16[4,128,1024]{2,1,0:T(8,128)(2,1)}, u32[]{:S(2)}, u32[]{:S(2)}) collective-permute-start(bf16[4,128,1024]{2,1,0:T(8,128)(2,1)} %all-to-all-done.2.refs_0_), channel_id=1, source_target_pairs={{0,4},{1,3},{2,6},{3,1},{4,0},{5,7},{6,2},{7,5},{8,12},{9,11},{10,... | collective-permute-start | bytes 3145736 | tf_op jit(solution)/shard_map/ppermute | solution.py:149
  161.3 5.3 %collective-permute-start.15 = (bf16[8,160,1024]{2,1,0:T(8,128)(2,1)}, bf16[8,160,1024]{2,1,0:T(8,128)(2,1)}, u32[]{:S(2)}, u32[]{:S(2)}) collective-permute-start(bf16[8,160,1024]{2,1,0:T(8,128)(2,1)} %collective-permute-done.6.refs_1_), channel_id=1, source_target_pairs={{0,1},{1,0},{2,3},{3,2},{4,5},{5,4},{6,7},{7,6},{8,9},{9,8},{10,11... | collective-permute-start | bytes 7864328 | tf_op jit(solution)/shard_map/ppermute | solution.py:149
  161.7 30.2 %collective-permute-start.11 = (bf16[4,128,1024]{2,1,0:T(8,128)(2,1)}, bf16[4,128,1024]{2,1,0:T(8,128)(2,1)}, u32[]{:S(2)}, u32[]{:S(2)}) collective-permute-start(bf16[4,128,1024]{2,1,0:T(8,128)(2,1)} %all-to-all-done.2.refs_0_), channel_id=1, source_target_pairs={{0,2},{1,5},{2,0},{3,7},{4,6},{5,1},{6,4},{7,3},{8,10},{9,13},{10,... | collective-permute-start | bytes 3145736 | tf_op jit(solution)/shard_map/ppermute | solution.py:149
  163.2 28.7 %collective-permute-start.12 = (bf16[4,128,1024]{2,1,0:T(8,128)(2,1)}, bf16[4,128,1024]{2,1,0:T(8,128)(2,1)}, u32[]{:S(2)}, u32[]{:S(2)}) collective-permute-start(bf16[4,128,1024]{2,1,0:T(8,128)(2,1)} %collective-permute-done.9.refs_1_), channel_id=1, source_target_pairs={{0,2},{1,5},{2,0},{3,7},{4,6},{5,1},{6,4},{7,3},{8,10},{9,13},{10,... | collective-permute-start | bytes 3145736 | tf_op jit(solution)/shard_map/ppermute | solution.py:149
  163.7 28.2 %collective-permute-start.13 = (bf16[4,128,1024]{2,1,0:T(8,128)(2,1)}, bf16[4,128,1024]{2,1,0:T(8,128)(2,1)}, u32[]{:S(2)}, u32[]{:S(2)}) collective-permute-start(bf16[4,128,1024]{2,1,0:T(8,128)(2,1)} %all-to-all-done.2.refs_0_), channel_id=1, source_target_pairs={{0,1},{1,0},{2,3},{3,2},{4,5},{5,4},{6,7},{7,6},{8,9},{9,8},{10,11... | collective-permute-start | bytes 3145736 | tf_op jit(solution)/shard_map/ppermute | solution.py:149
  163.7 28.2 %collective-permute-start.14 = (bf16[4,128,1024]{2,1,0:T(8,128)(2,1)}, bf16[4,128,1024]{2,1,0:T(8,128)(2,1)}, u32[]{:S(2)}, u32[]{:S(2)}) collective-permute-start(bf16[4,128,1024]{2,1,0:T(8,128)(2,1)} %collective-permute-done.9.refs_1_), channel_id=1, source_target_pairs={{0,1},{1,0},{2,3},{3,2},{4,5},{5,4},{6,7},{7,6},{8,9},{9,8},{10,11... | collective-permute-start | bytes 3145736 | tf_op jit(solution)/shard_map/ppermute | solution.py:149
  191.9 3.1 collective-permute-start.16
  192.3 4.1 collective-permute-start.17
  196.5 19.8 %collective-permute-start.18 = (bf16[4096,512]{1,0:T(8,128)(2,1)}, bf16[4096,512]{1,0:T(8,128)(2,1)}, u32[]{:S(2)}, u32[]{:S(2)}) collective-permute-start(bf16[4096,512]{1,0:T(8,128)(2,1)} %get-tuple-element.276.refs_0_), channel_id=1, source_target_pairs={{0,1},{1,0},{2,3},{3,2},{4,5},{5,4},{6,7},{7,6},{8,9},{9,8},{10,11... | collective-permute-start | bytes 12582920 | tf_op jit(solution)/shard_map/ppermute | solution.py:149
  213.2 3.1 collective-permute-start.19
  226.4 26.6 %collective-permute-start.20 = (bf16[8,128,1024]{2,1,0:T(8,128)(2,1)}, bf16[8,128,1024]{2,1,0:T(8,128)(2,1)}, u32[]{:S(2)}, u32[]{:S(2)}) collective-permute-start(bf16[8,128,1024]{2,1,0:T(8,128)(2,1)} %get-tuple-element.279), channel_id=1, source_target_pairs={{0,2},{1,5},{2,0},{3,7},{4,6},{5,1},{6,4},{7,3},{8,10},{9,13},{10,... | collective-permute-start | bytes 6291464 | tf_op jit(solution)/shard_map/ppermute | solution.py:149
  227.9 21.4 %collective-permute-start.21 = (bf16[1024,512]{1,0:T(8,128)(2,1)}, bf16[1024,512]{1,0:T(8,128)(2,1)}, u32[]{:S(2)}, u32[]{:S(2)}) collective-permute-start(bf16[1024,512]{1,0:T(8,128)(2,1)} %get-tuple-element.294.refs_0_), channel_id=1, source_target_pairs={{0,1},{1,0},{2,3},{3,2},{4,5},{5,4},{6,7},{7,6},{8,9},{9,8},{10,11... | collective-permute-start | bytes 3145736 | tf_op jit(solution)/shard_map/ppermute | solution.py:149
  248.3 3.1 collective-permute-start.22
  248.8 4.1 collective-permute-start.23
  248.9 9.8 %collective-permute-start.25 = (bf16[512,1024]{1,0:T(8,128)(2,1)}, bf16[512,1024]{1,0:T(8,128)(2,1)}, u32[]{:S(2)}, u32[]{:S(2)}) collective-permute-start(bf16[512,1024]{1,0:T(8,128)(2,1)} %get-tuple-element.300.refs_6_), channel_id=1, source_target_pairs={{0,1},{1,0},{2,3},{3,2},{4,5},{5,4},{6,7},{7,6},{8,9},{9,8},{10,11... | collective-permute-start | bytes 3145736 | tf_op jit(solution)/shard_map/ppermute | solution.py:149
  249.3 19.5 %collective-permute-start.28 = (bf16[1024,512]{1,0:T(8,128)(2,1)}, bf16[1024,512]{1,0:T(8,128)(2,1)}, u32[]{:S(2)}, u32[]{:S(2)}) collective-permute-start(bf16[1024,512]{1,0:T(8,128)(2,1)} %get-tuple-element.329.refs_2_), channel_id=1, source_target_pairs={{0,1},{1,0},{2,3},{3,2},{4,5},{5,4},{6,7},{7,6},{8,9},{9,8},{10,11... | collective-permute-start | bytes 3145736 | tf_op jit(solution)/shard_map/ppermute | solution.py:149
  251.4 7.2 %collective-permute-start.26 = (bf16[512,1024]{1,0:T(8,128)(2,1)}, bf16[512,1024]{1,0:T(8,128)(2,1)}, u32[]{:S(2)}, u32[]{:S(2)}) collective-permute-start(bf16[512,1024]{1,0:T(8,128)(2,1)} %get-tuple-element.301.refs_8_), channel_id=1, source_target_pairs={{0,1},{1,0},{2,3},{3,2},{4,5},{5,4},{6,7},{7,6},{8,9},{9,8},{10,11... | collective-permute-start | bytes 3145736 | tf_op jit(solution)/shard_map/ppermute | solution.py:149
  256.8 12.1 %collective-permute-start.27 = (bf16[1024,512]{1,0:T(8,128)(2,1)}, bf16[1024,512]{1,0:T(8,128)(2,1)}, u32[]{:S(2)}, u32[]{:S(2)}) collective-permute-start(bf16[1024,512]{1,0:T(8,128)(2,1)} %get-tuple-element.327.refs_0_), channel_id=1, source_target_pairs={{0,1},{1,0},{2,3},{3,2},{4,5},{5,4},{6,7},{7,6},{8,9},{9,8},{10,11... | collective-permute-start | bytes 3145736 | tf_op jit(solution)/shard_map/ppermute | solution.py:149
  257.1 15.1 %collective-permute-start.24 = (bf16[4,128,1024]{2,1,0:T(8,128)(2,1)}, bf16[4,128,1024]{2,1,0:T(8,128)(2,1)}, u32[]{:S(2)}, u32[]{:S(2)}) collective-permute-start(bf16[4,128,1024]{2,1,0:T(8,128)(2,1)} %get-tuple-element.291), channel_id=1, source_target_pairs={{0,4},{1,3},{2,6},{3,1},{4,0},{5,7},{6,2},{7,5},{8,12},{9,11},{10,... | collective-permute-start | bytes 3145736 | tf_op jit(solution)/shard_map/ppermute | solution.py:149
  258.7 13.6 %collective-permute-start.29 = (bf16[512,1024]{1,0:T(8,128)(2,1)}, bf16[512,1024]{1,0:T(8,128)(2,1)}, u32[]{:S(2)}, u32[]{:S(2)}) collective-permute-start(bf16[512,1024]{1,0:T(8,128)(2,1)} %get-tuple-element.331.d_out_ref.refs_4_), channel_id=1, source_target_pairs={{0,1},{1,0},{2,3},{3,2},{4,5},{5,4},{6,7},{7,6},{8,9},{9,8},{10,11... | collective-permute-start | bytes 3145736 | tf_op jit(solution)/shard_map/ppermute | solution.py:149
  274.8 33.4 %collective-permute-start.30 = (bf16[8,128,1024]{2,1,0:T(8,128)(2,1)}, bf16[8,128,1024]{2,1,0:T(8,128)(2,1)}, u32[]{:S(2)}, u32[]{:S(2)}) collective-permute-start(bf16[8,128,1024]{2,1,0:T(8,128)(2,1)} %get-tuple-element.311), channel_id=1, source_target_pairs={{0,2},{1,5},{2,0},{3,7},{4,6},{5,1},{6,4},{7,3},{8,10},{9,13},{10,... | collective-permute-start | bytes 6291464 | tf_op jit(solution)/shard_map/ppermute | solution.py:149
  275.8 32.4 %all-to-all-start.3 = ((bf16[4,128,1024]{2,1,0:T(8,128)(2,1)}), bf16[4,128,1024]{2,1,0:T(8,128)(2,1)}, u32[]{:S(2)}, u32[]{:S(2)}) async-start(bf16[4,128,1024]{2,1,0:T(8,128)(2,1)} %fold.9), calls=%async_computation.3 | async-start | bytes 2097152 | tf_op jit(solution)/shard_map/all_to_all | solution.py:157
  297.9 10.3 %collective-permute-start.31 = (bf16[512,1024]{1,0:T(8,128)(2,1)}, bf16[512,1024]{1,0:T(8,128)(2,1)}, u32[]{:S(2)}, u32[]{:S(2)}) collective-permute-start(bf16[512,1024]{1,0:T(8,128)(2,1)} %get-tuple-element.333.refs_0_.refs_6_), channel_id=1, source_target_pairs={{0,1},{1,0},{2,3},{3,2},{4,5},{5,4},{6,7},{7,6},{8,9},{9,8},{10,11... | collective-permute-start | bytes 3145736 | tf_op jit(solution)/shard_map/ppermute | solution.py:149
  297.9 10.3 %collective-permute-start.32 = (bf16[512,1024]{1,0:T(8,128)(2,1)}, bf16[512,1024]{1,0:T(8,128)(2,1)}, u32[]{:S(2)}, u32[]{:S(2)}) collective-permute-start(bf16[512,1024]{1,0:T(8,128)(2,1)} %get-tuple-element.335.refs_1_.refs_8_), channel_id=1, source_target_pairs={{0,1},{1,0},{2,3},{3,2},{4,5},{5,4},{6,7},{7,6},{8,9},{9,8},{10,11... | collective-permute-start | bytes 3145736 | tf_op jit(solution)/shard_map/ppermute | solution.py:149
  298.4 9.8 %collective-permute-start.33 = (bf16[512,1024]{1,0:T(8,128)(2,1)}, bf16[512,1024]{1,0:T(8,128)(2,1)}, u32[]{:S(2)}, u32[]{:S(2)}) collective-permute-start(bf16[512,1024]{1,0:T(8,128)(2,1)} %get-tuple-element.337.refs_2_.refs_10_), channel_id=1, source_target_pairs={{0,1},{1,0},{2,3},{3,2},{4,5},{5,4},{6,7},{7,6},{8,9},{9,8},{10,11... | collective-permute-start | bytes 3145736 | tf_op jit(solution)/shard_map/ppermute | solution.py:149
  311.7 15.6 %collective-permute-start.35 = (bf16[2048,512]{1,0:T(8,128)(2,1)}, bf16[2048,512]{1,0:T(8,128)(2,1)}, u32[]{:S(2)}, u32[]{:S(2)}) collective-permute-start(bf16[2048,512]{1,0:T(8,128)(2,1)} %get-tuple-element.362.refs_0_), channel_id=1, source_target_pairs={{0,1},{1,0},{2,3},{3,2},{4,5},{5,4},{6,7},{7,6},{8,9},{9,8},{10,11... | collective-permute-start | bytes 6291464 | tf_op jit(solution)/shard_map/ppermute | solution.py:149
  312.1 11.9 %collective-permute-start.36 = (bf16[512,1024]{1,0:T(8,128)(2,1)}, bf16[512,1024]{1,0:T(8,128)(2,1)}, u32[]{:S(2)}, u32[]{:S(2)}) collective-permute-start(bf16[512,1024]{1,0:T(8,128)(2,1)} %get-tuple-element.364.d_ref.refs_2_), channel_id=1, source_target_pairs={{0,1},{1,0},{2,3},{3,2},{4,5},{5,4},{6,7},{7,6},{8,9},{9,8},{10,11... | collective-permute-start | bytes 3145736 | tf_op jit(solution)/shard_map/ppermute | solution.py:149
  312.2 15.1 %collective-permute-start.34 = (bf16[4,128,1024]{2,1,0:T(8,128)(2,1)}, bf16[4,128,1024]{2,1,0:T(8,128)(2,1)}, u32[]{:S(2)}, u32[]{:S(2)}) collective-permute-start(bf16[4,128,1024]{2,1,0:T(8,128)(2,1)} %get-tuple-element.324), channel_id=1, source_target_pairs={{0,4},{1,3},{2,6},{3,1},{4,0},{5,7},{6,2},{7,5},{8,12},{9,11},{10,... | collective-permute-start | bytes 3145736 | tf_op jit(solution)/shard_map/ppermute | solution.py:149
  329.8 26.4 %collective-permute-start.37 = (bf16[8,128,1024]{2,1,0:T(8,128)(2,1)}, bf16[8,128,1024]{2,1,0:T(8,128)(2,1)}, u32[]{:S(2)}, u32[]{:S(2)}) collective-permute-start(bf16[8,128,1024]{2,1,0:T(8,128)(2,1)} %get-tuple-element.347), channel_id=1, source_target_pairs={{0,2},{1,5},{2,0},{3,7},{4,6},{5,1},{6,4},{7,3},{8,10},{9,13},{10,... | collective-permute-start | bytes 6291464 | tf_op jit(solution)/shard_map/ppermute | solution.py:149
  340.5 5.2 %collective-permute-start.38 = (bf16[16,32,1024]{2,1,0:T(8,128)(2,1)}, bf16[16,32,1024]{2,1,0:T(8,128)(2,1)}, u32[]{:S(2)}, u32[]{:S(2)}) collective-permute-start(bf16[16,32,1024]{2,1,0:T(8,128)(2,1)} %grads.8), channel_id=1, source_target_pairs={{0,1},{1,0},{2,3},{3,2},{4,5},{5,4},{6,7},{7,6},{8,9},{9,8},{10,11... | collective-permute-start | bytes 3145736 | tf_op jit(solution)/shard_map/ppermute | solution.py:149
  340.6 31.6 %all-to-all-start.4 = ((bf16[4,128,1024]{2,1,0:T(8,128)(2,1)}), bf16[4,128,1024]{2,1,0:T(8,128)(2,1)}, u32[]{:S(2)}, u32[]{:S(2)}) async-start(bf16[4,128,1024]{2,1,0:T(8,128)(2,1)} %fold.11), calls=%async_computation.4 | async-start | bytes 2097152 | tf_op jit(solution)/shard_map/all_to_all | solution.py:157
  359.5 26.4 %collective-permute-start.40 = (bf16[4,128,1024]{2,1,0:T(8,128)(2,1)}, bf16[4,128,1024]{2,1,0:T(8,128)(2,1)}, u32[]{:S(2)}, u32[]{:S(2)}) collective-permute-start(bf16[4,128,1024]{2,1,0:T(8,128)(2,1)} %get-tuple-element.374), channel_id=1, source_target_pairs={{0,4},{1,3},{2,6},{3,1},{4,0},{5,7},{6,2},{7,5},{8,12},{9,11},{10,... | collective-permute-start | bytes 3145736 | tf_op jit(solution)/shard_map/ppermute | solution.py:149
  361.0 32.4 %collective-permute-start.39 = (bf16[8,96,1024]{2,1,0:T(8,128)(2,1)}, bf16[8,96,1024]{2,1,0:T(8,128)(2,1)}, u32[]{:S(2)}, u32[]{:S(2)}) collective-permute-start(bf16[8,96,1024]{2,1,0:T(8,128)(2,1)} %get-tuple-element.373), channel_id=1, source_target_pairs={{0,2},{1,5},{2,0},{3,7},{4,6},{5,1},{6,4},{7,3},{8,10},{9,13},{10,... | collective-permute-start | bytes 4718600 | tf_op jit(solution)/shard_map/ppermute | solution.py:149
  388.4 25.1 %all-to-all-start.5 = ((bf16[4,128,1024]{2,1,0:T(8,128)(2,1)}), bf16[4,128,1024]{2,1,0:T(8,128)(2,1)}, u32[]{:S(2)}, u32[]{:S(2)}) async-start(bf16[4,128,1024]{2,1,0:T(8,128)(2,1)} %fold.13), calls=%async_computation.5 | async-start | bytes 2097152 | tf_op jit(solution)/shard_map/all_to_all | solution.py:157
  396.4 12.3 %collective-permute-start.41 = (bf16[4,96,1024]{2,1,0:T(8,128)(2,1)}, bf16[4,96,1024]{2,1,0:T(8,128)(2,1)}, u32[]{:S(2)}, u32[]{:S(2)}) collective-permute-start(bf16[4,96,1024]{2,1,0:T(8,128)(2,1)} %get-tuple-element.378), channel_id=1, source_target_pairs={{0,4},{1,3},{2,6},{3,1},{4,0},{5,7},{6,2},{7,5},{8,12},{9,11},{10,... | collective-permute-start | bytes 2359304 | tf_op jit(solution)/shard_map/ppermute | solution.py:149
  415.7 19.9 %all-to-all-start.6 = ((bf16[4,96,1024]{2,1,0:T(8,128)(2,1)}), bf16[4,96,1024]{2,1,0:T(8,128)(2,1)S(1)}, u32[]{:S(2)}, u32[]{:S(2)}) async-start(bf16[4,96,1024]{2,1,0:T(8,128)(2,1)} %fold.15), calls=%async_computation.6 | async-start | bytes 1572864 | tf_op jit(solution)/shard_map/all_to_all | solution.py:157
  421.3 5.2 %copy-start.3 = (f32[128,1024]{1,0:T(8,128)}, f32[128,1024]{1,0:T(8,128)S(1)}, u32[]{:S(2)}) copy-start(f32[128,1024]{1,0:T(8,128)S(1)} %convert_reduce_fusion.refs_3_) | copy-start | bytes 1572868
  423.5 0.8 copy-start.4
  424.3 28.8 %copy-start.11 = (f32[16]{0:T(128)S(1)}, f32[16]{0:T(128)}, u32[]{:S(2)}) copy-start(f32[16]{0:T(128)} %select_reduce_fusion) | copy-start | bytes 196
  426.5 0.8 copy-start.5
  435.8 0.8 copy-start.6

commit v7 on v6

--- a/solution.py
+++ b/solution.py
@@ -1300,8 +1300,8 @@
     if fast:
         turned = both(ffn_turned)
         d_hiddens = both(*d_hidden)
-        moved_0, turned, d_hiddens[:4], d_stream_mid, d_out = join(
-            moved_0, turned, d_hiddens[:4], d_stream_mid, d_out
+        moved_0, turned, d_hiddens[:2], d_stream_mid, d_out = join(
+            moved_0, turned, d_hiddens[:2], d_stream_mid, d_out
         )
         legs_0 = fold([legs_0[0]] + moved_0, near)
         moved_0 = hops(legs_0, "near")

time: 469 us -> 468 us (level)
  no operation moved by 1% of the time
where the time goes in v7:
time: 468 us; the launch traced here: 464 us
  Pallas kernels  207 us (44%)
  waiting for transfers between devices  141 us (30%)
  starting transfers between devices  61.6 us (13%)
  other arithmetic  17.6 us (4%)
  local copies, waits for them, and re-layouts  13.9 us (3%)
  blocking collectives  11.5 us (2%)
  between operations  10.9 us (2%)
    ppermute x42, waiting for transfers between devices, shift(): return lax.ppermute(x, AXES, grid.pairs(role, step))  92.8 us
    all_to_all x7, waiting for transfers between devices, swap_deep(): return lax.all_to_all(x, AXES, 0, 0, axis_index_groups=grid.lines())  48.1 us
    pallas_call x5, Pallas kernels, grads(): pl.pallas_call(partial(grads_kernel, plan, count, rows, legs, came is not...  41 us
    all_to_all x7, starting transfers between devices, swap_deep(): return lax.all_to_all(x, AXES, 0, 0, axis_index_groups=grid.lines())  34.3 us
    ppermute x42, starting transfers between devices, shift(): return lax.ppermute(x, AXES, grid.pairs(role, step))  27.3 us
    pallas_call x8, Pallas kernels, fold(): pl.pallas_call(partial(fold_kernel, legs), grid=(rows // tile,), in_specs...  23.2 us
    pallas_call x1, Pallas kernels, ffn_back(): pl.pallas_call(partial(ffn_back_kernel, at_gain), grid=(count,), in_specs...  20.4 us
    pallas_call x1, Pallas kernels, expand(): pl.pallas_call(partial(expand_kernel, len(pieces), blocks), grid=(blocks,...  17.4 us
  transfers between devices with their start and end apart: 49, of which 22 were waited for; matrix products, arithmetic and copies ran while one was open for 5% of the time, Pallas kernels for 38%

profile of v7, /device:TPU:0, one launch (start us, length us, event | category | flops | bytes accessed | tf_op | source)
XLA Modules:
  0.0 463.8 jit_solution(13520632812734588436)
XLA Ops:
  3.8 2.5 prepare.1
  6.4 6.5 %all-to-all-start = ((bf16[4,192,1024]{2,1,0:T(8,128)(2,1)}), bf16[4,192,1024]{2,1,0:T(8,128)(2,1)}, u32[]{:S(2)}, u32[]{:S(2)}) async-start(bf16[4,192,1024]{2,1,0:T(8,128)(2,1)} %prepare.1), calls=%async_computation | async-start | bytes 3145728 | tf_op jit(solution)/shard_map/all_to_all | solution.py:157
  16.1 1.5 collective-permute-start
  18.3 2.6 stack.7
  20.9 2.5 collective-permute-done.refs_1_
  23.5 3.4 stack.6
  26.9 23.0 %all-to-all-done.refs_0_ = bf16[4,192,1024]{2,1,0:T(8,128)(2,1)} async-done(((bf16[4,192,1024]{2,1,0:T(8,128)(2,1)}), bf16[4,192,1024]{2,1,0:T(8,128)(2,1)}, u32[]{:S(2)}, u32[]{:S(2)}) %all-to-all-start) | async-done | bytes 1572896 | tf_op jit(solution)/shard_map/all_to_all | solution.py:157
  49.9 4.5 all-to-all-start.1
  54.6 1.6 collective-permute-start.1
  57.5 17.7 %collective-permute-done.1.refs_1_ = bf16[4,192,1024]{2,1,0:T(8,128)(2,1)S(1)} collective-permute-done((bf16[4,192,1024]{2,1,0:T(8,128)(2,1)}, bf16[4,192,1024]{2,1,0:T(8,128)(2,1)S(1)}, u32[]{:S(2)}, u32[]{:S(2)}) %collective-permute-start.1) | collective-permute-done | bytes 1572896 | tf_op jit(solution)/shard_map/ppermute | solution.py:149
  80.4 1.8 copy.103
  82.2 2.3 copy.109
  85.6 1.7 add_convert_fusion
  90.3 5.6 %collective-permute-done.2.refs_2_ = bf16[4,192,1024]{2,1,0:T(8,128)(2,1)S(1)} collective-permute-done((bf16[4,192,1024]{2,1,0:T(8,128)(2,1)}, bf16[4,192,1024]{2,1,0:T(8,128)(2,1)S(1)}, u32[]{:S(2)}, u32[]{:S(2)}) %collective-permute-start.2) | collective-permute-done | bytes 1572896 | tf_op jit(solution)/shard_map/ppermute | solution.py:149
  95.9 17.0 %collective-permute-done.3.refs_3_ = bf16[4,192,1024]{2,1,0:T(8,128)(2,1)} collective-permute-done((bf16[4,192,1024]{2,1,0:T(8,128)(2,1)S(1)}, bf16[4,192,1024]{2,1,0:T(8,128)(2,1)}, u32[]{:S(2)}, u32[]{:S(2)}) %collective-permute-start.3) | collective-permute-done | bytes 1572896 | tf_op jit(solution)/shard_map/ppermute | solution.py:149
  114.0 4.5 all-to-all-start.2
  118.6 1.6 collective-permute-start.6
  121.4 11.4 %front.1 = (bf16[1024,1024]{1,0:T(8,128)(2,1)}, bf16[2048,1024]{1,0:T(8,128)(2,1)}, bf16[512,512]{1,0:T(8,128)(2,1)}, f32[512,1024]{1,0:T(8,128)}, bf16[2048,512...) custom-call(s32[1]{0:T(128)} %copy.124.speaker_ref, ...), custom_call_target="tpu_custom_call" | custom-call | tf_op jit(solution)/shard_map/front/pallas_call | solution.py:455
  132.8 8.2 %pack.1 = (bf16[3,1024,1024]{2,1,0:T(8,128)(2,1)}, bf16[3,512,1024]{2,1,0:T(8,128)(2,1)}) custom-call(s32[16]{0:T(128)} %get-tuple-element.224.own_ref, s32[16]{0:T(128)} %get-tuple-element.225.other_ref, bf16[4,192,1024]{2,1,0:T(8,128)(2,1)} %all-to-all-done.refs_0_, bf16[4,192,1024]{2,1,0:T(8,128)(2,1)} %copy-done, bf16[4,192,1024]{2,1,0:T(8,128)(2,1)} %copy-done.1, ...), custom_call_target="tpu_custom_call" | custom-call | tf_op jit(solution)/shard_map/pack/pallas_call | solution.py:513
  141.0 3.7 all-to-all-done.2.refs_0_
  144.6 1.5 collective-permute-start.9
  146.2 11.9 %attend.1 = (bf16[512,1024]{1,0:T(8,128)(2,1)}, f32[2,8,512]{2,1,0:T(8,128)}) custom-call(s32[1]{0:T(128)} %copy.121.length_ref, f32[16]{0:T(128)} %multiply_power_fusion.slope_ref, bf16[3,512,1024]{2,1,0:T(8,128)(2,1)} %get-tuple-element.308.packed_ref), custom_call_target="tpu_custom_call" | custom-call | tf_op jit(solution)/shard_map/attend/pallas_call | solution.py:223
  158.1 3.2 collective-permute-done.9.refs_1_
  164.2 2.4 collective-permute-done.15.refs_3_
  166.6 7.9 %mid.1 = (bf16[1024,1024]{1,0:T(8,128)(2,1)}, f32[512,1024]{1,0:T(8,128)}, bf16[512,1024]{1,0:T(8,128)(2,1)}, bf16[1024,512]{1,0:T(8,128)(2,1)}, bf16[1024,512]{1,0:T(8,128)(2,1)}) custom-call(s32[16]{0:T(128)} %get-tuple-element.249.own_ref, s32[16]{0:T(128)} %get-tuple-element.250.other_ref, bf16[8,160,1024]{2,1,0:T(8,128)(2,1)} %bitcast.10.refs_0_, ...), custom_call_target="tpu_custom_call" | custom-call | tf_op jit(solution)/shard_map/mid/pallas_call | solution.py:562
  174.4 17.4 %expand.1 = (bf16[4,1024,1024]{2,1,0:T(8,128)(2,1)}, bf16[512,4096]{1,0:T(8,128)(2,1)}, bf16[4096,512]{1,0:T(8,128)(2,1)}, bf16[512,4096]{1,0:T(8,128)(2,1)}) custom-call(s32[16]{0:T(128)} %get-tuple-element.249.own_ref, s32[16]{0:T(128)} %get-tuple-element.250.other_ref, bf16[8,160,1024]{2,1,0:T(8,128)(2,1)} %bitcast.10.refs_0_, ...), custom_call_target="tpu_custom_call" | custom-call | tf_op jit(solution)/shard_map/expand/pallas_call | solution.py:339
  192.5 2.5 collective-permute-done.16.refs_6_
  196.8 16.3 %head.1 = (bf16[4096,1024]{1,0:T(8,128)(2,1)}, f32[512,1024]{1,0:T(8,128)}, bf16[512,1024]{1,0:T(8,128)(2,1)}, f32[1024,80]{1,0:T(8,128)}, f32[1,1024]{1,0:T(1,128)}, /*index=5*/f32[1,1]{1,0:T(1,128)}) custom-call(f32[1,1]{1,0:T(1,128)} %get-tuple-element.246.share_ref, s32[16]{0:T(128)} %get-tuple-element.224.own_ref, s32[16]{0:T(128)} %get-tuple-element.225.other_ref, ...), custom_call_target="tpu_custom_call" | custom-call | tf_op jit(solution)/shard_map/head/pallas_call | solution.py:643
  213.4 2.9 collective-permute-done.19.refs_3_
  216.2 10.1 %grads.5 = (bf16[8,128,1024]{2,1,0:T(8,128)(2,1)}, bf16[8,128,1024]{2,1,0:T(8,128)(2,1)}) custom-call(s32[16]{0:T(128)} %get-tuple-element.272.idx_ref, bf16[4096,512]{1,0:T(8,128)(2,1)} %get-tuple-element.274.refs_0_, bf16[4096,512]{1,0:T(8,128)(2,1)} %collective-permute-done.18.refs_1_, bf16[512,1024]{1,0:T(8,128)(2,1)} %get-tuple-element.279.refs_2_.low_ref, ...), custom_call_target="tpu_custom_call" | custom-call | tf_op jit(solution)/shard_map/grads/pallas_call | solution.py:890
  226.4 1.6 collective-permute-start.20
  227.9 20.4 %ffn_back.1 = (f32[512,1024]{1,0:T(8,128)}, bf16[512,1024]{1,0:T(8,128)(2,1)}, f32[1,1024]{1,0:T(1,128)}, bf16[512,1024]{1,0:T(8,128)(2,1)}, bf16[512,1024]{1,0:...) custom-call(bf16[512,1024]{1,0:T(8,128)(2,1)} %get-tuple-element.279.refs_2_.low_ref, ...), custom_call_target="tpu_custom_call" | custom-call | tf_op jit(solution)/shard_map/ffn_back/pallas_call | solution.py:712
  249.4 2.0 collective-permute-done.22.refs_3_
  252.8 3.8 fold.8
  256.6 1.6 collective-permute-start.23
  258.3 10.1 %grads.6 = (bf16[8,128,1024]{2,1,0:T(8,128)(2,1)}, bf16[8,128,1024]{2,1,0:T(8,128)(2,1)}) custom-call(s32[16]{0:T(128)} %get-tuple-element.272.idx_ref, bf16[1024,512]{1,0:T(8,128)(2,1)} %get-tuple-element.291.refs_0_, bf16[1024,512]{1,0:T(8,128)(2,1)} %collective-permute-done.21.refs_1_, bf16[512,1024]{1,0:T(8,128)(2,1)} %get-tuple-element.293.refs_2_, ...), custom_call_target="tpu_custom_call" | custom-call | tf_op jit(solution)/shard_map/grads/pallas_call | solution.py:890
  268.5 3.3 collective-permute-done.23.refs_1_
  271.8 2.5 fold.9
  275.8 5.1 %all-to-all-start.3 = ((bf16[4,128,1024]{2,1,0:T(8,128)(2,1)}), bf16[4,128,1024]{2,1,0:T(8,128)(2,1)}, u32[]{:S(2)}, u32[]{:S(2)}) async-start(bf16[4,128,1024]{2,1,0:T(8,128)(2,1)} %fold.9), calls=%async_computation.3 | async-start | bytes 2097152 | tf_op jit(solution)/shard_map/all_to_all | solution.py:157
  280.9 17.0 %attend_back.1 = (bf16[512,1024]{1,0:T(8,128)(2,1)}, bf16[512,1024]{1,0:T(8,128)(2,1)}, bf16[512,1024]{1,0:T(8,128)(2,1)}) custom-call(s32[1]{0:T(128)} %copy.121.length_ref, f32[16]{0:T(128)} %multiply_power_fusion.slope_ref, bf16[3,512,1024]{2,1,0:T(8,128)(2,1)} %get-tuple-element.308.packed_ref, bf16[512,1024]{1,0:T(8,128)(2,1)} %get-tuple-element.327.d_out_ref.refs_4_, ...), custom_call_target="tpu_custom_call" | custom-call | tf_op jit(solution)/shard_map/attend_back/pallas_call | solution.py:274
  298.5 9.7 %pack_back.1 = (bf16[512,1024]{1,0:T(8,128)(2,1)}, f32[1,1024]{1,0:T(1,128)}) custom-call(bf16[512,1024]{1,0:T(8,128)(2,1)} %get-tuple-element.329.refs_0_.refs_6_, bf16[512,1024]{1,0:T(8,128)(2,1)} %get-tuple-element.331.refs_1_.refs_8_, bf16[512,1024]{1,0:T(8,128)(2,1)} %get-tuple-element.333.refs_2_.refs_10_, ...), custom_call_target="tpu_custom_call" | custom-call | tf_op jit(solution)/shard_map/pack_back/pallas_call | solution.py:759
  308.2 3.4 fold.10
  312.2 1.5 collective-permute-start.34
  313.7 10.3 %grads.7 = (bf16[8,128,1024]{2,1,0:T(8,128)(2,1)}, bf16[8,128,1024]{2,1,0:T(8,128)(2,1)}) custom-call(s32[16]{0:T(128)} %get-tuple-element.272.idx_ref, bf16[1024,512]{1,0:T(8,128)(2,1)} %get-tuple-element.323.refs_0_, bf16[1024,512]{1,0:T(8,128)(2,1)} %collective-permute-done.27.refs_1_, bf16[1024,512]{1,0:T(8,128)(2,1)} %get-tuple-element.325.refs_2_, ...), custom_call_target="tpu_custom_call" | custom-call | tf_op jit(solution)/shard_map/grads/pallas_call | solution.py:890
  324.0 3.3 collective-permute-done.34.refs_1_
  327.3 2.5 fold.11
  330.3 7.1 %tail.1 = (bf16[1024,768]{1,0:T(8,128)(2,1)}, bf16[512,128]{1,0:T(8,128)(2,1)}, bf16[1024,128]{1,0:T(8,128)(2,1)}) custom-call(bf16[512,1024]{1,0:T(8,128)(2,1)} %get-tuple-element.360.d_ref.refs_2_, bf16[2048,1024]{1,0:T(8,128)(2,1)} %get-tuple-element.348.skip_ref, bf16[1024,1024]{1,0:T(8,128)(2,1)} %get-tuple-element.349.small_ref, ...), custom_call_target="tpu_custom_call" | custom-call | tf_op jit(solution)/shard_map/tail/pallas_call | solution.py:804
  337.4 2.6 grads.8
  340.4 5.1 %all-to-all-start.4 = ((bf16[4,128,1024]{2,1,0:T(8,128)(2,1)}), bf16[4,128,1024]{2,1,0:T(8,128)(2,1)}, u32[]{:S(2)}, u32[]{:S(2)}) async-start(bf16[4,128,1024]{2,1,0:T(8,128)(2,1)} %fold.11), calls=%async_computation.4 | async-start | bytes 2097152 | tf_op jit(solution)/shard_map/all_to_all | solution.py:157
  345.4 7.9 %grads.9 = (bf16[8,96,1024]{2,1,0:T(8,128)(2,1)}, bf16[8,96,1024]{2,1,0:T(8,128)(2,1)}) custom-call(s32[16]{0:T(128)} %get-tuple-element.272.idx_ref, bf16[2048,512]{1,0:T(8,128)(2,1)} %get-tuple-element.358.refs_0_, bf16[2048,512]{1,0:T(8,128)(2,1)} %collective-permute-done.35.refs_1_, bf16[512,1024]{1,0:T(8,128)(2,1)} %get-tuple-element.360.d_ref.refs_2_, ...), custom_call_target="tpu_custom_call" | custom-call | tf_op jit(solution)/shard_map/grads/pallas_call | solution.py:890
  353.3 2.8 collective-permute-done.37.refs_1_.refs_3_
  356.1 3.4 fold.12
  363.2 8.5 %all-to-all-done.4 = bf16[4,128,1024]{2,1,0:T(8,128)(2,1)} async-done(((bf16[4,128,1024]{2,1,0:T(8,128)(2,1)}), bf16[4,128,1024]{2,1,0:T(8,128)(2,1)}, u32[]{:S(2)}, u32[]{:S(2)}) %all-to-all-start.4) | async-done | bytes 1048608 | tf_op jit(solution)/shard_map/all_to_all | solution.py:157
  371.7 14.3 %collective-permute-done.40.refs_1_ = bf16[4,128,1024]{2,1,0:T(8,128)(2,1)} collective-permute-done((bf16[4,128,1024]{2,1,0:T(8,128)(2,1)}, bf16[4,128,1024]{2,1,0:T(8,128)(2,1)}, u32[]{:S(2)}, u32[]{:S(2)}) %collective-permute-start.40) | collective-permute-done | bytes 1048608 | tf_op jit(solution)/shard_map/ppermute | solution.py:149
  385.9 2.4 fold.13
  388.4 5.1 %all-to-all-start.5 = ((bf16[4,128,1024]{2,1,0:T(8,128)(2,1)}), bf16[4,128,1024]{2,1,0:T(8,128)(2,1)}, u32[]{:S(2)}, u32[]{:S(2)}) async-start(bf16[4,128,1024]{2,1,0:T(8,128)(2,1)} %fold.13), calls=%async_computation.5 | async-start | bytes 2097152 | tf_op jit(solution)/shard_map/all_to_all | solution.py:157
  393.5 2.9 fold.14
  397.9 10.8 %collective-permute-done.41.refs_1_ = bf16[4,96,1024]{2,1,0:T(8,128)(2,1)} collective-permute-done((bf16[4,96,1024]{2,1,0:T(8,128)(2,1)}, bf16[4,96,1024]{2,1,0:T(8,128)(2,1)}, u32[]{:S(2)}, u32[]{:S(2)}) %collective-permute-start.41) | collective-permute-done | bytes 786464 | tf_op jit(solution)/shard_map/ppermute | solution.py:149
  408.7 4.8 %all-to-all-done.5 = bf16[4,128,1024]{2,1,0:T(8,128)(2,1)} async-done(((bf16[4,128,1024]{2,1,0:T(8,128)(2,1)}), bf16[4,128,1024]{2,1,0:T(8,128)(2,1)}, u32[]{:S(2)}, u32[]{:S(2)}) %all-to-all-start.5) | async-done | bytes 1048608 | tf_op jit(solution)/shard_map/all_to_all | solution.py:157
  413.5 2.2 fold.15
  415.7 3.5 all-to-all-start.6
  428.1 7.5 %all-to-all-done.6 = bf16[4,96,1024]{2,1,0:T(8,128)(2,1)S(1)} async-done(((bf16[4,96,1024]{2,1,0:T(8,128)(2,1)}), bf16[4,96,1024]{2,1,0:T(8,128)(2,1)S(1)}, u32[]{:S(2)}, u32[]{:S(2)}) %all-to-all-start.6) | async-done | bytes 786464 | tf_op jit(solution)/shard_map/all_to_all | solution.py:157
  439.9 11.5 %all_to_all.41 = f32[32,1,17]{2,1,0:T(1,128)S(1)} all-to-all(f32[32,1,17]{2,1,0:T(1,128)S(1)} %broadcast_in_dim.83), channel_id=1, replica_groups=mesh['wide'=8,'narrow'=4] {'wide','narrow'}, dimensions={0} | all-to-all | bytes 4352 | tf_op jit(solution)/shard_map/all_to_all | solution.py:169
  454.0 7.3 %adam.1 = (f32[32,672]{1,0:T(8,128)}, f32[16,128]{1,0:T(8,128)}, f32[64,1024]{1,0:T(8,128)}, f32[32,3072]{1,0:T(8,128)}, f32[32,1024]{1,0:T(8,128)}, /*index=5*/...) custom-call(f32[1]{0:T(128)} %bitcast.16.clip_ref, ...), custom_call_target="tpu_custom_call" | custom-call | tf_op jit(solution)/shard_map/adam/pallas_call | solution.py:1001
  (155 shorter events, 45.4 us)
Async XLA Ops:
  6.4 6.5 %copy-start.8 = (f32[32,4096]{1,0:T(8,128)S(1)}, f32[32,4096]{1,0:T(8,128)}, u32[]{:S(2)}) copy-start(f32[32,4096]{1,0:T(8,128)} %refs_9_.1) | copy-start | bytes 1572868
  6.4 6.5 %copy-start.9 = (f32[32,1024]{1,0:T(8,128)S(1)}, f32[32,1024]{1,0:T(8,128)}, u32[]{:S(2)}) copy-start(f32[32,1024]{1,0:T(8,128)} %refs_8_.3) | copy-start | bytes 393220
  6.4 11.2 %copy-start.7 = (f32[128,1024]{1,0:T(8,128)S(1)}, f32[128,1024]{1,0:T(8,128)}, u32[]{:S(2)}) copy-start(f32[128,1024]{1,0:T(8,128)} %refs_10_.1) | copy-start | bytes 1572868
  6.4 43.5 %all-to-all-start = ((bf16[4,192,1024]{2,1,0:T(8,128)(2,1)}), bf16[4,192,1024]{2,1,0:T(8,128)(2,1)}, u32[]{:S(2)}, u32[]{:S(2)}) async-start(bf16[4,192,1024]{2,1,0:T(8,128)(2,1)} %prepare.1), calls=%async_computation | async-start | bytes 3145728 | tf_op jit(solution)/shard_map/all_to_all | solution.py:157
  16.1 7.4 %collective-permute-start = (bf16[160,1024]{1,0:T(8,128)(2,1)}, bf16[160,1024]{1,0:T(8,128)(2,1)}, u32[]{:S(2)}, u32[]{:S(2)}) collective-permute-start(bf16[160,1024]{1,0:T(8,128)(2,1)} %slice_dynamic-update-slice_fusion.refs_0_), channel_id=1, source_target_pairs={{0,4},{1,3},{2,6},{3,1},{4,0},{5,7},{6,2},{7,5},{8,12},{9,11},{10,... | collective-permute-start | bytes 983048 | tf_op jit(solution)/shard_map/ppermute | solution.py:149
  49.9 63.5 %all-to-all-start.1 = ((bf16[4,2,160,1024]{3,2,1,0:T(8,128)(2,1)}), bf16[4,2,160,1024]{3,2,1,0:T(8,128)(2,1)}, u32[]{:S(2)}, u32[]{:S(2)}) async-start(bf16[4,2,160,1024]{3,2,1,0:T(8,128)(2,1)} %stack.6), calls=%async_computation.1 | async-start | bytes 5242880 | tf_op jit(solution)/shard_map/all_to_all | solution.py:157
  54.6 20.7 %collective-permute-start.1 = (bf16[4,192,1024]{2,1,0:T(8,128)(2,1)}, bf16[4,192,1024]{2,1,0:T(8,128)(2,1)S(1)}, u32[]{:S(2)}, u32[]{:S(2)}) collective-permute-start(bf16[4,192,1024]{2,1,0:T(8,128)(2,1)} %all-to-all-done.refs_0_), channel_id=1, source_target_pairs={{0,4},{1,3},{2,6},{3,1},{4,0},{5,7},{6,2},{7,5},{8,12},{9,11},{10,... | collective-permute-start | bytes 4718600 | tf_op jit(solution)/shard_map/ppermute | solution.py:149
  75.3 12.9 %copy-start = (bf16[4,192,1024]{2,1,0:T(8,128)(2,1)}, bf16[4,192,1024]{2,1,0:T(8,128)(2,1)S(1)}, u32[]{:S(2)}) copy-start(bf16[4,192,1024]{2,1,0:T(8,128)(2,1)S(1)} %collective-permute-done.1.refs_1_) | copy-start | bytes 4718596
  75.3 20.6 %collective-permute-start.2 = (bf16[4,192,1024]{2,1,0:T(8,128)(2,1)}, bf16[4,192,1024]{2,1,0:T(8,128)(2,1)S(1)}, u32[]{:S(2)}, u32[]{:S(2)}) collective-permute-start(bf16[4,192,1024]{2,1,0:T(8,128)(2,1)} %all-to-all-done.refs_0_), channel_id=1, source_target_pairs={{0,2},{1,5},{2,0},{3,7},{4,6},{5,1},{6,4},{7,3},{8,10},{9,13},{10,... | collective-permute-start | bytes 4718600 | tf_op jit(solution)/shard_map/ppermute | solution.py:149
  76.8 19.1 %collective-permute-start.4 = (bf16[4,192,1024]{2,1,0:T(8,128)(2,1)}, bf16[4,192,1024]{2,1,0:T(8,128)(2,1)}, u32[]{:S(2)}, u32[]{:S(2)}) collective-permute-start(bf16[4,192,1024]{2,1,0:T(8,128)(2,1)} %all-to-all-done.refs_0_), channel_id=1, source_target_pairs={{0,1},{1,0},{2,3},{3,2},{4,5},{5,4},{6,7},{7,6},{8,9},{9,8},{10,11... | collective-permute-start | bytes 4718600 | tf_op jit(solution)/shard_map/ppermute | solution.py:149
  76.8 36.1 %collective-permute-start.3 = (bf16[4,192,1024]{2,1,0:T(8,128)(2,1)S(1)}, bf16[4,192,1024]{2,1,0:T(8,128)(2,1)}, u32[]{:S(2)}, u32[]{:S(2)}) collective-permute-start(bf16[4,192,1024]{2,1,0:T(8,128)(2,1)S(1)} %collective-permute-done.1.refs_1_), channel_id=1, source_target_pairs={{0,2},{1,5},{2,0},{3,7},{4,6},{5,1},{6,4},{7,3},{8,10},{9,13},{10,... | collective-permute-start | bytes 4718600 | tf_op jit(solution)/shard_map/ppermute | solution.py:149
  77.3 35.6 %collective-permute-start.5 = (bf16[4,192,1024]{2,1,0:T(8,128)(2,1)S(1)}, bf16[4,192,1024]{2,1,0:T(8,128)(2,1)}, u32[]{:S(2)}, u32[]{:S(2)}) collective-permute-start(bf16[4,192,1024]{2,1,0:T(8,128)(2,1)S(1)} %collective-permute-done.1.refs_1_), channel_id=1, source_target_pairs={{0,1},{1,0},{2,3},{3,2},{4,5},{5,4},{6,7},{7,6},{8,9},{9,8},{10,11... | collective-permute-start | bytes 4718600 | tf_op jit(solution)/shard_map/ppermute | solution.py:149
  82.2 7.3 %copy-start.10 = (s32[512]{0:T(512)S(1)}, s32[512]{0:T(512)}, u32[]{:S(2)}) copy-start(s32[512]{0:T(512)} %param.39) | copy-start | bytes 6148
  95.9 17.6 %copy-start.1 = (bf16[4,192,1024]{2,1,0:T(8,128)(2,1)}, bf16[4,192,1024]{2,1,0:T(8,128)(2,1)S(1)}, u32[]{:S(2)}) copy-start(bf16[4,192,1024]{2,1,0:T(8,128)(2,1)S(1)} %collective-permute-done.2.refs_2_) | copy-start | bytes 4718596
  113.5 6.7 %collective-permute-start.7 = (bf16[4,192,1024]{2,1,0:T(8,128)(2,1)S(1)}, bf16[4,192,1024]{2,1,0:T(8,128)(2,1)S(1)}, u32[]{:S(2)}, u32[]{:S(2)}) collective-permute-start(bf16[4,192,1024]{2,1,0:T(8,128)(2,1)S(1)} %collective-permute-done.2.refs_2_), channel_id=1, source_target_pairs={{0,1},{1,0},{2,3},{3,2},{4,5},{5,4},{6,7},{7,6},{8,9},{9,8},{10,11... | collective-permute-start | bytes 4718600 | tf_op jit(solution)/shard_map/ppermute | solution.py:149
  113.5 7.9 %collective-permute-start.8 = (bf16[4,192,1024]{2,1,0:T(8,128)(2,1)}, bf16[4,192,1024]{2,1,0:T(8,128)(2,1)}, u32[]{:S(2)}, u32[]{:S(2)}) collective-permute-start(bf16[4,192,1024]{2,1,0:T(8,128)(2,1)} %collective-permute-done.3.refs_3_), channel_id=1, source_target_pairs={{0,1},{1,0},{2,3},{3,2},{4,5},{5,4},{6,7},{7,6},{8,9},{9,8},{10,11... | collective-permute-start | bytes 4718600 | tf_op jit(solution)/shard_map/ppermute | solution.py:149
  114.0 30.7 %all-to-all-start.2 = ((bf16[4,128,1024]{2,1,0:T(8,128)(2,1)}), bf16[4,128,1024]{2,1,0:T(8,128)(2,1)}, u32[]{:S(2)}, u32[]{:S(2)}) async-start(bf16[4,128,1024]{2,1,0:T(8,128)(2,1)} %bitcast.41), calls=%async_computation.2 | async-start | bytes 2097152 | tf_op jit(solution)/shard_map/all_to_all | solution.py:157
  118.5 42.8 %collective-permute-start.10 = (bf16[8,160,1024]{2,1,0:T(8,128)(2,1)}, bf16[8,160,1024]{2,1,0:T(8,128)(2,1)}, u32[]{:S(2)}, u32[]{:S(2)}) collective-permute-start(bf16[8,160,1024]{2,1,0:T(8,128)(2,1)} %bitcast.10.refs_0_), channel_id=1, source_target_pairs={{0,1},{1,0},{2,3},{3,2},{4,5},{5,4},{6,7},{7,6},{8,9},{9,8},{10,11... | collective-permute-start | bytes 7864328 | tf_op jit(solution)/shard_map/ppermute | solution.py:149
  118.6 42.7 %collective-permute-start.6 = (bf16[8,160,1024]{2,1,0:T(8,128)(2,1)}, bf16[8,160,1024]{2,1,0:T(8,128)(2,1)}, u32[]{:S(2)}, u32[]{:S(2)}) collective-permute-start(bf16[8,160,1024]{2,1,0:T(8,128)(2,1)} %bitcast.10.refs_0_), channel_id=1, source_target_pairs={{0,2},{1,5},{2,0},{3,7},{4,6},{5,1},{6,4},{7,3},{8,10},{9,13},{10,... | collective-permute-start | bytes 7864328 | tf_op jit(solution)/shard_map/ppermute | solution.py:149
  120.2 1.2 copy-start.2
  144.6 16.7 %collective-permute-start.9 = (bf16[4,128,1024]{2,1,0:T(8,128)(2,1)}, bf16[4,128,1024]{2,1,0:T(8,128)(2,1)}, u32[]{:S(2)}, u32[]{:S(2)}) collective-permute-start(bf16[4,128,1024]{2,1,0:T(8,128)(2,1)} %all-to-all-done.2.refs_0_), channel_id=1, source_target_pairs={{0,4},{1,3},{2,6},{3,1},{4,0},{5,7},{6,2},{7,5},{8,12},{9,11},{10,... | collective-permute-start | bytes 3145736 | tf_op jit(solution)/shard_map/ppermute | solution.py:149
  161.3 5.3 %collective-permute-start.15 = (bf16[8,160,1024]{2,1,0:T(8,128)(2,1)}, bf16[8,160,1024]{2,1,0:T(8,128)(2,1)}, u32[]{:S(2)}, u32[]{:S(2)}) collective-permute-start(bf16[8,160,1024]{2,1,0:T(8,128)(2,1)} %collective-permute-done.6.refs_1_), channel_id=1, source_target_pairs={{0,1},{1,0},{2,3},{3,2},{4,5},{5,4},{6,7},{7,6},{8,9},{9,8},{10,11... | collective-permute-start | bytes 7864328 | tf_op jit(solution)/shard_map/ppermute | solution.py:149
  161.7 30.2 %collective-permute-start.11 = (bf16[4,128,1024]{2,1,0:T(8,128)(2,1)}, bf16[4,128,1024]{2,1,0:T(8,128)(2,1)}, u32[]{:S(2)}, u32[]{:S(2)}) collective-permute-start(bf16[4,128,1024]{2,1,0:T(8,128)(2,1)} %all-to-all-done.2.refs_0_), channel_id=1, source_target_pairs={{0,2},{1,5},{2,0},{3,7},{4,6},{5,1},{6,4},{7,3},{8,10},{9,13},{10,... | collective-permute-start | bytes 3145736 | tf_op jit(solution)/shard_map/ppermute | solution.py:149
  163.2 28.7 %collective-permute-start.12 = (bf16[4,128,1024]{2,1,0:T(8,128)(2,1)}, bf16[4,128,1024]{2,1,0:T(8,128)(2,1)}, u32[]{:S(2)}, u32[]{:S(2)}) collective-permute-start(bf16[4,128,1024]{2,1,0:T(8,128)(2,1)} %collective-permute-done.9.refs_1_), channel_id=1, source_target_pairs={{0,2},{1,5},{2,0},{3,7},{4,6},{5,1},{6,4},{7,3},{8,10},{9,13},{10,... | collective-permute-start | bytes 3145736 | tf_op jit(solution)/shard_map/ppermute | solution.py:149
  163.7 28.2 %collective-permute-start.13 = (bf16[4,128,1024]{2,1,0:T(8,128)(2,1)}, bf16[4,128,1024]{2,1,0:T(8,128)(2,1)}, u32[]{:S(2)}, u32[]{:S(2)}) collective-permute-start(bf16[4,128,1024]{2,1,0:T(8,128)(2,1)} %all-to-all-done.2.refs_0_), channel_id=1, source_target_pairs={{0,1},{1,0},{2,3},{3,2},{4,5},{5,4},{6,7},{7,6},{8,9},{9,8},{10,11... | collective-permute-start | bytes 3145736 | tf_op jit(solution)/shard_map/ppermute | solution.py:149
  163.7 28.2 %collective-permute-start.14 = (bf16[4,128,1024]{2,1,0:T(8,128)(2,1)}, bf16[4,128,1024]{2,1,0:T(8,128)(2,1)}, u32[]{:S(2)}, u32[]{:S(2)}) collective-permute-start(bf16[4,128,1024]{2,1,0:T(8,128)(2,1)} %collective-permute-done.9.refs_1_), channel_id=1, source_target_pairs={{0,1},{1,0},{2,3},{3,2},{4,5},{5,4},{6,7},{7,6},{8,9},{9,8},{10,11... | collective-permute-start | bytes 3145736 | tf_op jit(solution)/shard_map/ppermute | solution.py:149
  191.9 3.1 collective-permute-start.16
  192.3 4.1 collective-permute-start.17
  196.5 19.8 %collective-permute-start.18 = (bf16[4096,512]{1,0:T(8,128)(2,1)}, bf16[4096,512]{1,0:T(8,128)(2,1)}, u32[]{:S(2)}, u32[]{:S(2)}) collective-permute-start(bf16[4096,512]{1,0:T(8,128)(2,1)} %get-tuple-element.274.refs_0_), channel_id=1, source_target_pairs={{0,1},{1,0},{2,3},{3,2},{4,5},{5,4},{6,7},{7,6},{8,9},{9,8},{10,11... | collective-permute-start | bytes 12582920 | tf_op jit(solution)/shard_map/ppermute | solution.py:149
  213.2 3.1 collective-permute-start.19
  226.4 26.4 %collective-permute-start.20 = (bf16[8,128,1024]{2,1,0:T(8,128)(2,1)}, bf16[8,128,1024]{2,1,0:T(8,128)(2,1)}, u32[]{:S(2)}, u32[]{:S(2)}) collective-permute-start(bf16[8,128,1024]{2,1,0:T(8,128)(2,1)} %get-tuple-element.277), channel_id=1, source_target_pairs={{0,2},{1,5},{2,0},{3,7},{4,6},{5,1},{6,4},{7,3},{8,10},{9,13},{10,... | collective-permute-start | bytes 6291464 | tf_op jit(solution)/shard_map/ppermute | solution.py:149
  227.9 21.4 %collective-permute-start.21 = (bf16[1024,512]{1,0:T(8,128)(2,1)}, bf16[1024,512]{1,0:T(8,128)(2,1)}, u32[]{:S(2)}, u32[]{:S(2)}) collective-permute-start(bf16[1024,512]{1,0:T(8,128)(2,1)} %get-tuple-element.291.refs_0_), channel_id=1, source_target_pairs={{0,1},{1,0},{2,3},{3,2},{4,5},{5,4},{6,7},{7,6},{8,9},{9,8},{10,11... | collective-permute-start | bytes 3145736 | tf_op jit(solution)/shard_map/ppermute | solution.py:149
  248.3 3.1 collective-permute-start.22
  248.8 7.8 %collective-permute-start.24 = (bf16[512,1024]{1,0:T(8,128)(2,1)}, bf16[512,1024]{1,0:T(8,128)(2,1)}, u32[]{:S(2)}, u32[]{:S(2)}) collective-permute-start(bf16[512,1024]{1,0:T(8,128)(2,1)} %get-tuple-element.295.refs_4_), channel_id=1, source_target_pairs={{0,1},{1,0},{2,3},{3,2},{4,5},{5,4},{6,7},{7,6},{8,9},{9,8},{10,11... | collective-permute-start | bytes 3145736 | tf_op jit(solution)/shard_map/ppermute | solution.py:149
  248.9 9.3 %collective-permute-start.25 = (bf16[512,1024]{1,0:T(8,128)(2,1)}, bf16[512,1024]{1,0:T(8,128)(2,1)}, u32[]{:S(2)}, u32[]{:S(2)}) collective-permute-start(bf16[512,1024]{1,0:T(8,128)(2,1)} %get-tuple-element.296.refs_6_), channel_id=1, source_target_pairs={{0,1},{1,0},{2,3},{3,2},{4,5},{5,4},{6,7},{7,6},{8,9},{9,8},{10,11... | collective-permute-start | bytes 3145736 | tf_op jit(solution)/shard_map/ppermute | solution.py:149
  249.3 19.1 %collective-permute-start.28 = (bf16[1024,512]{1,0:T(8,128)(2,1)}, bf16[1024,512]{1,0:T(8,128)(2,1)}, u32[]{:S(2)}, u32[]{:S(2)}) collective-permute-start(bf16[1024,512]{1,0:T(8,128)(2,1)} %get-tuple-element.325.refs_2_), channel_id=1, source_target_pairs={{0,1},{1,0},{2,3},{3,2},{4,5},{5,4},{6,7},{7,6},{8,9},{9,8},{10,11... | collective-permute-start | bytes 3145736 | tf_op jit(solution)/shard_map/ppermute | solution.py:149
  251.4 6.9 %collective-permute-start.26 = (bf16[512,1024]{1,0:T(8,128)(2,1)}, bf16[512,1024]{1,0:T(8,128)(2,1)}, u32[]{:S(2)}, u32[]{:S(2)}) collective-permute-start(bf16[512,1024]{1,0:T(8,128)(2,1)} %get-tuple-element.297.refs_8_), channel_id=1, source_target_pairs={{0,1},{1,0},{2,3},{3,2},{4,5},{5,4},{6,7},{7,6},{8,9},{9,8},{10,11... | collective-permute-start | bytes 3145736 | tf_op jit(solution)/shard_map/ppermute | solution.py:149
  256.6 11.8 %collective-permute-start.27 = (bf16[1024,512]{1,0:T(8,128)(2,1)}, bf16[1024,512]{1,0:T(8,128)(2,1)}, u32[]{:S(2)}, u32[]{:S(2)}) collective-permute-start(bf16[1024,512]{1,0:T(8,128)(2,1)} %get-tuple-element.323.refs_0_), channel_id=1, source_target_pairs={{0,1},{1,0},{2,3},{3,2},{4,5},{5,4},{6,7},{7,6},{8,9},{9,8},{10,11... | collective-permute-start | bytes 3145736 | tf_op jit(solution)/shard_map/ppermute | solution.py:149
  256.6 15.2 %collective-permute-start.23 = (bf16[4,128,1024]{2,1,0:T(8,128)(2,1)}, bf16[4,128,1024]{2,1,0:T(8,128)(2,1)}, u32[]{:S(2)}, u32[]{:S(2)}) collective-permute-start(bf16[4,128,1024]{2,1,0:T(8,128)(2,1)} %get-tuple-element.288), channel_id=1, source_target_pairs={{0,4},{1,3},{2,6},{3,1},{4,0},{5,7},{6,2},{7,5},{8,12},{9,11},{10,... | collective-permute-start | bytes 3145736 | tf_op jit(solution)/shard_map/ppermute | solution.py:149
  258.2 13.6 %collective-permute-start.29 = (bf16[512,1024]{1,0:T(8,128)(2,1)}, bf16[512,1024]{1,0:T(8,128)(2,1)}, u32[]{:S(2)}, u32[]{:S(2)}) collective-permute-start(bf16[512,1024]{1,0:T(8,128)(2,1)} %get-tuple-element.327.d_out_ref.refs_4_), channel_id=1, source_target_pairs={{0,1},{1,0},{2,3},{3,2},{4,5},{5,4},{6,7},{7,6},{8,9},{9,8},{10,11... | collective-permute-start | bytes 3145736 | tf_op jit(solution)/shard_map/ppermute | solution.py:149
  274.3 33.9 %collective-permute-start.30 = (bf16[8,128,1024]{2,1,0:T(8,128)(2,1)}, bf16[8,128,1024]{2,1,0:T(8,128)(2,1)}, u32[]{:S(2)}, u32[]{:S(2)}) collective-permute-start(bf16[8,128,1024]{2,1,0:T(8,128)(2,1)} %get-tuple-element.307), channel_id=1, source_target_pairs={{0,2},{1,5},{2,0},{3,7},{4,6},{5,1},{6,4},{7,3},{8,10},{9,13},{10,... | collective-permute-start | bytes 6291464 | tf_op jit(solution)/shard_map/ppermute | solution.py:149
  275.8 32.4 %all-to-all-start.3 = ((bf16[4,128,1024]{2,1,0:T(8,128)(2,1)}), bf16[4,128,1024]{2,1,0:T(8,128)(2,1)}, u32[]{:S(2)}, u32[]{:S(2)}) async-start(bf16[4,128,1024]{2,1,0:T(8,128)(2,1)} %fold.9), calls=%async_computation.3 | async-start | bytes 2097152 | tf_op jit(solution)/shard_map/all_to_all | solution.py:157
  297.9 10.3 %collective-permute-start.31 = (bf16[512,1024]{1,0:T(8,128)(2,1)}, bf16[512,1024]{1,0:T(8,128)(2,1)}, u32[]{:S(2)}, u32[]{:S(2)}) collective-permute-start(bf16[512,1024]{1,0:T(8,128)(2,1)} %get-tuple-element.329.refs_0_.refs_6_), channel_id=1, source_target_pairs={{0,1},{1,0},{2,3},{3,2},{4,5},{5,4},{6,7},{7,6},{8,9},{9,8},{10,11... | collective-permute-start | bytes 3145736 | tf_op jit(solution)/shard_map/ppermute | solution.py:149
  297.9 10.3 %collective-permute-start.32 = (bf16[512,1024]{1,0:T(8,128)(2,1)}, bf16[512,1024]{1,0:T(8,128)(2,1)}, u32[]{:S(2)}, u32[]{:S(2)}) collective-permute-start(bf16[512,1024]{1,0:T(8,128)(2,1)} %get-tuple-element.331.refs_1_.refs_8_), channel_id=1, source_target_pairs={{0,1},{1,0},{2,3},{3,2},{4,5},{5,4},{6,7},{7,6},{8,9},{9,8},{10,11... | collective-permute-start | bytes 3145736 | tf_op jit(solution)/shard_map/ppermute | solution.py:149
  298.4 9.8 %collective-permute-start.33 = (bf16[512,1024]{1,0:T(8,128)(2,1)}, bf16[512,1024]{1,0:T(8,128)(2,1)}, u32[]{:S(2)}, u32[]{:S(2)}) collective-permute-start(bf16[512,1024]{1,0:T(8,128)(2,1)} %get-tuple-element.333.refs_2_.refs_10_), channel_id=1, source_target_pairs={{0,1},{1,0},{2,3},{3,2},{4,5},{5,4},{6,7},{7,6},{8,9},{9,8},{10,11... | collective-permute-start | bytes 3145736 | tf_op jit(solution)/shard_map/ppermute | solution.py:149
  311.7 15.6 %collective-permute-start.35 = (bf16[2048,512]{1,0:T(8,128)(2,1)}, bf16[2048,512]{1,0:T(8,128)(2,1)}, u32[]{:S(2)}, u32[]{:S(2)}) collective-permute-start(bf16[2048,512]{1,0:T(8,128)(2,1)} %get-tuple-element.358.refs_0_), channel_id=1, source_target_pairs={{0,1},{1,0},{2,3},{3,2},{4,5},{5,4},{6,7},{7,6},{8,9},{9,8},{10,11... | collective-permute-start | bytes 6291464 | tf_op jit(solution)/shard_map/ppermute | solution.py:149
  312.1 11.9 %collective-permute-start.36 = (bf16[512,1024]{1,0:T(8,128)(2,1)}, bf16[512,1024]{1,0:T(8,128)(2,1)}, u32[]{:S(2)}, u32[]{:S(2)}) collective-permute-start(bf16[512,1024]{1,0:T(8,128)(2,1)} %get-tuple-element.360.d_ref.refs_2_), channel_id=1, source_target_pairs={{0,1},{1,0},{2,3},{3,2},{4,5},{5,4},{6,7},{7,6},{8,9},{9,8},{10,11... | collective-permute-start | bytes 3145736 | tf_op jit(solution)/shard_map/ppermute | solution.py:149
  312.2 15.1 %collective-permute-start.34 = (bf16[4,128,1024]{2,1,0:T(8,128)(2,1)}, bf16[4,128,1024]{2,1,0:T(8,128)(2,1)}, u32[]{:S(2)}, u32[]{:S(2)}) collective-permute-start(bf16[4,128,1024]{2,1,0:T(8,128)(2,1)} %get-tuple-element.320), channel_id=1, source_target_pairs={{0,4},{1,3},{2,6},{3,1},{4,0},{5,7},{6,2},{7,5},{8,12},{9,11},{10,... | collective-permute-start | bytes 3145736 | tf_op jit(solution)/shard_map/ppermute | solution.py:149
  329.8 26.4 %collective-permute-start.37 = (bf16[8,128,1024]{2,1,0:T(8,128)(2,1)}, bf16[8,128,1024]{2,1,0:T(8,128)(2,1)}, u32[]{:S(2)}, u32[]{:S(2)}) collective-permute-start(bf16[8,128,1024]{2,1,0:T(8,128)(2,1)} %get-tuple-element.343), channel_id=1, source_target_pairs={{0,2},{1,5},{2,0},{3,7},{4,6},{5,1},{6,4},{7,3},{8,10},{9,13},{10,... | collective-permute-start | bytes 6291464 | tf_op jit(solution)/shard_map/ppermute | solution.py:149
  340.0 5.4 %collective-permute-start.38 = (bf16[16,32,1024]{2,1,0:T(8,128)(2,1)}, bf16[16,32,1024]{2,1,0:T(8,128)(2,1)}, u32[]{:S(2)}, u32[]{:S(2)}) collective-permute-start(bf16[16,32,1024]{2,1,0:T(8,128)(2,1)} %grads.8), channel_id=1, source_target_pairs={{0,1},{1,0},{2,3},{3,2},{4,5},{5,4},{6,7},{7,6},{8,9},{9,8},{10,11... | collective-permute-start | bytes 3145736 | tf_op jit(solution)/shard_map/ppermute | solution.py:149
  340.4 31.3 %all-to-all-start.4 = ((bf16[4,128,1024]{2,1,0:T(8,128)(2,1)}), bf16[4,128,1024]{2,1,0:T(8,128)(2,1)}, u32[]{:S(2)}, u32[]{:S(2)}) async-start(bf16[4,128,1024]{2,1,0:T(8,128)(2,1)} %fold.11), calls=%async_computation.4 | async-start | bytes 2097152 | tf_op jit(solution)/shard_map/all_to_all | solution.py:157
  359.5 26.4 %collective-permute-start.40 = (bf16[4,128,1024]{2,1,0:T(8,128)(2,1)}, bf16[4,128,1024]{2,1,0:T(8,128)(2,1)}, u32[]{:S(2)}, u32[]{:S(2)}) collective-permute-start(bf16[4,128,1024]{2,1,0:T(8,128)(2,1)} %get-tuple-element.370), channel_id=1, source_target_pairs={{0,4},{1,3},{2,6},{3,1},{4,0},{5,7},{6,2},{7,5},{8,12},{9,11},{10,... | collective-permute-start | bytes 3145736 | tf_op jit(solution)/shard_map/ppermute | solution.py:149
  361.0 32.4 %collective-permute-start.39 = (bf16[8,96,1024]{2,1,0:T(8,128)(2,1)}, bf16[8,96,1024]{2,1,0:T(8,128)(2,1)}, u32[]{:S(2)}, u32[]{:S(2)}) collective-permute-start(bf16[8,96,1024]{2,1,0:T(8,128)(2,1)} %get-tuple-element.369), channel_id=1, source_target_pairs={{0,2},{1,5},{2,0},{3,7},{4,6},{5,1},{6,4},{7,3},{8,10},{9,13},{10,... | collective-permute-start | bytes 4718600 | tf_op jit(solution)/shard_map/ppermute | solution.py:149
  388.4 25.1 %all-to-all-start.5 = ((bf16[4,128,1024]{2,1,0:T(8,128)(2,1)}), bf16[4,128,1024]{2,1,0:T(8,128)(2,1)}, u32[]{:S(2)}, u32[]{:S(2)}) async-start(bf16[4,128,1024]{2,1,0:T(8,128)(2,1)} %fold.13), calls=%async_computation.5 | async-start | bytes 2097152 | tf_op jit(solution)/shard_map/all_to_all | solution.py:157
  396.4 12.3 %collective-permute-start.41 = (bf16[4,96,1024]{2,1,0:T(8,128)(2,1)}, bf16[4,96,1024]{2,1,0:T(8,128)(2,1)}, u32[]{:S(2)}, u32[]{:S(2)}) collective-permute-start(bf16[4,96,1024]{2,1,0:T(8,128)(2,1)} %get-tuple-element.374), channel_id=1, source_target_pairs={{0,4},{1,3},{2,6},{3,1},{4,0},{5,7},{6,2},{7,5},{8,12},{9,11},{10,... | collective-permute-start | bytes 2359304 | tf_op jit(solution)/shard_map/ppermute | solution.py:149
  415.7 19.9 %all-to-all-start.6 = ((bf16[4,96,1024]{2,1,0:T(8,128)(2,1)}), bf16[4,96,1024]{2,1,0:T(8,128)(2,1)S(1)}, u32[]{:S(2)}, u32[]{:S(2)}) async-start(bf16[4,96,1024]{2,1,0:T(8,128)(2,1)} %fold.15), calls=%async_computation.6 | async-start | bytes 1572864 | tf_op jit(solution)/shard_map/all_to_all | solution.py:157
  421.3 5.2 %copy-start.3 = (f32[128,1024]{1,0:T(8,128)}, f32[128,1024]{1,0:T(8,128)S(1)}, u32[]{:S(2)}) copy-start(f32[128,1024]{1,0:T(8,128)S(1)} %convert_reduce_fusion.refs_3_) | copy-start | bytes 1572868
  423.5 0.8 copy-start.4
  424.3 28.4 %copy-start.11 = (f32[16]{0:T(128)S(1)}, f32[16]{0:T(128)}, u32[]{:S(2)}) copy-start(f32[16]{0:T(128)} %select_reduce_fusion) | copy-start | bytes 196
  426.5 0.8 copy-start.5
  435.7 0.8 copy-start.6
